TPU v7x, 512 devices: a whole 4x4x16 slice. The times are simulated.
512 devices in a mesh: dp: 128 (over y_lo, z, x), mp: 4 (over y_hi, core).
Axes of the slice: x: 4, y: 4 (y_hi: 2, y_lo: 2; y = y_hi * 2 + y_lo), z: 16, core: 2. Of those that a mesh axis runs over, the one named last changes fastest.
Arguments:
- vision_encoder_output: bfloat16 [16384, 6144], P('dp', 'mp'), may hold values from -6 to 6
- sentence_encoder_output: bfloat16 [16384, 6144], P('dp', 'mp'), may hold values from -6 to 6
- vision_mapping_matrix: bfloat16 [6144, 512], P('mp'), may hold values from -0.078125 to 0.078125
- sentence_mapping_matrix: bfloat16 [6144, 512], P('mp'), may hold values from -0.078125 to 0.078125
- similarity_sharpness: float32 [1], replicated, may hold values from 20 to 60
- score_offset: float32 [1], replicated, may hold values from -4 to -1
Outputs:
- image_grad: bfloat16 [16384, 6144], P('dp', 'mp')
- text_grad: bfloat16 [16384, 6144], P('dp', 'mp')
All inputs are finite; a program needn't handle non-finite values.
Results may differ from a plain program's by a relative error of at most 0.033.
Values may be sent and summed in bfloat16 or wider, within the bound.
No kernel may reach another device: no remote copies, remote signals or barrier semaphores. Data moves between devices by JAX's collectives and lax.ppermute only.
A program may use at most 64 MiB of HBM per device.

v0:
```python
import jax
import jax.numpy as jnp
from jax import lax
from jax.sharding import PartitionSpec as P

EPS = 1e-06


def shifted(x, axis, by):
    peers = lax.axis_size(axis)
    return lax.ppermute(x, axis, [(i, (i + by) % peers) for i in range(peers)])


def normalize(embed):
    inv = lax.rsqrt(jnp.sum(embed * embed, axis=1, keepdims=True) + EPS)
    return (inv, embed * inv)


def backward(grad, inv, unit):
    along = jnp.sum(grad * unit, axis=1, keepdims=True)
    return (inv * (grad - along * unit)).astype(jnp.bfloat16)


def shards(
    vision_encoder_output,
    sentence_encoder_output,
    vision_mapping_matrix,
    sentence_mapping_matrix,
    similarity_sharpness,
    score_offset,
):
    rows = vision_encoder_output.shape[0]
    width = vision_mapping_matrix.shape[1]
    groups = lax.axis_size("mp")
    quarter = rows // groups
    member = lax.axis_index("mp")
    score_multiplier = similarity_sharpness[0]
    shift = score_offset[0]
    embedded = lax.psum_scatter(
        jnp.concatenate(
            [
                jnp.dot(
                    vision_encoder_output, vision_mapping_matrix, preferred_element_type=jnp.float32
                ),
                jnp.dot(
                    sentence_encoder_output,
                    sentence_mapping_matrix,
                    preferred_element_type=jnp.float32,
                ),
            ],
            axis=1,
        ),
        "mp",
        scatter_dimension=0,
        tiled=True,
    )
    img_quarter = embedded[:, :width]
    inv_txt, unit_txt = normalize(embedded[:, width:])
    txt_b = unit_txt.astype(jnp.bfloat16)
    inv_img, picture_unit_rows = normalize(img_quarter)
    img_b = lax.all_gather(picture_unit_rows.astype(jnp.bfloat16), "mp", axis=0, tiled=True)

    def tile_signed(block, sign):
        logits = (
            score_multiplier
            * lax.dot_general(
                img_b, block, (((1,), (1,)), ((), ())), preferred_element_type=jnp.float32
            )
            + shift
        )
        coef = (score_multiplier * -sign * jax.nn.sigmoid(-sign * logits)).astype(jnp.bfloat16)
        grad_rows = jnp.dot(coef, block, preferred_element_type=jnp.float32)
        grad_block = lax.dot_general(
            coef, img_b, (((0,), (0,)), ((), ())), preferred_element_type=jnp.float32
        )
        return (grad_rows, grad_block)

    def tile(block, own):
        if own:
            row_ids = jnp.arange(rows, dtype=jnp.int32)[:, None]
            column_indices = member * quarter + jnp.arange(block.shape[0], dtype=jnp.int32)[None, :]
            sign = jnp.where(row_ids == column_indices, jnp.float32(1.0), jnp.float32(-1.0))
        else:
            sign = jnp.float32(-1.0)
        return tile_signed(block, sign)

    cycle_len = lax.axis_size("dp")
    steps = cycle_len - 1
    grad_img, acc_own = tile(txt_b, True)

    def advance(index, carry):
        block, acc, total = carry
        block, acc = (
            shifted(block.astype(jnp.float32), "dp", 1).astype(block.dtype),
            shifted(acc, "dp", 1),
        )
        grad_rows, grad_block = tile(block, False)
        return (block, acc + grad_block, total + grad_rows)

    block, acc, grad_img = lax.fori_loop(0, steps, advance, (txt_b, acc_own, grad_img))
    caption_gradient = shifted(acc.astype(jnp.bfloat16), "dp", 1).astype(acc.dtype)
    delta_txt_part = backward(caption_gradient, inv_txt, unit_txt)
    grad_img_part = lax.psum_scatter(
        grad_img.astype(jnp.bfloat16), "mp", scatter_dimension=0, tiled=True
    ).astype(jnp.float32)
    delta_img_part = backward(grad_img_part, inv_img, picture_unit_rows)
    delta_img, delta_txt = (
        lax.all_gather(delta_img_part, "mp", axis=0, tiled=True),
        lax.all_gather(delta_txt_part, "mp", axis=0, tiled=True),
    )
    image_grad = lax.dot_general(
        delta_img,
        vision_mapping_matrix,
        (((1,), (1,)), ((), ())),
        preferred_element_type=jnp.float32,
    ).astype(jnp.bfloat16)
    text_grad = lax.dot_general(
        delta_txt,
        sentence_mapping_matrix,
        (((1,), (1,)), ((), ())),
        preferred_element_type=jnp.float32,
    ).astype(jnp.bfloat16)
    return (image_grad, text_grad)


def solution(mesh):
    in_specs = (P("dp", "mp"), P("dp", "mp"), P("mp", None), P("mp", None), P(), P())
    out_specs = (P("dp", "mp"), P("dp", "mp"))
    return jax.shard_map(shards, mesh=mesh, in_specs=in_specs, out_specs=out_specs, check_vma=False)
```

profile of v0, /device:TPU:1, one launch (start us, length us, event | category | flops | bytes accessed | tf_op | source)
XLA Modules:
  0.0 1712.1 jit_solution(16681082215139689566)
XLA Ops:
  11.9 48.5 %reduce-scatter.3.cloned.1.call-done = f32[32,1024]{1,0:T(8,128)} async-done(((f32[128,1024]{1,0:T(8,128)}), f32[32,1024]{1,0:T(8,128)}) %reduce-scatter.3.cloned.1.call-update) | async-done | bytes 131088 | tf_op jit(solution)/shard_map/reduce_scatter | solution.py:39
  62.4 7.4 all_gather.9
  70.3 1442.0 %while.14 = (s32[]{:T(128)}, bf16[32,512]{1,0:T(8,128)(2,1)S(1)}, f32[32,512]{1,0:T(8,128)S(1)}, f32[128,512]{1,0:T(8,128)S(1)}, f32[]{:T(128)}, /*index=5*/bf16[128,512]{1,0:T(8,128)(2,1)S(1)}, f32[]{:T(128)}, s32[]{:T(128)}) while((s32[]{:T(128)}, bf16[32,512]{1,0:T(8,128)(2,1)S(1)}, f32[32,512]{1,0:T(8,128)S(1)}, f32[128,512]{1,0:T(8,128)S(1)}, ...), condition=%wide.region_4.5_spmd, body=%wide.region_3.4_spmd.sunk | while | flops 12693506 | bytes 1466541 | solution.py:100
  86.8 5.0 collective-permute-done
  98.5 5.0 collective-permute-done
  132.3 5.0 collective-permute-done
  143.6 5.0 collective-permute-done
  154.9 5.0 collective-permute-done
  177.5 5.3 collective-permute-done
  188.8 5.0 collective-permute-done
  211.6 5.0 collective-permute-done
  245.8 5.0 collective-permute-done
  257.1 5.0 collective-permute-done
  268.4 5.0 collective-permute-done
  302.2 5.4 collective-permute-done
  313.5 5.0 collective-permute-done
  325.1 5.0 collective-permute-done
  336.4 5.0 collective-permute-done
  359.3 5.0 collective-permute-done
  370.6 5.0 collective-permute-done
  381.9 5.0 collective-permute-done
  415.7 5.0 collective-permute-done
  427.0 5.4 collective-permute-done
  438.3 5.0 collective-permute-done
  449.9 5.0 collective-permute-done
  461.1 5.0 collective-permute-done
  484.1 5.0 collective-permute-done
  495.4 5.0 collective-permute-done
  506.6 5.0 collective-permute-done
  529.2 5.0 collective-permute-done
  540.5 5.0 collective-permute-done
  551.8 5.4 collective-permute-done
  574.6 5.0 collective-permute-done
  585.9 5.0 collective-permute-done
  597.6 5.0 collective-permute-done
  608.8 5.0 collective-permute-done
  620.1 5.0 collective-permute-done
  654.0 5.0 collective-permute-done
  665.3 5.0 collective-permute-done
  676.6 5.4 collective-permute-done
  699.4 5.0 collective-permute-done
  722.3 5.0 collective-permute-done
  733.6 5.0 collective-permute-done
  767.5 5.0 collective-permute-done
  778.8 5.0 collective-permute-done
  790.1 5.0 collective-permute-done
  801.3 5.4 collective-permute-done
  847.1 5.0 collective-permute-done
  881.0 5.0 collective-permute-done
  892.3 5.0 collective-permute-done
  903.5 5.0 collective-permute-done
  926.1 5.4 collective-permute-done
  937.4 5.0 collective-permute-done
  960.2 5.0 collective-permute-done
  971.9 5.0 collective-permute-done
  994.5 5.0 collective-permute-done
  1050.9 5.4 collective-permute-done
  1175.7 5.4 collective-permute-done
  1300.4 5.4 collective-permute-done
  1425.2 5.4 collective-permute-done
  1515.1 6.9 collective-permute-done.2
  1522.0 163.8 %reduce-scatter.5.cloned.1.call-done = bf16[32,512]{1,0:T(8,128)(2,1)} async-done(((bf16[128,512]{1,0:T(8,128)(2,1)}), bf16[32,512]{1,0:T(8,128)(2,1)}) %reduce-scatter.5.cloned.1.call-update) | async-done | bytes 32784 | tf_op jit(solution)/shard_map/reduce_scatter | solution.py:103
  1687.6 7.9 all_gather.11
  1696.9 6.9 all_gather.10
  (988 shorter events, 1159.9 us)
Async XLA Ops:
  7.2 53.2 %reduce-scatter.3.cloned.1.call-start = ((), (), s32[]{:S(2)}) async-start(), calls=%async_computation.2 | async-start | bytes 655360 | tf_op jit(solution)/shard_map/reduce_scatter | solution.py:39
  10.5 1675.3 %reduce-scatter.5.cloned.1.call-start = ((), (), s32[]{:S(2)}) async-start(), calls=%async_computation.3 | async-start | bytes 163840 | tf_op jit(solution)/shard_map/reduce_scatter | solution.py:103
  70.3 9.3 collective-permute-start
  84.8 9.6 collective-permute-start.1
  130.4 9.2 collective-permute-start.1
  175.5 9.2 collective-permute-start.1
  186.8 9.5 collective-permute-start.1
  209.7 9.6 collective-permute-start.1
  243.9 9.2 collective-permute-start.1
  255.2 9.2 collective-permute-start.1
  298.4 9.2 collective-permute-start
  300.3 9.2 collective-permute-start.1
  311.6 9.5 collective-permute-start.1
  323.2 9.2 collective-permute-start.1
  334.4 9.6 collective-permute-start.1
  357.4 9.2 collective-permute-start.1
  368.7 9.2 collective-permute-start.1
  413.8 9.2 collective-permute-start.1
  423.2 9.2 collective-permute-start
  425.1 9.2 collective-permute-start.1
  436.4 9.5 collective-permute-start.1
  447.9 9.2 collective-permute-start.1
  459.2 9.6 collective-permute-start.1
  470.9 9.2 collective-permute-start.1
  482.1 9.2 collective-permute-start.1
  527.3 9.2 collective-permute-start.1
  538.6 9.2 collective-permute-start.1
  547.9 9.2 collective-permute-start
  561.1 9.5 collective-permute-start.1
  584.0 9.6 collective-permute-start.1
  595.6 9.2 collective-permute-start.1
  640.8 9.2 collective-permute-start.1
  652.1 9.2 collective-permute-start.1
  685.9 9.5 collective-permute-start.1
  708.8 9.6 collective-permute-start.1
  720.4 9.2 collective-permute-start.1
  765.6 9.2 collective-permute-start.1
  810.7 9.5 collective-permute-start.1
  833.5 9.6 collective-permute-start.1
  879.0 9.2 collective-permute-start.1
  890.3 9.2 collective-permute-start.1
  935.5 9.5 collective-permute-start.1
  958.3 9.6 collective-permute-start.1
  992.5 9.2 collective-permute-start.1
  1003.8 9.2 collective-permute-start.1
  1049.0 9.2 collective-permute-start.1
  1060.2 9.5 collective-permute-start.1
  1071.8 9.2 collective-permute-start.1
  1083.1 9.6 collective-permute-start.1
  1106.0 9.2 collective-permute-start.1
  1117.3 9.2 collective-permute-start.1
  1162.4 9.2 collective-permute-start.1
  1171.8 9.2 collective-permute-start
  1173.7 9.2 collective-permute-start.1
  1185.0 9.5 collective-permute-start.1
  1196.6 9.2 collective-permute-start.1
  1207.9 9.6 collective-permute-start.1
  1230.8 9.2 collective-permute-start.1
  1275.9 9.2 collective-permute-start.1
  1287.2 9.2 collective-permute-start.1
  1309.8 9.5 collective-permute-start.1
  1332.6 9.6 collective-permute-start.1
  1434.6 9.5 collective-permute-start.1
  1457.4 9.6 collective-permute-start.1
  (197 other events, 3550.7 us)
Sparse Core Ops, SparseCore 0:
  11.1 49.2 reduce-scatter.2
  1513.1 172.6 reduce-scatter.4
where the time goes:
time: 1730 us; the launch traced here: 1710 us
  waiting for transfers between devices  936 us (54%)
  starting transfers between devices  492 us (28%)
  matrix products  235 us (14%)
  blocking collectives  22.2 us (1%)
    ppermute x255, waiting for transfers between devices, shifted(): return lax.ppermute(x, axis, [(i, (i + by) % peers) for i in range(peers)])  724 us
    ppermute x255, starting transfers between devices, shifted(): return lax.ppermute(x, axis, [(i, (i + by) % peers) for i in range(peers)])  492 us
    dot_general x128, matrix products, tile_signed(): lax.dot_general(img_b, block, (((1,), (1,)), ((), ())), preferred_element...  185 us
    reduce_scatter x1, waiting for transfers between devices, shards(): lax.psum_scatter(grad_img.astype(jnp.bfloat16), 'mp', scatter_dimension=0...  164 us
    reduce_scatter x1, waiting for transfers between devices, shards(): lax.psum_scatter(jnp.concatenate([jnp.dot(vision_encoder_output, vision_m...  48.5 us
  transfers between devices with their start and end apart: 257, of which 257 were waited for; matrix products, arithmetic and copies ran while one was open for 12% of the time, Pallas kernels for 0%

commit v1 on v0

v1 whole, which is shorter than its diff:
```python
import jax
import jax.numpy as jnp
from jax import lax
from jax.sharding import Mesh
from jax.sharding import PartitionSpec as P

EPS = 1e-06
BF = jnp.bfloat16
F32 = jnp.float32
GROUP = ("yhi", "core")
LINE = "z"
PLANE = ("ylo", "x", "yhi", "core")


def normalize(embed):
    inv = lax.rsqrt(jnp.sum(embed * embed, axis=1, keepdims=True) + EPS)
    return (inv, embed * inv)


def backward(grad, inv, unit):
    along = jnp.sum(grad * unit, axis=1, keepdims=True)
    return (inv * (grad - along * unit)).astype(BF)


def exchange_sum(parts, axis):
    got = lax.all_to_all(parts.astype(BF), axis, 0, 0)
    return jnp.sum(got.astype(F32), axis=0)


def gather_rows(rows, axis):
    peers = lax.axis_size(axis)
    wide = jnp.broadcast_to(rows[None], (peers,) + rows.shape)
    return lax.all_to_all(wide, axis, 0, 0).reshape(peers * rows.shape[0], rows.shape[1])


def shards(vision, sentence, vision_map, sentence_map, sharpness, offset):
    rows = vision.shape[0]
    width = vision_map.shape[1]
    members = lax.axis_size(GROUP)
    quarter = rows // members
    t = sharpness[0]
    shift = offset[0]
    embed = jnp.concatenate(
        [
            jnp.dot(vision, vision_map, preferred_element_type=F32),
            jnp.dot(sentence, sentence_map, preferred_element_type=F32),
        ],
        axis=1,
    ).astype(BF)
    embed = exchange_sum(embed.reshape(members, quarter, 2 * width), GROUP)
    inv_img, unit_img = normalize(embed[:, :width])
    inv_txt, unit_txt = normalize(embed[:, width:])
    img_b = lax.all_gather(unit_img.astype(BF), LINE, axis=0, tiled=True)
    txt_b = gather_rows(unit_txt.astype(BF), PLANE)
    n_img, n_txt = img_b.shape[0], txt_b.shape[0]

    logits = t * lax.dot_general(img_b, txt_b, (((1,), (1,)), ((), ())), preferred_element_type=F32) + shift
    image_at = lax.broadcasted_iota(jnp.int32, (n_img, n_txt), 0) - lax.axis_index(LINE) * quarter
    text_at = lax.broadcasted_iota(jnp.int32, (n_img, n_txt), 1) - lax.axis_index(PLANE) * quarter
    own = (image_at == text_at) & (image_at >= 0) & (image_at < quarter)
    sign = jnp.where(own, F32(1.0), F32(-1.0))
    coef = (t * -sign * jax.nn.sigmoid(-sign * logits)).astype(BF)
    grad_img = jnp.dot(coef, txt_b, preferred_element_type=F32)
    grad_txt = lax.dot_general(coef, img_b, (((0,), (0,)), ((), ())), preferred_element_type=F32)

    grad_img = exchange_sum(grad_img.reshape(-1, quarter, width), LINE)
    grad_txt = exchange_sum(grad_txt.reshape(-1, quarter, width), PLANE)
    delta = jnp.concatenate(
        [backward(grad_img, inv_img, unit_img), backward(grad_txt, inv_txt, unit_txt)], axis=1
    )
    delta = lax.all_gather(delta, GROUP, axis=0, tiled=True)
    image_grad = lax.dot_general(
        delta[:, :width], vision_map, (((1,), (1,)), ((), ())), preferred_element_type=F32
    ).astype(BF)
    text_grad = lax.dot_general(
        delta[:, width:], sentence_map, (((1,), (1,)), ((), ())), preferred_element_type=F32
    ).astype(BF)
    return (image_grad, text_grad)


def solution(mesh):
    x, ylo = 4, 2
    z = mesh.shape["dp"] // (x * ylo)
    fine = Mesh(mesh.devices.reshape(ylo, z, x, 2, 2), ("ylo", "z", "x", "yhi", "core"))
    dp, mp = ("ylo", "z", "x"), ("yhi", "core")
    in_specs = (P(dp, mp), P(dp, mp), P(mp, None), P(mp, None), P(), P())
    out_specs = (P(dp, mp), P(dp, mp))
    return jax.shard_map(shards, mesh=fine, in_specs=in_specs, out_specs=out_specs, check_vma=False)
```

time: 1730 us -> 137 us (0.08); the launches traced: 1710 us -> 137 us
  waiting for transfers between devices: 936 us -> 36.8 us
  starting transfers between devices: 492 us -> 24.2 us
  matrix products: 235 us -> 11.7 us
  blocking collectives: 22.2 us -> 60.1 us
    ppermute x255 -> x0, waiting for transfers between devices: 724 us -> none  [shifted(): return lax.ppermute(x, axis, [(i, (i + by) % peers) for i in range(peers)])]
    ppermute x255 -> x0, starting transfers between devices: 492 us -> none  [shifted(): return lax.ppermute(x, axis, [(i, (i + by) % peers) for i in range(peers)])]
    dot_general x388 -> x7, matrix products: 235 us -> 11.7 us  [the longest x1 3.04 us: shards(): grad_img = jnp.dot(coef, txt_b, preferred_element_type=F32)]
    reduce_scatter x2 -> x0, waiting for transfers between devices: 212 us -> none  [the longest x1 164 us: shards(): lax.psum_scatter(grad_img.astype(jnp.bfloat16), 'mp', scatter_dimension=0...]
    all_to_all x0 -> x3, waiting for transfers between devices: none -> 36.8 us  [the longest x2 36.8 us: exchange_sum(): got = lax.all_to_all(parts.astype(BF), axis, 0, 0)]
    all_to_all x0 -> x3, starting transfers between devices: none -> 24.2 us  [the longest x2 19.6 us: exchange_sum(): got = lax.all_to_all(parts.astype(BF), axis, 0, 0)]
    all_gather x3 -> x2, blocking collectives: 22.2 us -> 44.3 us  [the longest x1 29.9 us: shards(): img_b = lax.all_gather(unit_img.astype(BF), LINE, axis=0, tiled=True)]
  transfers between devices with their start and end apart: 257 -> 3, of which waited for: 257 -> 2; matrix products, arithmetic and copies ran while one was open for 12% -> 2% of each run, Pallas kernels for 0% -> 0%
where the time goes in v1:
time: 137 us
  blocking collectives  60.1 us (44%)
  waiting for transfers between devices  36.8 us (27%)
  starting transfers between devices  24.2 us (18%)
  matrix products  11.7 us (9%)
  between operations  2.12 us (2%)
    all_to_all x2, waiting for transfers between devices, exchange_sum(): got = lax.all_to_all(parts.astype(BF), axis, 0, 0)  36.8 us
    all_gather x1, blocking collectives, shards(): img_b = lax.all_gather(unit_img.astype(BF), LINE, axis=0, tiled=True)  29.9 us
    all_to_all x2, starting transfers between devices, exchange_sum(): got = lax.all_to_all(parts.astype(BF), axis, 0, 0)  19.6 us
    all_to_all x1, blocking collectives, exchange_sum(): got = lax.all_to_all(parts.astype(BF), axis, 0, 0)  15.8 us
    all_gather x1, blocking collectives, shards(): delta = lax.all_gather(delta, GROUP, axis=0, tiled=True)  14.4 us
    all_to_all x1, starting transfers between devices, gather_rows(): lax.all_to_all(wide, axis, 0, 0)  4.62 us
    dot_general x1, matrix products, shards(): grad_img = jnp.dot(coef, txt_b, preferred_element_type=F32)  3.04 us
  transfers between devices with their start and end apart: 3, of which 2 were waited for; matrix products, arithmetic and copies ran while one was open for 2% of the time, Pallas kernels for 0%

profile of v1, /device:TPU:1, one launch (start us, length us, event | category | flops | bytes accessed | tf_op | source)
XLA Modules:
  0.0 136.8 jit_solution(18407089588258583726)
XLA Ops:
  0.6 0.0 copy-start
  0.6 0.0 copy-start.3
  0.7 2.0 %convolution_convert_fusion.5 = bf16[128,512]{1,0:T(8,128)(2,1)S(1)} fusion(bf16[128,1536]{1,0:T(8,128)(2,1)} %param.6, bf16[1536,512]{1,0:T(8,128)(2,1)} %param.8), kind=kOutput, calls=%fused_computation.7 | convolution fusion | flops 201392128 | bytes 2097152 | tf_op jit(solution)/shard_map/dot_general | solution.py:45
  2.7 0.0 copy-done
  2.7 0.0 copy-done.3
  2.7 0.4 convolution_convert_fusion.4
  3.1 15.8 %all_to_all.20 = bf16[4,32,1024]{2,1,0:T(8,128)(2,1)S(1)} all-to-all(bf16[4,32,1024]{2,1,0:T(8,128)(2,1)S(1)} %pad_maximum_fusion), channel_id=1, replica_groups=mesh['ylo'=2,'z'=16,'x'=4,'yhi'=2,'core'=2] {'yhi','core'}, dimensions={0} | all-to-all | bytes 524288 | tf_op jit(solution)/shard_map/all_to_all | solution.py:26
  18.9 0.1 multiply_reduce_fusion.2
  19.1 0.1 fusion.3
  19.2 1.1 broadcast_in_dim.20
  20.3 4.6 %all-to-all-start.1 = ((bf16[32,32,512]{2,1,0:T(8,128)(2,1)}), bf16[32,32,512]{2,1,0:T(8,128)(2,1)S(1)}, u32[]{:S(2)}, u32[]{:S(2)}) async-start(bf16[32,32,512]{2,1,0:T(8,128)(2,1)} %broadcast_in_dim.20), calls=%async_computation.1 | async-start | bytes 2097152 | tf_op jit(solution)/shard_map/all_to_all | solution.py:33
  26.2 29.9 %all_gather.6 = bf16[512,512]{1,0:T(8,128)(2,1)S(1)} all-gather(bf16[32,512]{1,0:T(8,128)(2,1)S(1)} %get-tuple-element.9), channel_id=1, replica_groups=mesh['ylo'=2,'z'=16,'x'=4,'yhi'=2,'core'=2] {'z'}, dimensions={0}, use_global_device_ids=true | all-gather | bytes 557056 | tf_op jit(solution)/shard_map/all_gather | solution.py:53
  56.2 0.0 all-to-all-done.1
  56.2 0.0 copy-start.2
  56.2 1.8 %multiply_convert_fusion = bf16[512,1024]{1,0:T(8,128)(2,1)S(1)} fusion(bf16[512,512]{1,0:T(8,128)(2,1)S(1)} %all_gather.6, bf16[1024,512]{1,0:T(8,128)(2,1)S(1)} %bitcast.23, f32[]{:T(128)} %bitcast.22, s32[1024]{0:T(1024)S(1)} %iota_subtract_fusion, f32[]{:T(128)} %bitcast.21, s32[512]{0:T(512)S(1)} %iota_subtract_fusion.1, ...), kind=kOutput, calls=%fused_computation.3 | convolution fusion | flops 544210944 | bytes 2628616 | tf_op jit(solution)/shard_map/dot_general | solution.py:57
  57.9 0.0 copy-done.2
  57.9 0.0 copy-start.4
  58.0 1.7 %convolution_convert_fusion.2 = bf16[1024,512]{1,0:T(8,128)(2,1)} fusion(bf16[512,1024]{1,0:T(8,128)(2,1)S(1)} %multiply_convert_fusion, bf16[512,512]{1,0:T(8,128)(2,1)S(1)} %all_gather.6), kind=kOutput, calls=%fused_computation.4 | convolution fusion | flops 537395200 | bytes 2621440 | tf_op jit(solution)/shard_map/dot_general | solution.py:64
  59.7 0.0 copy-done.4
  59.7 13.4 %all-to-all-start.3 = ((bf16[32,32,512]{2,1,0:T(8,128)(2,1)}), bf16[32,32,512]{2,1,0:T(8,128)(2,1)S(1)}, u32[]{:S(2)}, u32[]{:S(2)}) async-start(bf16[32,32,512]{2,1,0:T(8,128)(2,1)} %bitcast.25), calls=%async_computation.3 | async-start | bytes 2097152 | tf_op jit(solution)/shard_map/all_to_all | solution.py:26
  73.1 3.0 %convolution_convert_fusion.3 = bf16[16,32,512]{2,1,0:T(8,128)(2,1)} fusion(bf16[16,32,1024]{2,1,0:T(8,128)(2,1)} %bitcast.28, bf16[1024,512,1]{1,0,2:T(8,128)(2,1)} %bitcast.24), kind=kOutput, calls=%fused_computation.5 | convolution fusion | flops 537133056 | bytes 2621440 | tf_op jit(solution)/shard_map/dot_general | solution.py:63
  76.1 14.1 %all-to-all-done.3 = bf16[32,32,512]{2,1,0:T(8,128)(2,1)S(1)} async-done(((bf16[32,32,512]{2,1,0:T(8,128)(2,1)}), bf16[32,32,512]{2,1,0:T(8,128)(2,1)S(1)}, u32[]{:S(2)}, u32[]{:S(2)}) %all-to-all-start.3) | async-done | bytes 1048608 | tf_op jit(solution)/shard_map/all_to_all | solution.py:26
  90.2 6.2 %all-to-all-start.2 = ((bf16[16,32,512]{2,1,0:T(8,128)(2,1)}), bf16[16,32,512]{2,1,0:T(8,128)(2,1)S(1)}, u32[]{:S(2)}, u32[]{:S(2)}) async-start(bf16[16,32,512]{2,1,0:T(8,128)(2,1)} %convolution_convert_fusion.3), calls=%async_computation.2 | async-start | bytes 1048576 | tf_op jit(solution)/shard_map/all_to_all | solution.py:26
  96.4 0.2 convert_reduce_fusion
  96.6 22.7 %all-to-all-done.2 = bf16[16,32,512]{2,1,0:T(8,128)(2,1)S(1)} async-done(((bf16[16,32,512]{2,1,0:T(8,128)(2,1)}), bf16[16,32,512]{2,1,0:T(8,128)(2,1)S(1)}, u32[]{:S(2)}, u32[]{:S(2)}) %all-to-all-start.2) | async-done | bytes 524320 | tf_op jit(solution)/shard_map/all_to_all | solution.py:26
  119.3 0.1 convert_reduce_fusion.1
  119.3 0.0 copy-start.1
  119.3 0.2 multiply_reduce_fusion.1
  119.5 0.1 multiply_convert_fusion.2
  119.7 14.4 %all_gather.7 = bf16[128,1024]{1,0:T(8,128)(2,1)S(1)} all-gather(bf16[32,1024]{1,0:T(8,128)(2,1)S(1)} %pad_maximum_fusion.1), channel_id=1, replica_groups=mesh['ylo'=2,'z'=16,'x'=4,'yhi'=2,'core'=2] {'yhi','core'}, dimensions={0}, use_global_device_ids=true | all-gather | bytes 327680 | tf_op jit(solution)/shard_map/all_gather | solution.py:71
  134.0 1.4 %convolution_convert_fusion = bf16[128,1536]{1,0:T(8,128)(2,1)} fusion(bf16[1536,512]{1,0:T(8,128)(2,1)S(1)} %copy-done, bf16[128,1024]{1,0:T(8,128)(2,1)S(1)} %all_gather.7), kind=kOutput, calls=%fused_computation | convolution fusion | flops 201523200 | bytes 2097152 | tf_op jit(solution)/shard_map/dot_general | solution.py:75
  135.4 0.0 copy-done.1
  135.4 1.4 %convolution_convert_fusion.1 = bf16[128,1536]{1,0:T(8,128)(2,1)} fusion(bf16[1536,512]{1,0:T(8,128)(2,1)S(1)} %copy-done.1, bf16[128,1024]{1,0:T(8,128)(2,1)S(1)} %all_gather.7), kind=kOutput, calls=%fused_computation.1 | convolution fusion | flops 201523200 | bytes 2097152 | tf_op jit(solution)/shard_map/dot_general | solution.py:72
  (7 shorter events, 0.1 us)
Async XLA Ops:
  0.6 2.1 %copy-start = (bf16[1536,512]{1,0:T(8,128)(2,1)S(1)}, bf16[1536,512]{1,0:T(8,128)(2,1)}, u32[]{:S(2)}) copy-start(bf16[1536,512]{1,0:T(8,128)(2,1)} %param.9) | copy-start | bytes 4718596
  0.6 2.1 %copy-start.3 = (bf16[128,1536]{1,0:T(8,128)(2,1)S(1)}, bf16[128,1536]{1,0:T(8,128)(2,1)}, u32[]{:S(2)}) copy-start(bf16[128,1536]{1,0:T(8,128)(2,1)} %param.7) | copy-start | bytes 1179652
  20.3 35.9 %all-to-all-start.1 = ((bf16[32,32,512]{2,1,0:T(8,128)(2,1)}), bf16[32,32,512]{2,1,0:T(8,128)(2,1)S(1)}, u32[]{:S(2)}, u32[]{:S(2)}) async-start(bf16[32,32,512]{2,1,0:T(8,128)(2,1)} %broadcast_in_dim.20), calls=%async_computation.1 | async-start | bytes 2097152 | tf_op jit(solution)/shard_map/all_to_all | solution.py:33
  56.2 1.8 %copy-start.2 = (bf16[32,32,512]{2,1,0:T(8,128)(2,1)}, bf16[32,32,512]{2,1,0:T(8,128)(2,1)S(1)}, u32[]{:S(2)}) copy-start(bf16[32,32,512]{2,1,0:T(8,128)(2,1)S(1)} %all-to-all-done.1) | copy-start | bytes 3145732
  57.9 1.8 %copy-start.4 = (bf16[512,1024]{1,0:T(8,128)(2,1)}, bf16[512,1024]{1,0:T(8,128)(2,1)S(1)}, u32[]{:S(2)}) copy-start(bf16[512,1024]{1,0:T(8,128)(2,1)S(1)} %multiply_convert_fusion) | copy-start | bytes 3145732
  59.7 30.5 %all-to-all-start.3 = ((bf16[32,32,512]{2,1,0:T(8,128)(2,1)}), bf16[32,32,512]{2,1,0:T(8,128)(2,1)S(1)}, u32[]{:S(2)}, u32[]{:S(2)}) async-start(bf16[32,32,512]{2,1,0:T(8,128)(2,1)} %bitcast.25), calls=%async_computation.3 | async-start | bytes 2097152 | tf_op jit(solution)/shard_map/all_to_all | solution.py:26
  90.2 29.0 %all-to-all-start.2 = ((bf16[16,32,512]{2,1,0:T(8,128)(2,1)}), bf16[16,32,512]{2,1,0:T(8,128)(2,1)S(1)}, u32[]{:S(2)}, u32[]{:S(2)}) async-start(bf16[16,32,512]{2,1,0:T(8,128)(2,1)} %convolution_convert_fusion.3), calls=%async_computation.2 | async-start | bytes 1048576 | tf_op jit(solution)/shard_map/all_to_all | solution.py:26
  119.3 16.1 %copy-start.1 = (bf16[1536,512]{1,0:T(8,128)(2,1)S(1)}, bf16[1536,512]{1,0:T(8,128)(2,1)}, u32[]{:S(2)}) copy-start(bf16[1536,512]{1,0:T(8,128)(2,1)} %param.8) | copy-start | bytes 4718596

commit v2 on v1

v2 whole, which is shorter than its diff:
```python
import jax
import jax.numpy as jnp
from jax import lax
from jax.sharding import Mesh
from jax.sharding import PartitionSpec as P

EPS = 1e-06
BF = jnp.bfloat16
F32 = jnp.float32
GROUP = ("core", "yhi")


def normalize(embed):
    inv = lax.rsqrt(jnp.sum(embed * embed, axis=1, keepdims=True) + EPS)
    return (inv, embed * inv)


def backward(grad, inv, unit):
    along = jnp.sum(grad * unit, axis=1, keepdims=True)
    return (inv * (grad - along * unit)).astype(BF)


def shifted(x, axis, by):
    peers = lax.axis_size(axis)
    return lax.ppermute(x, axis, [(i, (i + by) % peers) for i in range(peers)])


def exchange_sum(parts, axis):
    got = lax.all_to_all(parts.astype(BF), axis, 0, 0)
    return jnp.sum(got.astype(F32), axis=0)


def mutual_sum(x, axis):
    x = x.astype(BF)
    return x.astype(F32) + shifted(x, axis, 1).astype(F32)


def other_half(x, core):
    return jnp.where(core == 0, x[1], x[0])


def own_half(x, core):
    return jnp.where(core == 0, x[0], x[1])


def gather_text(rows):
    rows = jnp.stack([rows, shifted(rows, "ylo", 1)])
    rows = jnp.stack([rows] + [shifted(rows, "x", k) for k in range(1, lax.axis_size("x"))])
    rows = jnp.stack([rows, shifted(rows, "core", 1)])
    return rows


def scatter_text(grad):
    grad = grad[0] + shifted(grad[1].astype(BF), "core", 1).astype(F32)
    back = [shifted(grad[k].astype(BF), "x", -k).astype(F32) for k in range(1, grad.shape[0])]
    grad = grad[0] + sum(back)
    grad = grad[0] + shifted(grad[1].astype(BF), "ylo", 1).astype(F32)
    return mutual_sum(grad, "yhi")


def shards(vision, sentence, vision_map, sentence_map, sharpness, offset):
    rows = vision.shape[0]
    width = vision_map.shape[1]
    quarter = rows // lax.axis_size(GROUP)
    half = 2 * quarter
    core, yhi, z = (lax.axis_index(a) for a in ("core", "yhi", "z"))
    depth = lax.axis_size("z")
    t = sharpness[0]
    shift = offset[0]

    img = jnp.dot(vision, vision_map, preferred_element_type=F32)
    img = exchange_sum(img.reshape(-1, quarter, width), GROUP)
    inv_img, unit_img = normalize(img)
    img_b = jnp.broadcast_to(unit_img.astype(BF)[None], (depth, quarter, width))
    img_b = lax.all_to_all(img_b, "z", 0, 0).reshape(depth * quarter, width)

    txt = jnp.dot(sentence, sentence_map, preferred_element_type=F32).reshape(2, half, width)
    txt = own_half(txt, core) + shifted(other_half(txt, core).astype(BF), "core", 1).astype(F32)
    txt = mutual_sum(txt, "yhi")
    inv_txt, unit_txt = normalize(txt)
    txt_b = gather_text(unit_txt.astype(BF))
    shape = txt_b.shape
    txt_b = txt_b.reshape(-1, width)
    n_img, n_txt = img_b.shape[0], txt_b.shape[0]

    logits = t * lax.dot_general(img_b, txt_b, (((1,), (1,)), ((), ())), preferred_element_type=F32) + shift
    image_at = lax.broadcasted_iota(jnp.int32, (n_img, n_txt), 0) - z * quarter
    text_at = lax.broadcasted_iota(jnp.int32, (n_img, n_txt), 1) - yhi * quarter
    own = (image_at == text_at) & (image_at >= 0) & (image_at < quarter)
    sign = jnp.where(own, F32(1.0), F32(-1.0))
    coef = (t * -sign * jax.nn.sigmoid(-sign * logits)).astype(BF)
    grad_img = jnp.dot(coef, txt_b, preferred_element_type=F32)
    grad_txt = lax.dot_general(coef, img_b, (((0,), (0,)), ((), ())), preferred_element_type=F32)

    grad_img = exchange_sum(grad_img.reshape(depth, quarter, width), "z")
    grad_txt = scatter_text(grad_txt.reshape(shape))
    delta_txt = lax.all_gather(backward(grad_txt, inv_txt, unit_txt), "core", axis=0, tiled=True)
    text_grad = lax.dot_general(
        delta_txt, sentence_map, (((1,), (1,)), ((), ())), preferred_element_type=F32
    ).astype(BF)
    delta_img = lax.all_gather(backward(grad_img, inv_img, unit_img), GROUP, axis=0, tiled=True)
    image_grad = lax.dot_general(
        delta_img, vision_map, (((1,), (1,)), ((), ())), preferred_element_type=F32
    ).astype(BF)
    return (image_grad, text_grad)


def solution(mesh):
    x, ylo = 4, 2
    z = mesh.shape["dp"] // (x * ylo)
    fine = Mesh(mesh.devices.reshape(ylo, z, x, 2, 2), ("ylo", "z", "x", "yhi", "core"))
    dp, mp = ("ylo", "z", "x"), ("yhi", "core")
    in_specs = (P(dp, mp), P(dp, mp), P(mp, None), P(mp, None), P(), P())
    out_specs = (P(dp, mp), P(dp, mp))
    return jax.shard_map(shards, mesh=fine, in_specs=in_specs, out_specs=out_specs, check_vma=False)
```

time: 137 us -> 138 us (level)
  starting transfers between devices: 24.2 us -> 74.6 us
  blocking collectives: 60.1 us -> 17.7 us
  waiting for transfers between devices: 36.8 us -> 24.6 us
  other arithmetic: 0.8 us -> 5.73 us
    ppermute x0 -> x13, starting transfers between devices: none -> 41.9 us  [shifted(): return lax.ppermute(x, axis, [(i, (i + by) % peers) for i in range(peers)])]
    all_to_all x2, waiting for transfers between devices: 36.8 us -> 2.72 us  [exchange_sum(): got = lax.all_to_all(parts.astype(BF), axis, 0, 0)]
    all_gather x2, blocking collectives: 44.3 us -> 17.7 us  [the longest x1 12.7 us: shards(): lax.all_gather(backward(grad_img, inv_img, unit_img), GROUP, axis=0, tile...]
    ppermute x0 -> x13, waiting for transfers between devices: none -> 21.9 us  [shifted(): return lax.ppermute(x, axis, [(i, (i + by) % peers) for i in range(peers)])]
    all_to_all x1 -> x0, blocking collectives: 15.8 us -> none  [exchange_sum(): got = lax.all_to_all(parts.astype(BF), axis, 0, 0)]
    all_to_all x1, starting transfers between devices: 4.62 us -> 10.7 us  [shards(): img_b = lax.all_to_all(img_b, 'z', 0, 0).reshape(depth * quarter, width)]
    another operation x0 -> x4, other arithmetic: none -> 3.49 us  [the longest x2 2.2 us: gather_text(): rows = jnp.stack([rows, shifted(rows, 'core', 1)])]
    all_to_all x2, starting transfers between devices: 19.6 us -> 22 us  [exchange_sum(): got = lax.all_to_all(parts.astype(BF), axis, 0, 0)]
  transfers between devices with their start and end apart: 3 -> 16, of which waited for: 2 -> 9; matrix products, arithmetic and copies ran while one was open for 2% -> 6% of each run, Pallas kernels for 0% -> 0%
where the time goes in v2:
time: 138 us; the launch traced here: 137 us
  starting transfers between devices  74.6 us (54%)
  waiting for transfers between devices  24.6 us (18%)
  blocking collectives  17.7 us (13%)
  matrix products  11.1 us (8%)
  other arithmetic  5.73 us (4%)
  between operations  2.27 us (2%)
    ppermute x13, starting transfers between devices, shifted(): return lax.ppermute(x, axis, [(i, (i + by) % peers) for i in range(peers)])  41.9 us
    all_to_all x2, starting transfers between devices, exchange_sum(): got = lax.all_to_all(parts.astype(BF), axis, 0, 0)  22 us
    ppermute x13, waiting for transfers between devices, shifted(): return lax.ppermute(x, axis, [(i, (i + by) % peers) for i in range(peers)])  21.9 us
    all_gather x1, blocking collectives, shards(): lax.all_gather(backward(grad_img, inv_img, unit_img), GROUP, axis=0, tile...  12.7 us
    all_to_all x1, starting transfers between devices, shards(): img_b = lax.all_to_all(img_b, 'z', 0, 0).reshape(depth * quarter, width)  10.7 us
    all_gather x1, blocking collectives, shards(): lax.all_gather(backward(grad_txt, inv_txt, unit_txt), 'core', axis=0, til...  5.03 us
    dot_general x1, matrix products, shards(): lax.dot_general(img_b, txt_b, (((1,), (1,)), ((), ())), preferred_element...  2.98 us
  transfers between devices with their start and end apart: 16, of which 9 were waited for; matrix products, arithmetic and copies ran while one was open for 6% of the time, Pallas kernels for 0%

profile of v2, /device:TPU:1, one launch (start us, length us, event | category | flops | bytes accessed | tf_op | source)
XLA Modules:
  0.0 137.0 jit_solution(1958305178546312084)
XLA Ops:
  0.6 0.0 copy-start
  0.6 0.0 copy-start.3
  0.7 2.7 %convolution_convert_fusion.3 = bf16[128,512]{1,0:T(8,128)(2,1)} fusion(bf16[128,1536]{1,0:T(8,128)(2,1)} %param.6, bf16[1536,512]{1,0:T(8,128)(2,1)} %param.8), kind=kOutput, calls=%fused_computation.4 | convolution fusion | flops 201392128 | bytes 2097152 | tf_op jit(solution)/shard_map/dot_general | solution.py:71
  3.4 10.2 %all-to-all-start = ((bf16[4,32,512]{2,1,0:T(8,128)(2,1)}), bf16[4,32,512]{2,1,0:T(8,128)(2,1)S(1)}, u32[]{:S(2)}, u32[]{:S(2)}) async-start(bf16[4,32,512]{2,1,0:T(8,128)(2,1)} %bitcast), calls=%async_computation | async-start | bytes 262144 | tf_op jit(solution)/shard_map/all_to_all | solution.py:29
  13.5 0.0 copy-done
  13.5 0.0 copy-done.3
  13.5 0.4 fusion.11
  13.9 2.0 %collective-permute-start = (bf16[64,512]{1,0:T(8,128)(2,1)S(1)}, bf16[64,512]{1,0:T(8,128)(2,1)S(1)}, u32[]{:S(2)}, u32[]{:S(2)}) collective-permute-start(bf16[64,512]{1,0:T(8,128)(2,1)S(1)} %select_convert_fusion), channel_id=1, source_target_pairs={{0,1},{1,0},{2,3},{3,2},{4,5},{5,4},{6,7},{7,6},{8,9},{9,8},{10,11... | collective-permute-start | bytes 196616 | tf_op jit(solution)/shard_map/ppermute | solution.py:25
  15.9 2.7 %all-to-all-done = bf16[4,32,512]{2,1,0:T(8,128)(2,1)S(1)} async-done(((bf16[4,32,512]{2,1,0:T(8,128)(2,1)}), bf16[4,32,512]{2,1,0:T(8,128)(2,1)S(1)}, u32[]{:S(2)}, u32[]{:S(2)}) %all-to-all-start) | async-done | bytes 131104 | tf_op jit(solution)/shard_map/all_to_all | solution.py:29
  18.6 0.1 multiply_reduce_fusion.3
  18.8 0.1 multiply_convert_fusion.3
  18.8 0.9 broadcast_in_dim.20
  19.7 10.7 %all-to-all-start.1 = ((bf16[16,32,512]{2,1,0:T(8,128)(2,1)}), bf16[16,32,512]{2,1,0:T(8,128)(2,1)S(1)}, u32[]{:S(2)}, u32[]{:S(2)}) async-start(bf16[16,32,512]{2,1,0:T(8,128)(2,1)} %broadcast_in_dim.20), calls=%async_computation.1 | async-start | bytes 1048576 | tf_op jit(solution)/shard_map/all_to_all | solution.py:75
  30.5 0.0 collective-permute-done
  30.5 2.4 %collective-permute-start.1 = (bf16[64,512]{1,0:T(8,128)(2,1)S(1)}, bf16[64,512]{1,0:T(8,128)(2,1)S(1)}, u32[]{:S(2)}, u32[]{:S(2)}) collective-permute-start(bf16[64,512]{1,0:T(8,128)(2,1)S(1)} %add_convert_fusion), channel_id=1, source_target_pairs={{0,2},{2,0},{1,3},{3,1},{4,6},{6,4},{5,7},{7,5},{8,10},{10,8},{9,1... | collective-permute-start | bytes 196616 | tf_op jit(solution)/shard_map/ppermute | solution.py:25
  33.0 4.1 %collective-permute-done.1 = bf16[64,512]{1,0:T(8,128)(2,1)S(1)} collective-permute-done((bf16[64,512]{1,0:T(8,128)(2,1)S(1)}, bf16[64,512]{1,0:T(8,128)(2,1)S(1)}, u32[]{:S(2)}, u32[]{:S(2)}) %collective-permute-start.1) | collective-permute-done | bytes 65568 | tf_op jit(solution)/shard_map/ppermute | solution.py:25
  37.0 0.1 multiply_reduce_fusion.1
  37.1 0.1 fusion.4
  37.2 2.3 %collective-permute-start.2 = (bf16[64,512]{1,0:T(8,128)(2,1)S(1)}, bf16[64,512]{1,0:T(8,128)(2,1)S(1)}, u32[]{:S(2)}, u32[]{:S(2)}) collective-permute-start(bf16[64,512]{1,0:T(8,128)(2,1)S(1)} %fusion.4), channel_id=1, source_target_pairs={{0,256},{256,0},{1,257},{257,1},{2,258},{258,2},{3,259},{259,3},{4... | collective-permute-start | bytes 196616 | tf_op jit(solution)/shard_map/ppermute | solution.py:25
  39.6 2.7 %collective-permute-done.2 = bf16[64,512]{1,0:T(8,128)(2,1)S(1)} collective-permute-done((bf16[64,512]{1,0:T(8,128)(2,1)S(1)}, bf16[64,512]{1,0:T(8,128)(2,1)S(1)}, u32[]{:S(2)}, u32[]{:S(2)}) %collective-permute-start.2) | collective-permute-done | bytes 65568 | tf_op jit(solution)/shard_map/ppermute | solution.py:25
  42.3 4.7 %collective-permute-start.4 = (bf16[2,64,512]{2,1,0:T(8,128)(2,1)S(1)}, bf16[2,64,512]{2,1,0:T(8,128)(2,1)S(1)}, u32[]{:S(2)}, u32[]{:S(2)}) collective-permute-start(bf16[2,64,512]{2,1,0:T(8,128)(2,1)S(1)} %get-tuple-element.10), channel_id=1, source_target_pairs={{0,8},{4,12},{8,0},{12,4},{1,9},{5,13},{9,1},{13,5},{2,10},{6,14},... | collective-permute-start | bytes 393224 | tf_op jit(solution)/shard_map/ppermute | solution.py:25
  46.9 2.2 %collective-permute-start.3 = (bf16[2,64,512]{2,1,0:T(8,128)(2,1)S(1)}, bf16[2,64,512]{2,1,0:T(8,128)(2,1)S(1)}, u32[]{:S(2)}, u32[]{:S(2)}) collective-permute-start(bf16[2,64,512]{2,1,0:T(8,128)(2,1)S(1)} %get-tuple-element.10), channel_id=1, source_target_pairs={{0,4},{4,8},{8,12},{12,0},{1,5},{5,9},{9,13},{13,1},{2,6},{6,10},{... | collective-permute-start | bytes 393224 | tf_op jit(solution)/shard_map/ppermute | solution.py:25
  49.2 4.3 %collective-permute-start.5 = (bf16[2,64,512]{2,1,0:T(8,128)(2,1)S(1)}, bf16[2,64,512]{2,1,0:T(8,128)(2,1)S(1)}, u32[]{:S(2)}, u32[]{:S(2)}) collective-permute-start(bf16[2,64,512]{2,1,0:T(8,128)(2,1)S(1)} %get-tuple-element.10), channel_id=1, source_target_pairs={{0,12},{4,0},{8,4},{12,8},{1,13},{5,1},{9,5},{13,9},{2,14},{6,2},{... | collective-permute-start | bytes 393224 | tf_op jit(solution)/shard_map/ppermute | solution.py:25
  53.4 0.0 collective-permute-done.4
  53.5 1.9 %collective-permute-done.3 = bf16[2,64,512]{2,1,0:T(8,128)(2,1)S(1)} collective-permute-done((bf16[2,64,512]{2,1,0:T(8,128)(2,1)S(1)}, bf16[2,64,512]{2,1,0:T(8,128)(2,1)S(1)}, u32[]{:S(2)}, u32[]{:S(2)}) %collective-permute-start.3) | collective-permute-done | bytes 131104 | tf_op jit(solution)/shard_map/ppermute | solution.py:25
  55.4 0.0 collective-permute-done.5
  55.4 0.1 fusion.9
  55.5 6.9 %collective-permute-start.6 = (bf16[4,2,64,512]{3,2,1,0:T(8,128)(2,1)S(1)}, bf16[4,2,64,512]{3,2,1,0:T(8,128)(2,1)}, u32[]{:S(2)}, u32[]{:S(2)}) collective-permute-start(bf16[4,2,64,512]{3,2,1,0:T(8,128)(2,1)S(1)} %get-tuple-element.8), channel_id=1, source_target_pairs={{0,1},{1,0},{2,3},{3,2},{4,5},{5,4},{6,7},{7,6},{8,9},{9,8},{10,11... | collective-permute-start | bytes 1572872 | tf_op jit(solution)/shard_map/ppermute | solution.py:25
  63.8 0.3 collective-permute-done.6
  64.1 2.1 %pad_maximum_fusion = bf16[2,4,2,64,512]{4,3,2,1,0:T(8,128)(2,1)} fusion(bf16[1,4,2,64,512]{4,3,2,1,0:T(8,128)(2,1)} %bitcast.10, bf16[1,4,2,64,512]{4,3,2,1,0:T(8,128)(2,1)S(1)} %get-tuple-element.7), kind=kLoop, calls=%fused_computation.6 | loop fusion | flops 524288 | bytes 2097152 | tf_op jit(solution)/shard_map/stack | solution.py:49
  66.2 0.0 all-to-all-done.1
  66.2 3.0 %multiply_convert_fusion = bf16[512,1024]{1,0:T(8,128)(2,1)S(1)} fusion(bf16[512,512]{1,0:T(8,128)(2,1)S(1)} %bitcast.55, bf16[1024,512]{1,0:T(8,128)(2,1)} %bitcast.58, f32[]{:T(128)} %bitcast.53, s32[1024]{0:T(1024)S(1)} %iota_subtract_fusion, f32[]{:T(128)} %bitcast.52, s32[512]{0:T(512)S(1)} %iota_subtract_fusion.1, ...), kind=kOutput, calls=%fused_computation.2 | convolution fusion | flops 544210944 | bytes 2628616 | tf_op jit(solution)/shard_map/dot_general | solution.py:86
  69.2 0.8 fusion.12
  69.9 0.0 copy-start.2
  69.9 0.1 slice.80
  70.0 2.4 %collective-permute-start.7 = (bf16[4,2,64,512]{3,2,1,0:T(8,128)(2,1)S(1)}, bf16[4,2,64,512]{3,2,1,0:T(8,128)(2,1)}, u32[]{:S(2)}, u32[]{:S(2)}) collective-permute-start(bf16[4,2,64,512]{3,2,1,0:T(8,128)(2,1)S(1)} %bitcast.60), channel_id=1, source_target_pairs={{0,1},{1,0},{2,3},{3,2},{4,5},{5,4},{6,7},{7,6},{8,9},{9,8},{10,11... | collective-permute-start | bytes 1572872 | tf_op jit(solution)/shard_map/ppermute | solution.py:25
  72.4 0.1 slice.53
  72.5 0.0 copy-done.2
  72.5 1.5 %convolution_convert_fusion.2 = bf16[16,32,512]{2,1,0:T(8,128)(2,1)} fusion(bf16[16,32,1024]{2,1,0:T(8,128)(2,1)S(1)} %bitcast.57, bf16[1024,512,1]{1,0,2:T(8,128)(2,1)S(1)} %bitcast.59), kind=kOutput, calls=%fused_computation.3 | convolution fusion | flops 537133056 | bytes 2621440 | tf_op jit(solution)/shard_map/dot_general | solution.py:92
  74.0 11.8 %all-to-all-start.2 = ((bf16[16,32,512]{2,1,0:T(8,128)(2,1)}), bf16[16,32,512]{2,1,0:T(8,128)(2,1)}, u32[]{:S(2)}, u32[]{:S(2)}) async-start(bf16[16,32,512]{2,1,0:T(8,128)(2,1)} %convolution_convert_fusion.2), calls=%async_computation.2 | async-start | bytes 1048576 | tf_op jit(solution)/shard_map/all_to_all | solution.py:29
  85.8 0.0 collective-permute-done.7
  85.8 1.3 fusion.10
  87.2 5.3 %collective-permute-start.8 = (bf16[2,64,512]{2,1,0:T(8,128)(2,1)S(1)}, bf16[2,64,512]{2,1,0:T(8,128)(2,1)S(1)}, u32[]{:S(2)}, u32[]{:S(2)}) collective-permute-start(bf16[2,64,512]{2,1,0:T(8,128)(2,1)S(1)} %get-tuple-element.4), channel_id=1, source_target_pairs={{0,12},{4,0},{8,4},{12,8},{1,13},{5,1},{9,5},{13,9},{2,14},{6,2},{... | collective-permute-start | bytes 393224 | tf_op jit(solution)/shard_map/ppermute | solution.py:25
  92.4 1.9 %collective-permute-start.10 = (bf16[2,64,512]{2,1,0:T(8,128)(2,1)S(1)}, bf16[2,64,512]{2,1,0:T(8,128)(2,1)S(1)}, u32[]{:S(2)}, u32[]{:S(2)}) collective-permute-start(bf16[2,64,512]{2,1,0:T(8,128)(2,1)S(1)} %get-tuple-element.5), channel_id=1, source_target_pairs={{0,4},{4,8},{8,12},{12,0},{1,5},{5,9},{9,13},{13,1},{2,6},{6,10},{... | collective-permute-start | bytes 393224 | tf_op jit(solution)/shard_map/ppermute | solution.py:25
  94.4 3.1 %collective-permute-start.9 = (bf16[2,64,512]{2,1,0:T(8,128)(2,1)S(1)}, bf16[2,64,512]{2,1,0:T(8,128)(2,1)S(1)}, u32[]{:S(2)}, u32[]{:S(2)}) collective-permute-start(bf16[2,64,512]{2,1,0:T(8,128)(2,1)S(1)} %get-tuple-element.6), channel_id=1, source_target_pairs={{0,8},{4,12},{8,0},{12,4},{1,9},{5,13},{9,1},{13,5},{2,10},{6,14},... | collective-permute-start | bytes 393224 | tf_op jit(solution)/shard_map/ppermute | solution.py:25
  97.5 0.0 collective-permute-done.8
  97.5 2.5 %collective-permute-done.10 = bf16[2,64,512]{2,1,0:T(8,128)(2,1)S(1)} collective-permute-done((bf16[2,64,512]{2,1,0:T(8,128)(2,1)S(1)}, bf16[2,64,512]{2,1,0:T(8,128)(2,1)S(1)}, u32[]{:S(2)}, u32[]{:S(2)}) %collective-permute-start.10) | collective-permute-done | bytes 131104 | tf_op jit(solution)/shard_map/ppermute | solution.py:25
  100.0 2.3 %collective-permute-done.9 = bf16[2,64,512]{2,1,0:T(8,128)(2,1)S(1)} collective-permute-done((bf16[2,64,512]{2,1,0:T(8,128)(2,1)S(1)}, bf16[2,64,512]{2,1,0:T(8,128)(2,1)S(1)}, u32[]{:S(2)}, u32[]{:S(2)}) %collective-permute-start.9) | collective-permute-done | bytes 131104 | tf_op jit(solution)/shard_map/ppermute | solution.py:25
  102.3 0.1 fusion
  102.4 0.0 copy-start.1
  102.4 2.4 %collective-permute-start.11 = (bf16[64,512]{1,0:T(8,128)(2,1)S(1)}, bf16[64,512]{1,0:T(8,128)(2,1)S(1)}, u32[]{:S(2)}, u32[]{:S(2)}) collective-permute-start(bf16[64,512]{1,0:T(8,128)(2,1)S(1)} %fusion.5), channel_id=1, source_target_pairs={{0,256},{256,0},{1,257},{257,1},{2,258},{258,2},{3,259},{259,3},{4... | collective-permute-start | bytes 196616 | tf_op jit(solution)/shard_map/ppermute | solution.py:25
  104.8 3.1 %collective-permute-done.11 = bf16[64,512]{1,0:T(8,128)(2,1)S(1)} collective-permute-done((bf16[64,512]{1,0:T(8,128)(2,1)S(1)}, bf16[64,512]{1,0:T(8,128)(2,1)S(1)}, u32[]{:S(2)}, u32[]{:S(2)}) %collective-permute-start.11) | collective-permute-done | bytes 65568 | tf_op jit(solution)/shard_map/ppermute | solution.py:25
  108.0 1.9 %collective-permute-start.12 = (bf16[64,512]{1,0:T(8,128)(2,1)S(1)}, bf16[64,512]{1,0:T(8,128)(2,1)S(1)}, u32[]{:S(2)}, u32[]{:S(2)}) collective-permute-start(bf16[64,512]{1,0:T(8,128)(2,1)S(1)} %fusion.2), channel_id=1, source_target_pairs={{0,2},{2,0},{1,3},{3,1},{4,6},{6,4},{5,7},{7,5},{8,10},{10,8},{9,1... | collective-permute-start | bytes 196616 | tf_op jit(solution)/shard_map/ppermute | solution.py:25
  109.9 5.0 %collective-permute-done.12 = bf16[64,512]{1,0:T(8,128)(2,1)S(1)} collective-permute-done((bf16[64,512]{1,0:T(8,128)(2,1)S(1)}, bf16[64,512]{1,0:T(8,128)(2,1)S(1)}, u32[]{:S(2)}, u32[]{:S(2)}) %collective-permute-start.12) | collective-permute-done | bytes 65568 | tf_op jit(solution)/shard_map/ppermute | solution.py:25
  114.9 0.2 multiply_reduce_fusion
  115.1 0.1 multiply_convert_fusion.1
  115.2 5.0 %all_gather.7 = bf16[128,512]{1,0:T(8,128)(2,1)S(1)} all-gather(bf16[64,512]{1,0:T(8,128)(2,1)S(1)} %multiply_convert_fusion.1), channel_id=1, replica_groups=mesh['ylo'=2,'z'=16,'x'=4,'yhi'=2,'core'=2] {'core'}, dimensions={0}, use_global_device_ids=true | all-gather | bytes 196608 | tf_op jit(solution)/shard_map/all_gather | solution.py:97
  120.2 1.4 %convolution_convert_fusion = bf16[128,1536]{1,0:T(8,128)(2,1)} fusion(bf16[128,512]{1,0:T(8,128)(2,1)S(1)} %all_gather.7, bf16[1536,512]{1,0:T(8,128)(2,1)S(1)} %copy-done), kind=kOutput, calls=%fused_computation | convolution fusion | flops 201523200 | bytes 2097152 | tf_op jit(solution)/shard_map/dot_general | solution.py:98
  121.6 0.0 all-to-all-done.2
  121.6 1.1 convert_reduce_fusion
  122.7 0.2 multiply_reduce_fusion.2
  122.9 0.1 multiply_convert_fusion.2
  123.0 12.7 %all_gather.6 = bf16[128,512]{1,0:T(8,128)(2,1)S(1)} all-gather(bf16[32,512]{1,0:T(8,128)(2,1)S(1)} %multiply_convert_fusion.2), channel_id=1, replica_groups=mesh['ylo'=2,'z'=16,'x'=4,'yhi'=2,'core'=2] {'core','yhi'}, dimensions={0}, use_global_device_ids=true | all-gather | bytes 163840 | tf_op jit(solution)/shard_map/all_gather | solution.py:101
  135.7 1.4 %convolution_convert_fusion.1 = bf16[128,1536]{1,0:T(8,128)(2,1)} fusion(bf16[128,512]{1,0:T(8,128)(2,1)S(1)} %all_gather.6, bf16[1536,512]{1,0:T(8,128)(2,1)S(1)} %copy-done.1), kind=kOutput, calls=%fused_computation.1 | convolution fusion | flops 201523200 | bytes 2097152 | tf_op jit(solution)/shard_map/dot_general | solution.py:102
  (13 shorter events, 0.2 us)
Async XLA Ops:
  0.6 12.9 %copy-start = (bf16[1536,512]{1,0:T(8,128)(2,1)S(1)}, bf16[1536,512]{1,0:T(8,128)(2,1)}, u32[]{:S(2)}) copy-start(bf16[1536,512]{1,0:T(8,128)(2,1)} %param.9) | copy-start | bytes 4718596
  0.6 12.9 %copy-start.3 = (bf16[128,1536]{1,0:T(8,128)(2,1)S(1)}, bf16[128,1536]{1,0:T(8,128)(2,1)}, u32[]{:S(2)}) copy-start(bf16[128,1536]{1,0:T(8,128)(2,1)} %param.7) | copy-start | bytes 1179652
  3.4 15.3 %all-to-all-start = ((bf16[4,32,512]{2,1,0:T(8,128)(2,1)}), bf16[4,32,512]{2,1,0:T(8,128)(2,1)S(1)}, u32[]{:S(2)}, u32[]{:S(2)}) async-start(bf16[4,32,512]{2,1,0:T(8,128)(2,1)} %bitcast), calls=%async_computation | async-start | bytes 262144 | tf_op jit(solution)/shard_map/all_to_all | solution.py:29
  13.9 16.5 %collective-permute-start = (bf16[64,512]{1,0:T(8,128)(2,1)S(1)}, bf16[64,512]{1,0:T(8,128)(2,1)S(1)}, u32[]{:S(2)}, u32[]{:S(2)}) collective-permute-start(bf16[64,512]{1,0:T(8,128)(2,1)S(1)} %select_convert_fusion), channel_id=1, source_target_pairs={{0,1},{1,0},{2,3},{3,2},{4,5},{5,4},{6,7},{7,6},{8,9},{9,8},{10,11... | collective-permute-start | bytes 196616 | tf_op jit(solution)/shard_map/ppermute | solution.py:25
  19.7 46.4 %all-to-all-start.1 = ((bf16[16,32,512]{2,1,0:T(8,128)(2,1)}), bf16[16,32,512]{2,1,0:T(8,128)(2,1)S(1)}, u32[]{:S(2)}, u32[]{:S(2)}) async-start(bf16[16,32,512]{2,1,0:T(8,128)(2,1)} %broadcast_in_dim.20), calls=%async_computation.1 | async-start | bytes 1048576 | tf_op jit(solution)/shard_map/all_to_all | solution.py:75
  30.5 6.5 %collective-permute-start.1 = (bf16[64,512]{1,0:T(8,128)(2,1)S(1)}, bf16[64,512]{1,0:T(8,128)(2,1)S(1)}, u32[]{:S(2)}, u32[]{:S(2)}) collective-permute-start(bf16[64,512]{1,0:T(8,128)(2,1)S(1)} %add_convert_fusion), channel_id=1, source_target_pairs={{0,2},{2,0},{1,3},{3,1},{4,6},{6,4},{5,7},{7,5},{8,10},{10,8},{9,1... | collective-permute-start | bytes 196616 | tf_op jit(solution)/shard_map/ppermute | solution.py:25
  37.2 5.0 %collective-permute-start.2 = (bf16[64,512]{1,0:T(8,128)(2,1)S(1)}, bf16[64,512]{1,0:T(8,128)(2,1)S(1)}, u32[]{:S(2)}, u32[]{:S(2)}) collective-permute-start(bf16[64,512]{1,0:T(8,128)(2,1)S(1)} %fusion.4), channel_id=1, source_target_pairs={{0,256},{256,0},{1,257},{257,1},{2,258},{258,2},{3,259},{259,3},{4... | collective-permute-start | bytes 196616 | tf_op jit(solution)/shard_map/ppermute | solution.py:25
  42.3 11.2 %collective-permute-start.4 = (bf16[2,64,512]{2,1,0:T(8,128)(2,1)S(1)}, bf16[2,64,512]{2,1,0:T(8,128)(2,1)S(1)}, u32[]{:S(2)}, u32[]{:S(2)}) collective-permute-start(bf16[2,64,512]{2,1,0:T(8,128)(2,1)S(1)} %get-tuple-element.10), channel_id=1, source_target_pairs={{0,8},{4,12},{8,0},{12,4},{1,9},{5,13},{9,1},{13,5},{2,10},{6,14},... | collective-permute-start | bytes 393224 | tf_op jit(solution)/shard_map/ppermute | solution.py:25
  46.9 8.4 %collective-permute-start.3 = (bf16[2,64,512]{2,1,0:T(8,128)(2,1)S(1)}, bf16[2,64,512]{2,1,0:T(8,128)(2,1)S(1)}, u32[]{:S(2)}, u32[]{:S(2)}) collective-permute-start(bf16[2,64,512]{2,1,0:T(8,128)(2,1)S(1)} %get-tuple-element.10), channel_id=1, source_target_pairs={{0,4},{4,8},{8,12},{12,0},{1,5},{5,9},{9,13},{13,1},{2,6},{6,10},{... | collective-permute-start | bytes 393224 | tf_op jit(solution)/shard_map/ppermute | solution.py:25
  49.2 6.2 %collective-permute-start.5 = (bf16[2,64,512]{2,1,0:T(8,128)(2,1)S(1)}, bf16[2,64,512]{2,1,0:T(8,128)(2,1)S(1)}, u32[]{:S(2)}, u32[]{:S(2)}) collective-permute-start(bf16[2,64,512]{2,1,0:T(8,128)(2,1)S(1)} %get-tuple-element.10), channel_id=1, source_target_pairs={{0,12},{4,0},{8,4},{12,8},{1,13},{5,1},{9,5},{13,9},{2,14},{6,2},{... | collective-permute-start | bytes 393224 | tf_op jit(solution)/shard_map/ppermute | solution.py:25
  55.5 8.6 %collective-permute-start.6 = (bf16[4,2,64,512]{3,2,1,0:T(8,128)(2,1)S(1)}, bf16[4,2,64,512]{3,2,1,0:T(8,128)(2,1)}, u32[]{:S(2)}, u32[]{:S(2)}) collective-permute-start(bf16[4,2,64,512]{3,2,1,0:T(8,128)(2,1)S(1)} %get-tuple-element.8), channel_id=1, source_target_pairs={{0,1},{1,0},{2,3},{3,2},{4,5},{5,4},{6,7},{7,6},{8,9},{9,8},{10,11... | collective-permute-start | bytes 1572872 | tf_op jit(solution)/shard_map/ppermute | solution.py:25
  69.9 2.6 %copy-start.2 = (bf16[2,4,2,64,512]{4,3,2,1,0:T(8,128)(2,1)S(1)}, bf16[2,4,2,64,512]{4,3,2,1,0:T(8,128)(2,1)}, u32[]{:S(2)}) copy-start(bf16[2,4,2,64,512]{4,3,2,1,0:T(8,128)(2,1)} %pad_maximum_fusion) | copy-start | bytes 3145732
  70.0 15.8 %collective-permute-start.7 = (bf16[4,2,64,512]{3,2,1,0:T(8,128)(2,1)S(1)}, bf16[4,2,64,512]{3,2,1,0:T(8,128)(2,1)}, u32[]{:S(2)}, u32[]{:S(2)}) collective-permute-start(bf16[4,2,64,512]{3,2,1,0:T(8,128)(2,1)S(1)} %bitcast.60), channel_id=1, source_target_pairs={{0,1},{1,0},{2,3},{3,2},{4,5},{5,4},{6,7},{7,6},{8,9},{9,8},{10,11... | collective-permute-start | bytes 1572872 | tf_op jit(solution)/shard_map/ppermute | solution.py:25
  74.0 47.5 %all-to-all-start.2 = ((bf16[16,32,512]{2,1,0:T(8,128)(2,1)}), bf16[16,32,512]{2,1,0:T(8,128)(2,1)}, u32[]{:S(2)}, u32[]{:S(2)}) async-start(bf16[16,32,512]{2,1,0:T(8,128)(2,1)} %convolution_convert_fusion.2), calls=%async_computation.2 | async-start | bytes 1048576 | tf_op jit(solution)/shard_map/all_to_all | solution.py:29
  87.2 10.3 %collective-permute-start.8 = (bf16[2,64,512]{2,1,0:T(8,128)(2,1)S(1)}, bf16[2,64,512]{2,1,0:T(8,128)(2,1)S(1)}, u32[]{:S(2)}, u32[]{:S(2)}) collective-permute-start(bf16[2,64,512]{2,1,0:T(8,128)(2,1)S(1)} %get-tuple-element.4), channel_id=1, source_target_pairs={{0,12},{4,0},{8,4},{12,8},{1,13},{5,1},{9,5},{13,9},{2,14},{6,2},{... | collective-permute-start | bytes 393224 | tf_op jit(solution)/shard_map/ppermute | solution.py:25
  92.4 7.5 %collective-permute-start.10 = (bf16[2,64,512]{2,1,0:T(8,128)(2,1)S(1)}, bf16[2,64,512]{2,1,0:T(8,128)(2,1)S(1)}, u32[]{:S(2)}, u32[]{:S(2)}) collective-permute-start(bf16[2,64,512]{2,1,0:T(8,128)(2,1)S(1)} %get-tuple-element.5), channel_id=1, source_target_pairs={{0,4},{4,8},{8,12},{12,0},{1,5},{5,9},{9,13},{13,1},{2,6},{6,10},{... | collective-permute-start | bytes 393224 | tf_op jit(solution)/shard_map/ppermute | solution.py:25
  94.4 7.9 %collective-permute-start.9 = (bf16[2,64,512]{2,1,0:T(8,128)(2,1)S(1)}, bf16[2,64,512]{2,1,0:T(8,128)(2,1)S(1)}, u32[]{:S(2)}, u32[]{:S(2)}) collective-permute-start(bf16[2,64,512]{2,1,0:T(8,128)(2,1)S(1)} %get-tuple-element.6), channel_id=1, source_target_pairs={{0,8},{4,12},{8,0},{12,4},{1,9},{5,13},{9,1},{13,5},{2,10},{6,14},... | collective-permute-start | bytes 393224 | tf_op jit(solution)/shard_map/ppermute | solution.py:25
  102.4 33.3 %copy-start.1 = (bf16[1536,512]{1,0:T(8,128)(2,1)S(1)}, bf16[1536,512]{1,0:T(8,128)(2,1)}, u32[]{:S(2)}) copy-start(bf16[1536,512]{1,0:T(8,128)(2,1)} %param.8) | copy-start | bytes 4718596
  102.4 5.5 %collective-permute-start.11 = (bf16[64,512]{1,0:T(8,128)(2,1)S(1)}, bf16[64,512]{1,0:T(8,128)(2,1)S(1)}, u32[]{:S(2)}, u32[]{:S(2)}) collective-permute-start(bf16[64,512]{1,0:T(8,128)(2,1)S(1)} %fusion.5), channel_id=1, source_target_pairs={{0,256},{256,0},{1,257},{257,1},{2,258},{258,2},{3,259},{259,3},{4... | collective-permute-start | bytes 196616 | tf_op jit(solution)/shard_map/ppermute | solution.py:25
  108.0 6.9 %collective-permute-start.12 = (bf16[64,512]{1,0:T(8,128)(2,1)S(1)}, bf16[64,512]{1,0:T(8,128)(2,1)S(1)}, u32[]{:S(2)}, u32[]{:S(2)}) collective-permute-start(bf16[64,512]{1,0:T(8,128)(2,1)S(1)} %fusion.2), channel_id=1, source_target_pairs={{0,2},{2,0},{1,3},{3,1},{4,6},{6,4},{5,7},{7,5},{8,10},{10,8},{9,1... | collective-permute-start | bytes 196616 | tf_op jit(solution)/shard_map/ppermute | solution.py:25

commit v3 on v1

v3 whole, which is shorter than its diff:
```python
import jax
import jax.numpy as jnp
from jax import lax
from jax.sharding import Mesh
from jax.sharding import PartitionSpec as P

EPS = 1e-06
BF = jnp.bfloat16
F32 = jnp.float32
AXES = ("ylo", "z", "x", "yhi", "core")
GROUP = ("yhi", "core")
PLANE = ("ylo", "x", "yhi")


def normalize(embed):
    inv = lax.rsqrt(jnp.sum(embed * embed, axis=1, keepdims=True) + EPS)
    return (inv, embed * inv)


def backward(grad, inv, unit):
    along = jnp.sum(grad * unit, axis=1, keepdims=True)
    return (inv * (grad - along * unit)).astype(BF)


def tower_groups(sizes):
    ylo, z, x, yhi, core = sizes

    def at(a, b, c, d, e):
        return (((a * z + b) * x + c) * yhi + d) * core + e

    lines = [[at(a, b, c, d, 0) for b in range(z)] for a in range(ylo) for c in range(x) for d in range(yhi)]
    planes = [[at(a, b, c, d, 1) for a in range(ylo) for c in range(x) for d in range(yhi)] for b in range(z)]
    return lines + planes


def shards(vision, sentence, vision_map, sentence_map, sharpness, offset):
    rows = vision.shape[0]
    width = vision_map.shape[1]
    own = rows // 2
    core, z, plane = (lax.axis_index(a) for a in ("core", "z", PLANE))
    groups = tower_groups([lax.axis_size(a) for a in AXES])
    peers = len(groups[0])
    t = sharpness[0]
    shift = offset[0]

    def meet(parts):
        return lax.all_to_all(parts, AXES, 0, 0, axis_index_groups=groups)

    parts = jnp.stack(
        [
            jnp.dot(vision, vision_map, preferred_element_type=F32).astype(BF).reshape(2, own, width),
            jnp.dot(sentence, sentence_map, preferred_element_type=F32).astype(BF).reshape(2, own, width),
        ],
        axis=1,
    ).reshape(4, own, width)
    embed = jnp.sum(lax.all_to_all(parts, GROUP, 0, 0).astype(F32), axis=0)
    inv, unit = normalize(embed)

    mine = meet(jnp.broadcast_to(unit.astype(BF)[None], (peers, own, width))).reshape(peers * own, width)
    other = lax.ppermute(mine, "core", [(0, 1), (1, 0)])
    logits = t * lax.dot_general(mine, other, (((1,), (1,)), ((), ())), preferred_element_type=F32) + shift
    mine_at = lax.broadcasted_iota(jnp.int32, logits.shape, 0) - jnp.where(core == 0, z, plane) * own
    other_at = lax.broadcasted_iota(jnp.int32, logits.shape, 1) - jnp.where(core == 0, plane, z) * own
    positive = (mine_at == other_at) & (mine_at >= 0) & (mine_at < own)
    sign = jnp.where(positive, F32(1.0), F32(-1.0))
    coef = (t * -sign * jax.nn.sigmoid(-sign * logits)).astype(BF)
    grad = jnp.dot(coef, other, preferred_element_type=F32).astype(BF)

    grad = jnp.sum(meet(grad.reshape(peers, own, width)).astype(F32), axis=0)
    delta = lax.all_gather(backward(grad, inv, unit), GROUP, axis=0).reshape(2, 2, own, width)
    image_grad = lax.dot_general(
        delta[:, 0].reshape(rows, width), vision_map, (((1,), (1,)), ((), ())), preferred_element_type=F32
    ).astype(BF)
    text_grad = lax.dot_general(
        delta[:, 1].reshape(rows, width), sentence_map, (((1,), (1,)), ((), ())), preferred_element_type=F32
    ).astype(BF)
    return (image_grad, text_grad)


def solution(mesh):
    x, ylo = 4, 2
    z = mesh.shape["dp"] // (x * ylo)
    fine = Mesh(mesh.devices.reshape(ylo, z, x, 2, 2), AXES)
    dp, mp = ("ylo", "z", "x"), ("yhi", "core")
    in_specs = (P(dp, mp), P(dp, mp), P(mp, None), P(mp, None), P(), P())
    out_specs = (P(dp, mp), P(dp, mp))
    return jax.shard_map(shards, mesh=fine, in_specs=in_specs, out_specs=out_specs, check_vma=False)
```

time: 137 us -> 121 us (0.88)
  waiting for transfers between devices: 36.8 us -> 1.27 us
  blocking collectives: 60.1 us -> 75 us
  starting transfers between devices: 24.2 us -> 29.6 us
    all_to_all x3 -> x0, waiting for transfers between devices: 36.8 us -> none  [the longest x2 36.8 us: exchange_sum(): got = lax.all_to_all(parts.astype(BF), axis, 0, 0)]
    all_to_all x1 -> x3, blocking collectives: 15.8 us -> 46.9 us  [the longest x2 31.1 us: meet(): return lax.all_to_all(parts, AXES, 0, 0, axis_index_groups=groups)]
    ppermute x0 -> x1, starting transfers between devices: none -> 29.6 us  [shards(): other = lax.ppermute(mine, 'core', [(0, 1), (1, 0)])]
    all_to_all x3 -> x0, starting transfers between devices: 24.2 us -> none  [the longest x2 19.6 us: exchange_sum(): got = lax.all_to_all(parts.astype(BF), axis, 0, 0)]
    all_gather x2 -> x1, blocking collectives: 44.3 us -> 28.1 us  [shards(): lax.all_gather(backward(grad, inv, unit), GROUP, axis=0)]
    dot_general x7 -> x5, matrix products: 11.7 us -> 10.7 us  [the longest x1 6.21 us: shards(): grad = jnp.dot(coef, other, preferred_element_type=F32).astype(BF)]
  transfers between devices with their start and end apart: 3 -> 1, of which waited for: 2 -> 1; matrix products, arithmetic and copies ran while one was open for 2% -> 0% of each run, Pallas kernels for 0% -> 0%
where the time goes in v3:
time: 121 us
  blocking collectives  75 us (62%)
  starting transfers between devices  29.6 us (24%)
  matrix products  10.7 us (9%)
  between operations  2.07 us (2%)
  local copies, waits for them, and re-layouts  1.51 us (1%)
  waiting for transfers between devices  1.27 us (1%)
    all_to_all x2, blocking collectives, meet(): return lax.all_to_all(parts, AXES, 0, 0, axis_index_groups=groups)  31.1 us
    ppermute x1, starting transfers between devices, shards(): other = lax.ppermute(mine, 'core', [(0, 1), (1, 0)])  29.6 us
    all_gather x1, blocking collectives, shards(): lax.all_gather(backward(grad, inv, unit), GROUP, axis=0)  28.1 us
    all_to_all x1, blocking collectives, shards(): embed = jnp.sum(lax.all_to_all(parts, GROUP, 0, 0).astype(F32), axis=0)  15.8 us
    dot_general x1, matrix products, shards(): grad = jnp.dot(coef, other, preferred_element_type=F32).astype(BF)  6.21 us
  transfers between devices with their start and end apart: 1, of which 1 were waited for; matrix products, arithmetic and copies ran while one was open for 0% of the time, Pallas kernels for 0%

profile of v3, /device:TPU:1, one launch (start us, length us, event | category | flops | bytes accessed | tf_op | source)
XLA Modules:
  0.0 120.9 jit_solution(8990849540521612508)
XLA Ops:
  0.6 0.0 copy-start
  0.6 0.0 copy-start.1
  0.7 0.0 copy-start.2
  0.7 1.4 %copy-done = bf16[1536,512]{1,0:T(8,128)(2,1)S(1)} copy-done((bf16[1536,512]{1,0:T(8,128)(2,1)S(1)}, bf16[1536,512]{1,0:T(8,128)(2,1)}, u32[]{:S(2)}) %copy-start) | copy-done | bytes 1572888
  2.0 1.4 %convolution_convert_fusion.4 = bf16[128,512]{1,0:T(8,128)(2,1)S(1)} fusion(bf16[128,1536]{1,0:T(8,128)(2,1)} %param.6, bf16[1536,512]{1,0:T(8,128)(2,1)S(1)} %copy-done), kind=kOutput, calls=%fused_computation.6 | convolution fusion | flops 201392128 | bytes 2097152 | tf_op jit(solution)/shard_map/dot_general | solution.py:51
  3.4 0.0 copy-done.1
  3.4 0.0 copy-done.2
  3.4 0.4 convolution_convert_fusion.3
  3.9 15.8 %all_to_all.15 = bf16[4,64,512]{2,1,0:T(8,128)(2,1)S(1)} all-to-all(bf16[4,64,512]{2,1,0:T(8,128)(2,1)S(1)} %bitcast.41), channel_id=1, replica_groups=mesh['ylo'=2,'z'=16,'x'=4,'yhi'=2,'core'=2] {'yhi','core'}, dimensions={0} | all-to-all | bytes 524288 | tf_op jit(solution)/shard_map/all_to_all | solution.py:56
  19.7 0.1 multiply_reduce_fusion.1
  19.8 0.1 multiply_convert_fusion.1
  19.9 0.1 broadcast_in_dim.18
  20.0 14.9 %all_to_all.16 = bf16[16,64,512]{2,1,0:T(8,128)(2,1)} all-to-all(bf16[16,64,512]{2,1,0:T(8,128)(2,1)S(1)} %broadcast_in_dim.18), channel_id=1, replica_groups={{0,16,32,48,64,80,96,112,128,144,160,176,192,208,224,240},{2,18,34,50,6..., dimensions={0} | all-to-all | bytes 2097152 | tf_op jit(solution)/shard_map/all_to_all | solution.py:47
  34.9 29.6 %collective-permute-start = (bf16[1024,512]{1,0:T(8,128)(2,1)}, bf16[1024,512]{1,0:T(8,128)(2,1)}, u32[]{:S(2)}, u32[]{:S(2)}) collective-permute-start(bf16[1024,512]{1,0:T(8,128)(2,1)} %bitcast.6), channel_id=1, source_target_pairs={{0,1},{1,0},{2,3},{3,2},{4,5},{5,4},{6,7},{7,6},{8,9},{9,8},{10,11... | collective-permute-start | bytes 3145736 | tf_op jit(solution)/shard_map/ppermute | solution.py:60
  65.9 1.3 %collective-permute-done = bf16[1024,512]{1,0:T(8,128)(2,1)} collective-permute-done((bf16[1024,512]{1,0:T(8,128)(2,1)}, bf16[1024,512]{1,0:T(8,128)(2,1)}, u32[]{:S(2)}, u32[]{:S(2)}) %collective-permute-start) | collective-permute-done | bytes 1048608 | tf_op jit(solution)/shard_map/ppermute | solution.py:60
  67.1 6.2 %convolution_convert_fusion.2 = bf16[1024,512]{1,0:T(8,128)(2,1)} fusion(bf16[1024,512]{1,0:T(8,128)(2,1)} %collective-permute-done, bf16[1024,512]{1,0:T(8,128)(2,1)} %bitcast.6, f32[]{:T(128)} %bitcast.38, s32[1024]{0:T(1024)S(1)} %get-tuple-element.6, f32[]{:T(128)} %bitcast.37, s32[1024]{0:T(1024)S(1)} %get-tuple-element.7, ...), kind=kOutput, calls=%fused_computation.4 | convolution fusion | flops 2162688000 | bytes 3155976 | tf_op jit(solution)/shard_map/dot_general | solution.py:67
  73.3 16.2 %all_to_all.17 = bf16[16,64,512]{2,1,0:T(8,128)(2,1)S(1)} all-to-all(bf16[16,64,512]{2,1,0:T(8,128)(2,1)} %bitcast.40), channel_id=1, replica_groups={{0,16,32,48,64,80,96,112,128,144,160,176,192,208,224,240},{2,18,34,50,6..., dimensions={0} | all-to-all | bytes 2097152 | tf_op jit(solution)/shard_map/all_to_all | solution.py:47
  89.6 0.1 convert_reduce_fusion
  89.7 0.2 multiply_reduce_fusion
  89.9 0.1 fusion.3
  90.0 28.1 %all_gather.4 = bf16[4,64,512]{2,1,0:T(8,128)(2,1)S(1)} all-gather(bf16[1,64,512]{2,1,0:T(8,128)(2,1)S(1)} %fusion.3), channel_id=1, replica_groups=mesh['ylo'=2,'z'=16,'x'=4,'yhi'=2,'core'=2] {'yhi','core'}, dimensions={0}, use_global_device_ids=true | all-gather | bytes 327680 | tf_op jit(solution)/shard_map/all_gather | solution.py:70
  118.1 1.4 %convolution_convert_fusion.1 = bf16[128,1536]{1,0:T(8,128)(2,1)} fusion(bf16[128,512]{1,0:T(8,128)(2,1)S(1)} %bitcast.43, bf16[1536,512]{1,0:T(8,128)(2,1)S(1)} %copy-done), kind=kOutput, calls=%fused_computation.2 | convolution fusion | flops 201523200 | bytes 2097152 | tf_op jit(solution)/shard_map/dot_general | solution.py:71
  119.5 1.4 %convolution_convert_fusion = bf16[128,1536]{1,0:T(8,128)(2,1)} fusion(bf16[128,512]{1,0:T(8,128)(2,1)S(1)} %bitcast.42, bf16[1536,512]{1,0:T(8,128)(2,1)S(1)} %copy-done.1), kind=kOutput, calls=%fused_computation.1 | convolution fusion | flops 201523200 | bytes 2097152 | tf_op jit(solution)/shard_map/dot_general | solution.py:74
  (6 shorter events, 0.1 us)
Async XLA Ops:
  0.6 1.4 %copy-start = (bf16[1536,512]{1,0:T(8,128)(2,1)S(1)}, bf16[1536,512]{1,0:T(8,128)(2,1)}, u32[]{:S(2)}) copy-start(bf16[1536,512]{1,0:T(8,128)(2,1)} %param.8) | copy-start | bytes 4718596
  0.6 2.8 %copy-start.1 = (bf16[1536,512]{1,0:T(8,128)(2,1)S(1)}, bf16[1536,512]{1,0:T(8,128)(2,1)}, u32[]{:S(2)}) copy-start(bf16[1536,512]{1,0:T(8,128)(2,1)} %param.9) | copy-start | bytes 4718596
  0.7 2.8 %copy-start.2 = (bf16[128,1536]{1,0:T(8,128)(2,1)S(1)}, bf16[128,1536]{1,0:T(8,128)(2,1)}, u32[]{:S(2)}) copy-start(bf16[128,1536]{1,0:T(8,128)(2,1)} %param.7) | copy-start | bytes 1179652
  34.9 32.2 %collective-permute-start = (bf16[1024,512]{1,0:T(8,128)(2,1)}, bf16[1024,512]{1,0:T(8,128)(2,1)}, u32[]{:S(2)}, u32[]{:S(2)}) collective-permute-start(bf16[1024,512]{1,0:T(8,128)(2,1)} %bitcast.6), channel_id=1, source_target_pairs={{0,1},{1,0},{2,3},{3,2},{4,5},{5,4},{6,7},{7,6},{8,9},{9,8},{10,11... | collective-permute-start | bytes 3145736 | tf_op jit(solution)/shard_map/ppermute | solution.py:60

commit v4 on v3

v4 whole, which is shorter than its diff:
```python
import math

import jax
import jax.numpy as jnp
import numpy as np
from jax import lax
from jax.sharding import Mesh
from jax.sharding import PartitionSpec as P

EPS = 1e-06
BF = jnp.bfloat16
F32 = jnp.float32
AXES = ("ylo", "zhi", "zlo", "x", "yhi", "core")
GROUP = ("yhi", "core")
DEPTH = (("zhi",), ("zlo",))
PLANE = (("x",), ("ylo", "yhi"))


def normalize(embed):
    inv = lax.rsqrt(jnp.sum(embed * embed, axis=1, keepdims=True) + EPS)
    return (inv, embed * inv)


def backward(grad, inv, unit):
    along = jnp.sum(grad * unit, axis=1, keepdims=True)
    return (inv * (grad - along * unit)).astype(BF)


def tower_groups(sizes, axes_by_core):
    ids = np.arange(math.prod(sizes)).reshape(sizes)
    groups = []
    for core, axes in enumerate(axes_by_core):
        kept = [i for i, name in enumerate(AXES[:-1]) if name not in axes]
        moved = [AXES.index(name) for name in axes]
        members = math.prod(sizes[i] for i in moved)
        groups += ids[..., core].transpose(kept + moved).reshape(-1, members).tolist()
    return groups


def shards(vision, sentence, vision_map, sentence_map, sharpness, offset):
    rows = vision.shape[0]
    width = vision_map.shape[1]
    own = rows // 2
    core = lax.axis_index("core")
    place = [
        jnp.where(core == 0, lax.axis_index(axes[0]), lax.axis_index(axes[1])) for axes in (PLANE, DEPTH)
    ]
    there = [
        jnp.where(core == 0, lax.axis_index(axes[1]), lax.axis_index(axes[0])) for axes in (PLANE, DEPTH)
    ]
    sizes = [lax.axis_size(a) for a in AXES]
    depth, plane = (tower_groups(sizes, axes) for axes in (DEPTH, PLANE))
    deep, wide = len(depth[0]), len(plane[0])
    t = sharpness[0]
    shift = offset[0]

    def meet(parts, groups):
        return lax.all_to_all(parts, AXES, 0, 0, axis_index_groups=groups)

    def gather(block, groups):
        return meet(jnp.broadcast_to(block[None], (len(groups[0]),) + block.shape), groups)

    def scatter(parts, groups):
        return jnp.sum(meet(parts.astype(BF), groups).astype(F32), axis=0)

    parts = jnp.stack(
        [
            jnp.dot(vision, vision_map, preferred_element_type=F32).astype(BF).reshape(2, own, width),
            jnp.dot(sentence, sentence_map, preferred_element_type=F32).astype(BF).reshape(2, own, width),
        ],
        axis=1,
    ).reshape(4, own, width)
    embed = jnp.sum(lax.all_to_all(parts, GROUP, 0, 0).astype(F32), axis=0)
    inv, unit = normalize(embed)

    mine = gather(gather(unit.astype(BF), depth), plane).reshape(wide * deep * own, width)
    other = lax.ppermute(mine, "core", [(0, 1), (1, 0)])
    logits = t * lax.dot_general(mine, other, (((1,), (1,)), ((), ())), preferred_element_type=F32) + shift
    mine_at = lax.broadcasted_iota(jnp.int32, logits.shape, 0) - (place[0] * deep + place[1]) * own
    other_at = lax.broadcasted_iota(jnp.int32, logits.shape, 1) - (there[0] * deep + there[1]) * own
    positive = (mine_at == other_at) & (mine_at >= 0) & (mine_at < own)
    sign = jnp.where(positive, F32(1.0), F32(-1.0))
    coef = (t * -sign * jax.nn.sigmoid(-sign * logits)).astype(BF)
    grad = jnp.dot(coef, other, preferred_element_type=F32)

    grad = scatter(scatter(grad.reshape(wide, deep, own, width), plane), depth)
    delta = lax.all_gather(backward(grad, inv, unit), GROUP, axis=0).reshape(2, 2, own, width)
    image_grad = lax.dot_general(
        delta[:, 0].reshape(rows, width), vision_map, (((1,), (1,)), ((), ())), preferred_element_type=F32
    ).astype(BF)
    text_grad = lax.dot_general(
        delta[:, 1].reshape(rows, width), sentence_map, (((1,), (1,)), ((), ())), preferred_element_type=F32
    ).astype(BF)
    return (image_grad, text_grad)


def solution(mesh):
    x, ylo = 4, 2
    zlo = 4
    zhi = mesh.shape["dp"] // (x * ylo * zlo)
    fine = Mesh(mesh.devices.reshape(ylo, zhi, zlo, x, 2, 2), AXES)
    dp, mp = ("ylo", "zhi", "zlo", "x"), ("yhi", "core")
    in_specs = (P(dp, mp), P(dp, mp), P(mp, None), P(mp, None), P(), P())
    out_specs = (P(dp, mp), P(dp, mp))
    return jax.shard_map(shards, mesh=fine, in_specs=in_specs, out_specs=out_specs, check_vma=False)
```

time: 121 us -> 122 us (level)
  starting transfers between devices: 29.6 us -> 23.7 us
  blocking collectives: 75 us -> 80.7 us
  other arithmetic: 0.71 us -> 2.02 us
    all_to_all x2 -> x4, blocking collectives: 31.1 us -> 47.9 us  [meet(): return lax.all_to_all(parts, AXES, 0, 0, axis_index_groups=groups)]
    all_gather x1, blocking collectives: 28.1 us -> 17 us  [shards(): lax.all_gather(backward(grad, inv, unit), GROUP, axis=0)]
    ppermute x1, starting transfers between devices: 29.6 us -> 23.7 us  [shards(): other = lax.ppermute(mine, 'core', [(0, 1), (1, 0)])]
    reduce_sum x1 -> x2, other arithmetic: 0.15 us -> 1.45 us  [scatter(): return jnp.sum(meet(parts.astype(BF), groups).astype(F32), axis=0)]
where the time goes in v4:
time: 122 us
  blocking collectives  80.7 us (66%)
  starting transfers between devices  23.7 us (19%)
  matrix products  10.7 us (9%)
  between operations  2.09 us (2%)
  other arithmetic  2.02 us (2%)
  local copies, waits for them, and re-layouts  1.53 us (1%)
  waiting for transfers between devices  1.26 us (1%)
    all_to_all x4, blocking collectives, meet(): return lax.all_to_all(parts, AXES, 0, 0, axis_index_groups=groups)  47.9 us
    ppermute x1, starting transfers between devices, shards(): other = lax.ppermute(mine, 'core', [(0, 1), (1, 0)])  23.7 us
    all_gather x1, blocking collectives, shards(): lax.all_gather(backward(grad, inv, unit), GROUP, axis=0)  17 us
    all_to_all x1, blocking collectives, shards(): embed = jnp.sum(lax.all_to_all(parts, GROUP, 0, 0).astype(F32), axis=0)  15.8 us
    dot_general x1, matrix products, shards(): grad = jnp.dot(coef, other, preferred_element_type=F32)  6.23 us
  transfers between devices with their start and end apart: 1, of which 1 were waited for; matrix products, arithmetic and copies ran while one was open for 0% of the time, Pallas kernels for 0%

profile of v4, /device:TPU:1, one launch (start us, length us, event | category | flops | bytes accessed | tf_op | source)
XLA Modules:
  0.0 122.0 jit_solution(16048956439139023775)
XLA Ops:
  0.6 0.0 copy-start
  0.6 0.0 copy-start.1
  0.7 0.0 copy-start.2
  0.7 1.4 %copy-done = bf16[1536,512]{1,0:T(8,128)(2,1)S(1)} copy-done((bf16[1536,512]{1,0:T(8,128)(2,1)S(1)}, bf16[1536,512]{1,0:T(8,128)(2,1)}, u32[]{:S(2)}) %copy-start) | copy-done | bytes 1572888
  2.0 1.4 %convolution_convert_fusion.4 = bf16[128,512]{1,0:T(8,128)(2,1)S(1)} fusion(bf16[128,1536]{1,0:T(8,128)(2,1)} %param.6, bf16[1536,512]{1,0:T(8,128)(2,1)S(1)} %copy-done), kind=kOutput, calls=%fused_computation.5 | convolution fusion | flops 201392128 | bytes 2097152 | tf_op jit(solution)/shard_map/dot_general | solution.py:68
  3.4 0.0 copy-done.1
  3.4 0.0 copy-done.2
  3.4 0.4 convolution_convert_fusion.3
  3.9 15.8 %all_to_all.25 = bf16[4,64,512]{2,1,0:T(8,128)(2,1)S(1)} all-to-all(bf16[4,64,512]{2,1,0:T(8,128)(2,1)S(1)} %bitcast.41), channel_id=1, replica_groups=mesh['ylo'=2,'zhi'=4,'zlo'=4,'x'=4,'yhi'=2,'core'=2] {'yhi','core'}, dimensions={0} | all-to-all | bytes 524288 | tf_op jit(solution)/shard_map/all_to_all | solution.py:73
  19.7 0.1 multiply_reduce_fusion.1
  19.8 0.1 multiply_convert_fusion.1
  19.9 8.4 %all_to_all.26 = bf16[4,64,512]{2,1,0:T(8,128)(2,1)S(1)} all-to-all(bf16[4,64,512]{2,1,0:T(8,128)(2,1)S(1)} %broadcast_in_dim.24), channel_id=1, replica_groups={{0,64,128,192},{2,66,130,194},{4,68,132,196},{6,70,134,198},{8,72,136,2..., dimensions={0} | all-to-all | bytes 524288 | tf_op jit(solution)/shard_map/all_to_all | solution.py:58
  28.3 0.1 broadcast_in_dim.25
  28.4 12.8 %all_to_all.27 = bf16[4,4,64,512]{3,2,1,0:T(8,128)(2,1)} all-to-all(bf16[4,4,64,512]{3,2,1,0:T(8,128)(2,1)S(1)} %broadcast_in_dim.25), channel_id=1, replica_groups={{0,4,8,12},{2,6,10,14},{16,20,24,28},{18,22,26,30},{32,36,40,44},{34,38..., dimensions={0} | all-to-all | bytes 2097152 | tf_op jit(solution)/shard_map/all_to_all | solution.py:58
  41.2 23.7 %collective-permute-start = (bf16[1024,512]{1,0:T(8,128)(2,1)}, bf16[1024,512]{1,0:T(8,128)(2,1)}, u32[]{:S(2)}, u32[]{:S(2)}) collective-permute-start(bf16[1024,512]{1,0:T(8,128)(2,1)} %bitcast.6), channel_id=1, source_target_pairs={{0,1},{1,0},{2,3},{3,2},{4,5},{5,4},{6,7},{7,6},{8,9},{9,8},{10,11... | collective-permute-start | bytes 3145736 | tf_op jit(solution)/shard_map/ppermute | solution.py:77
  66.2 1.3 %collective-permute-done = bf16[1024,512]{1,0:T(8,128)(2,1)} collective-permute-done((bf16[1024,512]{1,0:T(8,128)(2,1)}, bf16[1024,512]{1,0:T(8,128)(2,1)}, u32[]{:S(2)}, u32[]{:S(2)}) %collective-permute-start) | collective-permute-done | bytes 1048608 | tf_op jit(solution)/shard_map/ppermute | solution.py:77
  67.5 6.2 %convolution_convert_fusion.2 = bf16[1024,512]{1,0:T(8,128)(2,1)} fusion(bf16[1024,512]{1,0:T(8,128)(2,1)} %collective-permute-done, bf16[1024,512]{1,0:T(8,128)(2,1)} %bitcast.6, f32[]{:T(128)} %bitcast.38, s32[1024]{0:T(1024)S(1)} %get-tuple-element.6, f32[]{:T(128)} %bitcast.37, s32[1024]{0:T(1024)S(1)} %get-tuple-element.7, ...), kind=kOutput, calls=%fused_computation.3 | convolution fusion | flops 2162688000 | bytes 3155976 | tf_op jit(solution)/shard_map/dot_general | solution.py:84
  73.7 14.1 %all_to_all.28 = bf16[4,4,64,512]{3,2,1,0:T(8,128)(2,1)} all-to-all(bf16[4,4,64,512]{3,2,1,0:T(8,128)(2,1)} %bitcast.40), channel_id=1, replica_groups={{0,4,8,12},{2,6,10,14},{16,20,24,28},{18,22,26,30},{32,36,40,44},{34,38..., dimensions={0} | all-to-all | bytes 2097152 | tf_op jit(solution)/shard_map/all_to_all | solution.py:58
  87.8 1.4 %reduce_sum.54 = bf16[4,64,512]{2,1,0:T(8,128)(2,1)S(1)} reduce(bf16[4,4,64,512]{3,2,1,0:T(8,128)(2,1)} %all_to_all.28, bf16[]{:T(256)} %constant.43.clone.1), dimensions={0}, to_apply=%region_2.3 | reduce | flops 393216 | bytes 1310722 | tf_op jit(solution)/shard_map/reduce_sum | solution.py:64
  89.2 12.7 %all_to_all.29 = bf16[4,64,512]{2,1,0:T(8,128)(2,1)S(1)} all-to-all(bf16[4,64,512]{2,1,0:T(8,128)(2,1)S(1)} %reduce_sum.54), channel_id=1, replica_groups={{0,64,128,192},{2,66,130,194},{4,68,132,196},{6,70,134,198},{8,72,136,2..., dimensions={0} | all-to-all | bytes 524288 | tf_op jit(solution)/shard_map/all_to_all | solution.py:58
  101.9 0.2 multiply_reduce_fusion
  102.1 0.1 fusion.3
  102.2 17.0 %all_gather.4 = bf16[4,64,512]{2,1,0:T(8,128)(2,1)S(1)} all-gather(bf16[1,64,512]{2,1,0:T(8,128)(2,1)S(1)} %fusion.3), channel_id=1, replica_groups=mesh['ylo'=2,'zhi'=4,'zlo'=4,'x'=4,'yhi'=2,'core'=2] {'yhi','core'}, dimensions={0}, use_global_device_ids=true | all-gather | bytes 327680 | tf_op jit(solution)/shard_map/all_gather | solution.py:87
  119.3 1.4 %convolution_convert_fusion.1 = bf16[128,1536]{1,0:T(8,128)(2,1)} fusion(bf16[128,512]{1,0:T(8,128)(2,1)S(1)} %bitcast.43, bf16[1536,512]{1,0:T(8,128)(2,1)S(1)} %copy-done), kind=kOutput, calls=%fused_computation.2 | convolution fusion | flops 201523200 | bytes 2097152 | tf_op jit(solution)/shard_map/dot_general | solution.py:88
  120.6 1.4 %convolution_convert_fusion = bf16[128,1536]{1,0:T(8,128)(2,1)} fusion(bf16[128,512]{1,0:T(8,128)(2,1)S(1)} %bitcast.42, bf16[1536,512]{1,0:T(8,128)(2,1)S(1)} %copy-done.1), kind=kOutput, calls=%fused_computation.1 | convolution fusion | flops 201523200 | bytes 2097152 | tf_op jit(solution)/shard_map/dot_general | solution.py:91
  (8 shorter events, 0.2 us)
Async XLA Ops:
  0.6 1.4 %copy-start = (bf16[1536,512]{1,0:T(8,128)(2,1)S(1)}, bf16[1536,512]{1,0:T(8,128)(2,1)}, u32[]{:S(2)}) copy-start(bf16[1536,512]{1,0:T(8,128)(2,1)} %param.8) | copy-start | bytes 4718596
  0.6 2.8 %copy-start.1 = (bf16[1536,512]{1,0:T(8,128)(2,1)S(1)}, bf16[1536,512]{1,0:T(8,128)(2,1)}, u32[]{:S(2)}) copy-start(bf16[1536,512]{1,0:T(8,128)(2,1)} %param.9) | copy-start | bytes 4718596
  0.7 2.8 %copy-start.2 = (bf16[128,1536]{1,0:T(8,128)(2,1)S(1)}, bf16[128,1536]{1,0:T(8,128)(2,1)}, u32[]{:S(2)}) copy-start(bf16[128,1536]{1,0:T(8,128)(2,1)} %param.7) | copy-start | bytes 1179652
  41.2 26.3 %collective-permute-start = (bf16[1024,512]{1,0:T(8,128)(2,1)}, bf16[1024,512]{1,0:T(8,128)(2,1)}, u32[]{:S(2)}, u32[]{:S(2)}) collective-permute-start(bf16[1024,512]{1,0:T(8,128)(2,1)} %bitcast.6), channel_id=1, source_target_pairs={{0,1},{1,0},{2,3},{3,2},{4,5},{5,4},{6,7},{7,6},{8,9},{9,8},{10,11... | collective-permute-start | bytes 3145736 | tf_op jit(solution)/shard_map/ppermute | solution.py:77

commit v5 on v3

v5 whole, which is shorter than its diff:
```python
import math

import jax
import jax.numpy as jnp
import numpy as np
from jax import lax
from jax.experimental import pallas as pl
from jax.experimental.pallas import tpu as pltpu
from jax.sharding import Mesh
from jax.sharding import PartitionSpec as P

EPS = 1e-06
LOG2E = math.log2(math.e)
BF = jnp.bfloat16
F32 = jnp.float32
MIB = 2**20
AXES = ("ylo", "z", "x", "yhi", "core")
GROUP = ("yhi", "core")
MEET = (("z",), ("ylo", "x", "yhi"))

VMEM = pl.BlockSpec(memory_space=pltpu.VMEM)
SMEM = pl.BlockSpec(memory_space=pltpu.SMEM)
HBM = pl.BlockSpec(memory_space=pltpu.MemorySpace.HBM)


def normalize(embed):
    inv = lax.rsqrt(jnp.sum(embed * embed, axis=1, keepdims=True) + EPS)
    return (inv, embed * inv)


def backward(grad, inv, unit):
    along = jnp.sum(grad * unit, axis=1, keepdims=True)
    return (inv * (grad - along * unit)).astype(BF)


def tower_groups(sizes, axes_by_core):
    ids = np.arange(math.prod(sizes)).reshape(sizes)
    groups = []
    for core, axes in enumerate(axes_by_core):
        kept = [i for i, name in enumerate(AXES[:-1]) if name not in axes]
        moved = [AXES.index(name) for name in axes]
        members = math.prod(sizes[i] for i in moved)
        groups += ids[..., core].transpose(kept + moved).reshape(-1, members).tolist()
    return groups


def heads(vision, sentence, vision_map, sentence_map, chunks=3):
    rows, depth = vision.shape
    width = vision_map.shape[1]
    own, step = rows // 2, depth // chunks

    def kernel(v, s, wv, ws, out, vb, sb, wvb, wsb, sems):
        towers = ((v, wv, vb, wvb), (s, ws, sb, wsb))
        copies = []
        for tower, (x, w, xb, wb) in enumerate(towers):
            for c in range(chunks):
                cut = pl.ds(c * step, step)
                pair = (
                    pltpu.make_async_copy(x.at[:, cut], xb.at[:, cut], sems.at[tower, c, 0]),
                    pltpu.make_async_copy(w.at[cut], wb.at[cut], sems.at[tower, c, 1]),
                )
                for copy in pair:
                    copy.start()
                copies.append(pair)
        for tower, (_, _, xb, wb) in enumerate(towers):
            total = None
            for c in range(chunks):
                for copy in copies[tower * chunks + c]:
                    copy.wait()
                cut = slice(c * step, (c + 1) * step)
                part = jnp.dot(xb[:, cut], wb[cut], preferred_element_type=F32)
                total = part if total is None else total + part
            total = total.astype(BF)
            for half in range(2):
                out[2 * half + tower] = total[half * own : (half + 1) * own]

    return pl.pallas_call(
        kernel,
        out_shape=pltpu.VMEM((4, own, width), BF),
        in_specs=[HBM] * 4,
        out_specs=VMEM,
        scratch_shapes=[
            pltpu.VMEM((rows, depth), BF),
            pltpu.VMEM((rows, depth), BF),
            pltpu.VMEM((depth, width), BF),
            pltpu.VMEM((depth, width), BF),
            pltpu.SemaphoreType.DMA((2, chunks, 2)),
        ],
        compiler_params=pltpu.CompilerParams(vmem_limit_bytes=63 * MIB),
        name="heads",
    )(vision, sentence, vision_map, sentence_map)


def tile(mine, other, scale, place, own, block=256):
    n, width = mine.shape
    m = other.shape[0]
    blocks = n // block

    def kernel(scale_ref, place_ref, mine_ref, other_ref, out_ref):
        t, slope, start = scale_ref[0], scale_ref[1], scale_ref[2]
        first = place_ref[0] // block
        for i in range(blocks):
            at = pl.multiple_of(lax.rem(first + 1 + i, blocks) * block, block)
            dots = lax.dot_general(
                mine_ref[pl.ds(at, block)], other_ref[...], (((1,), (1,)), ((), ())), preferred_element_type=F32
            )
            e = jnp.exp2(dots * slope + start)
            coef = pl.reciprocal(1.0 + e, approx=True)
            if i == blocks - 1:
                col = lax.broadcasted_iota(jnp.int32, (1, m), 1) - place_ref[1]
                row = lax.broadcasted_iota(jnp.int32, (block, 1), 0) + (at - place_ref[0])
                row = jnp.where((row >= 0) & (row < own), row, -m)
                coef = jnp.where(row == col, -e, 1.0) * coef
            sums = jnp.dot(coef.astype(BF), other_ref[...], preferred_element_type=F32)
            out_ref[pl.ds(at, block)] = (t * sums).astype(BF)

    return pl.pallas_call(
        kernel,
        out_shape=pltpu.VMEM((n, width), BF),
        in_specs=[SMEM, SMEM, VMEM, VMEM],
        out_specs=VMEM,
        compiler_params=pltpu.CompilerParams(vmem_limit_bytes=40 * MIB),
        name="tile",
    )(scale, place, mine, other)


def heads_back(delta, vision_map, sentence_map, chunks=3):
    own, width = delta.shape[1:]
    rows, depth = 2 * own, vision_map.shape[0]
    step = depth // chunks

    def kernel(d, wv, ws, image, text, buf, sems):
        copies = []
        for tower, (w, out) in enumerate(((wv, image), (ws, text))):
            x = jnp.concatenate([d[tower], d[2 + tower]], axis=0)
            for c in range(chunks):
                cut = slice(c * step, (c + 1) * step)
                part = lax.dot_general(x, w[cut], (((1,), (1,)), ((), ())), preferred_element_type=F32)
                buf[tower, :, cut] = part.astype(BF)
                copy = pltpu.make_async_copy(buf.at[tower, :, cut], out.at[:, cut], sems.at[tower, c])
                copy.start()
                copies.append(copy)
        for copy in copies:
            copy.wait()

    return pl.pallas_call(
        kernel,
        out_shape=[jax.ShapeDtypeStruct((rows, depth), BF)] * 2,
        in_specs=[VMEM] * 3,
        out_specs=[HBM] * 2,
        scratch_shapes=[pltpu.VMEM((2, rows, depth), BF), pltpu.SemaphoreType.DMA((2, chunks))],
        compiler_params=pltpu.CompilerParams(vmem_limit_bytes=20 * MIB),
        name="heads_back",
    )(delta, vision_map, sentence_map)


def shards(vision, sentence, vision_map, sentence_map, sharpness, offset):
    width = vision_map.shape[1]
    own = vision.shape[0] // 2
    core = lax.axis_index("core")
    at_line, at_plane = (lax.axis_index(axes) * own for axes in MEET)
    place = jnp.where(core == 0, jnp.stack([at_line, at_plane]), jnp.stack([at_plane, at_line]))
    groups = tower_groups([lax.axis_size(a) for a in AXES], MEET)
    peers = len(groups[0])
    t = sharpness[0]
    scale = jnp.stack([t, -LOG2E * t, -LOG2E * offset[0]])

    def meet(parts):
        return lax.all_to_all(parts, AXES, 0, 0, axis_index_groups=groups)

    parts = heads(vision, sentence, vision_map, sentence_map)
    embed = jnp.sum(lax.all_to_all(parts, GROUP, 0, 0).astype(F32), axis=0)
    inv, unit = normalize(embed)

    mine = meet(jnp.broadcast_to(unit.astype(BF)[None], (peers, own, width))).reshape(peers * own, width)
    other = lax.ppermute(mine, "core", [(0, 1), (1, 0)])
    grad = tile(mine, other, scale, place, own)
    grad = jnp.sum(meet(grad.reshape(peers, own, width)).astype(F32), axis=0)
    delta = lax.all_gather(backward(grad, inv, unit), GROUP, axis=0)
    return tuple(heads_back(delta, vision_map, sentence_map))


def solution(mesh):
    x, ylo = 4, 2
    z = mesh.shape["dp"] // (x * ylo)
    fine = Mesh(mesh.devices.reshape(ylo, z, x, 2, 2), AXES)
    dp, mp = ("ylo", "z", "x"), ("yhi", "core")
    in_specs = (P(dp, mp), P(dp, mp), P(mp, None), P(mp, None), P(), P())
    out_specs = (P(dp, mp), P(dp, mp))
    return jax.shard_map(shards, mesh=fine, in_specs=in_specs, out_specs=out_specs, check_vma=False)
```

time: 121 us -> 116 us (0.959)
  matrix products: 10.7 us -> 0 us
  Pallas kernels: 0 us -> 7.46 us
  local copies, waits for them, and re-layouts: 1.51 us -> 0.1 us
    dot_general x5 -> x0, matrix products: 10.7 us -> none  [the longest x1 6.21 us: shards(): grad = jnp.dot(coef, other, preferred_element_type=F32).astype(BF)]
    pallas_call x0 -> x3, Pallas kernels: none -> 7.46 us  [the longest x1 3.16 us: tile(): pl.pallas_call(kernel, out_shape=pltpu.VMEM((n, width), BF), in_specs=[SM...]
    unnamed x6 -> x4, local copies, waits for them, and re-layouts: 1.39 us -> 0.01 us
where the time goes in v5:
time: 116 us
  blocking collectives  74.4 us (64%)
  starting transfers between devices  30.2 us (26%)
  Pallas kernels  7.46 us (6%)
  between operations  2.01 us (2%)
    all_to_all x2, blocking collectives, meet(): return lax.all_to_all(parts, AXES, 0, 0, axis_index_groups=groups)  30.4 us
    ppermute x1, starting transfers between devices, shards(): other = lax.ppermute(mine, 'core', [(0, 1), (1, 0)])  30.2 us
    all_gather x1, blocking collectives, shards(): delta = lax.all_gather(backward(grad, inv, unit), GROUP, axis=0)  28.2 us
    all_to_all x1, blocking collectives, shards(): embed = jnp.sum(lax.all_to_all(parts, GROUP, 0, 0).astype(F32), axis=0)  15.8 us
    pallas_call x1, Pallas kernels, tile(): pl.pallas_call(kernel, out_shape=pltpu.VMEM((n, width), BF), in_specs=[SM...  3.16 us
    pallas_call x1, Pallas kernels, heads(): pl.pallas_call(kernel, out_shape=pltpu.VMEM((4, own, width), BF), in_spec...  2.45 us
  transfers between devices with their start and end apart: 1, of which 1 were waited for; matrix products, arithmetic and copies ran while one was open for 0% of the time, Pallas kernels for 0%

profile of v5, /device:TPU:1, one launch (start us, length us, event | category | flops | bytes accessed | tf_op | source)
XLA Modules:
  0.0 115.8 jit_solution(4140947679052738511)
XLA Ops:
  0.6 2.5 %heads.1 = bf16[4,64,512]{2,1,0:T(8,128)(2,1)S(1)} custom-call(bf16[128,1536]{1,0:T(8,128)(2,1)} %v.1, bf16[128,1536]{1,0:T(8,128)(2,1)} %s.1, bf16[1536,512]{1,0:T(8,128)(2,1)} %wv.3, bf16[1536,512]{1,0:T(8,128)(2,1)} %ws.3), custom_call_target="tpu_custom_call" | custom-call | tf_op jit(solution)/shard_map/heads/pallas_call | solution.py:77
  3.1 15.8 %all_to_all.15 = bf16[4,64,512]{2,1,0:T(8,128)(2,1)S(1)} all-to-all(bf16[4,64,512]{2,1,0:T(8,128)(2,1)S(1)} %heads.1), channel_id=1, replica_groups=mesh['ylo'=2,'z'=16,'x'=4,'yhi'=2,'core'=2] {'yhi','core'}, dimensions={0} | all-to-all | bytes 524288 | tf_op jit(solution)/shard_map/all_to_all | solution.py:172
  18.9 0.1 multiply_reduce_fusion.1
  19.0 0.1 multiply_convert_fusion
  19.1 0.1 broadcast_in_dim.2
  19.2 14.3 %all_to_all.16 = bf16[16,64,512]{2,1,0:T(8,128)(2,1)S(1)} all-to-all(bf16[16,64,512]{2,1,0:T(8,128)(2,1)S(1)} %broadcast_in_dim.2), channel_id=1, replica_groups={{0,16,32,48,64,80,96,112,128,144,160,176,192,208,224,240},{2,18,34,50,6..., dimensions={0} | all-to-all | bytes 2097152 | tf_op jit(solution)/shard_map/all_to_all | solution.py:169
  33.5 30.2 %collective-permute-start = (bf16[1024,512]{1,0:T(8,128)(2,1)S(1)}, bf16[1024,512]{1,0:T(8,128)(2,1)S(1)}, u32[]{:S(2)}, u32[]{:S(2)}) collective-permute-start(bf16[1024,512]{1,0:T(8,128)(2,1)S(1)} %bitcast.16), channel_id=1, source_target_pairs={{0,1},{1,0},{2,3},{3,2},{4,5},{5,4},{6,7},{7,6},{8,9},{9,8},{10,11... | collective-permute-start | bytes 3145736 | tf_op jit(solution)/shard_map/ppermute | solution.py:176
  65.0 0.1 pad_maximum_fusion.scale_ref
  65.0 0.1 broadcast_select_fusion.place_ref
  65.1 0.8 collective-permute-done.other_ref
  65.9 3.2 %tile.1 = bf16[1024,512]{1,0:T(8,128)(2,1)S(1)} custom-call(f32[3]{0:T(128)S(1)} %pad_maximum_fusion.scale_ref, s32[2]{0:T(128)S(1)} %broadcast_select_fusion.place_ref, bf16[1024,512]{1,0:T(8,128)(2,1)S(1)} %bitcast.17, bf16[1024,512]{1,0:T(8,128)(2,1)S(1)} %collective-permute-done.other_ref), custom_call_target="tpu_custom_call" | custom-call | tf_op jit(solution)/shard_map/tile/pallas_call | solution.py:117
  69.1 0.0 copy-start.1
  69.1 16.2 %all_to_all.17 = bf16[16,64,512]{2,1,0:T(8,128)(2,1)S(1)} all-to-all(bf16[16,64,512]{2,1,0:T(8,128)(2,1)S(1)} %bitcast.18), channel_id=1, replica_groups={{0,16,32,48,64,80,96,112,128,144,160,176,192,208,224,240},{2,18,34,50,6..., dimensions={0} | all-to-all | bytes 2097152 | tf_op jit(solution)/shard_map/all_to_all | solution.py:169
  85.3 0.0 copy-start
  85.3 0.1 convert_reduce_fusion
  85.4 0.2 multiply_reduce_fusion
  85.6 0.1 fusion.3
  85.7 28.2 %all_gather.4.d = bf16[4,64,512]{2,1,0:T(8,128)(2,1)S(1)} all-gather(bf16[1,64,512]{2,1,0:T(8,128)(2,1)S(1)} %fusion.3), channel_id=1, replica_groups=mesh['ylo'=2,'z'=16,'x'=4,'yhi'=2,'core'=2] {'yhi','core'}, dimensions={0}, use_global_device_ids=true | all-gather | bytes 327680 | tf_op jit(solution)/shard_map/all_gather | solution.py:179
  113.9 0.0 copy-done.1
  113.9 0.0 copy-done
  113.9 1.8 %heads_back.1 = (bf16[128,1536]{1,0:T(8,128)(2,1)}, bf16[128,1536]{1,0:T(8,128)(2,1)}) custom-call(bf16[4,64,512]{2,1,0:T(8,128)(2,1)S(1)} %all_gather.4.d, bf16[1536,512]{1,0:T(8,128)(2,1)S(1)} %copy-done, bf16[1536,512]{1,0:T(8,128)(2,1)S(1)} %copy-done.1), custom_call_target="tpu_custom_call" | custom-call | tf_op jit(solution)/shard_map/heads_back/pallas_call | solution.py:146
  (2 shorter events, 0.0 us)
Async XLA Ops:
  33.5 32.4 %collective-permute-start = (bf16[1024,512]{1,0:T(8,128)(2,1)S(1)}, bf16[1024,512]{1,0:T(8,128)(2,1)S(1)}, u32[]{:S(2)}, u32[]{:S(2)}) collective-permute-start(bf16[1024,512]{1,0:T(8,128)(2,1)S(1)} %bitcast.16), channel_id=1, source_target_pairs={{0,1},{1,0},{2,3},{3,2},{4,5},{5,4},{6,7},{7,6},{8,9},{9,8},{10,11... | collective-permute-start | bytes 3145736 | tf_op jit(solution)/shard_map/ppermute | solution.py:176
  69.1 44.8 %copy-start.1 = (bf16[1536,512]{1,0:T(8,128)(2,1)S(1)}, bf16[1536,512]{1,0:T(8,128)(2,1)}, u32[]{:S(2)}) copy-start(bf16[1536,512]{1,0:T(8,128)(2,1)} %ws.3) | copy-start | bytes 4718596
  85.3 28.7 %copy-start = (bf16[1536,512]{1,0:T(8,128)(2,1)S(1)}, bf16[1536,512]{1,0:T(8,128)(2,1)}, u32[]{:S(2)}) copy-start(bf16[1536,512]{1,0:T(8,128)(2,1)} %wv.3) | copy-start | bytes 4718596

commit v6 on v5

--- a/solution.py
+++ b/solution.py
@@ -16,7 +16,8 @@
 MIB = 2**20
 AXES = ("ylo", "z", "x", "yhi", "core")
 GROUP = ("yhi", "core")
-MEET = (("z",), ("ylo", "x", "yhi"))
+PLANE = ("ylo", "x", "yhi")
+MEET = (("z",), PLANE)
 
 VMEM = pl.BlockSpec(memory_space=pltpu.VMEM)
 SMEM = pl.BlockSpec(memory_space=pltpu.SMEM)
@@ -26,11 +27,6 @@
 def normalize(embed):
     inv = lax.rsqrt(jnp.sum(embed * embed, axis=1, keepdims=True) + EPS)
     return (inv, embed * inv)
-
-
-def backward(grad, inv, unit):
-    along = jnp.sum(grad * unit, axis=1, keepdims=True)
-    return (inv * (grad - along * unit)).astype(BF)
 
 
 def tower_groups(sizes, axes_by_core):
@@ -47,7 +43,7 @@
 def heads(vision, sentence, vision_map, sentence_map, chunks=3):
     rows, depth = vision.shape
     width = vision_map.shape[1]
-    own, step = rows // 2, depth // chunks
+    own, step = rows // 4, depth // chunks
 
     def kernel(v, s, wv, ws, out, vb, sb, wvb, wsb, sems):
         towers = ((v, wv, vb, wvb), (s, ws, sb, wsb))
@@ -71,12 +67,12 @@
                 part = jnp.dot(xb[:, cut], wb[cut], preferred_element_type=F32)
                 total = part if total is None else total + part
             total = total.astype(BF)
-            for half in range(2):
-                out[2 * half + tower] = total[half * own : (half + 1) * own]
-
-    return pl.pallas_call(
-        kernel,
-        out_shape=pltpu.VMEM((4, own, width), BF),
+            for q in range(4):
+                out[q, :, tower * width : (tower + 1) * width] = total[q * own : (q + 1) * own]
+
+    return pl.pallas_call(
+        kernel,
+        out_shape=pltpu.VMEM((4, own, 2 * width), BF),
         in_specs=[HBM] * 4,
         out_specs=VMEM,
         scratch_shapes=[
@@ -91,37 +87,95 @@
     )(vision, sentence, vision_map, sentence_map)
 
 
-def tile(mine, other, scale, place, own, block=256):
-    n, width = mine.shape
-    m = other.shape[0]
-    blocks = n // block
-
-    def kernel(scale_ref, place_ref, mine_ref, other_ref, out_ref):
-        t, slope, start = scale_ref[0], scale_ref[1], scale_ref[2]
-        first = place_ref[0] // block
-        for i in range(blocks):
-            at = pl.multiple_of(lax.rem(first + 1 + i, blocks) * block, block)
-            dots = lax.dot_general(
-                mine_ref[pl.ds(at, block)], other_ref[...], (((1,), (1,)), ((), ())), preferred_element_type=F32
-            )
+def tile(sharpness, offset, near, far, text, own, block=256):
+    half, width = near.shape
+    n = text.shape[0]
+    members = half // own
+
+    def kernel(t_ref, b_ref, near_ref, far_ref, text_ref, out_ref):
+        t = t_ref[0]
+        slope, start = -LOG2E * t, -LOG2E * b_ref[0]
+        z = lax.axis_index("z")
+        plane = lax.axis_index(PLANE)
+
+        def sums(rows, other, positive=None):
+            dots = lax.dot_general(rows, other, (((1,), (1,)), ((), ())), preferred_element_type=F32)
             e = jnp.exp2(dots * slope + start)
             coef = pl.reciprocal(1.0 + e, approx=True)
-            if i == blocks - 1:
-                col = lax.broadcasted_iota(jnp.int32, (1, m), 1) - place_ref[1]
-                row = lax.broadcasted_iota(jnp.int32, (block, 1), 0) + (at - place_ref[0])
-                row = jnp.where((row >= 0) & (row < own), row, -m)
+            if positive is not None:
+                row = lax.broadcasted_iota(jnp.int32, (block, 1), 0) - positive[0]
+                row = jnp.where((row >= 0) & (row < own), row, -n)
+                col = lax.broadcasted_iota(jnp.int32, (1, other.shape[0]), 1) - positive[1]
                 coef = jnp.where(row == col, -e, 1.0) * coef
-            sums = jnp.dot(coef.astype(BF), other_ref[...], preferred_element_type=F32)
-            out_ref[pl.ds(at, block)] = (t * sums).astype(BF)
-
-    return pl.pallas_call(
-        kernel,
-        out_shape=pltpu.VMEM((n, width), BF),
-        in_specs=[SMEM, SMEM, VMEM, VMEM],
+            return jnp.dot(coef.astype(BF), other, preferred_element_type=F32)
+
+        def turn(blocks, place):
+            for i in range(blocks):
+                at = lax.rem(place // block + 1 + i, blocks) * block
+                yield i == blocks - 1, pl.multiple_of(at, block)
+
+        @pl.when(lax.axis_index("core") == 0)
+        def _():
+            for owner, rows_ref in enumerate((near_ref, far_ref)):
+                for last, at in turn(half // block, z * own):
+                    positive = (z * own - at, (2 * plane + owner) * own) if last else None
+                    total = t * sums(rows_ref[pl.ds(at, block)], text_ref[...], positive)
+                    some = block // own
+                    out_ref[pl.ds(at // own, some), owner] = total.astype(BF).reshape(some, own, width)
+
+        @pl.when(lax.axis_index("core") == 1)
+        def _():
+            for last, at in turn(n // block, 2 * plane * own):
+                rows = text_ref[pl.ds(at, block)]
+                total = 0.0
+                for owner, other_ref in ((1, near_ref), (0, far_ref)):
+                    positive = ((2 * plane + owner) * own - at, z * own) if last else None
+                    total = total + sums(rows, other_ref[:half], positive)
+                some = block // (2 * own)
+                total = (t * total).astype(BF).reshape(some, 2, own, width)
+                out_ref[pl.ds(at // (2 * own), some)] = total
+
+    return pl.pallas_call(
+        kernel,
+        out_shape=pltpu.VMEM((members, 2, own, width), BF),
+        in_specs=[SMEM, SMEM, VMEM, VMEM, VMEM],
         out_specs=VMEM,
         compiler_params=pltpu.CompilerParams(vmem_limit_bytes=40 * MIB),
         name="tile",
-    )(scale, place, mine, other)
+    )(sharpness, offset, near, far, text)
+
+
+def finish(sums, embed, far, own):
+    width = sums.shape[2]
+    tail = far.shape[0] - 4 * own
+
+    def kernel(sums_ref, embed_ref, far_ref, out_ref):
+        def piece(i):
+            return far_ref[tail + i * own : tail + (i + 1) * own].astype(F32)
+
+        for core in range(2):
+
+            @pl.when(lax.axis_index("core") == core)
+            def _():
+                for owner in range(2):
+                    if owner == core:
+                        rows = embed_ref[:, core * width : (core + 1) * width]
+                    else:
+                        rows = piece(2 * core) + piece(2 * core + 1)
+                    inv, unit = normalize(rows)
+                    at = slice(owner * own, (owner + 1) * own)
+                    grad = jnp.sum(sums_ref[:, at].astype(F32), axis=0)
+                    along = jnp.sum(grad * unit, axis=1, keepdims=True)
+                    out_ref[at] = (inv * (grad - along * unit)).astype(BF)
+
+    return pl.pallas_call(
+        kernel,
+        out_shape=pltpu.VMEM((2 * own, width), BF),
+        in_specs=[VMEM] * 3,
+        out_specs=VMEM,
+        compiler_params=pltpu.CompilerParams(vmem_limit_bytes=20 * MIB),
+        name="finish",
+    )(sums, embed, far)
 
 
 def heads_back(delta, vision_map, sentence_map, chunks=3):
@@ -156,27 +210,28 @@
 
 def shards(vision, sentence, vision_map, sentence_map, sharpness, offset):
     width = vision_map.shape[1]
-    own = vision.shape[0] // 2
-    core = lax.axis_index("core")
-    at_line, at_plane = (lax.axis_index(axes) * own for axes in MEET)
-    place = jnp.where(core == 0, jnp.stack([at_line, at_plane]), jnp.stack([at_plane, at_line]))
+    own = vision.shape[0] // 4
     groups = tower_groups([lax.axis_size(a) for a in AXES], MEET)
     peers = len(groups[0])
-    t = sharpness[0]
-    scale = jnp.stack([t, -LOG2E * t, -LOG2E * offset[0]])
-
-    def meet(parts):
-        return lax.all_to_all(parts, AXES, 0, 0, axis_index_groups=groups)
 
     parts = heads(vision, sentence, vision_map, sentence_map)
     embed = jnp.sum(lax.all_to_all(parts, GROUP, 0, 0).astype(F32), axis=0)
-    inv, unit = normalize(embed)
-
-    mine = meet(jnp.broadcast_to(unit.astype(BF)[None], (peers, own, width))).reshape(peers * own, width)
-    other = lax.ppermute(mine, "core", [(0, 1), (1, 0)])
-    grad = tile(mine, other, scale, place, own)
-    grad = jnp.sum(meet(grad.reshape(peers, own, width)).astype(F32), axis=0)
-    delta = lax.all_gather(backward(grad, inv, unit), GROUP, axis=0)
+    img, txt = embed[:, :width], embed[:, width:]
+    img_b, txt_b = (normalize(e)[1].astype(BF) for e in (img, txt))
+
+    text = jnp.broadcast_to(txt_b[None], (2 * peers, own, width))
+    text, img_b = lax.optimization_barrier((text, img_b))
+    text = lax.all_to_all(text, PLANE + ("core",), 0, 0).reshape(-1, width)
+    near = lax.all_gather(img_b, "z", axis=0, tiled=True)
+    terms = []
+    for e in (img, txt):
+        first = e.astype(BF)
+        terms += [first, (e - first.astype(F32)).astype(BF)]
+    far = lax.ppermute(jnp.concatenate([near] + terms), "core", [(0, 1), (1, 0)])
+    grad = tile(sharpness, offset, near, far, text, own)
+
+    grad = lax.all_to_all(grad.reshape(peers, 2 * own, width), AXES, 0, 0, axis_index_groups=groups)
+    delta = lax.all_gather(finish(grad, embed, far, own), GROUP, axis=0)
     return tuple(heads_back(delta, vision_map, sentence_map))
 
 

time: 116 us -> 114 us (0.983)
  starting transfers between devices: 30.2 us -> 12.9 us
  blocking collectives: 74.4 us -> 89.7 us
    all_gather x1 -> x2, blocking collectives: 28.2 us -> 55.4 us  [the longest x1 29.8 us: shards(): near = lax.all_gather(img_b, 'z', axis=0, tiled=True)]
    ppermute x1, starting transfers between devices: 30.2 us -> 8.32 us  [shards(): lax.ppermute(jnp.concatenate([near] + terms), 'core', [(0, 1), (1, 0)])]
    all_to_all x2 -> x1, blocking collectives: 30.4 us -> 18.5 us  [shards(): lax.all_to_all(grad.reshape(peers, 2 * own, width), AXES, 0, 0, axis_inde...]
    all_to_all x0 -> x1, starting transfers between devices: none -> 4.62 us  [shards(): text = lax.all_to_all(text, PLANE + ('core',), 0, 0).reshape(-1, width)]
    pallas_call x2 -> x3, Pallas kernels: 5.61 us -> 5.68 us  [the longest x1 2.98 us: tile(): pl.pallas_call(kernel, out_shape=pltpu.VMEM((members, 2, own, width), BF)...]
  transfers between devices with their start and end apart: 1 -> 2, of which waited for: 1 -> 1; matrix products, arithmetic and copies ran while one was open for 0% -> 0% of each run, Pallas kernels for 0% -> 0%
where the time goes in v6:
time: 114 us
  blocking collectives  89.7 us (79%)
  starting transfers between devices  12.9 us (11%)
  Pallas kernels  7.54 us (7%)
  between operations  2.02 us (2%)
  local copies, waits for them, and re-layouts  1.17 us (1%)
    all_gather x1, blocking collectives, shards(): near = lax.all_gather(img_b, 'z', axis=0, tiled=True)  29.8 us
    all_gather x1, blocking collectives, shards(): delta = lax.all_gather(finish(grad, embed, far, own), GROUP, axis=0)  25.7 us
    all_to_all x1, blocking collectives, shards(): lax.all_to_all(grad.reshape(peers, 2 * own, width), AXES, 0, 0, axis_inde...  18.5 us
    all_to_all x1, blocking collectives, shards(): embed = jnp.sum(lax.all_to_all(parts, GROUP, 0, 0).astype(F32), axis=0)  15.8 us
    ppermute x1, starting transfers between devices, shards(): lax.ppermute(jnp.concatenate([near] + terms), 'core', [(0, 1), (1, 0)])  8.32 us
    all_to_all x1, starting transfers between devices, shards(): text = lax.all_to_all(text, PLANE + ('core',), 0, 0).reshape(-1, width)  4.62 us
    pallas_call x1, Pallas kernels, tile(): pl.pallas_call(kernel, out_shape=pltpu.VMEM((members, 2, own, width), BF)...  2.98 us
    pallas_call x1, Pallas kernels, heads(): pl.pallas_call(kernel, out_shape=pltpu.VMEM((4, own, 2 * width), BF), in_...  2.45 us
  transfers between devices with their start and end apart: 2, of which 1 were waited for; matrix products, arithmetic and copies ran while one was open for 0% of the time, Pallas kernels for 0%

profile of v6, /device:TPU:1, one launch (start us, length us, event | category | flops | bytes accessed | tf_op | source)
XLA Modules:
  0.0 114.0 jit_solution(16091327886688620493)
XLA Ops:
  0.6 2.5 %heads.1 = bf16[4,32,1024]{2,1,0:T(8,128)(2,1)S(1)} custom-call(bf16[128,1536]{1,0:T(8,128)(2,1)} %v.1, bf16[128,1536]{1,0:T(8,128)(2,1)} %s.1, bf16[1536,512]{1,0:T(8,128)(2,1)} %wv.3, bf16[1536,512]{1,0:T(8,128)(2,1)} %ws.3), custom_call_target="tpu_custom_call" | custom-call | tf_op jit(solution)/shard_map/heads/pallas_call | solution.py:73
  3.1 15.8 %all_to_all.15 = bf16[4,32,1024]{2,1,0:T(8,128)(2,1)S(1)} all-to-all(bf16[4,32,1024]{2,1,0:T(8,128)(2,1)S(1)} %heads.1), channel_id=1, replica_groups=mesh['ylo'=2,'z'=16,'x'=4,'yhi'=2,'core'=2] {'yhi','core'}, dimensions={0} | all-to-all | bytes 524288 | tf_op jit(solution)/shard_map/all_to_all | solution.py:218
  18.9 0.1 multiply_reduce_fusion
  19.0 0.1 multiply_convert_fusion
  19.1 1.1 broadcast_in_dim.2
  20.2 4.6 %all-to-all-start.1 = ((bf16[32,32,512]{2,1,0:T(8,128)(2,1)}), bf16[32,32,512]{2,1,0:T(8,128)(2,1)S(1)}, u32[]{:S(2)}, u32[]{:S(2)}) async-start(bf16[32,32,512]{2,1,0:T(8,128)(2,1)} %broadcast_in_dim.2), calls=%async_computation.1 | async-start | bytes 2097152 | tf_op jit(solution)/shard_map/all_to_all | solution.py:224
  24.9 29.8 %all_gather.9.near_ref = bf16[512,512]{1,0:T(8,128)(2,1)S(1)} all-gather(bf16[32,512]{1,0:T(8,128)(2,1)S(1)} %get-tuple-element.4), channel_id=1, replica_groups=mesh['ylo'=2,'z'=16,'x'=4,'yhi'=2,'core'=2] {'z'}, dimensions={0}, use_global_device_ids=true | all-gather | bytes 557056 | tf_op jit(solution)/shard_map/all_gather | solution.py:225
  54.7 8.3 %collective-permute-start = (bf16[640,512]{1,0:T(8,128)(2,1)S(1)}, bf16[640,512]{1,0:T(8,128)(2,1)S(1)}, u32[]{:S(2)}, u32[]{:S(2)}) collective-permute-start(bf16[640,512]{1,0:T(8,128)(2,1)S(1)} %fusion.1), channel_id=1, source_target_pairs={{0,1},{1,0},{2,3},{3,2},{4,5},{5,4},{6,7},{7,6},{8,9},{9,8},{10,11... | collective-permute-start | bytes 1966088 | tf_op jit(solution)/shard_map/ppermute | solution.py:230
  64.3 0.4 collective-permute-done.far_ref
  64.7 0.0 all-to-all-done.1
  64.8 3.0 %tile.1 = bf16[16,2,32,512]{3,2,1,0:T(8,128)(2,1)S(1)} custom-call(f32[1]{0:T(128)S(6)} %copy.12.t_ref, f32[1]{0:T(128)S(6)} %copy.13.b_ref, bf16[512,512]{1,0:T(8,128)(2,1)S(1)} %all_gather.9.near_ref, bf16[640,512]{1,0:T(8,128)(2,1)S(1)} %collective-permute-done.far_ref, bf16[1024,512]{1,0:T(8,128)(2,1)S(1)} %bitcast.3), custom_call_target="tpu_custom_call" | custom-call | tf_op jit(solution)/shard_map/tile/pallas_call | solution.py:138
  67.7 0.0 copy-start.1
  67.8 18.5 %all_to_all.16.sums_ref = bf16[16,64,512]{2,1,0:T(8,128)(2,1)S(1)} all-to-all(bf16[16,64,512]{2,1,0:T(8,128)(2,1)S(1)} %bitcast.4), channel_id=1, replica_groups={{0,16,32,48,64,80,96,112,128,144,160,176,192,208,224,240},{2,18,34,50,6..., dimensions={0} | all-to-all | bytes 2097152 | tf_op jit(solution)/shard_map/all_to_all | solution.py:233
  86.2 0.0 copy-start
  86.2 0.2 finish.1
  86.5 25.7 %all-gather = bf16[256,512]{1,0:T(8,128)(2,1)S(1)} all-gather(bf16[64,512]{1,0:T(8,128)(2,1)S(1)} %finish.1), channel_id=2, replica_groups=mesh['ylo'=2,'z'=16,'x'=4,'yhi'=2,'core'=2] {'yhi','core'}, dimensions={0}, use_global_device_ids=true | all-gather | bytes 327680 | tf_op jit(solution)/shard_map/all_gather | solution.py:234
  112.2 0.0 copy-done.1
  112.2 0.0 copy-done
  112.2 1.9 %heads_back.1 = (bf16[128,1536]{1,0:T(8,128)(2,1)}, bf16[128,1536]{1,0:T(8,128)(2,1)}) custom-call(bf16[4,64,512]{2,1,0:T(8,128)(2,1)S(1)} %bitcast.5, bf16[1536,512]{1,0:T(8,128)(2,1)S(1)} %copy-done, bf16[1536,512]{1,0:T(8,128)(2,1)S(1)} %copy-done.1), custom_call_target="tpu_custom_call" | custom-call | tf_op jit(solution)/shard_map/heads_back/pallas_call | solution.py:200
  (7 shorter events, 0.1 us)
Async XLA Ops:
  20.2 44.5 %all-to-all-start.1 = ((bf16[32,32,512]{2,1,0:T(8,128)(2,1)}), bf16[32,32,512]{2,1,0:T(8,128)(2,1)S(1)}, u32[]{:S(2)}, u32[]{:S(2)}) async-start(bf16[32,32,512]{2,1,0:T(8,128)(2,1)} %broadcast_in_dim.2), calls=%async_computation.1 | async-start | bytes 2097152 | tf_op jit(solution)/shard_map/all_to_all | solution.py:224
  54.7 10.0 %collective-permute-start = (bf16[640,512]{1,0:T(8,128)(2,1)S(1)}, bf16[640,512]{1,0:T(8,128)(2,1)S(1)}, u32[]{:S(2)}, u32[]{:S(2)}) collective-permute-start(bf16[640,512]{1,0:T(8,128)(2,1)S(1)} %fusion.1), channel_id=1, source_target_pairs={{0,1},{1,0},{2,3},{3,2},{4,5},{5,4},{6,7},{7,6},{8,9},{9,8},{10,11... | collective-permute-start | bytes 1966088 | tf_op jit(solution)/shard_map/ppermute | solution.py:230
  67.7 44.4 %copy-start.1 = (bf16[1536,512]{1,0:T(8,128)(2,1)S(1)}, bf16[1536,512]{1,0:T(8,128)(2,1)}, u32[]{:S(2)}) copy-start(bf16[1536,512]{1,0:T(8,128)(2,1)} %ws.3) | copy-start | bytes 4718596
  86.2 25.9 %copy-start = (bf16[1536,512]{1,0:T(8,128)(2,1)S(1)}, bf16[1536,512]{1,0:T(8,128)(2,1)}, u32[]{:S(2)}) copy-start(bf16[1536,512]{1,0:T(8,128)(2,1)} %wv.3) | copy-start | bytes 4718596

commit v7 on v5

--- a/solution.py
+++ b/solution.py
@@ -14,9 +14,10 @@
 BF = jnp.bfloat16
 F32 = jnp.float32
 MIB = 2**20
-AXES = ("ylo", "z", "x", "yhi", "core")
+AXES = ("ylo", "zhi", "zlo", "x", "yhi", "core")
+LINE = ("zhi", "zlo")
+PLANE = ("ylo", "x", "yhi")
 GROUP = ("yhi", "core")
-MEET = (("z",), ("ylo", "x", "yhi"))
 
 VMEM = pl.BlockSpec(memory_space=pltpu.VMEM)
 SMEM = pl.BlockSpec(memory_space=pltpu.SMEM)
@@ -28,20 +29,14 @@
     return (inv, embed * inv)
 
 
-def backward(grad, inv, unit):
-    along = jnp.sum(grad * unit, axis=1, keepdims=True)
-    return (inv * (grad - along * unit)).astype(BF)
-
-
-def tower_groups(sizes, axes_by_core):
+def from_line(sizes, steps):
     ids = np.arange(math.prod(sizes)).reshape(sizes)
-    groups = []
-    for core, axes in enumerate(axes_by_core):
-        kept = [i for i, name in enumerate(AXES[:-1]) if name not in axes]
-        moved = [AXES.index(name) for name in axes]
-        members = math.prod(sizes[i] for i in moved)
-        groups += ids[..., core].transpose(kept + moved).reshape(-1, members).tolist()
-    return groups
+    pairs = []
+    for core, step in enumerate(steps):
+        target = ids[..., core].transpose(1, 2, 0, 3, 4).reshape(sizes[1] * sizes[2], -1)
+        source = np.roll(target, -step, axis=0)
+        pairs += zip(source.ravel().tolist(), target.ravel().tolist())
+    return pairs
 
 
 def heads(vision, sentence, vision_map, sentence_map, chunks=3):
@@ -72,11 +67,11 @@
                 total = part if total is None else total + part
             total = total.astype(BF)
             for half in range(2):
-                out[2 * half + tower] = total[half * own : (half + 1) * own]
-
-    return pl.pallas_call(
-        kernel,
-        out_shape=pltpu.VMEM((4, own, width), BF),
+                out[half, :, tower * width : (tower + 1) * width] = total[half * own : (half + 1) * own]
+
+    return pl.pallas_call(
+        kernel,
+        out_shape=pltpu.VMEM((2, own, 2 * width), BF),
         in_specs=[HBM] * 4,
         out_specs=VMEM,
         scratch_shapes=[
@@ -91,25 +86,79 @@
     )(vision, sentence, vision_map, sentence_map)
 
 
-def tile(mine, other, scale, place, own, block=256):
+def chip_sums(parts):
+    _, _, own, width = parts.shape
+
+    def kernel(parts_ref, given_ref, kept_ref):
+        for yhi in range(2):
+
+            @pl.when(lax.axis_index("yhi") == yhi)
+            def _():
+                total = [parts_ref[0, h].astype(F32) + parts_ref[1, h].astype(F32) for h in (yhi, 1 - yhi)]
+                kept_ref[...] = total[0]
+                given_ref[...] = total[1].astype(BF)
+
+    return pl.pallas_call(
+        kernel,
+        out_shape=[pltpu.VMEM((own, width), BF), pltpu.VMEM((own, width), F32)],
+        in_specs=[VMEM],
+        out_specs=[VMEM, VMEM],
+        compiler_params=pltpu.CompilerParams(vmem_limit_bytes=20 * MIB),
+        name="chip_sums",
+    )(parts)
+
+
+def units(kept, got, peers):
+    own, width = kept.shape[0], kept.shape[1] // 2
+
+    def kernel(kept_ref, got_ref, wide_ref, line_ref, embed_ref):
+        towers = [slice(0, width), slice(width, 2 * width)]
+        for yhi in range(2):
+            for core in range(2):
+
+                @pl.when((lax.axis_index("yhi") == yhi) & (lax.axis_index("core") == core))
+                def _():
+                    embed = [kept_ref[:, cut] + got_ref[1 - yhi, :, cut].astype(F32) for cut in towers]
+                    embed_ref[...] = embed[core]
+                    mine = normalize(embed[core])[1].astype(BF)
+                    for peer in range(peers):
+                        wide_ref[peer] = mine
+                    line_ref[...] = normalize(embed[1 - core])[1].astype(BF)
+
+    return pl.pallas_call(
+        kernel,
+        out_shape=[
+            pltpu.VMEM((peers, own, width), BF),
+            pltpu.VMEM((own, width), BF),
+            pltpu.VMEM((own, width), F32),
+        ],
+        in_specs=[VMEM] * 2,
+        out_specs=[VMEM] * 3,
+        compiler_params=pltpu.CompilerParams(vmem_limit_bytes=20 * MIB),
+        name="units",
+    )(kept, got)
+
+
+def tile(sharpness, offset, mine, other, own, block=256):
     n, width = mine.shape
     m = other.shape[0]
     blocks = n // block
 
-    def kernel(scale_ref, place_ref, mine_ref, other_ref, out_ref):
-        t, slope, start = scale_ref[0], scale_ref[1], scale_ref[2]
-        first = place_ref[0] // block
+    def kernel(t_ref, b_ref, mine_ref, other_ref, out_ref):
+        t = t_ref[0]
+        slope, start = -LOG2E * t, -LOG2E * b_ref[0]
+        mine_at, other_at = lax.axis_index(PLANE) * own, lax.axis_index("zhi") * own
         for i in range(blocks):
-            at = pl.multiple_of(lax.rem(first + 1 + i, blocks) * block, block)
+            at = pl.multiple_of(lax.rem(mine_at // block + 1 + i, blocks) * block, block)
             dots = lax.dot_general(
                 mine_ref[pl.ds(at, block)], other_ref[...], (((1,), (1,)), ((), ())), preferred_element_type=F32
             )
             e = jnp.exp2(dots * slope + start)
             coef = pl.reciprocal(1.0 + e, approx=True)
             if i == blocks - 1:
-                col = lax.broadcasted_iota(jnp.int32, (1, m), 1) - place_ref[1]
-                row = lax.broadcasted_iota(jnp.int32, (block, 1), 0) + (at - place_ref[0])
+                row = lax.broadcasted_iota(jnp.int32, (block, 1), 0) + (at - mine_at)
                 row = jnp.where((row >= 0) & (row < own), row, -m)
+                col = lax.broadcasted_iota(jnp.int32, (1, m), 1) - other_at
                 coef = jnp.where(row == col, -e, 1.0) * coef
             sums = jnp.dot(coef.astype(BF), other_ref[...], preferred_element_type=F32)
             out_ref[pl.ds(at, block)] = (t * sums).astype(BF)
@@ -121,7 +170,24 @@
         out_specs=VMEM,
         compiler_params=pltpu.CompilerParams(vmem_limit_bytes=40 * MIB),
         name="tile",
-    )(scale, place, mine, other)
+    )(sharpness, offset, mine, other)
+
+
+def finish(sums, embed):
+    def kernel(sums_ref, embed_ref, out_ref):
+        inv, unit = normalize(embed_ref[...])
+        grad = jnp.sum(sums_ref[...].astype(F32), axis=0)
+        along = jnp.sum(grad * unit, axis=1, keepdims=True)
+        out_ref[...] = (inv * (grad - along * unit)).astype(BF)
+
+    return pl.pallas_call(
+        kernel,
+        out_shape=pltpu.VMEM(embed.shape, BF),
+        in_specs=[VMEM] * 2,
+        out_specs=VMEM,
+        compiler_params=pltpu.CompilerParams(vmem_limit_bytes=20 * MIB),
+        name="finish",
+    )(sums, embed)
 
 
 def heads_back(delta, vision_map, sentence_map, chunks=3):
@@ -157,34 +223,29 @@
 def shards(vision, sentence, vision_map, sentence_map, sharpness, offset):
     width = vision_map.shape[1]
     own = vision.shape[0] // 2
-    core = lax.axis_index("core")
-    at_line, at_plane = (lax.axis_index(axes) * own for axes in MEET)
-    place = jnp.where(core == 0, jnp.stack([at_line, at_plane]), jnp.stack([at_plane, at_line]))
-    groups = tower_groups([lax.axis_size(a) for a in AXES], MEET)
-    peers = len(groups[0])
-    t = sharpness[0]
-    scale = jnp.stack([t, -LOG2E * t, -LOG2E * offset[0]])
-
-    def meet(parts):
-        return lax.all_to_all(parts, AXES, 0, 0, axis_index_groups=groups)
-
-    parts = heads(vision, sentence, vision_map, sentence_map)
-    embed = jnp.sum(lax.all_to_all(parts, GROUP, 0, 0).astype(F32), axis=0)
-    inv, unit = normalize(embed)
-
-    mine = meet(jnp.broadcast_to(unit.astype(BF)[None], (peers, own, width))).reshape(peers * own, width)
-    other = lax.ppermute(mine, "core", [(0, 1), (1, 0)])
-    grad = tile(mine, other, scale, place, own)
-    grad = jnp.sum(meet(grad.reshape(peers, own, width)).astype(F32), axis=0)
-    delta = lax.all_gather(backward(grad, inv, unit), GROUP, axis=0)
+    sizes = [lax.axis_size(a) for a in AXES]
+    peers = lax.axis_size(PLANE)
+
+    parts = lax.all_gather(heads(vision, sentence, vision_map, sentence_map), "core", axis=0)
+    given, kept = chip_sums(parts)
+    wide, line, embed = units(kept, lax.all_gather(given, "yhi", axis=0), peers)
+
+    wide, line = lax.optimization_barrier((wide, line))
+    mine = lax.all_to_all(wide, PLANE, 0, 0).reshape(peers * own, width)
+    line = lax.all_gather(line, "zhi", axis=0, tiled=True)
+    near = [lax.ppermute(line, AXES, from_line(sizes, steps)) for steps in ((1, 1), (-1, -1), (2, -2))]
+    grad = tile(sharpness, offset, mine, jnp.concatenate([line] + near), own)
+
+    grad = lax.all_to_all(grad.reshape(peers, own, width), PLANE, 0, 0)
+    delta = lax.all_gather(finish(grad, embed), GROUP, axis=0)
     return tuple(heads_back(delta, vision_map, sentence_map))
 
 
 def solution(mesh):
-    x, ylo = 4, 2
-    z = mesh.shape["dp"] // (x * ylo)
-    fine = Mesh(mesh.devices.reshape(ylo, z, x, 2, 2), AXES)
-    dp, mp = ("ylo", "z", "x"), ("yhi", "core")
+    x, ylo, zlo = 4, 2, 4
+    zhi = mesh.shape["dp"] // (x * ylo * zlo)
+    fine = Mesh(mesh.devices.reshape(ylo, zhi, zlo, x, 2, 2), AXES)
+    dp, mp = ("ylo", "zhi", "zlo", "x"), ("yhi", "core")
     in_specs = (P(dp, mp), P(dp, mp), P(mp, None), P(mp, None), P(), P())
     out_specs = (P(dp, mp), P(dp, mp))
     return jax.shard_map(shards, mesh=fine, in_specs=in_specs, out_specs=out_specs, check_vma=False)

time: 116 us -> 101 us (0.87)
  starting transfers between devices: 30.2 us -> 13.2 us
  waiting for transfers between devices: 0.8 us -> 7.23 us
  blocking collectives: 74.4 us -> 70.1 us
    all_to_all x3 -> x1, blocking collectives: 46.2 us -> 21.4 us  [shards(): grad = lax.all_to_all(grad.reshape(peers, own, width), PLANE, 0, 0)]
    ppermute x1 -> x3, starting transfers between devices: 30.2 us -> 9.51 us  [shards(): lax.ppermute(line, AXES, from_line(sizes, steps))]
    all_gather x1 -> x4, blocking collectives: 28.2 us -> 48.7 us  [the longest x1 22.6 us: shards(): line = lax.all_gather(line, 'zhi', axis=0, tiled=True)]
    ppermute x1 -> x3, waiting for transfers between devices: 0.8 us -> 7.23 us  [shards(): lax.ppermute(line, AXES, from_line(sizes, steps))]
    all_to_all x0 -> x1, starting transfers between devices: none -> 3.65 us  [shards(): mine = lax.all_to_all(wide, PLANE, 0, 0).reshape(peers * own, width)]
    pallas_call x1 -> x4, Pallas kernels: 2.45 us -> 3.89 us  [the longest x1 2.45 us: heads(): pl.pallas_call(kernel, out_shape=pltpu.VMEM((2, own, 2 * width), BF), in_...]
  transfers between devices with their start and end apart: 1 -> 4, of which waited for: 1 -> 3; matrix products, arithmetic and copies ran while one was open for 0% -> 0% of each run, Pallas kernels for 0% -> 0%
where the time goes in v7:
time: 101 us
  blocking collectives  70.1 us (69%)
  starting transfers between devices  13.2 us (13%)
  Pallas kernels  8.36 us (8%)
  waiting for transfers between devices  7.23 us (7%)
  between operations  2.01 us (2%)
    all_gather x1, blocking collectives, shards(): line = lax.all_gather(line, 'zhi', axis=0, tiled=True)  22.6 us
    all_to_all x1, blocking collectives, shards(): grad = lax.all_to_all(grad.reshape(peers, own, width), PLANE, 0, 0)  21.4 us
    all_gather x1, blocking collectives, shards(): delta = lax.all_gather(finish(grad, embed), GROUP, axis=0)  10.5 us
    ppermute x3, starting transfers between devices, shards(): lax.ppermute(line, AXES, from_line(sizes, steps))  9.51 us
    all_gather x1, blocking collectives, shards(): lax.all_gather(heads(vision, sentence, vision_map, sentence_map), 'core',...  8.69 us
    ppermute x3, waiting for transfers between devices, shards(): lax.ppermute(line, AXES, from_line(sizes, steps))  7.23 us
    all_gather x1, blocking collectives, shards(): wide, line, embed = units(kept, lax.all_gather(given, 'yhi', axis=0), peers)  6.89 us
    all_to_all x1, starting transfers between devices, shards(): mine = lax.all_to_all(wide, PLANE, 0, 0).reshape(peers * own, width)  3.65 us
  transfers between devices with their start and end apart: 4, of which 3 were waited for; matrix products, arithmetic and copies ran while one was open for 0% of the time, Pallas kernels for 0%

profile of v7, /device:TPU:1, one launch (start us, length us, event | category | flops | bytes accessed | tf_op | source)
XLA Modules:
  0.0 100.9 jit_solution(9152415279510447595)
XLA Ops:
  0.6 2.5 %heads.1 = bf16[2,64,1024]{2,1,0:T(8,128)(2,1)S(1)} custom-call(bf16[128,1536]{1,0:T(8,128)(2,1)} %v.1, bf16[128,1536]{1,0:T(8,128)(2,1)} %s.1, bf16[1536,512]{1,0:T(8,128)(2,1)} %wv.3, bf16[1536,512]{1,0:T(8,128)(2,1)} %ws.3), custom_call_target="tpu_custom_call" | custom-call | tf_op jit(solution)/shard_map/heads/pallas_call | solution.py:72
  3.1 8.7 %all-gather = bf16[4,64,1024]{2,1,0:T(8,128)(2,1)S(1)} all-gather(bf16[2,64,1024]{2,1,0:T(8,128)(2,1)S(1)} %heads.1), channel_id=2, replica_groups=mesh['ylo'=2,'zhi'=4,'zlo'=4,'x'=4,'yhi'=2,'core'=2] {'core'}, dimensions={0}, use_global_device_ids=true | all-gather | bytes 786432 | tf_op jit(solution)/shard_map/all_gather | solution.py:229
  11.8 0.1 chip_sums.1
  11.8 6.9 %all-gather.1 = bf16[128,1024]{1,0:T(8,128)(2,1)S(1)} all-gather(bf16[64,1024]{1,0:T(8,128)(2,1)S(1)} %get-tuple-element.10), channel_id=3, replica_groups=mesh['ylo'=2,'zhi'=4,'zlo'=4,'x'=4,'yhi'=2,'core'=2] {'yhi'}, dimensions={0}, use_global_device_ids=true | all-gather | bytes 393216 | tf_op jit(solution)/shard_map/all_gather | solution.py:231
  18.7 1.1 %units.1 = (bf16[16,64,512]{2,1,0:T(8,128)(2,1)}, bf16[64,512]{1,0:T(8,128)(2,1)S(1)}, f32[64,512]{1,0:T(8,128)S(1)}) custom-call(f32[64,1024]{1,0:T(8,128)S(1)} %get-tuple-element.9.kept_ref, bf16[2,64,1024]{2,1,0:T(8,128)(2,1)S(1)} %bitcast.8), custom_call_target="tpu_custom_call" | custom-call | tf_op jit(solution)/shard_map/units/pallas_call | solution.py:128
  19.9 3.7 %all-to-all-start = ((bf16[16,64,512]{2,1,0:T(8,128)(2,1)}), bf16[16,64,512]{2,1,0:T(8,128)(2,1)S(1)}, u32[]{:S(2)}, u32[]{:S(2)}) async-start(bf16[16,64,512]{2,1,0:T(8,128)(2,1)} %get-tuple-element.13), calls=%async_computation | async-start | bytes 2097152 | tf_op jit(solution)/shard_map/all_to_all | solution.py:234
  23.5 22.6 %all_gather.25 = bf16[256,512]{1,0:T(8,128)(2,1)S(1)} all-gather(bf16[64,512]{1,0:T(8,128)(2,1)S(1)} %get-tuple-element.14), channel_id=1, replica_groups=mesh['ylo'=2,'zhi'=4,'zlo'=4,'x'=4,'yhi'=2,'core'=2] {'zhi'}, dimensions={0}, use_global_device_ids=true | all-gather | bytes 327680 | tf_op jit(solution)/shard_map/all_gather | solution.py:235
  46.1 3.0 %collective-permute-start.2 = (bf16[256,512]{1,0:T(8,128)(2,1)S(1)}, bf16[256,512]{1,0:T(8,128)(2,1)S(1)}, u32[]{:S(2)}, u32[]{:S(2)}) collective-permute-start(bf16[256,512]{1,0:T(8,128)(2,1)S(1)} %all_gather.25), channel_id=1, source_target_pairs={{32,0},{34,2},{36,4},{38,6},{40,8},{42,10},{44,12},{46,14},{288,25... | collective-permute-start | bytes 786440 | tf_op jit(solution)/shard_map/ppermute | solution.py:236
  49.2 2.7 %collective-permute-start.1 = (bf16[256,512]{1,0:T(8,128)(2,1)S(1)}, bf16[256,512]{1,0:T(8,128)(2,1)S(1)}, u32[]{:S(2)}, u32[]{:S(2)}) collective-permute-start(bf16[256,512]{1,0:T(8,128)(2,1)S(1)} %all_gather.25), channel_id=1, source_target_pairs={{240,0},{242,2},{244,4},{246,6},{248,8},{250,10},{252,12},{254,14}... | collective-permute-start | bytes 786440 | tf_op jit(solution)/shard_map/ppermute | solution.py:236
  51.8 3.8 %collective-permute-start = (bf16[256,512]{1,0:T(8,128)(2,1)S(1)}, bf16[256,512]{1,0:T(8,128)(2,1)S(1)}, u32[]{:S(2)}, u32[]{:S(2)}) collective-permute-start(bf16[256,512]{1,0:T(8,128)(2,1)S(1)} %all_gather.25), channel_id=1, source_target_pairs={{16,0},{18,2},{20,4},{22,6},{24,8},{26,10},{28,12},{30,14},{272,25... | collective-permute-start | bytes 786440 | tf_op jit(solution)/shard_map/ppermute | solution.py:236
  57.0 0.1 collective-permute-done.2
  57.1 5.2 %collective-permute-done.1 = bf16[256,512]{1,0:T(8,128)(2,1)S(1)} collective-permute-done((bf16[256,512]{1,0:T(8,128)(2,1)S(1)}, bf16[256,512]{1,0:T(8,128)(2,1)S(1)}, u32[]{:S(2)}, u32[]{:S(2)}) %collective-permute-start.1) | collective-permute-done | bytes 262176 | tf_op jit(solution)/shard_map/ppermute | solution.py:236
  62.2 2.0 %collective-permute-done = bf16[256,512]{1,0:T(8,128)(2,1)S(1)} collective-permute-done((bf16[256,512]{1,0:T(8,128)(2,1)S(1)}, bf16[256,512]{1,0:T(8,128)(2,1)S(1)}, u32[]{:S(2)}, u32[]{:S(2)}) %collective-permute-start) | collective-permute-done | bytes 262176 | tf_op jit(solution)/shard_map/ppermute | solution.py:236
  64.2 0.1 pad_maximum_fusion.other_ref
  64.3 0.0 all-to-all-done
  64.3 2.6 %tile.1 = bf16[1024,512]{1,0:T(8,128)(2,1)S(1)} custom-call(f32[1]{0:T(128)S(6)} %copy.8.t_ref, f32[1]{0:T(128)S(6)} %copy.9.b_ref, bf16[1024,512]{1,0:T(8,128)(2,1)S(1)} %bitcast.5, bf16[1024,512]{1,0:T(8,128)(2,1)S(1)} %pad_maximum_fusion.other_ref), custom_call_target="tpu_custom_call" | custom-call | tf_op jit(solution)/shard_map/tile/pallas_call | solution.py:166
  66.9 0.0 copy-start
  66.9 0.0 copy-start.1
  66.9 21.4 %all_to_all.10.sums_ref = bf16[16,64,512]{2,1,0:T(8,128)(2,1)S(1)} all-to-all(bf16[16,64,512]{2,1,0:T(8,128)(2,1)S(1)} %bitcast.6), channel_id=1, replica_groups=mesh['ylo'=2,'zhi'=4,'zlo'=4,'x'=4,'yhi'=2,'core'=2] {'ylo','x','yhi'}, dimensions={0} | all-to-all | bytes 2097152 | tf_op jit(solution)/shard_map/all_to_all | solution.py:239
  88.3 0.2 finish.1
  88.5 10.5 %all-gather.2 = bf16[256,512]{1,0:T(8,128)(2,1)S(1)} all-gather(bf16[64,512]{1,0:T(8,128)(2,1)S(1)} %finish.1), channel_id=4, replica_groups=mesh['ylo'=2,'zhi'=4,'zlo'=4,'x'=4,'yhi'=2,'core'=2] {'yhi','core'}, dimensions={0}, use_global_device_ids=true | all-gather | bytes 327680 | tf_op jit(solution)/shard_map/all_gather | solution.py:240
  99.1 0.0 copy-done
  99.1 0.0 copy-done.1
  99.1 1.9 %heads_back.1 = (bf16[128,1536]{1,0:T(8,128)(2,1)}, bf16[128,1536]{1,0:T(8,128)(2,1)}) custom-call(bf16[4,64,512]{2,1,0:T(8,128)(2,1)S(1)} %bitcast.9, bf16[1536,512]{1,0:T(8,128)(2,1)S(1)} %copy-done, bf16[1536,512]{1,0:T(8,128)(2,1)S(1)} %copy-done.1), custom_call_target="tpu_custom_call" | custom-call | tf_op jit(solution)/shard_map/heads_back/pallas_call | solution.py:212
Async XLA Ops:
  19.9 44.4 %all-to-all-start = ((bf16[16,64,512]{2,1,0:T(8,128)(2,1)}), bf16[16,64,512]{2,1,0:T(8,128)(2,1)S(1)}, u32[]{:S(2)}, u32[]{:S(2)}) async-start(bf16[16,64,512]{2,1,0:T(8,128)(2,1)} %get-tuple-element.13), calls=%async_computation | async-start | bytes 2097152 | tf_op jit(solution)/shard_map/all_to_all | solution.py:234
  46.1 10.9 %collective-permute-start.2 = (bf16[256,512]{1,0:T(8,128)(2,1)S(1)}, bf16[256,512]{1,0:T(8,128)(2,1)S(1)}, u32[]{:S(2)}, u32[]{:S(2)}) collective-permute-start(bf16[256,512]{1,0:T(8,128)(2,1)S(1)} %all_gather.25), channel_id=1, source_target_pairs={{32,0},{34,2},{36,4},{38,6},{40,8},{42,10},{44,12},{46,14},{288,25... | collective-permute-start | bytes 786440 | tf_op jit(solution)/shard_map/ppermute | solution.py:236
  49.2 13.1 %collective-permute-start.1 = (bf16[256,512]{1,0:T(8,128)(2,1)S(1)}, bf16[256,512]{1,0:T(8,128)(2,1)S(1)}, u32[]{:S(2)}, u32[]{:S(2)}) collective-permute-start(bf16[256,512]{1,0:T(8,128)(2,1)S(1)} %all_gather.25), channel_id=1, source_target_pairs={{240,0},{242,2},{244,4},{246,6},{248,8},{250,10},{252,12},{254,14}... | collective-permute-start | bytes 786440 | tf_op jit(solution)/shard_map/ppermute | solution.py:236
  51.8 12.4 %collective-permute-start = (bf16[256,512]{1,0:T(8,128)(2,1)S(1)}, bf16[256,512]{1,0:T(8,128)(2,1)S(1)}, u32[]{:S(2)}, u32[]{:S(2)}) collective-permute-start(bf16[256,512]{1,0:T(8,128)(2,1)S(1)} %all_gather.25), channel_id=1, source_target_pairs={{16,0},{18,2},{20,4},{22,6},{24,8},{26,10},{28,12},{30,14},{272,25... | collective-permute-start | bytes 786440 | tf_op jit(solution)/shard_map/ppermute | solution.py:236
  66.9 32.2 %copy-start = (bf16[1536,512]{1,0:T(8,128)(2,1)S(1)}, bf16[1536,512]{1,0:T(8,128)(2,1)}, u32[]{:S(2)}) copy-start(bf16[1536,512]{1,0:T(8,128)(2,1)} %wv.3) | copy-start | bytes 4718596
  66.9 32.2 %copy-start.1 = (bf16[1536,512]{1,0:T(8,128)(2,1)S(1)}, bf16[1536,512]{1,0:T(8,128)(2,1)}, u32[]{:S(2)}) copy-start(bf16[1536,512]{1,0:T(8,128)(2,1)} %ws.3) | copy-start | bytes 4718596

commit v8 on v7

--- a/solution.py
+++ b/solution.py
@@ -15,9 +15,9 @@
 F32 = jnp.float32
 MIB = 2**20
 AXES = ("ylo", "zhi", "zlo", "x", "yhi", "core")
-LINE = ("zhi", "zlo")
-PLANE = ("ylo", "x", "yhi")
 GROUP = ("yhi", "core")
+SUMS = (("ylo", "x", "yhi"), ("x", "zlo"))
+RING = (("zhi", "zlo"), ("yhi", "ylo"))
 
 VMEM = pl.BlockSpec(memory_space=pltpu.VMEM)
 SMEM = pl.BlockSpec(memory_space=pltpu.SMEM)
@@ -29,13 +29,30 @@
     return (inv, embed * inv)
 
 
-def from_line(sizes, steps):
+def device_groups(sizes, axes_by_core, flip=False):
+    ids = np.arange(math.prod(sizes)).reshape(sizes)
+    groups = []
+    for core, axes in enumerate(axes_by_core):
+        kept = [i for i, name in enumerate(AXES[:-1]) if name not in axes]
+        moved = [AXES.index(name) for name in axes]
+        members = math.prod(sizes[i] for i in moved)
+        part = ids[..., core].transpose(kept + moved).reshape(-1, members)
+        groups += (part[:, ::-1] if flip and core == 1 else part).tolist()
+    return groups
+
+
+def from_ring(sizes, step):
     ids = np.arange(math.prod(sizes)).reshape(sizes)
     pairs = []
-    for core, step in enumerate(steps):
-        target = ids[..., core].transpose(1, 2, 0, 3, 4).reshape(sizes[1] * sizes[2], -1)
-        source = np.roll(target, -step, axis=0)
-        pairs += zip(source.ravel().tolist(), target.ravel().tolist())
+    for core, axes in enumerate(RING):
+        kept = [i for i, name in enumerate(AXES[:-1]) if name not in axes]
+        moved = [AXES.index(name) for name in axes]
+        places = math.prod(sizes[i] for i in moved)
+        target = ids[..., core].transpose(moved + kept).reshape(places, -1)
+        for place in range(places):
+            back = step == 2 and place % 2 == 1
+            source = target[(place + (-step if back else step)) % places]
+            pairs += zip(source.tolist(), target[place].tolist())
     return pairs
 
 
@@ -147,7 +164,10 @@
     def kernel(t_ref, b_ref, mine_ref, other_ref, out_ref):
         t = t_ref[0]
         slope, start = -LOG2E * t, -LOG2E * b_ref[0]
-        mine_at, other_at = lax.axis_index(PLANE) * own, lax.axis_index("zhi") * own
+        zhi, last = lax.axis_index("zhi"), lax.axis_size("zhi") - 1
+        first_core = lax.axis_index("core") == 0
+        mine_at = jnp.where(first_core, lax.axis_index(SUMS[0]), lax.axis_index(SUMS[1])) * own
+        other_at = jnp.where(first_core, zhi, last - zhi) * own
         for i in range(blocks):
             at = pl.multiple_of(lax.rem(mine_at // block + 1 + i, blocks) * block, block)
             dots = lax.dot_general(
@@ -224,19 +244,24 @@
     width = vision_map.shape[1]
     own = vision.shape[0] // 2
     sizes = [lax.axis_size(a) for a in AXES]
-    peers = lax.axis_size(PLANE)
+    groups = device_groups(sizes, SUMS)
+    peers = len(groups[0])
+
+    def meet(x):
+        return lax.all_to_all(x, AXES, 0, 0, axis_index_groups=groups)
 
     parts = lax.all_gather(heads(vision, sentence, vision_map, sentence_map), "core", axis=0)
     given, kept = chip_sums(parts)
     wide, line, embed = units(kept, lax.all_gather(given, "yhi", axis=0), peers)
 
     wide, line = lax.optimization_barrier((wide, line))
-    mine = lax.all_to_all(wide, PLANE, 0, 0).reshape(peers * own, width)
-    line = lax.all_gather(line, "zhi", axis=0, tiled=True)
-    near = [lax.ppermute(line, AXES, from_line(sizes, steps)) for steps in ((1, 1), (-1, -1), (2, -2))]
+    mine = meet(wide).reshape(peers * own, width)
+    far = device_groups(sizes, (("zhi",), ("zhi",)), flip=True)
+    line = lax.all_gather(line, AXES, axis=0, tiled=True, axis_index_groups=far)
+    near = [lax.ppermute(line, AXES, from_ring(sizes, step)) for step in (1, -1, 2)]
     grad = tile(sharpness, offset, mine, jnp.concatenate([line] + near), own)
 
-    grad = lax.all_to_all(grad.reshape(peers, own, width), PLANE, 0, 0)
+    grad = meet(grad.reshape(peers, own, width))
     delta = lax.all_gather(finish(grad, embed), GROUP, axis=0)
     return tuple(heads_back(delta, vision_map, sentence_map))
 

time: 101 us -> 106 us (1.050)
  blocking collectives: 70.1 us -> 78.5 us
  waiting for transfers between devices: 7.23 us -> 1.99 us
  starting transfers between devices: 13.2 us -> 15 us
    all_to_all x1, blocking collectives: 21.4 us -> 28.2 us  [meet(): return lax.all_to_all(x, AXES, 0, 0, axis_index_groups=groups)]
    ppermute x3, waiting for transfers between devices: 7.23 us -> 1.99 us  [shards(): lax.ppermute(line, AXES, from_ring(sizes, step))]
    all_gather x1, blocking collectives: 22.6 us -> 27.3 us  [shards(): line = lax.all_gather(line, AXES, axis=0, tiled=True, axis_index_groups=far)]
    all_gather x1, blocking collectives: 10.5 us -> 7.36 us  [shards(): delta = lax.all_gather(finish(grad, embed), GROUP, axis=0)]
    ppermute x3, starting transfers between devices: 9.51 us -> 11.4 us  [shards(): lax.ppermute(line, AXES, from_ring(sizes, step))]
  transfers between devices with their start and end apart: 4 -> 4, of which waited for: 3 -> 2; matrix products, arithmetic and copies ran while one was open for 0% -> 0% of each run, Pallas kernels for 0% -> 0%
where the time goes in v8:
time: 106 us
  blocking collectives  78.5 us (74%)
  starting transfers between devices  15 us (14%)
  Pallas kernels  8.37 us (8%)
  between operations  2.02 us (2%)
  waiting for transfers between devices  1.99 us (2%)
    all_to_all x1, blocking collectives, meet(): return lax.all_to_all(x, AXES, 0, 0, axis_index_groups=groups)  28.2 us
    all_gather x1, blocking collectives, shards(): line = lax.all_gather(line, AXES, axis=0, tiled=True, axis_index_groups=far)  27.3 us
    ppermute x3, starting transfers between devices, shards(): lax.ppermute(line, AXES, from_ring(sizes, step))  11.4 us
    all_gather x1, blocking collectives, shards(): lax.all_gather(heads(vision, sentence, vision_map, sentence_map), 'core',...  8.69 us
    all_gather x1, blocking collectives, shards(): delta = lax.all_gather(finish(grad, embed), GROUP, axis=0)  7.36 us
    all_gather x1, blocking collectives, shards(): wide, line, embed = units(kept, lax.all_gather(given, 'yhi', axis=0), peers)  6.89 us
    all_to_all x1, starting transfers between devices, meet(): return lax.all_to_all(x, AXES, 0, 0, axis_index_groups=groups)  3.65 us
    pallas_call x1, Pallas kernels, tile(): pl.pallas_call(kernel, out_shape=pltpu.VMEM((n, width), BF), in_specs=[SM...  2.62 us
  transfers between devices with their start and end apart: 4, of which 2 were waited for; matrix products, arithmetic and copies ran while one was open for 0% of the time, Pallas kernels for 0%

profile of v8, /device:TPU:1, one launch (start us, length us, event | category | flops | bytes accessed | tf_op | source)
XLA Modules:
  0.0 105.9 jit_solution(10788206177935356037)
XLA Ops:
  0.6 2.5 %heads.1 = bf16[2,64,1024]{2,1,0:T(8,128)(2,1)S(1)} custom-call(bf16[128,1536]{1,0:T(8,128)(2,1)} %v.1, bf16[128,1536]{1,0:T(8,128)(2,1)} %s.1, bf16[1536,512]{1,0:T(8,128)(2,1)} %wv.3, bf16[1536,512]{1,0:T(8,128)(2,1)} %ws.3), custom_call_target="tpu_custom_call" | custom-call | tf_op jit(solution)/shard_map/heads/pallas_call | solution.py:89
  3.1 8.7 %all-gather = bf16[4,64,1024]{2,1,0:T(8,128)(2,1)S(1)} all-gather(bf16[2,64,1024]{2,1,0:T(8,128)(2,1)S(1)} %heads.1), channel_id=2, replica_groups=mesh['ylo'=2,'zhi'=4,'zlo'=4,'x'=4,'yhi'=2,'core'=2] {'core'}, dimensions={0}, use_global_device_ids=true | all-gather | bytes 786432 | tf_op jit(solution)/shard_map/all_gather | solution.py:253
  11.8 0.1 chip_sums.1
  11.8 6.9 %all-gather.1 = bf16[128,1024]{1,0:T(8,128)(2,1)S(1)} all-gather(bf16[64,1024]{1,0:T(8,128)(2,1)S(1)} %get-tuple-element.10), channel_id=3, replica_groups=mesh['ylo'=2,'zhi'=4,'zlo'=4,'x'=4,'yhi'=2,'core'=2] {'yhi'}, dimensions={0}, use_global_device_ids=true | all-gather | bytes 393216 | tf_op jit(solution)/shard_map/all_gather | solution.py:255
  18.7 1.1 %units.1 = (bf16[16,64,512]{2,1,0:T(8,128)(2,1)}, bf16[64,512]{1,0:T(8,128)(2,1)S(1)}, f32[64,512]{1,0:T(8,128)S(1)}) custom-call(f32[64,1024]{1,0:T(8,128)S(1)} %get-tuple-element.9.kept_ref, bf16[2,64,1024]{2,1,0:T(8,128)(2,1)S(1)} %bitcast.8), custom_call_target="tpu_custom_call" | custom-call | tf_op jit(solution)/shard_map/units/pallas_call | solution.py:145
  19.9 3.7 %all-to-all-start = ((bf16[16,64,512]{2,1,0:T(8,128)(2,1)}), bf16[16,64,512]{2,1,0:T(8,128)(2,1)S(1)}, u32[]{:S(2)}, u32[]{:S(2)}) async-start(bf16[16,64,512]{2,1,0:T(8,128)(2,1)} %get-tuple-element.13), calls=%async_computation | async-start | bytes 2097152 | tf_op jit(solution)/shard_map/all_to_all | solution.py:251
  23.5 27.3 %all_gather.25 = bf16[256,512]{1,0:T(8,128)(2,1)S(1)} all-gather(bf16[64,512]{1,0:T(8,128)(2,1)S(1)} %get-tuple-element.14), channel_id=1, replica_groups={{0,64,128,192},{2,66,130,194},{4,68,132,196},{6,70,134,198},{8,72,136,2..., dimensions={0}, use_global_device_ids=true | all-gather | bytes 327680 | tf_op jit(solution)/shard_map/all_gather | solution.py:260
  50.8 4.9 %collective-permute-start.2 = (bf16[256,512]{1,0:T(8,128)(2,1)S(1)}, bf16[256,512]{1,0:T(8,128)(2,1)S(1)}, u32[]{:S(2)}, u32[]{:S(2)}) collective-permute-start(bf16[256,512]{1,0:T(8,128)(2,1)S(1)} %all_gather.25), channel_id=1, source_target_pairs={{32,0},{34,2},{36,4},{38,6},{40,8},{42,10},{44,12},{46,14},{288,25... | collective-permute-start | bytes 786440 | tf_op jit(solution)/shard_map/ppermute | solution.py:261
  55.7 2.3 %collective-permute-start.1 = (bf16[256,512]{1,0:T(8,128)(2,1)S(1)}, bf16[256,512]{1,0:T(8,128)(2,1)S(1)}, u32[]{:S(2)}, u32[]{:S(2)}) collective-permute-start(bf16[256,512]{1,0:T(8,128)(2,1)S(1)} %all_gather.25), channel_id=1, source_target_pairs={{240,0},{242,2},{244,4},{246,6},{248,8},{250,10},{252,12},{254,14}... | collective-permute-start | bytes 786440 | tf_op jit(solution)/shard_map/ppermute | solution.py:261
  58.0 4.1 %collective-permute-start = (bf16[256,512]{1,0:T(8,128)(2,1)S(1)}, bf16[256,512]{1,0:T(8,128)(2,1)S(1)}, u32[]{:S(2)}, u32[]{:S(2)}) collective-permute-start(bf16[256,512]{1,0:T(8,128)(2,1)S(1)} %all_gather.25), channel_id=1, source_target_pairs={{16,0},{18,2},{20,4},{22,6},{24,8},{26,10},{28,12},{30,14},{272,25... | collective-permute-start | bytes 786440 | tf_op jit(solution)/shard_map/ppermute | solution.py:261
  63.5 0.0 collective-permute-done.2
  63.5 0.8 collective-permute-done.1
  64.3 1.2 %collective-permute-done = bf16[256,512]{1,0:T(8,128)(2,1)S(1)} collective-permute-done((bf16[256,512]{1,0:T(8,128)(2,1)S(1)}, bf16[256,512]{1,0:T(8,128)(2,1)S(1)}, u32[]{:S(2)}, u32[]{:S(2)}) %collective-permute-start) | collective-permute-done | bytes 262176 | tf_op jit(solution)/shard_map/ppermute | solution.py:261
  65.5 0.1 pad_maximum_fusion.other_ref
  65.6 0.0 all-to-all-done
  65.6 2.6 %tile.1 = bf16[1024,512]{1,0:T(8,128)(2,1)S(1)} custom-call(f32[1]{0:T(128)S(6)} %copy.8.t_ref, f32[1]{0:T(128)S(6)} %copy.9.b_ref, bf16[1024,512]{1,0:T(8,128)(2,1)S(1)} %bitcast.5, bf16[1024,512]{1,0:T(8,128)(2,1)S(1)} %pad_maximum_fusion.other_ref), custom_call_target="tpu_custom_call" | custom-call | tf_op jit(solution)/shard_map/tile/pallas_call | solution.py:186
  68.2 0.0 copy-start
  68.2 0.0 copy-start.1
  68.2 28.2 %all_to_all.10.sums_ref = bf16[16,64,512]{2,1,0:T(8,128)(2,1)S(1)} all-to-all(bf16[16,64,512]{2,1,0:T(8,128)(2,1)S(1)} %bitcast.6), channel_id=1, replica_groups={{0,2,4,6,8,10,12,14,256,258,260,262,264,266,268,270},{16,18,20,22,24,26..., dimensions={0} | all-to-all | bytes 2097152 | tf_op jit(solution)/shard_map/all_to_all | solution.py:251
  96.5 0.2 finish.1
  96.7 7.4 %all-gather.2 = bf16[256,512]{1,0:T(8,128)(2,1)S(1)} all-gather(bf16[64,512]{1,0:T(8,128)(2,1)S(1)} %finish.1), channel_id=4, replica_groups=mesh['ylo'=2,'zhi'=4,'zlo'=4,'x'=4,'yhi'=2,'core'=2] {'yhi','core'}, dimensions={0}, use_global_device_ids=true | all-gather | bytes 327680 | tf_op jit(solution)/shard_map/all_gather | solution.py:265
  104.1 0.0 copy-done
  104.1 0.0 copy-done.1
  104.1 1.9 %heads_back.1 = (bf16[128,1536]{1,0:T(8,128)(2,1)}, bf16[128,1536]{1,0:T(8,128)(2,1)}) custom-call(bf16[4,64,512]{2,1,0:T(8,128)(2,1)S(1)} %bitcast.9, bf16[1536,512]{1,0:T(8,128)(2,1)S(1)} %copy-done, bf16[1536,512]{1,0:T(8,128)(2,1)S(1)} %copy-done.1), custom_call_target="tpu_custom_call" | custom-call | tf_op jit(solution)/shard_map/heads_back/pallas_call | solution.py:232
Async XLA Ops:
  19.9 45.7 %all-to-all-start = ((bf16[16,64,512]{2,1,0:T(8,128)(2,1)}), bf16[16,64,512]{2,1,0:T(8,128)(2,1)S(1)}, u32[]{:S(2)}, u32[]{:S(2)}) async-start(bf16[16,64,512]{2,1,0:T(8,128)(2,1)} %get-tuple-element.13), calls=%async_computation | async-start | bytes 2097152 | tf_op jit(solution)/shard_map/all_to_all | solution.py:251
  50.8 12.7 %collective-permute-start.2 = (bf16[256,512]{1,0:T(8,128)(2,1)S(1)}, bf16[256,512]{1,0:T(8,128)(2,1)S(1)}, u32[]{:S(2)}, u32[]{:S(2)}) collective-permute-start(bf16[256,512]{1,0:T(8,128)(2,1)S(1)} %all_gather.25), channel_id=1, source_target_pairs={{32,0},{34,2},{36,4},{38,6},{40,8},{42,10},{44,12},{46,14},{288,25... | collective-permute-start | bytes 786440 | tf_op jit(solution)/shard_map/ppermute | solution.py:261
  55.7 8.6 %collective-permute-start.1 = (bf16[256,512]{1,0:T(8,128)(2,1)S(1)}, bf16[256,512]{1,0:T(8,128)(2,1)S(1)}, u32[]{:S(2)}, u32[]{:S(2)}) collective-permute-start(bf16[256,512]{1,0:T(8,128)(2,1)S(1)} %all_gather.25), channel_id=1, source_target_pairs={{240,0},{242,2},{244,4},{246,6},{248,8},{250,10},{252,12},{254,14}... | collective-permute-start | bytes 786440 | tf_op jit(solution)/shard_map/ppermute | solution.py:261
  58.0 7.4 %collective-permute-start = (bf16[256,512]{1,0:T(8,128)(2,1)S(1)}, bf16[256,512]{1,0:T(8,128)(2,1)S(1)}, u32[]{:S(2)}, u32[]{:S(2)}) collective-permute-start(bf16[256,512]{1,0:T(8,128)(2,1)S(1)} %all_gather.25), channel_id=1, source_target_pairs={{16,0},{18,2},{20,4},{22,6},{24,8},{26,10},{28,12},{30,14},{272,25... | collective-permute-start | bytes 786440 | tf_op jit(solution)/shard_map/ppermute | solution.py:261
  68.2 35.9 %copy-start = (bf16[1536,512]{1,0:T(8,128)(2,1)S(1)}, bf16[1536,512]{1,0:T(8,128)(2,1)}, u32[]{:S(2)}) copy-start(bf16[1536,512]{1,0:T(8,128)(2,1)} %wv.3) | copy-start | bytes 4718596
  68.2 35.9 %copy-start.1 = (bf16[1536,512]{1,0:T(8,128)(2,1)S(1)}, bf16[1536,512]{1,0:T(8,128)(2,1)}, u32[]{:S(2)}) copy-start(bf16[1536,512]{1,0:T(8,128)(2,1)} %ws.3) | copy-start | bytes 4718596

commit v9 on v7

--- a/solution.py
+++ b/solution.py
@@ -27,6 +27,15 @@
 def normalize(embed):
     inv = lax.rsqrt(jnp.sum(embed * embed, axis=1, keepdims=True) + EPS)
     return (inv, embed * inv)
+
+
+def far_groups(sizes):
+    ids = np.arange(math.prod(sizes)).reshape(sizes)
+    groups = []
+    for core in range(2):
+        part = np.moveaxis(ids[..., core], 1, -1).reshape(-1, sizes[1])
+        groups += (part[:, ::-1] if core == 1 else part).tolist()
+    return groups
 
 
 def from_line(sizes, steps):
@@ -139,15 +148,18 @@
     )(kept, got)
 
 
-def tile(sharpness, offset, mine, other, own, block=256):
+def tile(sharpness, offset, mine, other, total, own, final=False, block=256):
     n, width = mine.shape
     m = other.shape[0]
     blocks = n // block
 
-    def kernel(t_ref, b_ref, mine_ref, other_ref, out_ref):
+    def kernel(t_ref, b_ref, mine_ref, other_ref, *rest):
+        out_ref = rest[-1]
         t = t_ref[0]
         slope, start = -LOG2E * t, -LOG2E * b_ref[0]
-        mine_at, other_at = lax.axis_index(PLANE) * own, lax.axis_index("zhi") * own
+        zhi, last = lax.axis_index("zhi"), lax.axis_size("zhi") - 1
+        mine_at = lax.axis_index(PLANE) * own
+        other_at = jnp.where(lax.axis_index("core") == 0, zhi, last - zhi) * own
         for i in range(blocks):
             at = pl.multiple_of(lax.rem(mine_at // block + 1 + i, blocks) * block, block)
             dots = lax.dot_general(
@@ -155,22 +167,28 @@
             )
             e = jnp.exp2(dots * slope + start)
             coef = pl.reciprocal(1.0 + e, approx=True)
-            if i == blocks - 1:
+            if total is None and i == blocks - 1:
                 row = lax.broadcasted_iota(jnp.int32, (block, 1), 0) + (at - mine_at)
                 row = jnp.where((row >= 0) & (row < own), row, -m)
                 col = lax.broadcasted_iota(jnp.int32, (1, m), 1) - other_at
                 coef = jnp.where(row == col, -e, 1.0) * coef
             sums = jnp.dot(coef.astype(BF), other_ref[...], preferred_element_type=F32)
-            out_ref[pl.ds(at, block)] = (t * sums).astype(BF)
-
-    return pl.pallas_call(
-        kernel,
-        out_shape=pltpu.VMEM((n, width), BF),
-        in_specs=[SMEM, SMEM, VMEM, VMEM],
+            if total is not None:
+                sums = sums + rest[0][pl.ds(at, block)]
+            out_ref[pl.ds(at, block)] = (t * sums).astype(BF) if final else sums
+
+    totals = [] if total is None else [total]
+    return pl.pallas_call(
+        kernel,
+        out_shape=pltpu.VMEM((n, width), BF if final else F32),
+        in_specs=[SMEM, SMEM, VMEM, VMEM] + [VMEM] * len(totals),
         out_specs=VMEM,
-        compiler_params=pltpu.CompilerParams(vmem_limit_bytes=40 * MIB),
+        compiler_params=pltpu.CompilerParams(vmem_limit_bytes=30 * MIB),
+        cost_estimate=pl.CostEstimate(
+            flops=4 * n * m * width, bytes_accessed=2 * width * (n + m), transcendentals=2 * n * m
+        ),
         name="tile",
-    )(sharpness, offset, mine, other)
+    )(sharpness, offset, mine, other, *totals)
 
 
 def finish(sums, embed):
@@ -232,9 +250,11 @@
 
     wide, line = lax.optimization_barrier((wide, line))
     mine = lax.all_to_all(wide, PLANE, 0, 0).reshape(peers * own, width)
-    line = lax.all_gather(line, "zhi", axis=0, tiled=True)
+    line = lax.all_gather(line, AXES, axis=0, tiled=True, axis_index_groups=far_groups(sizes))
     near = [lax.ppermute(line, AXES, from_line(sizes, steps)) for steps in ((1, 1), (-1, -1), (2, -2))]
-    grad = tile(sharpness, offset, mine, jnp.concatenate([line] + near), own)
+    grad = tile(sharpness, offset, mine, line, None, own)
+    for other in near:
+        grad = tile(sharpness, offset, mine, other, grad, own, final=other is near[-1])
 
     grad = lax.all_to_all(grad.reshape(peers, own, width), PLANE, 0, 0)
     delta = lax.all_gather(finish(grad, embed), GROUP, axis=0)

time: 101 us -> 101 us (level)
  Pallas kernels: 8.36 us -> 10.2 us
  starting transfers between devices: 13.2 us -> 12 us
    pallas_call x1 -> x4, Pallas kernels: 2.62 us -> 4.5 us  [tile(): pl.pallas_call(kernel, out_shape=pltpu.VMEM((n, width), BF if final else...]
    ppermute x3, starting transfers between devices: 9.51 us -> 8.31 us  [shards(): lax.ppermute(line, AXES, from_line(sizes, steps))]
  transfers between devices with their start and end apart: 4 -> 4, of which waited for: 3 -> 1; matrix products, arithmetic and copies ran while one was open for 0% -> 0% of each run, Pallas kernels for 0% -> 3%
where the time goes in v9:
time: 101 us
  blocking collectives  69.9 us (69%)
  starting transfers between devices  12 us (12%)
  Pallas kernels  10.2 us (10%)
  waiting for transfers between devices  6.8 us (7%)
  between operations  2.04 us (2%)
    all_gather x1, blocking collectives, shards(): lax.all_gather(line, AXES, axis=0, tiled=True, axis_index_groups=far_grou...  22.6 us
    all_to_all x1, blocking collectives, shards(): grad = lax.all_to_all(grad.reshape(peers, own, width), PLANE, 0, 0)  21.2 us
    all_gather x1, blocking collectives, shards(): delta = lax.all_gather(finish(grad, embed), GROUP, axis=0)  10.5 us
    all_gather x1, blocking collectives, shards(): lax.all_gather(heads(vision, sentence, vision_map, sentence_map), 'core',...  8.69 us
    ppermute x3, starting transfers between devices, shards(): lax.ppermute(line, AXES, from_line(sizes, steps))  8.31 us
    all_gather x1, blocking collectives, shards(): wide, line, embed = units(kept, lax.all_gather(given, 'yhi', axis=0), peers)  6.89 us
    ppermute x3, waiting for transfers between devices, shards(): lax.ppermute(line, AXES, from_line(sizes, steps))  6.79 us
    pallas_call x4, Pallas kernels, tile(): pl.pallas_call(kernel, out_shape=pltpu.VMEM((n, width), BF if final else...  4.5 us
  transfers between devices with their start and end apart: 4, of which 1 were waited for; matrix products, arithmetic and copies ran while one was open for 0% of the time, Pallas kernels for 3%

profile of v9, /device:TPU:1, one launch (start us, length us, event | category | flops | bytes accessed | tf_op | source)
XLA Modules:
  0.0 100.9 jit_solution(14935434295856588075)
XLA Ops:
  0.6 2.5 %heads.1 = bf16[2,64,1024]{2,1,0:T(8,128)(2,1)S(1)} custom-call(bf16[128,1536]{1,0:T(8,128)(2,1)} %v.1, bf16[128,1536]{1,0:T(8,128)(2,1)} %s.1, bf16[1536,512]{1,0:T(8,128)(2,1)} %wv.3, bf16[1536,512]{1,0:T(8,128)(2,1)} %ws.3), custom_call_target="tpu_custom_call" | custom-call | tf_op jit(solution)/shard_map/heads/pallas_call | solution.py:81
  3.1 8.7 %all-gather = bf16[4,64,1024]{2,1,0:T(8,128)(2,1)S(1)} all-gather(bf16[2,64,1024]{2,1,0:T(8,128)(2,1)S(1)} %heads.1), channel_id=2, replica_groups=mesh['ylo'=2,'zhi'=4,'zlo'=4,'x'=4,'yhi'=2,'core'=2] {'core'}, dimensions={0}, use_global_device_ids=true | all-gather | bytes 786432 | tf_op jit(solution)/shard_map/all_gather | solution.py:247
  11.8 0.1 chip_sums.1
  11.8 6.9 %all-gather.1 = bf16[128,1024]{1,0:T(8,128)(2,1)S(1)} all-gather(bf16[64,1024]{1,0:T(8,128)(2,1)S(1)} %get-tuple-element.10), channel_id=3, replica_groups=mesh['ylo'=2,'zhi'=4,'zlo'=4,'x'=4,'yhi'=2,'core'=2] {'yhi'}, dimensions={0}, use_global_device_ids=true | all-gather | bytes 393216 | tf_op jit(solution)/shard_map/all_gather | solution.py:249
  18.7 1.1 %units.1 = (bf16[16,64,512]{2,1,0:T(8,128)(2,1)}, bf16[64,512]{1,0:T(8,128)(2,1)S(1)}, f32[64,512]{1,0:T(8,128)S(1)}) custom-call(f32[64,1024]{1,0:T(8,128)S(1)} %get-tuple-element.9.kept_ref, bf16[2,64,1024]{2,1,0:T(8,128)(2,1)S(1)} %bitcast.11), custom_call_target="tpu_custom_call" | custom-call | tf_op jit(solution)/shard_map/units/pallas_call | solution.py:137
  19.9 3.7 %all-to-all-start = ((bf16[16,64,512]{2,1,0:T(8,128)(2,1)}), bf16[16,64,512]{2,1,0:T(8,128)(2,1)S(1)}, u32[]{:S(2)}, u32[]{:S(2)}) async-start(bf16[16,64,512]{2,1,0:T(8,128)(2,1)} %get-tuple-element.13), calls=%async_computation | async-start | bytes 2097152 | tf_op jit(solution)/shard_map/all_to_all | solution.py:252
  23.5 22.6 %all_gather.25.other_ref = bf16[256,512]{1,0:T(8,128)(2,1)S(1)} all-gather(bf16[64,512]{1,0:T(8,128)(2,1)S(1)} %get-tuple-element.14), channel_id=1, replica_groups={{0,64,128,192},{2,66,130,194},{4,68,132,196},{6,70,134,198},{8,72,136,2..., dimensions={0}, use_global_device_ids=true | all-gather | bytes 327680 | tf_op jit(solution)/shard_map/all_gather | solution.py:253
  46.1 3.5 %collective-permute-start.2 = (bf16[256,512]{1,0:T(8,128)(2,1)S(1)}, bf16[256,512]{1,0:T(8,128)(2,1)S(1)}, u32[]{:S(2)}, u32[]{:S(2)}) collective-permute-start(bf16[256,512]{1,0:T(8,128)(2,1)S(1)} %all_gather.25.other_ref), channel_id=1, source_target_pairs={{16,0},{18,2},{20,4},{22,6},{24,8},{26,10},{28,12},{30,14},{272,25... | collective-permute-start | bytes 786440 | tf_op jit(solution)/shard_map/ppermute | solution.py:254
  49.6 1.9 %collective-permute-start.1 = (bf16[256,512]{1,0:T(8,128)(2,1)S(1)}, bf16[256,512]{1,0:T(8,128)(2,1)S(1)}, u32[]{:S(2)}, u32[]{:S(2)}) collective-permute-start(bf16[256,512]{1,0:T(8,128)(2,1)S(1)} %all_gather.25.other_ref), channel_id=1, source_target_pairs={{240,0},{242,2},{244,4},{246,6},{248,8},{250,10},{252,12},{254,14}... | collective-permute-start | bytes 786440 | tf_op jit(solution)/shard_map/ppermute | solution.py:254
  51.5 2.9 %collective-permute-start = (bf16[256,512]{1,0:T(8,128)(2,1)S(1)}, bf16[256,512]{1,0:T(8,128)(2,1)S(1)}, u32[]{:S(2)}, u32[]{:S(2)}) collective-permute-start(bf16[256,512]{1,0:T(8,128)(2,1)S(1)} %all_gather.25.other_ref), channel_id=1, source_target_pairs={{32,0},{34,2},{36,4},{38,6},{40,8},{42,10},{44,12},{46,14},{288,25... | collective-permute-start | bytes 786440 | tf_op jit(solution)/shard_map/ppermute | solution.py:254
  55.8 0.0 all-to-all-done
  55.8 1.1 %tile.4.rest_0_ = f32[1024,512]{1,0:T(8,128)S(1)} custom-call(f32[1]{0:T(128)S(6)} %copy.8.t_ref, f32[1]{0:T(128)S(6)} %copy.9.b_ref, bf16[1024,512]{1,0:T(8,128)(2,1)S(1)} %bitcast.5, bf16[256,512]{1,0:T(8,128)(2,1)S(1)} %all_gather.25.other_ref), custom_call_target="tpu_custom_call" | custom-call | flops 536870912 | bytes 1310720 | tf_op jit(solution)/shard_map/tile/pallas_call | solution.py:181
  56.9 0.0 collective-permute-done.2.other_ref
  56.9 1.1 %tile.5.rest_0_ = f32[1024,512]{1,0:T(8,128)S(1)} custom-call(f32[1]{0:T(128)S(6)} %copy.8.t_ref, f32[1]{0:T(128)S(6)} %copy.9.b_ref, bf16[1024,512]{1,0:T(8,128)(2,1)S(1)} %bitcast.6, bf16[256,512]{1,0:T(8,128)(2,1)S(1)} %collective-permute-done.2.other_ref, f32[1024,512]{1,0:T(8,128)S(1)} %tile.4.rest_0_), custom_call_target="tpu_custom_call" | custom-call | flops 536870912 | bytes 1310720 | tf_op jit(solution)/shard_map/tile/pallas_call | solution.py:181
  58.0 0.0 collective-permute-done.1.other_ref
  58.0 1.1 %tile.6.rest_0_ = f32[1024,512]{1,0:T(8,128)S(1)} custom-call(f32[1]{0:T(128)S(6)} %copy.8.t_ref, f32[1]{0:T(128)S(6)} %copy.9.b_ref, bf16[1024,512]{1,0:T(8,128)(2,1)S(1)} %bitcast.7, bf16[256,512]{1,0:T(8,128)(2,1)S(1)} %collective-permute-done.1.other_ref, f32[1024,512]{1,0:T(8,128)S(1)} %tile.5.rest_0_), custom_call_target="tpu_custom_call" | custom-call | flops 536870912 | bytes 1310720 | tf_op jit(solution)/shard_map/tile/pallas_call | solution.py:181
  59.2 6.8 %collective-permute-done.other_ref = bf16[256,512]{1,0:T(8,128)(2,1)S(1)} collective-permute-done((bf16[256,512]{1,0:T(8,128)(2,1)S(1)}, bf16[256,512]{1,0:T(8,128)(2,1)S(1)}, u32[]{:S(2)}, u32[]{:S(2)}) %collective-permute-start) | collective-permute-done | bytes 262176 | tf_op jit(solution)/shard_map/ppermute | solution.py:254
  66.0 1.1 %tile.7 = bf16[1024,512]{1,0:T(8,128)(2,1)S(1)} custom-call(f32[1]{0:T(128)S(6)} %copy.8.t_ref, f32[1]{0:T(128)S(6)} %copy.9.b_ref, bf16[1024,512]{1,0:T(8,128)(2,1)S(1)} %bitcast.8, bf16[256,512]{1,0:T(8,128)(2,1)S(1)} %collective-permute-done.other_ref, f32[1024,512]{1,0:T(8,128)S(1)} %tile.6.rest_0_), custom_call_target="tpu_custom_call" | custom-call | flops 536870912 | bytes 1310720 | tf_op jit(solution)/shard_map/tile/pallas_call | solution.py:181
  67.1 0.0 copy-start
  67.1 0.0 copy-start.1
  67.1 21.2 %all_to_all.10.sums_ref = bf16[16,64,512]{2,1,0:T(8,128)(2,1)S(1)} all-to-all(bf16[16,64,512]{2,1,0:T(8,128)(2,1)S(1)} %bitcast.9), channel_id=1, replica_groups=mesh['ylo'=2,'zhi'=4,'zlo'=4,'x'=4,'yhi'=2,'core'=2] {'ylo','x','yhi'}, dimensions={0} | all-to-all | bytes 2097152 | tf_op jit(solution)/shard_map/all_to_all | solution.py:259
  88.3 0.2 finish.1
  88.5 10.5 %all-gather.2 = bf16[256,512]{1,0:T(8,128)(2,1)S(1)} all-gather(bf16[64,512]{1,0:T(8,128)(2,1)S(1)} %finish.1), channel_id=4, replica_groups=mesh['ylo'=2,'zhi'=4,'zlo'=4,'x'=4,'yhi'=2,'core'=2] {'yhi','core'}, dimensions={0}, use_global_device_ids=true | all-gather | bytes 327680 | tf_op jit(solution)/shard_map/all_gather | solution.py:260
  99.0 0.0 copy-done
  99.0 0.0 copy-done.1
  99.0 1.8 %heads_back.1 = (bf16[128,1536]{1,0:T(8,128)(2,1)}, bf16[128,1536]{1,0:T(8,128)(2,1)}) custom-call(bf16[4,64,512]{2,1,0:T(8,128)(2,1)S(1)} %bitcast.12, bf16[1536,512]{1,0:T(8,128)(2,1)S(1)} %copy-done, bf16[1536,512]{1,0:T(8,128)(2,1)S(1)} %copy-done.1), custom_call_target="tpu_custom_call" | custom-call | tf_op jit(solution)/shard_map/heads_back/pallas_call | solution.py:230
Async XLA Ops:
  19.9 35.9 %all-to-all-start = ((bf16[16,64,512]{2,1,0:T(8,128)(2,1)}), bf16[16,64,512]{2,1,0:T(8,128)(2,1)S(1)}, u32[]{:S(2)}, u32[]{:S(2)}) async-start(bf16[16,64,512]{2,1,0:T(8,128)(2,1)} %get-tuple-element.13), calls=%async_computation | async-start | bytes 2097152 | tf_op jit(solution)/shard_map/all_to_all | solution.py:252
  46.1 10.8 %collective-permute-start.2 = (bf16[256,512]{1,0:T(8,128)(2,1)S(1)}, bf16[256,512]{1,0:T(8,128)(2,1)S(1)}, u32[]{:S(2)}, u32[]{:S(2)}) collective-permute-start(bf16[256,512]{1,0:T(8,128)(2,1)S(1)} %all_gather.25.other_ref), channel_id=1, source_target_pairs={{16,0},{18,2},{20,4},{22,6},{24,8},{26,10},{28,12},{30,14},{272,25... | collective-permute-start | bytes 786440 | tf_op jit(solution)/shard_map/ppermute | solution.py:254
  49.6 8.4 %collective-permute-start.1 = (bf16[256,512]{1,0:T(8,128)(2,1)S(1)}, bf16[256,512]{1,0:T(8,128)(2,1)S(1)}, u32[]{:S(2)}, u32[]{:S(2)}) collective-permute-start(bf16[256,512]{1,0:T(8,128)(2,1)S(1)} %all_gather.25.other_ref), channel_id=1, source_target_pairs={{240,0},{242,2},{244,4},{246,6},{248,8},{250,10},{252,12},{254,14}... | collective-permute-start | bytes 786440 | tf_op jit(solution)/shard_map/ppermute | solution.py:254
  51.5 14.4 %collective-permute-start = (bf16[256,512]{1,0:T(8,128)(2,1)S(1)}, bf16[256,512]{1,0:T(8,128)(2,1)S(1)}, u32[]{:S(2)}, u32[]{:S(2)}) collective-permute-start(bf16[256,512]{1,0:T(8,128)(2,1)S(1)} %all_gather.25.other_ref), channel_id=1, source_target_pairs={{32,0},{34,2},{36,4},{38,6},{40,8},{42,10},{44,12},{46,14},{288,25... | collective-permute-start | bytes 786440 | tf_op jit(solution)/shard_map/ppermute | solution.py:254
  67.1 31.9 %copy-start = (bf16[1536,512]{1,0:T(8,128)(2,1)S(1)}, bf16[1536,512]{1,0:T(8,128)(2,1)}, u32[]{:S(2)}) copy-start(bf16[1536,512]{1,0:T(8,128)(2,1)} %wv.3) | copy-start | bytes 4718596
  67.1 31.9 %copy-start.1 = (bf16[1536,512]{1,0:T(8,128)(2,1)S(1)}, bf16[1536,512]{1,0:T(8,128)(2,1)}, u32[]{:S(2)}) copy-start(bf16[1536,512]{1,0:T(8,128)(2,1)} %ws.3) | copy-start | bytes 4718596

commit v10 on v9

--- a/solution.py
+++ b/solution.py
@@ -42,18 +42,19 @@
     ids = np.arange(math.prod(sizes)).reshape(sizes)
     pairs = []
     for core, step in enumerate(steps):
-        target = ids[..., core].transpose(1, 2, 0, 3, 4).reshape(sizes[1] * sizes[2], -1)
-        source = np.roll(target, -step, axis=0)
-        pairs += zip(source.ravel().tolist(), target.ravel().tolist())
+        target, other = (
+            ids[..., c].transpose(1, 2, 0, 3, 4).reshape(sizes[1] * sizes[2], -1) for c in (core, 1 - core)
+        )
+        pairs += zip(np.roll(other, -step, axis=0).ravel().tolist(), target.ravel().tolist())
     return pairs
 
 
 def heads(vision, sentence, vision_map, sentence_map, chunks=3):
     rows, depth = vision.shape
     width = vision_map.shape[1]
-    own, step = rows // 2, depth // chunks
-
-    def kernel(v, s, wv, ws, out, vb, sb, wvb, wsb, sems):
+    step = depth // chunks
+
+    def kernel(v, s, wv, ws, given, kept, vb, sb, wvb, wsb, sems):
         towers = ((v, wv, vb, wvb), (s, ws, sb, wsb))
         copies = []
         for tower, (x, w, xb, wb) in enumerate(towers):
@@ -74,15 +75,20 @@
                 cut = slice(c * step, (c + 1) * step)
                 part = jnp.dot(xb[:, cut], wb[cut], preferred_element_type=F32)
                 total = part if total is None else total + part
-            total = total.astype(BF)
-            for half in range(2):
-                out[half, :, tower * width : (tower + 1) * width] = total[half * own : (half + 1) * own]
-
-    return pl.pallas_call(
-        kernel,
-        out_shape=pltpu.VMEM((2, own, 2 * width), BF),
+
+            @pl.when(lax.axis_index("core") == tower)
+            def _():
+                kept[...] = total
+
+            @pl.when(lax.axis_index("core") != tower)
+            def _():
+                given[...] = total.astype(BF)
+
+    return pl.pallas_call(
+        kernel,
+        out_shape=[pltpu.VMEM((rows, width), BF), pltpu.VMEM((rows, width), F32)],
         in_specs=[HBM] * 4,
-        out_specs=VMEM,
+        out_specs=[VMEM] * 2,
         scratch_shapes=[
             pltpu.VMEM((rows, depth), BF),
             pltpu.VMEM((rows, depth), BF),
@@ -95,44 +101,43 @@
     )(vision, sentence, vision_map, sentence_map)
 
 
-def chip_sums(parts):
-    _, _, own, width = parts.shape
-
-    def kernel(parts_ref, given_ref, kept_ref):
+def chip_sums(kept, got):
+    own, width = kept.shape[0] // 2, kept.shape[1]
+
+    def kernel(kept_ref, got_ref, given_ref, sums_ref):
+        for core in range(2):
+            for yhi in range(2):
+
+                @pl.when((lax.axis_index("core") == core) & (lax.axis_index("yhi") == yhi))
+                def _():
+                    total = kept_ref[...] + got_ref[1 - core].astype(F32)
+                    sums_ref[...] = total[yhi * own : (yhi + 1) * own]
+                    given_ref[...] = total[(1 - yhi) * own : (2 - yhi) * own].astype(BF)
+
+    return pl.pallas_call(
+        kernel,
+        out_shape=[pltpu.VMEM((own, width), BF), pltpu.VMEM((own, width), F32)],
+        in_specs=[VMEM] * 2,
+        out_specs=[VMEM] * 2,
+        compiler_params=pltpu.CompilerParams(vmem_limit_bytes=20 * MIB),
+        name="chip_sums",
+    )(kept, got)
+
+
+def units(sums, got, peers):
+    own, width = sums.shape
+
+    def kernel(sums_ref, got_ref, wide_ref, unit_ref, embed_ref):
         for yhi in range(2):
 
             @pl.when(lax.axis_index("yhi") == yhi)
             def _():
-                total = [parts_ref[0, h].astype(F32) + parts_ref[1, h].astype(F32) for h in (yhi, 1 - yhi)]
-                kept_ref[...] = total[0]
-                given_ref[...] = total[1].astype(BF)
-
-    return pl.pallas_call(
-        kernel,
-        out_shape=[pltpu.VMEM((own, width), BF), pltpu.VMEM((own, width), F32)],
-        in_specs=[VMEM],
-        out_specs=[VMEM, VMEM],
-        compiler_params=pltpu.CompilerParams(vmem_limit_bytes=20 * MIB),
-        name="chip_sums",
-    )(parts)
-
-
-def units(kept, got, peers):
-    own, width = kept.shape[0], kept.shape[1] // 2
-
-    def kernel(kept_ref, got_ref, wide_ref, line_ref, embed_ref):
-        towers = [slice(0, width), slice(width, 2 * width)]
-        for yhi in range(2):
-            for core in range(2):
-
-                @pl.when((lax.axis_index("yhi") == yhi) & (lax.axis_index("core") == core))
-                def _():
-                    embed = [kept_ref[:, cut] + got_ref[1 - yhi, :, cut].astype(F32) for cut in towers]
-                    embed_ref[...] = embed[core]
-                    mine = normalize(embed[core])[1].astype(BF)
-                    for peer in range(peers):
-                        wide_ref[peer] = mine
-                    line_ref[...] = normalize(embed[1 - core])[1].astype(BF)
+                embed = sums_ref[...] + got_ref[1 - yhi].astype(F32)
+                embed_ref[...] = embed
+                unit = normalize(embed)[1].astype(BF)
+                unit_ref[...] = unit
+                for peer in range(peers):
+                    wide_ref[peer] = unit
 
     return pl.pallas_call(
         kernel,
@@ -145,50 +150,53 @@
         out_specs=[VMEM] * 3,
         compiler_params=pltpu.CompilerParams(vmem_limit_bytes=20 * MIB),
         name="units",
-    )(kept, got)
-
-
-def tile(sharpness, offset, mine, other, total, own, final=False, block=256):
+    )(sums, got)
+
+
+def tile(sharpness, offset, mine, others, total, own, positives=False, final=False, block=256):
     n, width = mine.shape
-    m = other.shape[0]
+    m = others[0].shape[0]
     blocks = n // block
 
-    def kernel(t_ref, b_ref, mine_ref, other_ref, *rest):
+    def kernel(t_ref, b_ref, mine_ref, *rest):
         out_ref = rest[-1]
         t = t_ref[0]
         slope, start = -LOG2E * t, -LOG2E * b_ref[0]
         zhi, last = lax.axis_index("zhi"), lax.axis_size("zhi") - 1
         mine_at = lax.axis_index(PLANE) * own
-        other_at = jnp.where(lax.axis_index("core") == 0, zhi, last - zhi) * own
+        other_at = jnp.where(lax.axis_index("core") == 0, last - zhi, zhi) * own
         for i in range(blocks):
             at = pl.multiple_of(lax.rem(mine_at // block + 1 + i, blocks) * block, block)
-            dots = lax.dot_general(
-                mine_ref[pl.ds(at, block)], other_ref[...], (((1,), (1,)), ((), ())), preferred_element_type=F32
-            )
-            e = jnp.exp2(dots * slope + start)
-            coef = pl.reciprocal(1.0 + e, approx=True)
-            if total is None and i == blocks - 1:
-                row = lax.broadcasted_iota(jnp.int32, (block, 1), 0) + (at - mine_at)
-                row = jnp.where((row >= 0) & (row < own), row, -m)
-                col = lax.broadcasted_iota(jnp.int32, (1, m), 1) - other_at
-                coef = jnp.where(row == col, -e, 1.0) * coef
-            sums = jnp.dot(coef.astype(BF), other_ref[...], preferred_element_type=F32)
-            if total is not None:
-                sums = sums + rest[0][pl.ds(at, block)]
+            sums = None if total is None else rest[len(others)][pl.ds(at, block)]
+            for other_ref in rest[: len(others)]:
+                dots = lax.dot_general(
+                    mine_ref[pl.ds(at, block)], other_ref[...], (((1,), (1,)), ((), ())), preferred_element_type=F32
+                )
+                e = jnp.exp2(dots * slope + start)
+                coef = pl.reciprocal(1.0 + e, approx=True)
+                if positives and i == blocks - 1:
+                    row = lax.broadcasted_iota(jnp.int32, (block, 1), 0) + (at - mine_at)
+                    row = jnp.where((row >= 0) & (row < own), row, -m)
+                    col = lax.broadcasted_iota(jnp.int32, (1, m), 1) - other_at
+                    coef = jnp.where(row == col, -e, 1.0) * coef
+                part = jnp.dot(coef.astype(BF), other_ref[...], preferred_element_type=F32)
+                sums = part if sums is None else sums + part
             out_ref[pl.ds(at, block)] = (t * sums).astype(BF) if final else sums
 
     totals = [] if total is None else [total]
     return pl.pallas_call(
         kernel,
         out_shape=pltpu.VMEM((n, width), BF if final else F32),
-        in_specs=[SMEM, SMEM, VMEM, VMEM] + [VMEM] * len(totals),
+        in_specs=[SMEM, SMEM, VMEM] + [VMEM] * (len(others) + len(totals)),
         out_specs=VMEM,
         compiler_params=pltpu.CompilerParams(vmem_limit_bytes=30 * MIB),
         cost_estimate=pl.CostEstimate(
-            flops=4 * n * m * width, bytes_accessed=2 * width * (n + m), transcendentals=2 * n * m
+            flops=4 * n * m * width * len(others),
+            bytes_accessed=2 * width * (n + m * len(others)),
+            transcendentals=2 * n * m * len(others),
         ),
         name="tile",
-    )(sharpness, offset, mine, other, *totals)
+    )(sharpness, offset, mine, *others, *totals)
 
 
 def finish(sums, embed):
@@ -244,17 +252,19 @@
     sizes = [lax.axis_size(a) for a in AXES]
     peers = lax.axis_size(PLANE)
 
-    parts = lax.all_gather(heads(vision, sentence, vision_map, sentence_map), "core", axis=0)
-    given, kept = chip_sums(parts)
-    wide, line, embed = units(kept, lax.all_gather(given, "yhi", axis=0), peers)
-
-    wide, line = lax.optimization_barrier((wide, line))
+    given, kept = heads(vision, sentence, vision_map, sentence_map)
+    given, sums = chip_sums(kept, lax.all_gather(given, "core", axis=0))
+    wide, unit, embed = units(sums, lax.all_gather(given, "yhi", axis=0), peers)
+
+    wide, unit = lax.optimization_barrier((wide, unit))
     mine = lax.all_to_all(wide, PLANE, 0, 0).reshape(peers * own, width)
-    line = lax.all_gather(line, AXES, axis=0, tiled=True, axis_index_groups=far_groups(sizes))
-    near = [lax.ppermute(line, AXES, from_line(sizes, steps)) for steps in ((1, 1), (-1, -1), (2, -2))]
-    grad = tile(sharpness, offset, mine, line, None, own)
-    for other in near:
-        grad = tile(sharpness, offset, mine, other, grad, own, final=other is near[-1])
+    line = lax.all_gather(unit, AXES, axis=0, tiled=True, axis_index_groups=far_groups(sizes))
+    first, second, third, here = (
+        lax.ppermute(line, AXES, from_line(sizes, steps)) for steps in ((1, 1), (-1, -1), (2, -2), (0, 0))
+    )
+    grad = tile(sharpness, offset, mine, [first], None, own)
+    grad = tile(sharpness, offset, mine, [here], grad, own, positives=True)
+    grad = tile(sharpness, offset, mine, [second, third], grad, own, final=True)
 
     grad = lax.all_to_all(grad.reshape(peers, own, width), PLANE, 0, 0)
     delta = lax.all_gather(finish(grad, embed), GROUP, axis=0)

time: 101 us -> 104 us (1.030)
  starting transfers between devices: 12 us -> 17.9 us
  waiting for transfers between devices: 6.8 us -> 4.66 us
    ppermute x3 -> x4, starting transfers between devices: 8.31 us -> 14.2 us  [shards(): lax.ppermute(line, AXES, from_line(sizes, steps))]
    all_to_all x1, blocking collectives: 21.2 us -> 23.8 us  [shards(): grad = lax.all_to_all(grad.reshape(peers, own, width), PLANE, 0, 0)]
    ppermute x3 -> x4, waiting for transfers between devices: 6.79 us -> 4.66 us  [shards(): lax.ppermute(line, AXES, from_line(sizes, steps))]
    all_gather x1, blocking collectives: 10.5 us -> 8.47 us  [shards(): delta = lax.all_gather(finish(grad, embed), GROUP, axis=0)]
    all_gather x3, blocking collectives: 38.2 us -> 36.6 us  [the longest x1 22.7 us: shards(): lax.all_gather(unit, AXES, axis=0, tiled=True, axis_index_groups=far_grou...]
    pallas_call x4 -> x3, Pallas kernels: 4.5 us -> 4 us  [tile(): pl.pallas_call(kernel, out_shape=pltpu.VMEM((n, width), BF if final else...]
  transfers between devices with their start and end apart: 4 -> 5, of which waited for: 1 -> 2; matrix products, arithmetic and copies ran while one was open for 0% -> 0% of each run, Pallas kernels for 3% -> 2%
where the time goes in v10:
time: 104 us; the launch traced here: 103 us
  blocking collectives  68.9 us (66%)
  starting transfers between devices  17.9 us (17%)
  Pallas kernels  9.71 us (9%)
  waiting for transfers between devices  4.66 us (4%)
  between operations  2.04 us (2%)
    all_to_all x1, blocking collectives, shards(): grad = lax.all_to_all(grad.reshape(peers, own, width), PLANE, 0, 0)  23.8 us
    all_gather x1, blocking collectives, shards(): lax.all_gather(unit, AXES, axis=0, tiled=True, axis_index_groups=far_grou...  22.7 us
    ppermute x4, starting transfers between devices, shards(): lax.ppermute(line, AXES, from_line(sizes, steps))  14.2 us
    all_gather x1, blocking collectives, shards(): given, sums = chip_sums(kept, lax.all_gather(given, 'core', axis=0))  8.52 us
    all_gather x1, blocking collectives, shards(): delta = lax.all_gather(finish(grad, embed), GROUP, axis=0)  8.47 us
    all_gather x1, blocking collectives, shards(): wide, unit, embed = units(sums, lax.all_gather(given, 'yhi', axis=0), peers)  5.3 us
    ppermute x4, waiting for transfers between devices, shards(): lax.ppermute(line, AXES, from_line(sizes, steps))  4.66 us
    pallas_call x3, Pallas kernels, tile(): pl.pallas_call(kernel, out_shape=pltpu.VMEM((n, width), BF if final else...  4 us
  transfers between devices with their start and end apart: 5, of which 2 were waited for; matrix products, arithmetic and copies ran while one was open for 0% of the time, Pallas kernels for 2%

profile of v10, /device:TPU:1, one launch (start us, length us, event | category | flops | bytes accessed | tf_op | source)
XLA Modules:
  0.0 103.2 jit_solution(8385286950023040209)
XLA Ops:
  0.6 2.5 %heads.1 = (bf16[128,512]{1,0:T(8,128)(2,1)S(1)}, f32[128,512]{1,0:T(8,128)S(1)}) custom-call(bf16[128,1536]{1,0:T(8,128)(2,1)} %v.1, bf16[128,1536]{1,0:T(8,128)(2,1)} %s.1, bf16[1536,512]{1,0:T(8,128)(2,1)} %wv.3, bf16[1536,512]{1,0:T(8,128)(2,1)} %ws.3), custom_call_target="tpu_custom_call" | custom-call | tf_op jit(solution)/shard_map/heads/pallas_call | solution.py:87
  3.1 8.5 %all-gather = bf16[256,512]{1,0:T(8,128)(2,1)S(1)} all-gather(bf16[128,512]{1,0:T(8,128)(2,1)S(1)} %get-tuple-element.12), channel_id=2, replica_groups=mesh['ylo'=2,'zhi'=4,'zlo'=4,'x'=4,'yhi'=2,'core'=2] {'core'}, dimensions={0}, use_global_device_ids=true | all-gather | bytes 393216 | tf_op jit(solution)/shard_map/all_gather | solution.py:256
  11.6 5.3 %all-gather.1 = bf16[128,512]{1,0:T(8,128)(2,1)S(1)} all-gather(bf16[64,512]{1,0:T(8,128)(2,1)S(1)} %get-tuple-element.14), channel_id=3, replica_groups=mesh['ylo'=2,'zhi'=4,'zlo'=4,'x'=4,'yhi'=2,'core'=2] {'yhi'}, dimensions={0}, use_global_device_ids=true | all-gather | bytes 196608 | tf_op jit(solution)/shard_map/all_gather | solution.py:257
  16.9 1.1 %units.1 = (bf16[16,64,512]{2,1,0:T(8,128)(2,1)}, bf16[64,512]{1,0:T(8,128)(2,1)S(1)}, f32[64,512]{1,0:T(8,128)S(1)}) custom-call(f32[64,512]{1,0:T(8,128)S(1)} %get-tuple-element.13.sums_ref, bf16[2,64,512]{2,1,0:T(8,128)(2,1)S(1)} %bitcast.11), custom_call_target="tpu_custom_call" | custom-call | tf_op jit(solution)/shard_map/units/pallas_call | solution.py:142
  18.1 3.7 %all-to-all-start = ((bf16[16,64,512]{2,1,0:T(8,128)(2,1)}), bf16[16,64,512]{2,1,0:T(8,128)(2,1)S(1)}, u32[]{:S(2)}, u32[]{:S(2)}) async-start(bf16[16,64,512]{2,1,0:T(8,128)(2,1)} %get-tuple-element.17), calls=%async_computation | async-start | bytes 2097152 | tf_op jit(solution)/shard_map/all_to_all | solution.py:260
  21.7 22.7 %all_gather.25 = bf16[256,512]{1,0:T(8,128)(2,1)S(1)} all-gather(bf16[64,512]{1,0:T(8,128)(2,1)S(1)} %get-tuple-element.18), channel_id=1, replica_groups={{0,64,128,192},{2,66,130,194},{4,68,132,196},{6,70,134,198},{8,72,136,2..., dimensions={0}, use_global_device_ids=true | all-gather | bytes 327680 | tf_op jit(solution)/shard_map/all_gather | solution.py:261
  44.5 6.2 %collective-permute-start.3 = (bf16[256,512]{1,0:T(8,128)(2,1)S(1)}, bf16[256,512]{1,0:T(8,128)(2,1)S(1)}, u32[]{:S(2)}, u32[]{:S(2)}) collective-permute-start(bf16[256,512]{1,0:T(8,128)(2,1)S(1)} %all_gather.25), channel_id=1, source_target_pairs={{17,0},{19,2},{21,4},{23,6},{25,8},{27,10},{29,12},{31,14},{273,25... | collective-permute-start | bytes 786440 | tf_op jit(solution)/shard_map/ppermute | solution.py:263
  50.7 2.3 %collective-permute-start.2 = (bf16[256,512]{1,0:T(8,128)(2,1)S(1)}, bf16[256,512]{1,0:T(8,128)(2,1)S(1)}, u32[]{:S(2)}, u32[]{:S(2)}) collective-permute-start(bf16[256,512]{1,0:T(8,128)(2,1)S(1)} %all_gather.25), channel_id=1, source_target_pairs={{1,0},{3,2},{5,4},{7,6},{9,8},{11,10},{13,12},{15,14},{257,256},{2... | collective-permute-start | bytes 786440 | tf_op jit(solution)/shard_map/ppermute | solution.py:263
  53.0 3.6 %collective-permute-start = (bf16[256,512]{1,0:T(8,128)(2,1)S(1)}, bf16[256,512]{1,0:T(8,128)(2,1)S(1)}, u32[]{:S(2)}, u32[]{:S(2)}) collective-permute-start(bf16[256,512]{1,0:T(8,128)(2,1)S(1)} %all_gather.25), channel_id=1, source_target_pairs={{241,0},{243,2},{245,4},{247,6},{249,8},{251,10},{253,12},{255,14}... | collective-permute-start | bytes 786440 | tf_op jit(solution)/shard_map/ppermute | solution.py:263
  56.6 2.1 %collective-permute-start.1 = (bf16[256,512]{1,0:T(8,128)(2,1)S(1)}, bf16[256,512]{1,0:T(8,128)(2,1)S(1)}, u32[]{:S(2)}, u32[]{:S(2)}) collective-permute-start(bf16[256,512]{1,0:T(8,128)(2,1)S(1)} %all_gather.25), channel_id=1, source_target_pairs={{33,0},{35,2},{37,4},{39,6},{41,8},{43,10},{45,12},{47,14},{289,25... | collective-permute-start | bytes 786440 | tf_op jit(solution)/shard_map/ppermute | solution.py:263
  60.0 0.0 collective-permute-done.3.rest_0_
  60.1 0.0 all-to-all-done
  60.1 1.1 %tile.3.rest_1_ = f32[1024,512]{1,0:T(8,128)S(1)} custom-call(f32[1]{0:T(128)S(6)} %copy.8.t_ref, f32[1]{0:T(128)S(6)} %copy.9.b_ref, bf16[1024,512]{1,0:T(8,128)(2,1)S(1)} %bitcast.5, bf16[256,512]{1,0:T(8,128)(2,1)S(1)} %collective-permute-done.3.rest_0_), custom_call_target="tpu_custom_call" | custom-call | flops 536870912 | bytes 1310720 | tf_op jit(solution)/shard_map/tile/pallas_call | solution.py:187
  61.2 0.0 collective-permute-done.2.rest_0_
  61.2 1.1 %tile.4.rest_2_ = f32[1024,512]{1,0:T(8,128)S(1)} custom-call(f32[1]{0:T(128)S(6)} %copy.8.t_ref, f32[1]{0:T(128)S(6)} %copy.9.b_ref, bf16[1024,512]{1,0:T(8,128)(2,1)S(1)} %bitcast.6, bf16[256,512]{1,0:T(8,128)(2,1)S(1)} %collective-permute-done.2.rest_0_, f32[1024,512]{1,0:T(8,128)S(1)} %tile.3.rest_1_), custom_call_target="tpu_custom_call" | custom-call | flops 536870912 | bytes 1310720 | tf_op jit(solution)/shard_map/tile/pallas_call | solution.py:187
  62.3 2.2 %collective-permute-done.rest_0_ = bf16[256,512]{1,0:T(8,128)(2,1)S(1)} collective-permute-done((bf16[256,512]{1,0:T(8,128)(2,1)S(1)}, bf16[256,512]{1,0:T(8,128)(2,1)S(1)}, u32[]{:S(2)}, u32[]{:S(2)}) %collective-permute-start) | collective-permute-done | bytes 262176 | tf_op jit(solution)/shard_map/ppermute | solution.py:263
  64.5 2.5 %collective-permute-done.1.rest_1_ = bf16[256,512]{1,0:T(8,128)(2,1)S(1)} collective-permute-done((bf16[256,512]{1,0:T(8,128)(2,1)S(1)}, bf16[256,512]{1,0:T(8,128)(2,1)S(1)}, u32[]{:S(2)}, u32[]{:S(2)}) %collective-permute-start.1) | collective-permute-done | bytes 262176 | tf_op jit(solution)/shard_map/ppermute | solution.py:263
  67.0 1.7 %tile.5 = bf16[1024,512]{1,0:T(8,128)(2,1)S(1)} custom-call(f32[1]{0:T(128)S(6)} %copy.8.t_ref, f32[1]{0:T(128)S(6)} %copy.9.b_ref, bf16[1024,512]{1,0:T(8,128)(2,1)S(1)} %bitcast.7, bf16[256,512]{1,0:T(8,128)(2,1)S(1)} %collective-permute-done.rest_0_, bf16[256,512]{1,0:T(8,128)(2,1)S(1)} %collective-permute-done.1.rest_1_, f32[1024,512]{1,0:T(8,128)S(1)} %tile.4.rest_2_), custom_call_target="tpu_custom_call" | custom-call | flops 1073741824 | bytes 1572864 | tf_op jit(solution)/shard_map/tile/pallas_call | solution.py:187
  68.8 0.0 copy-start
  68.8 0.0 copy-start.1
  68.8 23.8 %all_to_all.10.sums_ref = bf16[16,64,512]{2,1,0:T(8,128)(2,1)S(1)} all-to-all(bf16[16,64,512]{2,1,0:T(8,128)(2,1)S(1)} %bitcast.8), channel_id=1, replica_groups=mesh['ylo'=2,'zhi'=4,'zlo'=4,'x'=4,'yhi'=2,'core'=2] {'ylo','x','yhi'}, dimensions={0} | all-to-all | bytes 2097152 | tf_op jit(solution)/shard_map/all_to_all | solution.py:269
  92.6 0.2 finish.1
  92.8 8.5 %all-gather.2 = bf16[256,512]{1,0:T(8,128)(2,1)S(1)} all-gather(bf16[64,512]{1,0:T(8,128)(2,1)S(1)} %finish.1), channel_id=4, replica_groups=mesh['ylo'=2,'zhi'=4,'zlo'=4,'x'=4,'yhi'=2,'core'=2] {'yhi','core'}, dimensions={0}, use_global_device_ids=true | all-gather | bytes 327680 | tf_op jit(solution)/shard_map/all_gather | solution.py:270
  101.3 0.0 copy-done
  101.3 0.0 copy-done.1
  101.3 1.8 %heads_back.1 = (bf16[128,1536]{1,0:T(8,128)(2,1)}, bf16[128,1536]{1,0:T(8,128)(2,1)}) custom-call(bf16[4,64,512]{2,1,0:T(8,128)(2,1)S(1)} %bitcast.10, bf16[1536,512]{1,0:T(8,128)(2,1)S(1)} %copy-done, bf16[1536,512]{1,0:T(8,128)(2,1)S(1)} %copy-done.1), custom_call_target="tpu_custom_call" | custom-call | tf_op jit(solution)/shard_map/heads_back/pallas_call | solution.py:238
  (1 shorter events, 0.0 us)
Async XLA Ops:
  18.1 42.0 %all-to-all-start = ((bf16[16,64,512]{2,1,0:T(8,128)(2,1)}), bf16[16,64,512]{2,1,0:T(8,128)(2,1)S(1)}, u32[]{:S(2)}, u32[]{:S(2)}) async-start(bf16[16,64,512]{2,1,0:T(8,128)(2,1)} %get-tuple-element.17), calls=%async_computation | async-start | bytes 2097152 | tf_op jit(solution)/shard_map/all_to_all | solution.py:260
  44.5 15.6 %collective-permute-start.3 = (bf16[256,512]{1,0:T(8,128)(2,1)S(1)}, bf16[256,512]{1,0:T(8,128)(2,1)S(1)}, u32[]{:S(2)}, u32[]{:S(2)}) collective-permute-start(bf16[256,512]{1,0:T(8,128)(2,1)S(1)} %all_gather.25), channel_id=1, source_target_pairs={{17,0},{19,2},{21,4},{23,6},{25,8},{27,10},{29,12},{31,14},{273,25... | collective-permute-start | bytes 786440 | tf_op jit(solution)/shard_map/ppermute | solution.py:263
  50.7 10.5 %collective-permute-start.2 = (bf16[256,512]{1,0:T(8,128)(2,1)S(1)}, bf16[256,512]{1,0:T(8,128)(2,1)S(1)}, u32[]{:S(2)}, u32[]{:S(2)}) collective-permute-start(bf16[256,512]{1,0:T(8,128)(2,1)S(1)} %all_gather.25), channel_id=1, source_target_pairs={{1,0},{3,2},{5,4},{7,6},{9,8},{11,10},{13,12},{15,14},{257,256},{2... | collective-permute-start | bytes 786440 | tf_op jit(solution)/shard_map/ppermute | solution.py:263
  53.0 11.6 %collective-permute-start = (bf16[256,512]{1,0:T(8,128)(2,1)S(1)}, bf16[256,512]{1,0:T(8,128)(2,1)S(1)}, u32[]{:S(2)}, u32[]{:S(2)}) collective-permute-start(bf16[256,512]{1,0:T(8,128)(2,1)S(1)} %all_gather.25), channel_id=1, source_target_pairs={{241,0},{243,2},{245,4},{247,6},{249,8},{251,10},{253,12},{255,14}... | collective-permute-start | bytes 786440 | tf_op jit(solution)/shard_map/ppermute | solution.py:263
  56.6 10.4 %collective-permute-start.1 = (bf16[256,512]{1,0:T(8,128)(2,1)S(1)}, bf16[256,512]{1,0:T(8,128)(2,1)S(1)}, u32[]{:S(2)}, u32[]{:S(2)}) collective-permute-start(bf16[256,512]{1,0:T(8,128)(2,1)S(1)} %all_gather.25), channel_id=1, source_target_pairs={{33,0},{35,2},{37,4},{39,6},{41,8},{43,10},{45,12},{47,14},{289,25... | collective-permute-start | bytes 786440 | tf_op jit(solution)/shard_map/ppermute | solution.py:263
  68.8 32.6 %copy-start = (bf16[1536,512]{1,0:T(8,128)(2,1)S(1)}, bf16[1536,512]{1,0:T(8,128)(2,1)}, u32[]{:S(2)}) copy-start(bf16[1536,512]{1,0:T(8,128)(2,1)} %wv.3) | copy-start | bytes 4718596
  68.8 32.6 %copy-start.1 = (bf16[1536,512]{1,0:T(8,128)(2,1)S(1)}, bf16[1536,512]{1,0:T(8,128)(2,1)}, u32[]{:S(2)}) copy-start(bf16[1536,512]{1,0:T(8,128)(2,1)} %ws.3) | copy-start | bytes 4718596

commit v11 on v9

--- a/solution.py
+++ b/solution.py
@@ -148,12 +148,12 @@
     )(kept, got)
 
 
-def tile(sharpness, offset, mine, other, total, own, final=False, block=256):
+def tile(sharpness, offset, mine, others, total, own, positives=False, final=False, block=256):
     n, width = mine.shape
-    m = other.shape[0]
+    m = others[0].shape[0]
     blocks = n // block
 
-    def kernel(t_ref, b_ref, mine_ref, other_ref, *rest):
+    def kernel(t_ref, b_ref, mine_ref, *rest):
         out_ref = rest[-1]
         t = t_ref[0]
         slope, start = -LOG2E * t, -LOG2E * b_ref[0]
@@ -162,33 +162,36 @@
         other_at = jnp.where(lax.axis_index("core") == 0, zhi, last - zhi) * own
         for i in range(blocks):
             at = pl.multiple_of(lax.rem(mine_at // block + 1 + i, blocks) * block, block)
-            dots = lax.dot_general(
-                mine_ref[pl.ds(at, block)], other_ref[...], (((1,), (1,)), ((), ())), preferred_element_type=F32
-            )
-            e = jnp.exp2(dots * slope + start)
-            coef = pl.reciprocal(1.0 + e, approx=True)
-            if total is None and i == blocks - 1:
-                row = lax.broadcasted_iota(jnp.int32, (block, 1), 0) + (at - mine_at)
-                row = jnp.where((row >= 0) & (row < own), row, -m)
-                col = lax.broadcasted_iota(jnp.int32, (1, m), 1) - other_at
-                coef = jnp.where(row == col, -e, 1.0) * coef
-            sums = jnp.dot(coef.astype(BF), other_ref[...], preferred_element_type=F32)
-            if total is not None:
-                sums = sums + rest[0][pl.ds(at, block)]
+            sums = None if total is None else rest[len(others)][pl.ds(at, block)]
+            for other_ref in rest[: len(others)]:
+                dots = lax.dot_general(
+                    mine_ref[pl.ds(at, block)], other_ref[...], (((1,), (1,)), ((), ())), preferred_element_type=F32
+                )
+                e = jnp.exp2(dots * slope + start)
+                coef = pl.reciprocal(1.0 + e, approx=True)
+                if positives and i == blocks - 1:
+                    row = lax.broadcasted_iota(jnp.int32, (block, 1), 0) + (at - mine_at)
+                    row = jnp.where((row >= 0) & (row < own), row, -m)
+                    col = lax.broadcasted_iota(jnp.int32, (1, m), 1) - other_at
+                    coef = jnp.where(row == col, -e, 1.0) * coef
+                part = jnp.dot(coef.astype(BF), other_ref[...], preferred_element_type=F32)
+                sums = part if sums is None else sums + part
             out_ref[pl.ds(at, block)] = (t * sums).astype(BF) if final else sums
 
     totals = [] if total is None else [total]
     return pl.pallas_call(
         kernel,
         out_shape=pltpu.VMEM((n, width), BF if final else F32),
-        in_specs=[SMEM, SMEM, VMEM, VMEM] + [VMEM] * len(totals),
+        in_specs=[SMEM, SMEM, VMEM] + [VMEM] * (len(others) + len(totals)),
         out_specs=VMEM,
         compiler_params=pltpu.CompilerParams(vmem_limit_bytes=30 * MIB),
         cost_estimate=pl.CostEstimate(
-            flops=4 * n * m * width, bytes_accessed=2 * width * (n + m), transcendentals=2 * n * m
+            flops=4 * n * m * width * len(others),
+            bytes_accessed=2 * width * (n + m * len(others)),
+            transcendentals=2 * n * m * len(others),
         ),
         name="tile",
-    )(sharpness, offset, mine, other, *totals)
+    )(sharpness, offset, mine, *others, *totals)
 
 
 def finish(sums, embed):
@@ -251,10 +254,12 @@
     wide, line = lax.optimization_barrier((wide, line))
     mine = lax.all_to_all(wide, PLANE, 0, 0).reshape(peers * own, width)
     line = lax.all_gather(line, AXES, axis=0, tiled=True, axis_index_groups=far_groups(sizes))
-    near = [lax.ppermute(line, AXES, from_line(sizes, steps)) for steps in ((1, 1), (-1, -1), (2, -2))]
-    grad = tile(sharpness, offset, mine, line, None, own)
-    for other in near:
-        grad = tile(sharpness, offset, mine, other, grad, own, final=other is near[-1])
+    first, second, third = (
+        lax.ppermute(line, AXES, from_line(sizes, steps)) for steps in ((1, 1), (-1, -1), (2, -2))
+    )
+    grad = tile(sharpness, offset, mine, [line], None, own, positives=True)
+    grad = tile(sharpness, offset, mine, [first], grad, own)
+    grad = tile(sharpness, offset, mine, [second, third], grad, own, final=True)
 
     grad = lax.all_to_all(grad.reshape(peers, own, width), PLANE, 0, 0)
     delta = lax.all_gather(finish(grad, embed), GROUP, axis=0)

time: 101 us -> 102 us (level)
  waiting for transfers between devices: 6.8 us -> 7.93 us
    ppermute x3, waiting for transfers between devices: 6.79 us -> 7.92 us  [shards(): lax.ppermute(line, AXES, from_line(sizes, steps))]
    pallas_call x4 -> x3, Pallas kernels: 4.5 us -> 3.99 us  [tile(): pl.pallas_call(kernel, out_shape=pltpu.VMEM((n, width), BF if final else...]
  transfers between devices with their start and end apart: 4 -> 4, of which waited for: 1 -> 1; matrix products, arithmetic and copies ran while one was open for 0% -> 0% of each run, Pallas kernels for 3% -> 2%
where the time goes in v11:
time: 102 us; the launch traced here: 101 us
  blocking collectives  69.8 us (68%)
  starting transfers between devices  12 us (12%)
  Pallas kernels  9.73 us (10%)
  waiting for transfers between devices  7.93 us (8%)
  between operations  2.03 us (2%)
    all_gather x1, blocking collectives, shards(): lax.all_gather(line, AXES, axis=0, tiled=True, axis_index_groups=far_grou...  22.6 us
    all_to_all x1, blocking collectives, shards(): grad = lax.all_to_all(grad.reshape(peers, own, width), PLANE, 0, 0)  22.1 us
    all_gather x1, blocking collectives, shards(): delta = lax.all_gather(finish(grad, embed), GROUP, axis=0)  9.56 us
    all_gather x1, blocking collectives, shards(): lax.all_gather(heads(vision, sentence, vision_map, sentence_map), 'core',...  8.69 us
    ppermute x3, starting transfers between devices, shards(): lax.ppermute(line, AXES, from_line(sizes, steps))  8.31 us
    ppermute x3, waiting for transfers between devices, shards(): lax.ppermute(line, AXES, from_line(sizes, steps))  7.92 us
    all_gather x1, blocking collectives, shards(): wide, line, embed = units(kept, lax.all_gather(given, 'yhi', axis=0), peers)  6.89 us
    pallas_call x3, Pallas kernels, tile(): pl.pallas_call(kernel, out_shape=pltpu.VMEM((n, width), BF if final else...  3.99 us
  transfers between devices with their start and end apart: 4, of which 1 were waited for; matrix products, arithmetic and copies ran while one was open for 0% of the time, Pallas kernels for 2%

profile of v11, /device:TPU:1, one launch (start us, length us, event | category | flops | bytes accessed | tf_op | source)
XLA Modules:
  0.0 101.4 jit_solution(13313980094081197260)
XLA Ops:
  0.6 2.5 %heads.1 = bf16[2,64,1024]{2,1,0:T(8,128)(2,1)S(1)} custom-call(bf16[128,1536]{1,0:T(8,128)(2,1)} %v.1, bf16[128,1536]{1,0:T(8,128)(2,1)} %s.1, bf16[1536,512]{1,0:T(8,128)(2,1)} %wv.3, bf16[1536,512]{1,0:T(8,128)(2,1)} %ws.3), custom_call_target="tpu_custom_call" | custom-call | tf_op jit(solution)/shard_map/heads/pallas_call | solution.py:81
  3.1 8.7 %all-gather = bf16[4,64,1024]{2,1,0:T(8,128)(2,1)S(1)} all-gather(bf16[2,64,1024]{2,1,0:T(8,128)(2,1)S(1)} %heads.1), channel_id=2, replica_groups=mesh['ylo'=2,'zhi'=4,'zlo'=4,'x'=4,'yhi'=2,'core'=2] {'core'}, dimensions={0}, use_global_device_ids=true | all-gather | bytes 786432 | tf_op jit(solution)/shard_map/all_gather | solution.py:250
  11.8 0.1 chip_sums.1
  11.8 6.9 %all-gather.1 = bf16[128,1024]{1,0:T(8,128)(2,1)S(1)} all-gather(bf16[64,1024]{1,0:T(8,128)(2,1)S(1)} %get-tuple-element.10), channel_id=3, replica_groups=mesh['ylo'=2,'zhi'=4,'zlo'=4,'x'=4,'yhi'=2,'core'=2] {'yhi'}, dimensions={0}, use_global_device_ids=true | all-gather | bytes 393216 | tf_op jit(solution)/shard_map/all_gather | solution.py:252
  18.7 1.1 %units.1 = (bf16[16,64,512]{2,1,0:T(8,128)(2,1)}, bf16[64,512]{1,0:T(8,128)(2,1)S(1)}, f32[64,512]{1,0:T(8,128)S(1)}) custom-call(f32[64,1024]{1,0:T(8,128)S(1)} %get-tuple-element.9.kept_ref, bf16[2,64,1024]{2,1,0:T(8,128)(2,1)S(1)} %bitcast.10), custom_call_target="tpu_custom_call" | custom-call | tf_op jit(solution)/shard_map/units/pallas_call | solution.py:137
  19.9 3.7 %all-to-all-start = ((bf16[16,64,512]{2,1,0:T(8,128)(2,1)}), bf16[16,64,512]{2,1,0:T(8,128)(2,1)S(1)}, u32[]{:S(2)}, u32[]{:S(2)}) async-start(bf16[16,64,512]{2,1,0:T(8,128)(2,1)} %get-tuple-element.13), calls=%async_computation | async-start | bytes 2097152 | tf_op jit(solution)/shard_map/all_to_all | solution.py:255
  23.5 22.6 %all_gather.25.rest_0_ = bf16[256,512]{1,0:T(8,128)(2,1)S(1)} all-gather(bf16[64,512]{1,0:T(8,128)(2,1)S(1)} %get-tuple-element.14), channel_id=1, replica_groups={{0,64,128,192},{2,66,130,194},{4,68,132,196},{6,70,134,198},{8,72,136,2..., dimensions={0}, use_global_device_ids=true | all-gather | bytes 327680 | tf_op jit(solution)/shard_map/all_gather | solution.py:256
  46.1 3.5 %collective-permute-start.2 = (bf16[256,512]{1,0:T(8,128)(2,1)S(1)}, bf16[256,512]{1,0:T(8,128)(2,1)S(1)}, u32[]{:S(2)}, u32[]{:S(2)}) collective-permute-start(bf16[256,512]{1,0:T(8,128)(2,1)S(1)} %all_gather.25.rest_0_), channel_id=1, source_target_pairs={{16,0},{18,2},{20,4},{22,6},{24,8},{26,10},{28,12},{30,14},{272,25... | collective-permute-start | bytes 786440 | tf_op jit(solution)/shard_map/ppermute | solution.py:258
  49.6 1.9 %collective-permute-start = (bf16[256,512]{1,0:T(8,128)(2,1)S(1)}, bf16[256,512]{1,0:T(8,128)(2,1)S(1)}, u32[]{:S(2)}, u32[]{:S(2)}) collective-permute-start(bf16[256,512]{1,0:T(8,128)(2,1)S(1)} %all_gather.25.rest_0_), channel_id=1, source_target_pairs={{240,0},{242,2},{244,4},{246,6},{248,8},{250,10},{252,12},{254,14}... | collective-permute-start | bytes 786440 | tf_op jit(solution)/shard_map/ppermute | solution.py:258
  51.5 2.9 %collective-permute-start.1 = (bf16[256,512]{1,0:T(8,128)(2,1)S(1)}, bf16[256,512]{1,0:T(8,128)(2,1)S(1)}, u32[]{:S(2)}, u32[]{:S(2)}) collective-permute-start(bf16[256,512]{1,0:T(8,128)(2,1)S(1)} %all_gather.25.rest_0_), channel_id=1, source_target_pairs={{32,0},{34,2},{36,4},{38,6},{40,8},{42,10},{44,12},{46,14},{288,25... | collective-permute-start | bytes 786440 | tf_op jit(solution)/shard_map/ppermute | solution.py:258
  55.8 0.0 all-to-all-done
  55.8 1.1 %tile.3.rest_1_ = f32[1024,512]{1,0:T(8,128)S(1)} custom-call(f32[1]{0:T(128)S(6)} %copy.8.t_ref, f32[1]{0:T(128)S(6)} %copy.9.b_ref, bf16[1024,512]{1,0:T(8,128)(2,1)S(1)} %bitcast.5, bf16[256,512]{1,0:T(8,128)(2,1)S(1)} %all_gather.25.rest_0_), custom_call_target="tpu_custom_call" | custom-call | flops 536870912 | bytes 1310720 | tf_op jit(solution)/shard_map/tile/pallas_call | solution.py:182
  56.9 0.0 collective-permute-done.2.rest_0_
  56.9 1.1 %tile.4.rest_2_ = f32[1024,512]{1,0:T(8,128)S(1)} custom-call(f32[1]{0:T(128)S(6)} %copy.8.t_ref, f32[1]{0:T(128)S(6)} %copy.9.b_ref, bf16[1024,512]{1,0:T(8,128)(2,1)S(1)} %bitcast.6, bf16[256,512]{1,0:T(8,128)(2,1)S(1)} %collective-permute-done.2.rest_0_, f32[1024,512]{1,0:T(8,128)S(1)} %tile.3.rest_1_), custom_call_target="tpu_custom_call" | custom-call | flops 536870912 | bytes 1310720 | tf_op jit(solution)/shard_map/tile/pallas_call | solution.py:182
  58.0 0.0 collective-permute-done.rest_0_
  58.0 7.9 %collective-permute-done.1.rest_1_ = bf16[256,512]{1,0:T(8,128)(2,1)S(1)} collective-permute-done((bf16[256,512]{1,0:T(8,128)(2,1)S(1)}, bf16[256,512]{1,0:T(8,128)(2,1)S(1)}, u32[]{:S(2)}, u32[]{:S(2)}) %collective-permute-start.1) | collective-permute-done | bytes 262176 | tf_op jit(solution)/shard_map/ppermute | solution.py:258
  66.0 1.7 %tile.5 = bf16[1024,512]{1,0:T(8,128)(2,1)S(1)} custom-call(f32[1]{0:T(128)S(6)} %copy.8.t_ref, f32[1]{0:T(128)S(6)} %copy.9.b_ref, bf16[1024,512]{1,0:T(8,128)(2,1)S(1)} %bitcast.7, bf16[256,512]{1,0:T(8,128)(2,1)S(1)} %collective-permute-done.rest_0_, bf16[256,512]{1,0:T(8,128)(2,1)S(1)} %collective-permute-done.1.rest_1_, f32[1024,512]{1,0:T(8,128)S(1)} %tile.4.rest_2_), custom_call_target="tpu_custom_call" | custom-call | flops 1073741824 | bytes 1572864 | tf_op jit(solution)/shard_map/tile/pallas_call | solution.py:182
  67.7 0.0 copy-start
  67.7 0.0 copy-start.1
  67.7 22.1 %all_to_all.10.sums_ref = bf16[16,64,512]{2,1,0:T(8,128)(2,1)S(1)} all-to-all(bf16[16,64,512]{2,1,0:T(8,128)(2,1)S(1)} %bitcast.8), channel_id=1, replica_groups=mesh['ylo'=2,'zhi'=4,'zlo'=4,'x'=4,'yhi'=2,'core'=2] {'ylo','x','yhi'}, dimensions={0} | all-to-all | bytes 2097152 | tf_op jit(solution)/shard_map/all_to_all | solution.py:264
  89.8 0.2 finish.1
  90.0 9.6 %all-gather.2 = bf16[256,512]{1,0:T(8,128)(2,1)S(1)} all-gather(bf16[64,512]{1,0:T(8,128)(2,1)S(1)} %finish.1), channel_id=4, replica_groups=mesh['ylo'=2,'zhi'=4,'zlo'=4,'x'=4,'yhi'=2,'core'=2] {'yhi','core'}, dimensions={0}, use_global_device_ids=true | all-gather | bytes 327680 | tf_op jit(solution)/shard_map/all_gather | solution.py:265
  99.6 0.0 copy-done
  99.6 0.0 copy-done.1
  99.6 1.9 %heads_back.1 = (bf16[128,1536]{1,0:T(8,128)(2,1)}, bf16[128,1536]{1,0:T(8,128)(2,1)}) custom-call(bf16[4,64,512]{2,1,0:T(8,128)(2,1)S(1)} %bitcast.11, bf16[1536,512]{1,0:T(8,128)(2,1)S(1)} %copy-done, bf16[1536,512]{1,0:T(8,128)(2,1)S(1)} %copy-done.1), custom_call_target="tpu_custom_call" | custom-call | tf_op jit(solution)/shard_map/heads_back/pallas_call | solution.py:233
Async XLA Ops:
  19.9 35.9 %all-to-all-start = ((bf16[16,64,512]{2,1,0:T(8,128)(2,1)}), bf16[16,64,512]{2,1,0:T(8,128)(2,1)S(1)}, u32[]{:S(2)}, u32[]{:S(2)}) async-start(bf16[16,64,512]{2,1,0:T(8,128)(2,1)} %get-tuple-element.13), calls=%async_computation | async-start | bytes 2097152 | tf_op jit(solution)/shard_map/all_to_all | solution.py:255
  46.1 10.8 %collective-permute-start.2 = (bf16[256,512]{1,0:T(8,128)(2,1)S(1)}, bf16[256,512]{1,0:T(8,128)(2,1)S(1)}, u32[]{:S(2)}, u32[]{:S(2)}) collective-permute-start(bf16[256,512]{1,0:T(8,128)(2,1)S(1)} %all_gather.25.rest_0_), channel_id=1, source_target_pairs={{16,0},{18,2},{20,4},{22,6},{24,8},{26,10},{28,12},{30,14},{272,25... | collective-permute-start | bytes 786440 | tf_op jit(solution)/shard_map/ppermute | solution.py:258
  49.6 8.4 %collective-permute-start = (bf16[256,512]{1,0:T(8,128)(2,1)S(1)}, bf16[256,512]{1,0:T(8,128)(2,1)S(1)}, u32[]{:S(2)}, u32[]{:S(2)}) collective-permute-start(bf16[256,512]{1,0:T(8,128)(2,1)S(1)} %all_gather.25.rest_0_), channel_id=1, source_target_pairs={{240,0},{242,2},{244,4},{246,6},{248,8},{250,10},{252,12},{254,14}... | collective-permute-start | bytes 786440 | tf_op jit(solution)/shard_map/ppermute | solution.py:258
  51.5 14.4 %collective-permute-start.1 = (bf16[256,512]{1,0:T(8,128)(2,1)S(1)}, bf16[256,512]{1,0:T(8,128)(2,1)S(1)}, u32[]{:S(2)}, u32[]{:S(2)}) collective-permute-start(bf16[256,512]{1,0:T(8,128)(2,1)S(1)} %all_gather.25.rest_0_), channel_id=1, source_target_pairs={{32,0},{34,2},{36,4},{38,6},{40,8},{42,10},{44,12},{46,14},{288,25... | collective-permute-start | bytes 786440 | tf_op jit(solution)/shard_map/ppermute | solution.py:258
  67.7 31.9 %copy-start = (bf16[1536,512]{1,0:T(8,128)(2,1)S(1)}, bf16[1536,512]{1,0:T(8,128)(2,1)}, u32[]{:S(2)}) copy-start(bf16[1536,512]{1,0:T(8,128)(2,1)} %wv.3) | copy-start | bytes 4718596
  67.7 31.9 %copy-start.1 = (bf16[1536,512]{1,0:T(8,128)(2,1)S(1)}, bf16[1536,512]{1,0:T(8,128)(2,1)}, u32[]{:S(2)}) copy-start(bf16[1536,512]{1,0:T(8,128)(2,1)} %ws.3) | copy-start | bytes 4718596

commit v12 on v11

--- a/solution.py
+++ b/solution.py
@@ -120,7 +120,7 @@
 def units(kept, got, peers):
     own, width = kept.shape[0], kept.shape[1] // 2
 
-    def kernel(kept_ref, got_ref, wide_ref, line_ref, embed_ref):
+    def kernel(kept_ref, got_ref, wide_ref, line_ref, embed_ref, mine, sems):
         towers = [slice(0, width), slice(width, 2 * width)]
         for yhi in range(2):
             for core in range(2):
@@ -129,20 +129,25 @@
                 def _():
                     embed = [kept_ref[:, cut] + got_ref[1 - yhi, :, cut].astype(F32) for cut in towers]
                     embed_ref[...] = embed[core]
-                    mine = normalize(embed[core])[1].astype(BF)
-                    for peer in range(peers):
-                        wide_ref[peer] = mine
+                    mine[...] = normalize(embed[core])[1].astype(BF)
                     line_ref[...] = normalize(embed[1 - core])[1].astype(BF)
 
+        copies = [pltpu.make_async_copy(mine, wide_ref.at[peer], sems.at[peer]) for peer in range(peers)]
+        for copy in copies:
+            copy.start()
+        for copy in copies:
+            copy.wait()
+
     return pl.pallas_call(
         kernel,
         out_shape=[
-            pltpu.VMEM((peers, own, width), BF),
+            jax.ShapeDtypeStruct((peers, own, width), BF),
             pltpu.VMEM((own, width), BF),
             pltpu.VMEM((own, width), F32),
         ],
         in_specs=[VMEM] * 2,
-        out_specs=[VMEM] * 3,
+        out_specs=[HBM, VMEM, VMEM],
+        scratch_shapes=[pltpu.VMEM((own, width), BF), pltpu.SemaphoreType.DMA((peers,))],
         compiler_params=pltpu.CompilerParams(vmem_limit_bytes=20 * MIB),
         name="units",
     )(kept, got)
@@ -168,7 +173,7 @@
                     mine_ref[pl.ds(at, block)], other_ref[...], (((1,), (1,)), ((), ())), preferred_element_type=F32
                 )
                 e = jnp.exp2(dots * slope + start)
-                coef = pl.reciprocal(1.0 + e, approx=True)
+                coef = pl.reciprocal(1.0 + e)
                 if positives and i == blocks - 1:
                     row = lax.broadcasted_iota(jnp.int32, (block, 1), 0) + (at - mine_at)
                     row = jnp.where((row >= 0) & (row < own), row, -m)
@@ -258,8 +263,8 @@
         lax.ppermute(line, AXES, from_line(sizes, steps)) for steps in ((1, 1), (-1, -1), (2, -2))
     )
     grad = tile(sharpness, offset, mine, [line], None, own, positives=True)
-    grad = tile(sharpness, offset, mine, [first], grad, own)
-    grad = tile(sharpness, offset, mine, [second, third], grad, own, final=True)
+    grad = tile(sharpness, offset, mine, [third], grad, own)
+    grad = tile(sharpness, offset, mine, [first, second], grad, own, final=True)
 
     grad = lax.all_to_all(grad.reshape(peers, own, width), PLANE, 0, 0)
     delta = lax.all_gather(finish(grad, embed), GROUP, axis=0)

time: 102 us -> 97.8 us (0.959)
  waiting for transfers between devices: 7.93 us -> 3.02 us
    ppermute x3, waiting for transfers between devices: 7.92 us -> 3.01 us  [shards(): lax.ppermute(line, AXES, from_line(sizes, steps))]
    all_gather x1, blocking collectives: 9.56 us -> 12.8 us  [shards(): delta = lax.all_gather(finish(grad, embed), GROUP, axis=0)]
    all_to_all x1, blocking collectives: 22.1 us -> 19 us  [shards(): grad = lax.all_to_all(grad.reshape(peers, own, width), PLANE, 0, 0)]
where the time goes in v12:
time: 97.8 us; the launch traced here: 97.4 us
  blocking collectives  70 us (72%)
  starting transfers between devices  12.5 us (13%)
  Pallas kernels  9.83 us (10%)
  waiting for transfers between devices  3.02 us (3%)
  between operations  2.03 us (2%)
    all_gather x1, blocking collectives, shards(): lax.all_gather(line, AXES, axis=0, tiled=True, axis_index_groups=far_grou...  22.6 us
    all_to_all x1, blocking collectives, shards(): grad = lax.all_to_all(grad.reshape(peers, own, width), PLANE, 0, 0)  19 us
    all_gather x1, blocking collectives, shards(): delta = lax.all_gather(finish(grad, embed), GROUP, axis=0)  12.8 us
    ppermute x3, starting transfers between devices, shards(): lax.ppermute(line, AXES, from_line(sizes, steps))  8.88 us
    all_gather x1, blocking collectives, shards(): lax.all_gather(heads(vision, sentence, vision_map, sentence_map), 'core',...  8.69 us
    all_gather x1, blocking collectives, shards(): wide, line, embed = units(kept, lax.all_gather(given, 'yhi', axis=0), peers)  6.89 us
    pallas_call x3, Pallas kernels, tile(): pl.pallas_call(kernel, out_shape=pltpu.VMEM((n, width), BF if final else...  3.99 us
    all_to_all x1, starting transfers between devices, shards(): mine = lax.all_to_all(wide, PLANE, 0, 0).reshape(peers * own, width)  3.66 us
  transfers between devices with their start and end apart: 4, of which 1 were waited for; matrix products, arithmetic and copies ran while one was open for 0% of the time, Pallas kernels for 2%

profile of v12, /device:TPU:1, one launch (start us, length us, event | category | flops | bytes accessed | tf_op | source)
XLA Modules:
  0.0 97.4 jit_solution(14309700707029190388)
XLA Ops:
  0.6 2.5 %heads.1 = bf16[2,64,1024]{2,1,0:T(8,128)(2,1)S(1)} custom-call(bf16[128,1536]{1,0:T(8,128)(2,1)} %v.1, bf16[128,1536]{1,0:T(8,128)(2,1)} %s.1, bf16[1536,512]{1,0:T(8,128)(2,1)} %wv.3, bf16[1536,512]{1,0:T(8,128)(2,1)} %ws.3), custom_call_target="tpu_custom_call" | custom-call | tf_op jit(solution)/shard_map/heads/pallas_call | solution.py:81
  3.1 8.7 %all-gather = bf16[4,64,1024]{2,1,0:T(8,128)(2,1)S(1)} all-gather(bf16[2,64,1024]{2,1,0:T(8,128)(2,1)S(1)} %heads.1), channel_id=2, replica_groups=mesh['ylo'=2,'zhi'=4,'zlo'=4,'x'=4,'yhi'=2,'core'=2] {'core'}, dimensions={0}, use_global_device_ids=true | all-gather | bytes 786432 | tf_op jit(solution)/shard_map/all_gather | solution.py:255
  11.8 0.1 chip_sums.1
  11.8 6.9 %all-gather.1 = bf16[128,1024]{1,0:T(8,128)(2,1)S(1)} all-gather(bf16[64,1024]{1,0:T(8,128)(2,1)S(1)} %get-tuple-element.10), channel_id=3, replica_groups=mesh['ylo'=2,'zhi'=4,'zlo'=4,'x'=4,'yhi'=2,'core'=2] {'yhi'}, dimensions={0}, use_global_device_ids=true | all-gather | bytes 393216 | tf_op jit(solution)/shard_map/all_gather | solution.py:257
  18.7 1.2 %units.1 = (bf16[16,64,512]{2,1,0:T(8,128)(2,1)}, bf16[64,512]{1,0:T(8,128)(2,1)S(1)}, f32[64,512]{1,0:T(8,128)S(1)}) custom-call(f32[64,1024]{1,0:T(8,128)S(1)} %get-tuple-element.9.kept_ref, bf16[2,64,1024]{2,1,0:T(8,128)(2,1)S(1)} %bitcast.10), custom_call_target="tpu_custom_call" | custom-call | tf_op jit(solution)/shard_map/units/pallas_call | solution.py:141
  20.0 3.7 %all-to-all-start = ((bf16[16,64,512]{2,1,0:T(8,128)(2,1)}), bf16[16,64,512]{2,1,0:T(8,128)(2,1)S(1)}, u32[]{:S(2)}, u32[]{:S(2)}) async-start(bf16[16,64,512]{2,1,0:T(8,128)(2,1)} %get-tuple-element.13), calls=%async_computation | async-start | bytes 2097152 | tf_op jit(solution)/shard_map/all_to_all | solution.py:260
  23.6 22.6 %all_gather.25.rest_0_ = bf16[256,512]{1,0:T(8,128)(2,1)S(1)} all-gather(bf16[64,512]{1,0:T(8,128)(2,1)S(1)} %get-tuple-element.14), channel_id=1, replica_groups={{0,64,128,192},{2,66,130,194},{4,68,132,196},{6,70,134,198},{8,72,136,2..., dimensions={0}, use_global_device_ids=true | all-gather | bytes 327680 | tf_op jit(solution)/shard_map/all_gather | solution.py:261
  46.2 3.0 %collective-permute-start.2 = (bf16[256,512]{1,0:T(8,128)(2,1)S(1)}, bf16[256,512]{1,0:T(8,128)(2,1)S(1)}, u32[]{:S(2)}, u32[]{:S(2)}) collective-permute-start(bf16[256,512]{1,0:T(8,128)(2,1)S(1)} %all_gather.25.rest_0_), channel_id=1, source_target_pairs={{32,0},{34,2},{36,4},{38,6},{40,8},{42,10},{44,12},{46,14},{288,25... | collective-permute-start | bytes 786440 | tf_op jit(solution)/shard_map/ppermute | solution.py:263
  49.3 3.9 %collective-permute-start = (bf16[256,512]{1,0:T(8,128)(2,1)S(1)}, bf16[256,512]{1,0:T(8,128)(2,1)S(1)}, u32[]{:S(2)}, u32[]{:S(2)}) collective-permute-start(bf16[256,512]{1,0:T(8,128)(2,1)S(1)} %all_gather.25.rest_0_), channel_id=1, source_target_pairs={{16,0},{18,2},{20,4},{22,6},{24,8},{26,10},{28,12},{30,14},{272,25... | collective-permute-start | bytes 786440 | tf_op jit(solution)/shard_map/ppermute | solution.py:263
  53.2 1.9 %collective-permute-start.1 = (bf16[256,512]{1,0:T(8,128)(2,1)S(1)}, bf16[256,512]{1,0:T(8,128)(2,1)S(1)}, u32[]{:S(2)}, u32[]{:S(2)}) collective-permute-start(bf16[256,512]{1,0:T(8,128)(2,1)S(1)} %all_gather.25.rest_0_), channel_id=1, source_target_pairs={{240,0},{242,2},{244,4},{246,6},{248,8},{250,10},{252,12},{254,14}... | collective-permute-start | bytes 786440 | tf_op jit(solution)/shard_map/ppermute | solution.py:263
  56.5 0.0 all-to-all-done
  56.5 1.1 %tile.3.rest_1_ = f32[1024,512]{1,0:T(8,128)S(1)} custom-call(f32[1]{0:T(128)S(6)} %copy.8.t_ref, f32[1]{0:T(128)S(6)} %copy.9.b_ref, bf16[1024,512]{1,0:T(8,128)(2,1)S(1)} %bitcast.5, bf16[256,512]{1,0:T(8,128)(2,1)S(1)} %all_gather.25.rest_0_), custom_call_target="tpu_custom_call" | custom-call | flops 536870912 | bytes 1310720 | tf_op jit(solution)/shard_map/tile/pallas_call | solution.py:187
  57.6 0.0 collective-permute-done.2.rest_0_
  57.6 1.1 %tile.4.rest_2_ = f32[1024,512]{1,0:T(8,128)S(1)} custom-call(f32[1]{0:T(128)S(6)} %copy.8.t_ref, f32[1]{0:T(128)S(6)} %copy.9.b_ref, bf16[1024,512]{1,0:T(8,128)(2,1)S(1)} %bitcast.6, bf16[256,512]{1,0:T(8,128)(2,1)S(1)} %collective-permute-done.2.rest_0_, f32[1024,512]{1,0:T(8,128)S(1)} %tile.3.rest_1_), custom_call_target="tpu_custom_call" | custom-call | flops 536870912 | bytes 1310720 | tf_op jit(solution)/shard_map/tile/pallas_call | solution.py:187
  58.7 3.0 %collective-permute-done.rest_0_ = bf16[256,512]{1,0:T(8,128)(2,1)S(1)} collective-permute-done((bf16[256,512]{1,0:T(8,128)(2,1)S(1)}, bf16[256,512]{1,0:T(8,128)(2,1)S(1)}, u32[]{:S(2)}, u32[]{:S(2)}) %collective-permute-start) | collective-permute-done | bytes 262176 | tf_op jit(solution)/shard_map/ppermute | solution.py:263
  61.7 0.0 collective-permute-done.1.rest_1_
  61.7 1.7 %tile.5 = bf16[1024,512]{1,0:T(8,128)(2,1)S(1)} custom-call(f32[1]{0:T(128)S(6)} %copy.8.t_ref, f32[1]{0:T(128)S(6)} %copy.9.b_ref, bf16[1024,512]{1,0:T(8,128)(2,1)S(1)} %bitcast.7, bf16[256,512]{1,0:T(8,128)(2,1)S(1)} %collective-permute-done.rest_0_, bf16[256,512]{1,0:T(8,128)(2,1)S(1)} %collective-permute-done.1.rest_1_, f32[1024,512]{1,0:T(8,128)S(1)} %tile.4.rest_2_), custom_call_target="tpu_custom_call" | custom-call | flops 1073741824 | bytes 1572864 | tf_op jit(solution)/shard_map/tile/pallas_call | solution.py:187
  63.5 0.0 copy-start
  63.5 0.0 copy-start.1
  63.5 19.0 %all_to_all.10.sums_ref = bf16[16,64,512]{2,1,0:T(8,128)(2,1)S(1)} all-to-all(bf16[16,64,512]{2,1,0:T(8,128)(2,1)S(1)} %bitcast.8), channel_id=1, replica_groups=mesh['ylo'=2,'zhi'=4,'zlo'=4,'x'=4,'yhi'=2,'core'=2] {'ylo','x','yhi'}, dimensions={0} | all-to-all | bytes 2097152 | tf_op jit(solution)/shard_map/all_to_all | solution.py:269
  82.5 0.2 finish.1
  82.7 12.8 %all-gather.2 = bf16[256,512]{1,0:T(8,128)(2,1)S(1)} all-gather(bf16[64,512]{1,0:T(8,128)(2,1)S(1)} %finish.1), channel_id=4, replica_groups=mesh['ylo'=2,'zhi'=4,'zlo'=4,'x'=4,'yhi'=2,'core'=2] {'yhi','core'}, dimensions={0}, use_global_device_ids=true | all-gather | bytes 327680 | tf_op jit(solution)/shard_map/all_gather | solution.py:270
  95.5 0.0 copy-done
  95.5 0.0 copy-done.1
  95.5 1.9 %heads_back.1 = (bf16[128,1536]{1,0:T(8,128)(2,1)}, bf16[128,1536]{1,0:T(8,128)(2,1)}) custom-call(bf16[4,64,512]{2,1,0:T(8,128)(2,1)S(1)} %bitcast.11, bf16[1536,512]{1,0:T(8,128)(2,1)S(1)} %copy-done, bf16[1536,512]{1,0:T(8,128)(2,1)S(1)} %copy-done.1), custom_call_target="tpu_custom_call" | custom-call | tf_op jit(solution)/shard_map/heads_back/pallas_call | solution.py:238
Async XLA Ops:
  20.0 36.5 %all-to-all-start = ((bf16[16,64,512]{2,1,0:T(8,128)(2,1)}), bf16[16,64,512]{2,1,0:T(8,128)(2,1)S(1)}, u32[]{:S(2)}, u32[]{:S(2)}) async-start(bf16[16,64,512]{2,1,0:T(8,128)(2,1)} %get-tuple-element.13), calls=%async_computation | async-start | bytes 2097152 | tf_op jit(solution)/shard_map/all_to_all | solution.py:260
  46.2 11.3 %collective-permute-start.2 = (bf16[256,512]{1,0:T(8,128)(2,1)S(1)}, bf16[256,512]{1,0:T(8,128)(2,1)S(1)}, u32[]{:S(2)}, u32[]{:S(2)}) collective-permute-start(bf16[256,512]{1,0:T(8,128)(2,1)S(1)} %all_gather.25.rest_0_), channel_id=1, source_target_pairs={{32,0},{34,2},{36,4},{38,6},{40,8},{42,10},{44,12},{46,14},{288,25... | collective-permute-start | bytes 786440 | tf_op jit(solution)/shard_map/ppermute | solution.py:263
  49.3 12.5 %collective-permute-start = (bf16[256,512]{1,0:T(8,128)(2,1)S(1)}, bf16[256,512]{1,0:T(8,128)(2,1)S(1)}, u32[]{:S(2)}, u32[]{:S(2)}) collective-permute-start(bf16[256,512]{1,0:T(8,128)(2,1)S(1)} %all_gather.25.rest_0_), channel_id=1, source_target_pairs={{16,0},{18,2},{20,4},{22,6},{24,8},{26,10},{28,12},{30,14},{272,25... | collective-permute-start | bytes 786440 | tf_op jit(solution)/shard_map/ppermute | solution.py:263
  53.2 8.5 %collective-permute-start.1 = (bf16[256,512]{1,0:T(8,128)(2,1)S(1)}, bf16[256,512]{1,0:T(8,128)(2,1)S(1)}, u32[]{:S(2)}, u32[]{:S(2)}) collective-permute-start(bf16[256,512]{1,0:T(8,128)(2,1)S(1)} %all_gather.25.rest_0_), channel_id=1, source_target_pairs={{240,0},{242,2},{244,4},{246,6},{248,8},{250,10},{252,12},{254,14}... | collective-permute-start | bytes 786440 | tf_op jit(solution)/shard_map/ppermute | solution.py:263
  63.5 32.1 %copy-start = (bf16[1536,512]{1,0:T(8,128)(2,1)S(1)}, bf16[1536,512]{1,0:T(8,128)(2,1)}, u32[]{:S(2)}) copy-start(bf16[1536,512]{1,0:T(8,128)(2,1)} %wv.3) | copy-start | bytes 4718596
  63.5 32.0 %copy-start.1 = (bf16[1536,512]{1,0:T(8,128)(2,1)S(1)}, bf16[1536,512]{1,0:T(8,128)(2,1)}, u32[]{:S(2)}) copy-start(bf16[1536,512]{1,0:T(8,128)(2,1)} %ws.3) | copy-start | bytes 4718596

commit v13 on v11

--- a/solution.py
+++ b/solution.py
@@ -29,11 +29,11 @@
     return (inv, embed * inv)
 
 
-def far_groups(sizes):
+def opposite_groups(sizes, axis):
     ids = np.arange(math.prod(sizes)).reshape(sizes)
     groups = []
     for core in range(2):
-        part = np.moveaxis(ids[..., core], 1, -1).reshape(-1, sizes[1])
+        part = np.moveaxis(ids[..., core], AXES.index(axis), -1).reshape(-1, sizes[AXES.index(axis)])
         groups += (part[:, ::-1] if core == 1 else part).tolist()
     return groups
 
@@ -127,7 +127,8 @@
 
                 @pl.when((lax.axis_index("yhi") == yhi) & (lax.axis_index("core") == core))
                 def _():
-                    embed = [kept_ref[:, cut] + got_ref[1 - yhi, :, cut].astype(F32) for cut in towers]
+                    other = 1 - yhi if core == 0 else yhi
+                    embed = [kept_ref[:, cut] + got_ref[other, :, cut].astype(F32) for cut in towers]
                     embed_ref[...] = embed[core]
                     mine = normalize(embed[core])[1].astype(BF)
                     for peer in range(peers):
@@ -168,7 +169,7 @@
                     mine_ref[pl.ds(at, block)], other_ref[...], (((1,), (1,)), ((), ())), preferred_element_type=F32
                 )
                 e = jnp.exp2(dots * slope + start)
-                coef = pl.reciprocal(1.0 + e, approx=True)
+                coef = pl.reciprocal(1.0 + e)
                 if positives and i == blocks - 1:
                     row = lax.broadcasted_iota(jnp.int32, (block, 1), 0) + (at - mine_at)
                     row = jnp.where((row >= 0) & (row < own), row, -m)
@@ -247,15 +248,18 @@
     sizes = [lax.axis_size(a) for a in AXES]
     peers = lax.axis_size(PLANE)
 
+    def gather(x, axis):
+        return lax.all_gather(x, AXES, axis=0, axis_index_groups=opposite_groups(sizes, axis))
+
     parts = lax.all_gather(heads(vision, sentence, vision_map, sentence_map), "core", axis=0)
     given, kept = chip_sums(parts)
-    wide, line, embed = units(kept, lax.all_gather(given, "yhi", axis=0), peers)
+    wide, line, embed = units(kept, gather(given, "yhi"), peers)
 
     wide, line = lax.optimization_barrier((wide, line))
     mine = lax.all_to_all(wide, PLANE, 0, 0).reshape(peers * own, width)
-    line = lax.all_gather(line, AXES, axis=0, tiled=True, axis_index_groups=far_groups(sizes))
+    line = gather(line, "zhi").reshape(-1, width)
     first, second, third = (
-        lax.ppermute(line, AXES, from_line(sizes, steps)) for steps in ((1, 1), (-1, -1), (2, -2))
+        lax.ppermute(line, AXES, from_line(sizes, steps)) for steps in ((2, -2), (-1, 1), (1, -1))
     )
     grad = tile(sharpness, offset, mine, [line], None, own, positives=True)
     grad = tile(sharpness, offset, mine, [first], grad, own)

time: 102 us -> 100 us (0.980)
  waiting for transfers between devices: 7.93 us -> 5.35 us
    ppermute x3, waiting for transfers between devices: 7.92 us -> 5.35 us  [shards(): lax.ppermute(line, AXES, from_line(sizes, steps))]
  transfers between devices with their start and end apart: 4 -> 4, of which waited for: 1 -> 2; matrix products, arithmetic and copies ran while one was open for 0% -> 0% of each run, Pallas kernels for 2% -> 2%
where the time goes in v13:
time: 100 us; the launch traced here: 99.6 us
  blocking collectives  70 us (70%)
  starting transfers between devices  12.5 us (12%)
  Pallas kernels  9.74 us (10%)
  waiting for transfers between devices  5.35 us (5%)
  between operations  2.02 us (2%)
    all_gather x2, blocking collectives, gather(): lax.all_gather(x, AXES, axis=0, axis_index_groups=opposite_groups(sizes,...  29.5 us
    all_to_all x1, blocking collectives, shards(): grad = lax.all_to_all(grad.reshape(peers, own, width), PLANE, 0, 0)  22.2 us
    all_gather x1, blocking collectives, shards(): delta = lax.all_gather(finish(grad, embed), GROUP, axis=0)  9.61 us
    ppermute x3, starting transfers between devices, shards(): lax.ppermute(line, AXES, from_line(sizes, steps))  8.88 us
    all_gather x1, blocking collectives, shards(): lax.all_gather(heads(vision, sentence, vision_map, sentence_map), 'core',...  8.69 us
    ppermute x3, waiting for transfers between devices, shards(): lax.ppermute(line, AXES, from_line(sizes, steps))  5.35 us
    pallas_call x3, Pallas kernels, tile(): pl.pallas_call(kernel, out_shape=pltpu.VMEM((n, width), BF if final else...  3.99 us
    all_to_all x1, starting transfers between devices, shards(): mine = lax.all_to_all(wide, PLANE, 0, 0).reshape(peers * own, width)  3.65 us
  transfers between devices with their start and end apart: 4, of which 2 were waited for; matrix products, arithmetic and copies ran while one was open for 0% of the time, Pallas kernels for 2%

profile of v13, /device:TPU:1, one launch (start us, length us, event | category | flops | bytes accessed | tf_op | source)
XLA Modules:
  0.0 99.6 jit_solution(2795726431624785897)
XLA Ops:
  0.6 2.5 %heads.1 = bf16[2,64,1024]{2,1,0:T(8,128)(2,1)S(1)} custom-call(bf16[128,1536]{1,0:T(8,128)(2,1)} %v.1, bf16[128,1536]{1,0:T(8,128)(2,1)} %s.1, bf16[1536,512]{1,0:T(8,128)(2,1)} %wv.3, bf16[1536,512]{1,0:T(8,128)(2,1)} %ws.3), custom_call_target="tpu_custom_call" | custom-call | tf_op jit(solution)/shard_map/heads/pallas_call | solution.py:81
  3.1 8.7 %all-gather = bf16[4,64,1024]{2,1,0:T(8,128)(2,1)S(1)} all-gather(bf16[2,64,1024]{2,1,0:T(8,128)(2,1)S(1)} %heads.1), channel_id=2, replica_groups=mesh['ylo'=2,'zhi'=4,'zlo'=4,'x'=4,'yhi'=2,'core'=2] {'core'}, dimensions={0}, use_global_device_ids=true | all-gather | bytes 786432 | tf_op jit(solution)/shard_map/all_gather | solution.py:254
  11.8 0.1 chip_sums.1
  11.8 6.9 %all-gather.1 = bf16[128,1024]{1,0:T(8,128)(2,1)S(1)} all-gather(bf16[64,1024]{1,0:T(8,128)(2,1)S(1)} %get-tuple-element.10), channel_id=3, replica_groups={{0,2},{4,6},{8,10},{12,14},{16,18},{20,22},{24,26},{28,30},{32,34},{36,..., dimensions={0}, use_global_device_ids=true | all-gather | bytes 393216 | tf_op jit(solution)/shard_map/all_gather | solution.py:252
  18.7 1.1 %units.1 = (bf16[16,64,512]{2,1,0:T(8,128)(2,1)}, bf16[64,512]{1,0:T(8,128)(2,1)S(1)}, f32[64,512]{1,0:T(8,128)S(1)}) custom-call(f32[64,1024]{1,0:T(8,128)S(1)} %get-tuple-element.9.kept_ref, bf16[2,64,1024]{2,1,0:T(8,128)(2,1)S(1)} %bitcast.10), custom_call_target="tpu_custom_call" | custom-call | tf_op jit(solution)/shard_map/units/pallas_call | solution.py:138
  19.9 3.7 %all-to-all-start = ((bf16[16,64,512]{2,1,0:T(8,128)(2,1)}), bf16[16,64,512]{2,1,0:T(8,128)(2,1)S(1)}, u32[]{:S(2)}, u32[]{:S(2)}) async-start(bf16[16,64,512]{2,1,0:T(8,128)(2,1)} %get-tuple-element.13), calls=%async_computation | async-start | bytes 2097152 | tf_op jit(solution)/shard_map/all_to_all | solution.py:259
  23.5 22.6 %all-gather.2.rest_0_ = bf16[256,512]{1,0:T(8,128)(2,1)S(1)} all-gather(bf16[64,512]{1,0:T(8,128)(2,1)S(1)} %get-tuple-element.14), channel_id=4, replica_groups={{0,64,128,192},{2,66,130,194},{4,68,132,196},{6,70,134,198},{8,72,136,2..., dimensions={0}, use_global_device_ids=true | all-gather | bytes 327680 | tf_op jit(solution)/shard_map/all_gather | solution.py:252
  46.1 3.0 %collective-permute-start.2 = (bf16[256,512]{1,0:T(8,128)(2,1)S(1)}, bf16[256,512]{1,0:T(8,128)(2,1)S(1)}, u32[]{:S(2)}, u32[]{:S(2)}) collective-permute-start(bf16[256,512]{1,0:T(8,128)(2,1)S(1)} %all-gather.2.rest_0_), channel_id=1, source_target_pairs={{32,0},{34,2},{36,4},{38,6},{40,8},{42,10},{44,12},{46,14},{288,25... | collective-permute-start | bytes 786440 | tf_op jit(solution)/shard_map/ppermute | solution.py:262
  49.2 3.9 %collective-permute-start = (bf16[256,512]{1,0:T(8,128)(2,1)S(1)}, bf16[256,512]{1,0:T(8,128)(2,1)S(1)}, u32[]{:S(2)}, u32[]{:S(2)}) collective-permute-start(bf16[256,512]{1,0:T(8,128)(2,1)S(1)} %all-gather.2.rest_0_), channel_id=1, source_target_pairs={{240,0},{242,2},{244,4},{246,6},{248,8},{250,10},{252,12},{254,14}... | collective-permute-start | bytes 786440 | tf_op jit(solution)/shard_map/ppermute | solution.py:262
  53.1 1.9 %collective-permute-start.1 = (bf16[256,512]{1,0:T(8,128)(2,1)S(1)}, bf16[256,512]{1,0:T(8,128)(2,1)S(1)}, u32[]{:S(2)}, u32[]{:S(2)}) collective-permute-start(bf16[256,512]{1,0:T(8,128)(2,1)S(1)} %all-gather.2.rest_0_), channel_id=1, source_target_pairs={{16,0},{18,2},{20,4},{22,6},{24,8},{26,10},{28,12},{30,14},{272,25... | collective-permute-start | bytes 786440 | tf_op jit(solution)/shard_map/ppermute | solution.py:262
  56.3 0.0 all-to-all-done
  56.3 1.1 %tile.3.rest_1_ = f32[1024,512]{1,0:T(8,128)S(1)} custom-call(f32[1]{0:T(128)S(6)} %copy.8.t_ref, f32[1]{0:T(128)S(6)} %copy.9.b_ref, bf16[1024,512]{1,0:T(8,128)(2,1)S(1)} %bitcast.5, bf16[256,512]{1,0:T(8,128)(2,1)S(1)} %all-gather.2.rest_0_), custom_call_target="tpu_custom_call" | custom-call | flops 536870912 | bytes 1310720 | tf_op jit(solution)/shard_map/tile/pallas_call | solution.py:183
  57.5 0.0 collective-permute-done.2.rest_0_
  57.5 1.1 %tile.4.rest_2_ = f32[1024,512]{1,0:T(8,128)S(1)} custom-call(f32[1]{0:T(128)S(6)} %copy.8.t_ref, f32[1]{0:T(128)S(6)} %copy.9.b_ref, bf16[1024,512]{1,0:T(8,128)(2,1)S(1)} %bitcast.6, bf16[256,512]{1,0:T(8,128)(2,1)S(1)} %collective-permute-done.2.rest_0_, f32[1024,512]{1,0:T(8,128)S(1)} %tile.3.rest_1_), custom_call_target="tpu_custom_call" | custom-call | flops 536870912 | bytes 1310720 | tf_op jit(solution)/shard_map/tile/pallas_call | solution.py:183
  58.6 3.0 %collective-permute-done.rest_0_ = bf16[256,512]{1,0:T(8,128)(2,1)S(1)} collective-permute-done((bf16[256,512]{1,0:T(8,128)(2,1)S(1)}, bf16[256,512]{1,0:T(8,128)(2,1)S(1)}, u32[]{:S(2)}, u32[]{:S(2)}) %collective-permute-start) | collective-permute-done | bytes 262176 | tf_op jit(solution)/shard_map/ppermute | solution.py:262
  61.6 2.3 %collective-permute-done.1.rest_1_ = bf16[256,512]{1,0:T(8,128)(2,1)S(1)} collective-permute-done((bf16[256,512]{1,0:T(8,128)(2,1)S(1)}, bf16[256,512]{1,0:T(8,128)(2,1)S(1)}, u32[]{:S(2)}, u32[]{:S(2)}) %collective-permute-start.1) | collective-permute-done | bytes 262176 | tf_op jit(solution)/shard_map/ppermute | solution.py:262
  64.0 1.7 %tile.5 = bf16[1024,512]{1,0:T(8,128)(2,1)S(1)} custom-call(f32[1]{0:T(128)S(6)} %copy.8.t_ref, f32[1]{0:T(128)S(6)} %copy.9.b_ref, bf16[1024,512]{1,0:T(8,128)(2,1)S(1)} %bitcast.7, bf16[256,512]{1,0:T(8,128)(2,1)S(1)} %collective-permute-done.rest_0_, bf16[256,512]{1,0:T(8,128)(2,1)S(1)} %collective-permute-done.1.rest_1_, f32[1024,512]{1,0:T(8,128)S(1)} %tile.4.rest_2_), custom_call_target="tpu_custom_call" | custom-call | flops 1073741824 | bytes 1572864 | tf_op jit(solution)/shard_map/tile/pallas_call | solution.py:183
  65.7 0.0 copy-start
  65.7 0.0 copy-start.1
  65.7 22.2 %all_to_all.10.sums_ref = bf16[16,64,512]{2,1,0:T(8,128)(2,1)S(1)} all-to-all(bf16[16,64,512]{2,1,0:T(8,128)(2,1)S(1)} %bitcast.8), channel_id=1, replica_groups=mesh['ylo'=2,'zhi'=4,'zlo'=4,'x'=4,'yhi'=2,'core'=2] {'ylo','x','yhi'}, dimensions={0} | all-to-all | bytes 2097152 | tf_op jit(solution)/shard_map/all_to_all | solution.py:268
  87.9 0.2 finish.1
  88.2 9.6 %all-gather.3 = bf16[256,512]{1,0:T(8,128)(2,1)S(1)} all-gather(bf16[64,512]{1,0:T(8,128)(2,1)S(1)} %finish.1), channel_id=5, replica_groups=mesh['ylo'=2,'zhi'=4,'zlo'=4,'x'=4,'yhi'=2,'core'=2] {'yhi','core'}, dimensions={0}, use_global_device_ids=true | all-gather | bytes 327680 | tf_op jit(solution)/shard_map/all_gather | solution.py:269
  97.8 0.0 copy-done
  97.8 0.0 copy-done.1
  97.8 1.9 %heads_back.1 = (bf16[128,1536]{1,0:T(8,128)(2,1)}, bf16[128,1536]{1,0:T(8,128)(2,1)}) custom-call(bf16[4,64,512]{2,1,0:T(8,128)(2,1)S(1)} %bitcast.11, bf16[1536,512]{1,0:T(8,128)(2,1)S(1)} %copy-done, bf16[1536,512]{1,0:T(8,128)(2,1)S(1)} %copy-done.1), custom_call_target="tpu_custom_call" | custom-call | tf_op jit(solution)/shard_map/heads_back/pallas_call | solution.py:234
Async XLA Ops:
  19.9 36.5 %all-to-all-start = ((bf16[16,64,512]{2,1,0:T(8,128)(2,1)}), bf16[16,64,512]{2,1,0:T(8,128)(2,1)S(1)}, u32[]{:S(2)}, u32[]{:S(2)}) async-start(bf16[16,64,512]{2,1,0:T(8,128)(2,1)} %get-tuple-element.13), calls=%async_computation | async-start | bytes 2097152 | tf_op jit(solution)/shard_map/all_to_all | solution.py:259
  46.1 11.3 %collective-permute-start.2 = (bf16[256,512]{1,0:T(8,128)(2,1)S(1)}, bf16[256,512]{1,0:T(8,128)(2,1)S(1)}, u32[]{:S(2)}, u32[]{:S(2)}) collective-permute-start(bf16[256,512]{1,0:T(8,128)(2,1)S(1)} %all-gather.2.rest_0_), channel_id=1, source_target_pairs={{32,0},{34,2},{36,4},{38,6},{40,8},{42,10},{44,12},{46,14},{288,25... | collective-permute-start | bytes 786440 | tf_op jit(solution)/shard_map/ppermute | solution.py:262
  49.2 12.5 %collective-permute-start = (bf16[256,512]{1,0:T(8,128)(2,1)S(1)}, bf16[256,512]{1,0:T(8,128)(2,1)S(1)}, u32[]{:S(2)}, u32[]{:S(2)}) collective-permute-start(bf16[256,512]{1,0:T(8,128)(2,1)S(1)} %all-gather.2.rest_0_), channel_id=1, source_target_pairs={{240,0},{242,2},{244,4},{246,6},{248,8},{250,10},{252,12},{254,14}... | collective-permute-start | bytes 786440 | tf_op jit(solution)/shard_map/ppermute | solution.py:262
  53.1 10.8 %collective-permute-start.1 = (bf16[256,512]{1,0:T(8,128)(2,1)S(1)}, bf16[256,512]{1,0:T(8,128)(2,1)S(1)}, u32[]{:S(2)}, u32[]{:S(2)}) collective-permute-start(bf16[256,512]{1,0:T(8,128)(2,1)S(1)} %all-gather.2.rest_0_), channel_id=1, source_target_pairs={{16,0},{18,2},{20,4},{22,6},{24,8},{26,10},{28,12},{30,14},{272,25... | collective-permute-start | bytes 786440 | tf_op jit(solution)/shard_map/ppermute | solution.py:262
  65.7 32.1 %copy-start = (bf16[1536,512]{1,0:T(8,128)(2,1)S(1)}, bf16[1536,512]{1,0:T(8,128)(2,1)}, u32[]{:S(2)}) copy-start(bf16[1536,512]{1,0:T(8,128)(2,1)} %wv.3) | copy-start | bytes 4718596
  65.7 32.1 %copy-start.1 = (bf16[1536,512]{1,0:T(8,128)(2,1)S(1)}, bf16[1536,512]{1,0:T(8,128)(2,1)}, u32[]{:S(2)}) copy-start(bf16[1536,512]{1,0:T(8,128)(2,1)} %ws.3) | copy-start | bytes 4718596

commit v14 on v11

--- a/solution.py
+++ b/solution.py
@@ -168,7 +168,7 @@
                     mine_ref[pl.ds(at, block)], other_ref[...], (((1,), (1,)), ((), ())), preferred_element_type=F32
                 )
                 e = jnp.exp2(dots * slope + start)
-                coef = pl.reciprocal(1.0 + e, approx=True)
+                coef = pl.reciprocal(1.0 + e)
                 if positives and i == blocks - 1:
                     row = lax.broadcasted_iota(jnp.int32, (block, 1), 0) + (at - mine_at)
                     row = jnp.where((row >= 0) & (row < own), row, -m)
@@ -258,8 +258,8 @@
         lax.ppermute(line, AXES, from_line(sizes, steps)) for steps in ((1, 1), (-1, -1), (2, -2))
     )
     grad = tile(sharpness, offset, mine, [line], None, own, positives=True)
-    grad = tile(sharpness, offset, mine, [first], grad, own)
-    grad = tile(sharpness, offset, mine, [second, third], grad, own, final=True)
+    grad = tile(sharpness, offset, mine, [third], grad, own)
+    grad = tile(sharpness, offset, mine, [second, first], grad, own, final=True)
 
     grad = lax.all_to_all(grad.reshape(peers, own, width), PLANE, 0, 0)
     delta = lax.all_gather(finish(grad, embed), GROUP, axis=0)

time: 102 us -> 100 us (0.980)
  waiting for transfers between devices: 7.93 us -> 4.95 us
  starting transfers between devices: 12 us -> 13.2 us
    ppermute x3, waiting for transfers between devices: 7.92 us -> 4.95 us  [shards(): lax.ppermute(line, AXES, from_line(sizes, steps))]
    ppermute x3, starting transfers between devices: 8.31 us -> 9.52 us  [shards(): lax.ppermute(line, AXES, from_line(sizes, steps))]
  transfers between devices with their start and end apart: 4 -> 4, of which waited for: 1 -> 2; matrix products, arithmetic and copies ran while one was open for 0% -> 0% of each run, Pallas kernels for 2% -> 2%
where the time goes in v14:
time: 100 us
  blocking collectives  70.1 us (70%)
  starting transfers between devices  13.2 us (13%)
  Pallas kernels  9.74 us (10%)
  waiting for transfers between devices  4.95 us (5%)
  between operations  2.02 us (2%)
    all_gather x1, blocking collectives, shards(): lax.all_gather(line, AXES, axis=0, tiled=True, axis_index_groups=far_grou...  22.6 us
    all_to_all x1, blocking collectives, shards(): grad = lax.all_to_all(grad.reshape(peers, own, width), PLANE, 0, 0)  21.4 us
    all_gather x1, blocking collectives, shards(): delta = lax.all_gather(finish(grad, embed), GROUP, axis=0)  10.5 us
    ppermute x3, starting transfers between devices, shards(): lax.ppermute(line, AXES, from_line(sizes, steps))  9.52 us
    all_gather x1, blocking collectives, shards(): lax.all_gather(heads(vision, sentence, vision_map, sentence_map), 'core',...  8.69 us
    all_gather x1, blocking collectives, shards(): wide, line, embed = units(kept, lax.all_gather(given, 'yhi', axis=0), peers)  6.89 us
    ppermute x3, waiting for transfers between devices, shards(): lax.ppermute(line, AXES, from_line(sizes, steps))  4.95 us
    pallas_call x3, Pallas kernels, tile(): pl.pallas_call(kernel, out_shape=pltpu.VMEM((n, width), BF if final else...  3.99 us
  transfers between devices with their start and end apart: 4, of which 2 were waited for; matrix products, arithmetic and copies ran while one was open for 0% of the time, Pallas kernels for 2%

profile of v14, /device:TPU:1, one launch (start us, length us, event | category | flops | bytes accessed | tf_op | source)
XLA Modules:
  0.0 100.0 jit_solution(13230442034121559323)
XLA Ops:
  0.6 2.5 %heads.1 = bf16[2,64,1024]{2,1,0:T(8,128)(2,1)S(1)} custom-call(bf16[128,1536]{1,0:T(8,128)(2,1)} %v.1, bf16[128,1536]{1,0:T(8,128)(2,1)} %s.1, bf16[1536,512]{1,0:T(8,128)(2,1)} %wv.3, bf16[1536,512]{1,0:T(8,128)(2,1)} %ws.3), custom_call_target="tpu_custom_call" | custom-call | tf_op jit(solution)/shard_map/heads/pallas_call | solution.py:81
  3.1 8.7 %all-gather = bf16[4,64,1024]{2,1,0:T(8,128)(2,1)S(1)} all-gather(bf16[2,64,1024]{2,1,0:T(8,128)(2,1)S(1)} %heads.1), channel_id=2, replica_groups=mesh['ylo'=2,'zhi'=4,'zlo'=4,'x'=4,'yhi'=2,'core'=2] {'core'}, dimensions={0}, use_global_device_ids=true | all-gather | bytes 786432 | tf_op jit(solution)/shard_map/all_gather | solution.py:250
  11.8 0.1 chip_sums.1
  11.8 6.9 %all-gather.1 = bf16[128,1024]{1,0:T(8,128)(2,1)S(1)} all-gather(bf16[64,1024]{1,0:T(8,128)(2,1)S(1)} %get-tuple-element.10), channel_id=3, replica_groups=mesh['ylo'=2,'zhi'=4,'zlo'=4,'x'=4,'yhi'=2,'core'=2] {'yhi'}, dimensions={0}, use_global_device_ids=true | all-gather | bytes 393216 | tf_op jit(solution)/shard_map/all_gather | solution.py:252
  18.7 1.1 %units.1 = (bf16[16,64,512]{2,1,0:T(8,128)(2,1)}, bf16[64,512]{1,0:T(8,128)(2,1)S(1)}, f32[64,512]{1,0:T(8,128)S(1)}) custom-call(f32[64,1024]{1,0:T(8,128)S(1)} %get-tuple-element.9.kept_ref, bf16[2,64,1024]{2,1,0:T(8,128)(2,1)S(1)} %bitcast.10), custom_call_target="tpu_custom_call" | custom-call | tf_op jit(solution)/shard_map/units/pallas_call | solution.py:137
  19.9 3.7 %all-to-all-start = ((bf16[16,64,512]{2,1,0:T(8,128)(2,1)}), bf16[16,64,512]{2,1,0:T(8,128)(2,1)S(1)}, u32[]{:S(2)}, u32[]{:S(2)}) async-start(bf16[16,64,512]{2,1,0:T(8,128)(2,1)} %get-tuple-element.13), calls=%async_computation | async-start | bytes 2097152 | tf_op jit(solution)/shard_map/all_to_all | solution.py:255
  23.5 22.6 %all_gather.25.rest_0_ = bf16[256,512]{1,0:T(8,128)(2,1)S(1)} all-gather(bf16[64,512]{1,0:T(8,128)(2,1)S(1)} %get-tuple-element.14), channel_id=1, replica_groups={{0,64,128,192},{2,66,130,194},{4,68,132,196},{6,70,134,198},{8,72,136,2..., dimensions={0}, use_global_device_ids=true | all-gather | bytes 327680 | tf_op jit(solution)/shard_map/all_gather | solution.py:256
  46.1 3.0 %collective-permute-start.2 = (bf16[256,512]{1,0:T(8,128)(2,1)S(1)}, bf16[256,512]{1,0:T(8,128)(2,1)S(1)}, u32[]{:S(2)}, u32[]{:S(2)}) collective-permute-start(bf16[256,512]{1,0:T(8,128)(2,1)S(1)} %all_gather.25.rest_0_), channel_id=1, source_target_pairs={{32,0},{34,2},{36,4},{38,6},{40,8},{42,10},{44,12},{46,14},{288,25... | collective-permute-start | bytes 786440 | tf_op jit(solution)/shard_map/ppermute | solution.py:258
  49.2 2.7 %collective-permute-start = (bf16[256,512]{1,0:T(8,128)(2,1)S(1)}, bf16[256,512]{1,0:T(8,128)(2,1)S(1)}, u32[]{:S(2)}, u32[]{:S(2)}) collective-permute-start(bf16[256,512]{1,0:T(8,128)(2,1)S(1)} %all_gather.25.rest_0_), channel_id=1, source_target_pairs={{240,0},{242,2},{244,4},{246,6},{248,8},{250,10},{252,12},{254,14}... | collective-permute-start | bytes 786440 | tf_op jit(solution)/shard_map/ppermute | solution.py:258
  51.8 3.8 %collective-permute-start.1 = (bf16[256,512]{1,0:T(8,128)(2,1)S(1)}, bf16[256,512]{1,0:T(8,128)(2,1)S(1)}, u32[]{:S(2)}, u32[]{:S(2)}) collective-permute-start(bf16[256,512]{1,0:T(8,128)(2,1)S(1)} %all_gather.25.rest_0_), channel_id=1, source_target_pairs={{16,0},{18,2},{20,4},{22,6},{24,8},{26,10},{28,12},{30,14},{272,25... | collective-permute-start | bytes 786440 | tf_op jit(solution)/shard_map/ppermute | solution.py:258
  57.0 0.0 all-to-all-done
  57.0 1.1 %tile.3.rest_1_ = f32[1024,512]{1,0:T(8,128)S(1)} custom-call(f32[1]{0:T(128)S(6)} %copy.8.t_ref, f32[1]{0:T(128)S(6)} %copy.9.b_ref, bf16[1024,512]{1,0:T(8,128)(2,1)S(1)} %bitcast.5, bf16[256,512]{1,0:T(8,128)(2,1)S(1)} %all_gather.25.rest_0_), custom_call_target="tpu_custom_call" | custom-call | flops 536870912 | bytes 1310720 | tf_op jit(solution)/shard_map/tile/pallas_call | solution.py:182
  58.1 0.0 collective-permute-done.2.rest_0_
  58.1 1.1 %tile.4.rest_2_ = f32[1024,512]{1,0:T(8,128)S(1)} custom-call(f32[1]{0:T(128)S(6)} %copy.8.t_ref, f32[1]{0:T(128)S(6)} %copy.9.b_ref, bf16[1024,512]{1,0:T(8,128)(2,1)S(1)} %bitcast.6, bf16[256,512]{1,0:T(8,128)(2,1)S(1)} %collective-permute-done.2.rest_0_, f32[1024,512]{1,0:T(8,128)S(1)} %tile.3.rest_1_), custom_call_target="tpu_custom_call" | custom-call | flops 536870912 | bytes 1310720 | tf_op jit(solution)/shard_map/tile/pallas_call | solution.py:182
  59.2 2.8 %collective-permute-done.rest_0_ = bf16[256,512]{1,0:T(8,128)(2,1)S(1)} collective-permute-done((bf16[256,512]{1,0:T(8,128)(2,1)S(1)}, bf16[256,512]{1,0:T(8,128)(2,1)S(1)}, u32[]{:S(2)}, u32[]{:S(2)}) %collective-permute-start) | collective-permute-done | bytes 262176 | tf_op jit(solution)/shard_map/ppermute | solution.py:258
  62.1 2.1 %collective-permute-done.1.rest_1_ = bf16[256,512]{1,0:T(8,128)(2,1)S(1)} collective-permute-done((bf16[256,512]{1,0:T(8,128)(2,1)S(1)}, bf16[256,512]{1,0:T(8,128)(2,1)S(1)}, u32[]{:S(2)}, u32[]{:S(2)}) %collective-permute-start.1) | collective-permute-done | bytes 262176 | tf_op jit(solution)/shard_map/ppermute | solution.py:258
  64.2 1.7 %tile.5 = bf16[1024,512]{1,0:T(8,128)(2,1)S(1)} custom-call(f32[1]{0:T(128)S(6)} %copy.8.t_ref, f32[1]{0:T(128)S(6)} %copy.9.b_ref, bf16[1024,512]{1,0:T(8,128)(2,1)S(1)} %bitcast.7, bf16[256,512]{1,0:T(8,128)(2,1)S(1)} %collective-permute-done.rest_0_, bf16[256,512]{1,0:T(8,128)(2,1)S(1)} %collective-permute-done.1.rest_1_, f32[1024,512]{1,0:T(8,128)S(1)} %tile.4.rest_2_), custom_call_target="tpu_custom_call" | custom-call | flops 1073741824 | bytes 1572864 | tf_op jit(solution)/shard_map/tile/pallas_call | solution.py:182
  65.9 0.0 copy-start
  66.0 0.0 copy-start.1
  66.0 21.4 %all_to_all.10.sums_ref = bf16[16,64,512]{2,1,0:T(8,128)(2,1)S(1)} all-to-all(bf16[16,64,512]{2,1,0:T(8,128)(2,1)S(1)} %bitcast.8), channel_id=1, replica_groups=mesh['ylo'=2,'zhi'=4,'zlo'=4,'x'=4,'yhi'=2,'core'=2] {'ylo','x','yhi'}, dimensions={0} | all-to-all | bytes 2097152 | tf_op jit(solution)/shard_map/all_to_all | solution.py:264
  87.3 0.2 finish.1
  87.6 10.5 %all-gather.2 = bf16[256,512]{1,0:T(8,128)(2,1)S(1)} all-gather(bf16[64,512]{1,0:T(8,128)(2,1)S(1)} %finish.1), channel_id=4, replica_groups=mesh['ylo'=2,'zhi'=4,'zlo'=4,'x'=4,'yhi'=2,'core'=2] {'yhi','core'}, dimensions={0}, use_global_device_ids=true | all-gather | bytes 327680 | tf_op jit(solution)/shard_map/all_gather | solution.py:265
  98.1 0.0 copy-done
  98.1 0.0 copy-done.1
  98.1 1.9 %heads_back.1 = (bf16[128,1536]{1,0:T(8,128)(2,1)}, bf16[128,1536]{1,0:T(8,128)(2,1)}) custom-call(bf16[4,64,512]{2,1,0:T(8,128)(2,1)S(1)} %bitcast.11, bf16[1536,512]{1,0:T(8,128)(2,1)S(1)} %copy-done, bf16[1536,512]{1,0:T(8,128)(2,1)S(1)} %copy-done.1), custom_call_target="tpu_custom_call" | custom-call | tf_op jit(solution)/shard_map/heads_back/pallas_call | solution.py:233
Async XLA Ops:
  19.9 37.1 %all-to-all-start = ((bf16[16,64,512]{2,1,0:T(8,128)(2,1)}), bf16[16,64,512]{2,1,0:T(8,128)(2,1)S(1)}, u32[]{:S(2)}, u32[]{:S(2)}) async-start(bf16[16,64,512]{2,1,0:T(8,128)(2,1)} %get-tuple-element.13), calls=%async_computation | async-start | bytes 2097152 | tf_op jit(solution)/shard_map/all_to_all | solution.py:255
  46.1 12.0 %collective-permute-start.2 = (bf16[256,512]{1,0:T(8,128)(2,1)S(1)}, bf16[256,512]{1,0:T(8,128)(2,1)S(1)}, u32[]{:S(2)}, u32[]{:S(2)}) collective-permute-start(bf16[256,512]{1,0:T(8,128)(2,1)S(1)} %all_gather.25.rest_0_), channel_id=1, source_target_pairs={{32,0},{34,2},{36,4},{38,6},{40,8},{42,10},{44,12},{46,14},{288,25... | collective-permute-start | bytes 786440 | tf_op jit(solution)/shard_map/ppermute | solution.py:258
  49.2 12.9 %collective-permute-start = (bf16[256,512]{1,0:T(8,128)(2,1)S(1)}, bf16[256,512]{1,0:T(8,128)(2,1)S(1)}, u32[]{:S(2)}, u32[]{:S(2)}) collective-permute-start(bf16[256,512]{1,0:T(8,128)(2,1)S(1)} %all_gather.25.rest_0_), channel_id=1, source_target_pairs={{240,0},{242,2},{244,4},{246,6},{248,8},{250,10},{252,12},{254,14}... | collective-permute-start | bytes 786440 | tf_op jit(solution)/shard_map/ppermute | solution.py:258
  51.8 12.4 %collective-permute-start.1 = (bf16[256,512]{1,0:T(8,128)(2,1)S(1)}, bf16[256,512]{1,0:T(8,128)(2,1)S(1)}, u32[]{:S(2)}, u32[]{:S(2)}) collective-permute-start(bf16[256,512]{1,0:T(8,128)(2,1)S(1)} %all_gather.25.rest_0_), channel_id=1, source_target_pairs={{16,0},{18,2},{20,4},{22,6},{24,8},{26,10},{28,12},{30,14},{272,25... | collective-permute-start | bytes 786440 | tf_op jit(solution)/shard_map/ppermute | solution.py:258
  65.9 32.2 %copy-start = (bf16[1536,512]{1,0:T(8,128)(2,1)S(1)}, bf16[1536,512]{1,0:T(8,128)(2,1)}, u32[]{:S(2)}) copy-start(bf16[1536,512]{1,0:T(8,128)(2,1)} %wv.3) | copy-start | bytes 4718596
  66.0 32.2 %copy-start.1 = (bf16[1536,512]{1,0:T(8,128)(2,1)S(1)}, bf16[1536,512]{1,0:T(8,128)(2,1)}, u32[]{:S(2)}) copy-start(bf16[1536,512]{1,0:T(8,128)(2,1)} %ws.3) | copy-start | bytes 4718596

commit v15 on v12

--- a/solution.py
+++ b/solution.py
@@ -260,7 +260,7 @@
     mine = lax.all_to_all(wide, PLANE, 0, 0).reshape(peers * own, width)
     line = lax.all_gather(line, AXES, axis=0, tiled=True, axis_index_groups=far_groups(sizes))
     first, second, third = (
-        lax.ppermute(line, AXES, from_line(sizes, steps)) for steps in ((1, 1), (-1, -1), (2, -2))
+        lax.ppermute(line, AXES, from_line(sizes, steps)) for steps in ((1, -1), (-1, 1), (2, -2))
     )
     grad = tile(sharpness, offset, mine, [line], None, own, positives=True)
     grad = tile(sharpness, offset, mine, [third], grad, own)

time: 97.8 us -> 100 us (1.022)
  waiting for transfers between devices: 3.02 us -> 4.95 us
    all_to_all x1, blocking collectives: 19 us -> 21.3 us  [shards(): grad = lax.all_to_all(grad.reshape(peers, own, width), PLANE, 0, 0)]
    all_gather x1, blocking collectives: 12.8 us -> 10.5 us  [shards(): delta = lax.all_gather(finish(grad, embed), GROUP, axis=0)]
    ppermute x3, waiting for transfers between devices: 3.01 us -> 4.95 us  [shards(): lax.ppermute(line, AXES, from_line(sizes, steps))]
  transfers between devices with their start and end apart: 4 -> 4, of which waited for: 1 -> 2; matrix products, arithmetic and copies ran while one was open for 0% -> 0% of each run, Pallas kernels for 2% -> 2%
where the time goes in v15:
time: 100 us
  blocking collectives  70.1 us (70%)
  starting transfers between devices  13.2 us (13%)
  Pallas kernels  9.83 us (10%)
  waiting for transfers between devices  4.95 us (5%)
  between operations  2.03 us (2%)
    all_gather x1, blocking collectives, shards(): lax.all_gather(line, AXES, axis=0, tiled=True, axis_index_groups=far_grou...  22.6 us
    all_to_all x1, blocking collectives, shards(): grad = lax.all_to_all(grad.reshape(peers, own, width), PLANE, 0, 0)  21.3 us
    all_gather x1, blocking collectives, shards(): delta = lax.all_gather(finish(grad, embed), GROUP, axis=0)  10.5 us
    ppermute x3, starting transfers between devices, shards(): lax.ppermute(line, AXES, from_line(sizes, steps))  9.52 us
    all_gather x1, blocking collectives, shards(): lax.all_gather(heads(vision, sentence, vision_map, sentence_map), 'core',...  8.69 us
    all_gather x1, blocking collectives, shards(): wide, line, embed = units(kept, lax.all_gather(given, 'yhi', axis=0), peers)  6.89 us
    ppermute x3, waiting for transfers between devices, shards(): lax.ppermute(line, AXES, from_line(sizes, steps))  4.95 us
    pallas_call x3, Pallas kernels, tile(): pl.pallas_call(kernel, out_shape=pltpu.VMEM((n, width), BF if final else...  3.99 us
  transfers between devices with their start and end apart: 4, of which 2 were waited for; matrix products, arithmetic and copies ran while one was open for 0% of the time, Pallas kernels for 2%

profile of v15, /device:TPU:1, one launch (start us, length us, event | category | flops | bytes accessed | tf_op | source)
XLA Modules:
  0.0 100.1 jit_solution(3357987665675139080)
XLA Ops:
  0.6 2.5 %heads.1 = bf16[2,64,1024]{2,1,0:T(8,128)(2,1)S(1)} custom-call(bf16[128,1536]{1,0:T(8,128)(2,1)} %v.1, bf16[128,1536]{1,0:T(8,128)(2,1)} %s.1, bf16[1536,512]{1,0:T(8,128)(2,1)} %wv.3, bf16[1536,512]{1,0:T(8,128)(2,1)} %ws.3), custom_call_target="tpu_custom_call" | custom-call | tf_op jit(solution)/shard_map/heads/pallas_call | solution.py:81
  3.1 8.7 %all-gather = bf16[4,64,1024]{2,1,0:T(8,128)(2,1)S(1)} all-gather(bf16[2,64,1024]{2,1,0:T(8,128)(2,1)S(1)} %heads.1), channel_id=2, replica_groups=mesh['ylo'=2,'zhi'=4,'zlo'=4,'x'=4,'yhi'=2,'core'=2] {'core'}, dimensions={0}, use_global_device_ids=true | all-gather | bytes 786432 | tf_op jit(solution)/shard_map/all_gather | solution.py:255
  11.8 0.1 chip_sums.1
  11.8 6.9 %all-gather.1 = bf16[128,1024]{1,0:T(8,128)(2,1)S(1)} all-gather(bf16[64,1024]{1,0:T(8,128)(2,1)S(1)} %get-tuple-element.10), channel_id=3, replica_groups=mesh['ylo'=2,'zhi'=4,'zlo'=4,'x'=4,'yhi'=2,'core'=2] {'yhi'}, dimensions={0}, use_global_device_ids=true | all-gather | bytes 393216 | tf_op jit(solution)/shard_map/all_gather | solution.py:257
  18.7 1.2 %units.1 = (bf16[16,64,512]{2,1,0:T(8,128)(2,1)}, bf16[64,512]{1,0:T(8,128)(2,1)S(1)}, f32[64,512]{1,0:T(8,128)S(1)}) custom-call(f32[64,1024]{1,0:T(8,128)S(1)} %get-tuple-element.9.kept_ref, bf16[2,64,1024]{2,1,0:T(8,128)(2,1)S(1)} %bitcast.10), custom_call_target="tpu_custom_call" | custom-call | tf_op jit(solution)/shard_map/units/pallas_call | solution.py:141
  20.0 3.7 %all-to-all-start = ((bf16[16,64,512]{2,1,0:T(8,128)(2,1)}), bf16[16,64,512]{2,1,0:T(8,128)(2,1)S(1)}, u32[]{:S(2)}, u32[]{:S(2)}) async-start(bf16[16,64,512]{2,1,0:T(8,128)(2,1)} %get-tuple-element.13), calls=%async_computation | async-start | bytes 2097152 | tf_op jit(solution)/shard_map/all_to_all | solution.py:260
  23.6 22.6 %all_gather.25.rest_0_ = bf16[256,512]{1,0:T(8,128)(2,1)S(1)} all-gather(bf16[64,512]{1,0:T(8,128)(2,1)S(1)} %get-tuple-element.14), channel_id=1, replica_groups={{0,64,128,192},{2,66,130,194},{4,68,132,196},{6,70,134,198},{8,72,136,2..., dimensions={0}, use_global_device_ids=true | all-gather | bytes 327680 | tf_op jit(solution)/shard_map/all_gather | solution.py:261
  46.2 3.0 %collective-permute-start.2 = (bf16[256,512]{1,0:T(8,128)(2,1)S(1)}, bf16[256,512]{1,0:T(8,128)(2,1)S(1)}, u32[]{:S(2)}, u32[]{:S(2)}) collective-permute-start(bf16[256,512]{1,0:T(8,128)(2,1)S(1)} %all_gather.25.rest_0_), channel_id=1, source_target_pairs={{32,0},{34,2},{36,4},{38,6},{40,8},{42,10},{44,12},{46,14},{288,25... | collective-permute-start | bytes 786440 | tf_op jit(solution)/shard_map/ppermute | solution.py:263
  49.3 2.7 %collective-permute-start = (bf16[256,512]{1,0:T(8,128)(2,1)S(1)}, bf16[256,512]{1,0:T(8,128)(2,1)S(1)}, u32[]{:S(2)}, u32[]{:S(2)}) collective-permute-start(bf16[256,512]{1,0:T(8,128)(2,1)S(1)} %all_gather.25.rest_0_), channel_id=1, source_target_pairs={{16,0},{18,2},{20,4},{22,6},{24,8},{26,10},{28,12},{30,14},{272,25... | collective-permute-start | bytes 786440 | tf_op jit(solution)/shard_map/ppermute | solution.py:263
  51.9 3.8 %collective-permute-start.1 = (bf16[256,512]{1,0:T(8,128)(2,1)S(1)}, bf16[256,512]{1,0:T(8,128)(2,1)S(1)}, u32[]{:S(2)}, u32[]{:S(2)}) collective-permute-start(bf16[256,512]{1,0:T(8,128)(2,1)S(1)} %all_gather.25.rest_0_), channel_id=1, source_target_pairs={{240,0},{242,2},{244,4},{246,6},{248,8},{250,10},{252,12},{254,14}... | collective-permute-start | bytes 786440 | tf_op jit(solution)/shard_map/ppermute | solution.py:263
  57.1 0.0 all-to-all-done
  57.1 1.1 %tile.3.rest_1_ = f32[1024,512]{1,0:T(8,128)S(1)} custom-call(f32[1]{0:T(128)S(6)} %copy.8.t_ref, f32[1]{0:T(128)S(6)} %copy.9.b_ref, bf16[1024,512]{1,0:T(8,128)(2,1)S(1)} %bitcast.5, bf16[256,512]{1,0:T(8,128)(2,1)S(1)} %all_gather.25.rest_0_), custom_call_target="tpu_custom_call" | custom-call | flops 536870912 | bytes 1310720 | tf_op jit(solution)/shard_map/tile/pallas_call | solution.py:187
  58.2 0.0 collective-permute-done.2.rest_0_
  58.2 1.1 %tile.4.rest_2_ = f32[1024,512]{1,0:T(8,128)S(1)} custom-call(f32[1]{0:T(128)S(6)} %copy.8.t_ref, f32[1]{0:T(128)S(6)} %copy.9.b_ref, bf16[1024,512]{1,0:T(8,128)(2,1)S(1)} %bitcast.6, bf16[256,512]{1,0:T(8,128)(2,1)S(1)} %collective-permute-done.2.rest_0_, f32[1024,512]{1,0:T(8,128)S(1)} %tile.3.rest_1_), custom_call_target="tpu_custom_call" | custom-call | flops 536870912 | bytes 1310720 | tf_op jit(solution)/shard_map/tile/pallas_call | solution.py:187
  59.4 1.4 %collective-permute-done.rest_0_ = bf16[256,512]{1,0:T(8,128)(2,1)S(1)} collective-permute-done((bf16[256,512]{1,0:T(8,128)(2,1)S(1)}, bf16[256,512]{1,0:T(8,128)(2,1)S(1)}, u32[]{:S(2)}, u32[]{:S(2)}) %collective-permute-start) | collective-permute-done | bytes 262176 | tf_op jit(solution)/shard_map/ppermute | solution.py:263
  60.8 3.5 %collective-permute-done.1.rest_1_ = bf16[256,512]{1,0:T(8,128)(2,1)S(1)} collective-permute-done((bf16[256,512]{1,0:T(8,128)(2,1)S(1)}, bf16[256,512]{1,0:T(8,128)(2,1)S(1)}, u32[]{:S(2)}, u32[]{:S(2)}) %collective-permute-start.1) | collective-permute-done | bytes 262176 | tf_op jit(solution)/shard_map/ppermute | solution.py:263
  64.3 1.7 %tile.5 = bf16[1024,512]{1,0:T(8,128)(2,1)S(1)} custom-call(f32[1]{0:T(128)S(6)} %copy.8.t_ref, f32[1]{0:T(128)S(6)} %copy.9.b_ref, bf16[1024,512]{1,0:T(8,128)(2,1)S(1)} %bitcast.7, bf16[256,512]{1,0:T(8,128)(2,1)S(1)} %collective-permute-done.rest_0_, bf16[256,512]{1,0:T(8,128)(2,1)S(1)} %collective-permute-done.1.rest_1_, f32[1024,512]{1,0:T(8,128)S(1)} %tile.4.rest_2_), custom_call_target="tpu_custom_call" | custom-call | flops 1073741824 | bytes 1572864 | tf_op jit(solution)/shard_map/tile/pallas_call | solution.py:187
  66.1 0.0 copy-start
  66.1 0.0 copy-start.1
  66.1 21.3 %all_to_all.10.sums_ref = bf16[16,64,512]{2,1,0:T(8,128)(2,1)S(1)} all-to-all(bf16[16,64,512]{2,1,0:T(8,128)(2,1)S(1)} %bitcast.8), channel_id=1, replica_groups=mesh['ylo'=2,'zhi'=4,'zlo'=4,'x'=4,'yhi'=2,'core'=2] {'ylo','x','yhi'}, dimensions={0} | all-to-all | bytes 2097152 | tf_op jit(solution)/shard_map/all_to_all | solution.py:269
  87.4 0.2 finish.1
  87.7 10.5 %all-gather.2 = bf16[256,512]{1,0:T(8,128)(2,1)S(1)} all-gather(bf16[64,512]{1,0:T(8,128)(2,1)S(1)} %finish.1), channel_id=4, replica_groups=mesh['ylo'=2,'zhi'=4,'zlo'=4,'x'=4,'yhi'=2,'core'=2] {'yhi','core'}, dimensions={0}, use_global_device_ids=true | all-gather | bytes 327680 | tf_op jit(solution)/shard_map/all_gather | solution.py:270
  98.2 0.0 copy-done
  98.2 0.0 copy-done.1
  98.2 1.9 %heads_back.1 = (bf16[128,1536]{1,0:T(8,128)(2,1)}, bf16[128,1536]{1,0:T(8,128)(2,1)}) custom-call(bf16[4,64,512]{2,1,0:T(8,128)(2,1)S(1)} %bitcast.11, bf16[1536,512]{1,0:T(8,128)(2,1)S(1)} %copy-done, bf16[1536,512]{1,0:T(8,128)(2,1)S(1)} %copy-done.1), custom_call_target="tpu_custom_call" | custom-call | tf_op jit(solution)/shard_map/heads_back/pallas_call | solution.py:238
Async XLA Ops:
  20.0 37.1 %all-to-all-start = ((bf16[16,64,512]{2,1,0:T(8,128)(2,1)}), bf16[16,64,512]{2,1,0:T(8,128)(2,1)S(1)}, u32[]{:S(2)}, u32[]{:S(2)}) async-start(bf16[16,64,512]{2,1,0:T(8,128)(2,1)} %get-tuple-element.13), calls=%async_computation | async-start | bytes 2097152 | tf_op jit(solution)/shard_map/all_to_all | solution.py:260
  46.2 12.0 %collective-permute-start.2 = (bf16[256,512]{1,0:T(8,128)(2,1)S(1)}, bf16[256,512]{1,0:T(8,128)(2,1)S(1)}, u32[]{:S(2)}, u32[]{:S(2)}) collective-permute-start(bf16[256,512]{1,0:T(8,128)(2,1)S(1)} %all_gather.25.rest_0_), channel_id=1, source_target_pairs={{32,0},{34,2},{36,4},{38,6},{40,8},{42,10},{44,12},{46,14},{288,25... | collective-permute-start | bytes 786440 | tf_op jit(solution)/shard_map/ppermute | solution.py:263
  49.3 11.5 %collective-permute-start = (bf16[256,512]{1,0:T(8,128)(2,1)S(1)}, bf16[256,512]{1,0:T(8,128)(2,1)S(1)}, u32[]{:S(2)}, u32[]{:S(2)}) collective-permute-start(bf16[256,512]{1,0:T(8,128)(2,1)S(1)} %all_gather.25.rest_0_), channel_id=1, source_target_pairs={{16,0},{18,2},{20,4},{22,6},{24,8},{26,10},{28,12},{30,14},{272,25... | collective-permute-start | bytes 786440 | tf_op jit(solution)/shard_map/ppermute | solution.py:263
  51.9 12.4 %collective-permute-start.1 = (bf16[256,512]{1,0:T(8,128)(2,1)S(1)}, bf16[256,512]{1,0:T(8,128)(2,1)S(1)}, u32[]{:S(2)}, u32[]{:S(2)}) collective-permute-start(bf16[256,512]{1,0:T(8,128)(2,1)S(1)} %all_gather.25.rest_0_), channel_id=1, source_target_pairs={{240,0},{242,2},{244,4},{246,6},{248,8},{250,10},{252,12},{254,14}... | collective-permute-start | bytes 786440 | tf_op jit(solution)/shard_map/ppermute | solution.py:263
  66.1 32.2 %copy-start = (bf16[1536,512]{1,0:T(8,128)(2,1)S(1)}, bf16[1536,512]{1,0:T(8,128)(2,1)}, u32[]{:S(2)}) copy-start(bf16[1536,512]{1,0:T(8,128)(2,1)} %wv.3) | copy-start | bytes 4718596
  66.1 32.2 %copy-start.1 = (bf16[1536,512]{1,0:T(8,128)(2,1)S(1)}, bf16[1536,512]{1,0:T(8,128)(2,1)}, u32[]{:S(2)}) copy-start(bf16[1536,512]{1,0:T(8,128)(2,1)} %ws.3) | copy-start | bytes 4718596

commit v16 on v12

--- a/solution.py
+++ b/solution.py
@@ -29,11 +29,14 @@
     return (inv, embed * inv)
 
 
-def far_groups(sizes):
+def opposite_groups(sizes, axes):
     ids = np.arange(math.prod(sizes)).reshape(sizes)
+    kept = [i for i, name in enumerate(AXES[:-1]) if name not in axes]
+    moved = [AXES.index(name) for name in axes]
+    members = math.prod(sizes[i] for i in moved)
     groups = []
     for core in range(2):
-        part = np.moveaxis(ids[..., core], 1, -1).reshape(-1, sizes[1])
+        part = ids[..., core].transpose(kept + moved).reshape(-1, members)
         groups += (part[:, ::-1] if core == 1 else part).tolist()
     return groups
 
@@ -163,7 +166,8 @@
         t = t_ref[0]
         slope, start = -LOG2E * t, -LOG2E * b_ref[0]
         zhi, last = lax.axis_index("zhi"), lax.axis_size("zhi") - 1
-        mine_at = lax.axis_index(PLANE) * own
+        plane, most = lax.axis_index(PLANE), lax.axis_size(PLANE) - 1
+        mine_at = jnp.where(lax.axis_index("core") == 0, plane, most - plane) * own
         other_at = jnp.where(lax.axis_index("core") == 0, zhi, last - zhi) * own
         for i in range(blocks):
             at = pl.multiple_of(lax.rem(mine_at // block + 1 + i, blocks) * block, block)
@@ -252,13 +256,16 @@
     sizes = [lax.axis_size(a) for a in AXES]
     peers = lax.axis_size(PLANE)
 
+    def meet(x):
+        return lax.all_to_all(x, AXES, 0, 0, axis_index_groups=opposite_groups(sizes, PLANE))
+
     parts = lax.all_gather(heads(vision, sentence, vision_map, sentence_map), "core", axis=0)
     given, kept = chip_sums(parts)
     wide, line, embed = units(kept, lax.all_gather(given, "yhi", axis=0), peers)
 
     wide, line = lax.optimization_barrier((wide, line))
-    mine = lax.all_to_all(wide, PLANE, 0, 0).reshape(peers * own, width)
-    line = lax.all_gather(line, AXES, axis=0, tiled=True, axis_index_groups=far_groups(sizes))
+    mine = meet(wide).reshape(peers * own, width)
+    line = lax.all_gather(line, AXES, axis=0, tiled=True, axis_index_groups=opposite_groups(sizes, ("zhi",)))
     first, second, third = (
         lax.ppermute(line, AXES, from_line(sizes, steps)) for steps in ((1, 1), (-1, -1), (2, -2))
     )
@@ -266,7 +273,7 @@
     grad = tile(sharpness, offset, mine, [third], grad, own)
     grad = tile(sharpness, offset, mine, [first, second], grad, own, final=True)
 
-    grad = lax.all_to_all(grad.reshape(peers, own, width), PLANE, 0, 0)
+    grad = meet(grad.reshape(peers, own, width))
     delta = lax.all_gather(finish(grad, embed), GROUP, axis=0)
     return tuple(heads_back(delta, vision_map, sentence_map))
 

time: 97.8 us -> 98.6 us (level)
  starting transfers between devices: 12.5 us -> 15.8 us
  blocking collectives: 70 us -> 67.4 us
    all_to_all x1, blocking collectives: 19 us -> 14.8 us  [meet(): lax.all_to_all(x, AXES, 0, 0, axis_index_groups=opposite_groups(sizes, PL...]
    all_gather x1, blocking collectives: 12.8 us -> 16.1 us  [shards(): delta = lax.all_gather(finish(grad, embed), GROUP, axis=0)]
    all_to_all x1, starting transfers between devices: 3.66 us -> 6.09 us  [meet(): lax.all_to_all(x, AXES, 0, 0, axis_index_groups=opposite_groups(sizes, PL...]
    all_gather x1, blocking collectives: 22.6 us -> 20.9 us  [shards(): lax.all_gather(line, AXES, axis=0, tiled=True, axis_index_groups=opposite...]
where the time goes in v16:
time: 98.6 us; the launch traced here: 98.3 us
  blocking collectives  67.4 us (68%)
  starting transfers between devices  15.8 us (16%)
  Pallas kernels  9.83 us (10%)
  waiting for transfers between devices  3.27 us (3%)
  between operations  2.02 us (2%)
    all_gather x1, blocking collectives, shards(): lax.all_gather(line, AXES, axis=0, tiled=True, axis_index_groups=opposite...  20.9 us
    all_gather x1, blocking collectives, shards(): delta = lax.all_gather(finish(grad, embed), GROUP, axis=0)  16.1 us
    all_to_all x1, blocking collectives, meet(): lax.all_to_all(x, AXES, 0, 0, axis_index_groups=opposite_groups(sizes, PL...  14.8 us
    ppermute x3, starting transfers between devices, shards(): lax.ppermute(line, AXES, from_line(sizes, steps))  9.68 us
    all_gather x1, blocking collectives, shards(): lax.all_gather(heads(vision, sentence, vision_map, sentence_map), 'core',...  8.69 us
    all_gather x1, blocking collectives, shards(): wide, line, embed = units(kept, lax.all_gather(given, 'yhi', axis=0), peers)  6.89 us
    all_to_all x1, starting transfers between devices, meet(): lax.all_to_all(x, AXES, 0, 0, axis_index_groups=opposite_groups(sizes, PL...  6.09 us
    pallas_call x3, Pallas kernels, tile(): pl.pallas_call(kernel, out_shape=pltpu.VMEM((n, width), BF if final else...  3.99 us
  transfers between devices with their start and end apart: 4, of which 1 were waited for; matrix products, arithmetic and copies ran while one was open for 0% of the time, Pallas kernels for 2%

profile of v16, /device:TPU:1, one launch (start us, length us, event | category | flops | bytes accessed | tf_op | source)
XLA Modules:
  0.0 98.3 jit_solution(10202950448974928040)
XLA Ops:
  0.6 2.5 %heads.1 = bf16[2,64,1024]{2,1,0:T(8,128)(2,1)S(1)} custom-call(bf16[128,1536]{1,0:T(8,128)(2,1)} %v.1, bf16[128,1536]{1,0:T(8,128)(2,1)} %s.1, bf16[1536,512]{1,0:T(8,128)(2,1)} %wv.3, bf16[1536,512]{1,0:T(8,128)(2,1)} %ws.3), custom_call_target="tpu_custom_call" | custom-call | tf_op jit(solution)/shard_map/heads/pallas_call | solution.py:84
  3.1 8.7 %all-gather = bf16[4,64,1024]{2,1,0:T(8,128)(2,1)S(1)} all-gather(bf16[2,64,1024]{2,1,0:T(8,128)(2,1)S(1)} %heads.1), channel_id=2, replica_groups=mesh['ylo'=2,'zhi'=4,'zlo'=4,'x'=4,'yhi'=2,'core'=2] {'core'}, dimensions={0}, use_global_device_ids=true | all-gather | bytes 786432 | tf_op jit(solution)/shard_map/all_gather | solution.py:262
  11.8 0.1 chip_sums.1
  11.8 6.9 %all-gather.1 = bf16[128,1024]{1,0:T(8,128)(2,1)S(1)} all-gather(bf16[64,1024]{1,0:T(8,128)(2,1)S(1)} %get-tuple-element.10), channel_id=3, replica_groups=mesh['ylo'=2,'zhi'=4,'zlo'=4,'x'=4,'yhi'=2,'core'=2] {'yhi'}, dimensions={0}, use_global_device_ids=true | all-gather | bytes 393216 | tf_op jit(solution)/shard_map/all_gather | solution.py:264
  18.7 1.2 %units.1 = (bf16[16,64,512]{2,1,0:T(8,128)(2,1)}, bf16[64,512]{1,0:T(8,128)(2,1)S(1)}, f32[64,512]{1,0:T(8,128)S(1)}) custom-call(f32[64,1024]{1,0:T(8,128)S(1)} %get-tuple-element.9.kept_ref, bf16[2,64,1024]{2,1,0:T(8,128)(2,1)S(1)} %bitcast.10), custom_call_target="tpu_custom_call" | custom-call | tf_op jit(solution)/shard_map/units/pallas_call | solution.py:144
  20.0 6.1 %all-to-all-start = ((bf16[16,64,512]{2,1,0:T(8,128)(2,1)}), bf16[16,64,512]{2,1,0:T(8,128)(2,1)S(1)}, u32[]{:S(2)}, u32[]{:S(2)}) async-start(bf16[16,64,512]{2,1,0:T(8,128)(2,1)} %get-tuple-element.13), calls=%async_computation | async-start | bytes 2097152 | tf_op jit(solution)/shard_map/all_to_all | solution.py:260
  26.1 20.9 %all_gather.25.rest_0_ = bf16[256,512]{1,0:T(8,128)(2,1)S(1)} all-gather(bf16[64,512]{1,0:T(8,128)(2,1)S(1)} %get-tuple-element.14), channel_id=1, replica_groups={{0,64,128,192},{2,66,130,194},{4,68,132,196},{6,70,134,198},{8,72,136,2..., dimensions={0}, use_global_device_ids=true | all-gather | bytes 327680 | tf_op jit(solution)/shard_map/all_gather | solution.py:268
  46.9 3.9 %collective-permute-start.2 = (bf16[256,512]{1,0:T(8,128)(2,1)S(1)}, bf16[256,512]{1,0:T(8,128)(2,1)S(1)}, u32[]{:S(2)}, u32[]{:S(2)}) collective-permute-start(bf16[256,512]{1,0:T(8,128)(2,1)S(1)} %all_gather.25.rest_0_), channel_id=1, source_target_pairs={{32,0},{34,2},{36,4},{38,6},{40,8},{42,10},{44,12},{46,14},{288,25... | collective-permute-start | bytes 786440 | tf_op jit(solution)/shard_map/ppermute | solution.py:270
  50.8 3.9 %collective-permute-start = (bf16[256,512]{1,0:T(8,128)(2,1)S(1)}, bf16[256,512]{1,0:T(8,128)(2,1)S(1)}, u32[]{:S(2)}, u32[]{:S(2)}) collective-permute-start(bf16[256,512]{1,0:T(8,128)(2,1)S(1)} %all_gather.25.rest_0_), channel_id=1, source_target_pairs={{16,0},{18,2},{20,4},{22,6},{24,8},{26,10},{28,12},{30,14},{272,25... | collective-permute-start | bytes 786440 | tf_op jit(solution)/shard_map/ppermute | solution.py:270
  54.7 1.9 %collective-permute-start.1 = (bf16[256,512]{1,0:T(8,128)(2,1)S(1)}, bf16[256,512]{1,0:T(8,128)(2,1)S(1)}, u32[]{:S(2)}, u32[]{:S(2)}) collective-permute-start(bf16[256,512]{1,0:T(8,128)(2,1)S(1)} %all_gather.25.rest_0_), channel_id=1, source_target_pairs={{240,0},{242,2},{244,4},{246,6},{248,8},{250,10},{252,12},{254,14}... | collective-permute-start | bytes 786440 | tf_op jit(solution)/shard_map/ppermute | solution.py:270
  58.0 0.0 all-to-all-done
  58.0 1.1 %tile.3.rest_1_ = f32[1024,512]{1,0:T(8,128)S(1)} custom-call(f32[1]{0:T(128)S(6)} %copy.8.t_ref, f32[1]{0:T(128)S(6)} %copy.9.b_ref, bf16[1024,512]{1,0:T(8,128)(2,1)S(1)} %bitcast.5, bf16[256,512]{1,0:T(8,128)(2,1)S(1)} %all_gather.25.rest_0_), custom_call_target="tpu_custom_call" | custom-call | flops 536870912 | bytes 1310720 | tf_op jit(solution)/shard_map/tile/pallas_call | solution.py:191
  59.1 0.0 collective-permute-done.2.rest_0_
  59.1 1.1 %tile.4.rest_2_ = f32[1024,512]{1,0:T(8,128)S(1)} custom-call(f32[1]{0:T(128)S(6)} %copy.8.t_ref, f32[1]{0:T(128)S(6)} %copy.9.b_ref, bf16[1024,512]{1,0:T(8,128)(2,1)S(1)} %bitcast.6, bf16[256,512]{1,0:T(8,128)(2,1)S(1)} %collective-permute-done.2.rest_0_, f32[1024,512]{1,0:T(8,128)S(1)} %tile.3.rest_1_), custom_call_target="tpu_custom_call" | custom-call | flops 536870912 | bytes 1310720 | tf_op jit(solution)/shard_map/tile/pallas_call | solution.py:191
  60.2 3.3 %collective-permute-done.rest_0_ = bf16[256,512]{1,0:T(8,128)(2,1)S(1)} collective-permute-done((bf16[256,512]{1,0:T(8,128)(2,1)S(1)}, bf16[256,512]{1,0:T(8,128)(2,1)S(1)}, u32[]{:S(2)}, u32[]{:S(2)}) %collective-permute-start) | collective-permute-done | bytes 262176 | tf_op jit(solution)/shard_map/ppermute | solution.py:270
  63.5 0.0 collective-permute-done.1.rest_1_
  63.5 1.7 %tile.5 = bf16[1024,512]{1,0:T(8,128)(2,1)S(1)} custom-call(f32[1]{0:T(128)S(6)} %copy.8.t_ref, f32[1]{0:T(128)S(6)} %copy.9.b_ref, bf16[1024,512]{1,0:T(8,128)(2,1)S(1)} %bitcast.7, bf16[256,512]{1,0:T(8,128)(2,1)S(1)} %collective-permute-done.rest_0_, bf16[256,512]{1,0:T(8,128)(2,1)S(1)} %collective-permute-done.1.rest_1_, f32[1024,512]{1,0:T(8,128)S(1)} %tile.4.rest_2_), custom_call_target="tpu_custom_call" | custom-call | flops 1073741824 | bytes 1572864 | tf_op jit(solution)/shard_map/tile/pallas_call | solution.py:191
  65.2 0.0 copy-start
  65.3 0.0 copy-start.1
  65.3 14.8 %all_to_all.10.sums_ref = bf16[16,64,512]{2,1,0:T(8,128)(2,1)S(1)} all-to-all(bf16[16,64,512]{2,1,0:T(8,128)(2,1)S(1)} %bitcast.8), channel_id=1, replica_groups={{0,2,4,6,8,10,12,14,256,258,260,262,264,266,268,270},{16,18,20,22,24,26..., dimensions={0} | all-to-all | bytes 2097152 | tf_op jit(solution)/shard_map/all_to_all | solution.py:260
  80.1 0.2 finish.1
  80.3 16.1 %all-gather.2 = bf16[256,512]{1,0:T(8,128)(2,1)S(1)} all-gather(bf16[64,512]{1,0:T(8,128)(2,1)S(1)} %finish.1), channel_id=4, replica_groups=mesh['ylo'=2,'zhi'=4,'zlo'=4,'x'=4,'yhi'=2,'core'=2] {'yhi','core'}, dimensions={0}, use_global_device_ids=true | all-gather | bytes 327680 | tf_op jit(solution)/shard_map/all_gather | solution.py:277
  96.4 0.0 copy-done
  96.4 0.0 copy-done.1
  96.4 1.9 %heads_back.1 = (bf16[128,1536]{1,0:T(8,128)(2,1)}, bf16[128,1536]{1,0:T(8,128)(2,1)}) custom-call(bf16[4,64,512]{2,1,0:T(8,128)(2,1)S(1)} %bitcast.11, bf16[1536,512]{1,0:T(8,128)(2,1)S(1)} %copy-done, bf16[1536,512]{1,0:T(8,128)(2,1)S(1)} %copy-done.1), custom_call_target="tpu_custom_call" | custom-call | tf_op jit(solution)/shard_map/heads_back/pallas_call | solution.py:242
Async XLA Ops:
  20.0 38.0 %all-to-all-start = ((bf16[16,64,512]{2,1,0:T(8,128)(2,1)}), bf16[16,64,512]{2,1,0:T(8,128)(2,1)S(1)}, u32[]{:S(2)}, u32[]{:S(2)}) async-start(bf16[16,64,512]{2,1,0:T(8,128)(2,1)} %get-tuple-element.13), calls=%async_computation | async-start | bytes 2097152 | tf_op jit(solution)/shard_map/all_to_all | solution.py:260
  46.9 12.1 %collective-permute-start.2 = (bf16[256,512]{1,0:T(8,128)(2,1)S(1)}, bf16[256,512]{1,0:T(8,128)(2,1)S(1)}, u32[]{:S(2)}, u32[]{:S(2)}) collective-permute-start(bf16[256,512]{1,0:T(8,128)(2,1)S(1)} %all_gather.25.rest_0_), channel_id=1, source_target_pairs={{32,0},{34,2},{36,4},{38,6},{40,8},{42,10},{44,12},{46,14},{288,25... | collective-permute-start | bytes 786440 | tf_op jit(solution)/shard_map/ppermute | solution.py:270
  50.8 12.7 %collective-permute-start = (bf16[256,512]{1,0:T(8,128)(2,1)S(1)}, bf16[256,512]{1,0:T(8,128)(2,1)S(1)}, u32[]{:S(2)}, u32[]{:S(2)}) collective-permute-start(bf16[256,512]{1,0:T(8,128)(2,1)S(1)} %all_gather.25.rest_0_), channel_id=1, source_target_pairs={{16,0},{18,2},{20,4},{22,6},{24,8},{26,10},{28,12},{30,14},{272,25... | collective-permute-start | bytes 786440 | tf_op jit(solution)/shard_map/ppermute | solution.py:270
  54.7 8.8 %collective-permute-start.1 = (bf16[256,512]{1,0:T(8,128)(2,1)S(1)}, bf16[256,512]{1,0:T(8,128)(2,1)S(1)}, u32[]{:S(2)}, u32[]{:S(2)}) collective-permute-start(bf16[256,512]{1,0:T(8,128)(2,1)S(1)} %all_gather.25.rest_0_), channel_id=1, source_target_pairs={{240,0},{242,2},{244,4},{246,6},{248,8},{250,10},{252,12},{254,14}... | collective-permute-start | bytes 786440 | tf_op jit(solution)/shard_map/ppermute | solution.py:270
  65.2 31.2 %copy-start = (bf16[1536,512]{1,0:T(8,128)(2,1)S(1)}, bf16[1536,512]{1,0:T(8,128)(2,1)}, u32[]{:S(2)}) copy-start(bf16[1536,512]{1,0:T(8,128)(2,1)} %wv.3) | copy-start | bytes 4718596
  65.3 31.2 %copy-start.1 = (bf16[1536,512]{1,0:T(8,128)(2,1)S(1)}, bf16[1536,512]{1,0:T(8,128)(2,1)}, u32[]{:S(2)}) copy-start(bf16[1536,512]{1,0:T(8,128)(2,1)} %ws.3) | copy-start | bytes 4718596

commit v17 on v15

--- a/solution.py
+++ b/solution.py
@@ -260,7 +260,7 @@
     mine = lax.all_to_all(wide, PLANE, 0, 0).reshape(peers * own, width)
     line = lax.all_gather(line, AXES, axis=0, tiled=True, axis_index_groups=far_groups(sizes))
     first, second, third = (
-        lax.ppermute(line, AXES, from_line(sizes, steps)) for steps in ((1, -1), (-1, 1), (2, -2))
+        lax.ppermute(line, AXES, from_line(sizes, steps)) for steps in ((1, 1), (-1, -1), (-2, 2))
     )
     grad = tile(sharpness, offset, mine, [line], None, own, positives=True)
     grad = tile(sharpness, offset, mine, [third], grad, own)

time: 100 us -> 102 us (1.020)
  waiting for transfers between devices: 4.95 us -> 6.84 us
    ppermute x3, waiting for transfers between devices: 4.95 us -> 6.84 us  [shards(): lax.ppermute(line, AXES, from_line(sizes, steps))]
where the time goes in v17:
time: 102 us; the launch traced here: 101 us
  blocking collectives  70.4 us (69%)
  starting transfers between devices  12.3 us (12%)
  Pallas kernels  9.83 us (10%)
  waiting for transfers between devices  6.84 us (7%)
  between operations  2.02 us (2%)
    all_gather x1, blocking collectives, shards(): lax.all_gather(line, AXES, axis=0, tiled=True, axis_index_groups=far_grou...  22.6 us
    all_to_all x1, blocking collectives, shards(): grad = lax.all_to_all(grad.reshape(peers, own, width), PLANE, 0, 0)  22 us
    all_gather x1, blocking collectives, shards(): delta = lax.all_gather(finish(grad, embed), GROUP, axis=0)  10.2 us
    all_gather x1, blocking collectives, shards(): lax.all_gather(heads(vision, sentence, vision_map, sentence_map), 'core',...  8.69 us
    ppermute x3, starting transfers between devices, shards(): lax.ppermute(line, AXES, from_line(sizes, steps))  8.67 us
    all_gather x1, blocking collectives, shards(): wide, line, embed = units(kept, lax.all_gather(given, 'yhi', axis=0), peers)  6.89 us
    ppermute x3, waiting for transfers between devices, shards(): lax.ppermute(line, AXES, from_line(sizes, steps))  6.84 us
    pallas_call x3, Pallas kernels, tile(): pl.pallas_call(kernel, out_shape=pltpu.VMEM((n, width), BF if final else...  3.99 us
  transfers between devices with their start and end apart: 4, of which 2 were waited for; matrix products, arithmetic and copies ran while one was open for 0% of the time, Pallas kernels for 2%

profile of v17, /device:TPU:1, one launch (start us, length us, event | category | flops | bytes accessed | tf_op | source)
XLA Modules:
  0.0 101.5 jit_solution(9959273359989016728)
XLA Ops:
  0.6 2.5 %heads.1 = bf16[2,64,1024]{2,1,0:T(8,128)(2,1)S(1)} custom-call(bf16[128,1536]{1,0:T(8,128)(2,1)} %v.1, bf16[128,1536]{1,0:T(8,128)(2,1)} %s.1, bf16[1536,512]{1,0:T(8,128)(2,1)} %wv.3, bf16[1536,512]{1,0:T(8,128)(2,1)} %ws.3), custom_call_target="tpu_custom_call" | custom-call | tf_op jit(solution)/shard_map/heads/pallas_call | solution.py:81
  3.1 8.7 %all-gather = bf16[4,64,1024]{2,1,0:T(8,128)(2,1)S(1)} all-gather(bf16[2,64,1024]{2,1,0:T(8,128)(2,1)S(1)} %heads.1), channel_id=2, replica_groups=mesh['ylo'=2,'zhi'=4,'zlo'=4,'x'=4,'yhi'=2,'core'=2] {'core'}, dimensions={0}, use_global_device_ids=true | all-gather | bytes 786432 | tf_op jit(solution)/shard_map/all_gather | solution.py:255
  11.8 0.1 chip_sums.1
  11.8 6.9 %all-gather.1 = bf16[128,1024]{1,0:T(8,128)(2,1)S(1)} all-gather(bf16[64,1024]{1,0:T(8,128)(2,1)S(1)} %get-tuple-element.10), channel_id=3, replica_groups=mesh['ylo'=2,'zhi'=4,'zlo'=4,'x'=4,'yhi'=2,'core'=2] {'yhi'}, dimensions={0}, use_global_device_ids=true | all-gather | bytes 393216 | tf_op jit(solution)/shard_map/all_gather | solution.py:257
  18.7 1.2 %units.1 = (bf16[16,64,512]{2,1,0:T(8,128)(2,1)}, bf16[64,512]{1,0:T(8,128)(2,1)S(1)}, f32[64,512]{1,0:T(8,128)S(1)}) custom-call(f32[64,1024]{1,0:T(8,128)S(1)} %get-tuple-element.9.kept_ref, bf16[2,64,1024]{2,1,0:T(8,128)(2,1)S(1)} %bitcast.10), custom_call_target="tpu_custom_call" | custom-call | tf_op jit(solution)/shard_map/units/pallas_call | solution.py:141
  20.0 3.7 %all-to-all-start = ((bf16[16,64,512]{2,1,0:T(8,128)(2,1)}), bf16[16,64,512]{2,1,0:T(8,128)(2,1)S(1)}, u32[]{:S(2)}, u32[]{:S(2)}) async-start(bf16[16,64,512]{2,1,0:T(8,128)(2,1)} %get-tuple-element.13), calls=%async_computation | async-start | bytes 2097152 | tf_op jit(solution)/shard_map/all_to_all | solution.py:260
  23.6 22.6 %all_gather.25.rest_0_ = bf16[256,512]{1,0:T(8,128)(2,1)S(1)} all-gather(bf16[64,512]{1,0:T(8,128)(2,1)S(1)} %get-tuple-element.14), channel_id=1, replica_groups={{0,64,128,192},{2,66,130,194},{4,68,132,196},{6,70,134,198},{8,72,136,2..., dimensions={0}, use_global_device_ids=true | all-gather | bytes 327680 | tf_op jit(solution)/shard_map/all_gather | solution.py:261
  46.2 3.4 %collective-permute-start.2 = (bf16[256,512]{1,0:T(8,128)(2,1)S(1)}, bf16[256,512]{1,0:T(8,128)(2,1)S(1)}, u32[]{:S(2)}, u32[]{:S(2)}) collective-permute-start(bf16[256,512]{1,0:T(8,128)(2,1)S(1)} %all_gather.25.rest_0_), channel_id=1, source_target_pairs={{224,0},{226,2},{228,4},{230,6},{232,8},{234,10},{236,12},{238,14}... | collective-permute-start | bytes 786440 | tf_op jit(solution)/shard_map/ppermute | solution.py:263
  49.6 2.2 %collective-permute-start = (bf16[256,512]{1,0:T(8,128)(2,1)S(1)}, bf16[256,512]{1,0:T(8,128)(2,1)S(1)}, u32[]{:S(2)}, u32[]{:S(2)}) collective-permute-start(bf16[256,512]{1,0:T(8,128)(2,1)S(1)} %all_gather.25.rest_0_), channel_id=1, source_target_pairs={{16,0},{18,2},{20,4},{22,6},{24,8},{26,10},{28,12},{30,14},{272,25... | collective-permute-start | bytes 786440 | tf_op jit(solution)/shard_map/ppermute | solution.py:263
  51.8 3.1 %collective-permute-start.1 = (bf16[256,512]{1,0:T(8,128)(2,1)S(1)}, bf16[256,512]{1,0:T(8,128)(2,1)S(1)}, u32[]{:S(2)}, u32[]{:S(2)}) collective-permute-start(bf16[256,512]{1,0:T(8,128)(2,1)S(1)} %all_gather.25.rest_0_), channel_id=1, source_target_pairs={{240,0},{242,2},{244,4},{246,6},{248,8},{250,10},{252,12},{254,14}... | collective-permute-start | bytes 786440 | tf_op jit(solution)/shard_map/ppermute | solution.py:263
  56.2 0.0 all-to-all-done
  56.3 1.1 %tile.3.rest_1_ = f32[1024,512]{1,0:T(8,128)S(1)} custom-call(f32[1]{0:T(128)S(6)} %copy.8.t_ref, f32[1]{0:T(128)S(6)} %copy.9.b_ref, bf16[1024,512]{1,0:T(8,128)(2,1)S(1)} %bitcast.5, bf16[256,512]{1,0:T(8,128)(2,1)S(1)} %all_gather.25.rest_0_), custom_call_target="tpu_custom_call" | custom-call | flops 536870912 | bytes 1310720 | tf_op jit(solution)/shard_map/tile/pallas_call | solution.py:187
  57.4 0.0 collective-permute-done.2.rest_0_
  57.4 1.1 %tile.4.rest_2_ = f32[1024,512]{1,0:T(8,128)S(1)} custom-call(f32[1]{0:T(128)S(6)} %copy.8.t_ref, f32[1]{0:T(128)S(6)} %copy.9.b_ref, bf16[1024,512]{1,0:T(8,128)(2,1)S(1)} %bitcast.6, bf16[256,512]{1,0:T(8,128)(2,1)S(1)} %collective-permute-done.2.rest_0_, f32[1024,512]{1,0:T(8,128)S(1)} %tile.3.rest_1_), custom_call_target="tpu_custom_call" | custom-call | flops 536870912 | bytes 1310720 | tf_op jit(solution)/shard_map/tile/pallas_call | solution.py:187
  58.5 4.1 %collective-permute-done.rest_0_ = bf16[256,512]{1,0:T(8,128)(2,1)S(1)} collective-permute-done((bf16[256,512]{1,0:T(8,128)(2,1)S(1)}, bf16[256,512]{1,0:T(8,128)(2,1)S(1)}, u32[]{:S(2)}, u32[]{:S(2)}) %collective-permute-start) | collective-permute-done | bytes 262176 | tf_op jit(solution)/shard_map/ppermute | solution.py:263
  62.6 2.8 %collective-permute-done.1.rest_1_ = bf16[256,512]{1,0:T(8,128)(2,1)S(1)} collective-permute-done((bf16[256,512]{1,0:T(8,128)(2,1)S(1)}, bf16[256,512]{1,0:T(8,128)(2,1)S(1)}, u32[]{:S(2)}, u32[]{:S(2)}) %collective-permute-start.1) | collective-permute-done | bytes 262176 | tf_op jit(solution)/shard_map/ppermute | solution.py:263
  65.3 1.7 %tile.5 = bf16[1024,512]{1,0:T(8,128)(2,1)S(1)} custom-call(f32[1]{0:T(128)S(6)} %copy.8.t_ref, f32[1]{0:T(128)S(6)} %copy.9.b_ref, bf16[1024,512]{1,0:T(8,128)(2,1)S(1)} %bitcast.7, bf16[256,512]{1,0:T(8,128)(2,1)S(1)} %collective-permute-done.rest_0_, bf16[256,512]{1,0:T(8,128)(2,1)S(1)} %collective-permute-done.1.rest_1_, f32[1024,512]{1,0:T(8,128)S(1)} %tile.4.rest_2_), custom_call_target="tpu_custom_call" | custom-call | flops 1073741824 | bytes 1572864 | tf_op jit(solution)/shard_map/tile/pallas_call | solution.py:187
  67.1 0.0 copy-start
  67.1 0.0 copy-start.1
  67.1 22.0 %all_to_all.10.sums_ref = bf16[16,64,512]{2,1,0:T(8,128)(2,1)S(1)} all-to-all(bf16[16,64,512]{2,1,0:T(8,128)(2,1)S(1)} %bitcast.8), channel_id=1, replica_groups=mesh['ylo'=2,'zhi'=4,'zlo'=4,'x'=4,'yhi'=2,'core'=2] {'ylo','x','yhi'}, dimensions={0} | all-to-all | bytes 2097152 | tf_op jit(solution)/shard_map/all_to_all | solution.py:269
  89.1 0.2 finish.1
  89.4 10.2 %all-gather.2 = bf16[256,512]{1,0:T(8,128)(2,1)S(1)} all-gather(bf16[64,512]{1,0:T(8,128)(2,1)S(1)} %finish.1), channel_id=4, replica_groups=mesh['ylo'=2,'zhi'=4,'zlo'=4,'x'=4,'yhi'=2,'core'=2] {'yhi','core'}, dimensions={0}, use_global_device_ids=true | all-gather | bytes 327680 | tf_op jit(solution)/shard_map/all_gather | solution.py:270
  99.6 0.0 copy-done
  99.6 0.0 copy-done.1
  99.6 1.9 %heads_back.1 = (bf16[128,1536]{1,0:T(8,128)(2,1)}, bf16[128,1536]{1,0:T(8,128)(2,1)}) custom-call(bf16[4,64,512]{2,1,0:T(8,128)(2,1)S(1)} %bitcast.11, bf16[1536,512]{1,0:T(8,128)(2,1)S(1)} %copy-done, bf16[1536,512]{1,0:T(8,128)(2,1)S(1)} %copy-done.1), custom_call_target="tpu_custom_call" | custom-call | tf_op jit(solution)/shard_map/heads_back/pallas_call | solution.py:238
Async XLA Ops:
  20.0 36.3 %all-to-all-start = ((bf16[16,64,512]{2,1,0:T(8,128)(2,1)}), bf16[16,64,512]{2,1,0:T(8,128)(2,1)S(1)}, u32[]{:S(2)}, u32[]{:S(2)}) async-start(bf16[16,64,512]{2,1,0:T(8,128)(2,1)} %get-tuple-element.13), calls=%async_computation | async-start | bytes 2097152 | tf_op jit(solution)/shard_map/all_to_all | solution.py:260
  46.2 11.2 %collective-permute-start.2 = (bf16[256,512]{1,0:T(8,128)(2,1)S(1)}, bf16[256,512]{1,0:T(8,128)(2,1)S(1)}, u32[]{:S(2)}, u32[]{:S(2)}) collective-permute-start(bf16[256,512]{1,0:T(8,128)(2,1)S(1)} %all_gather.25.rest_0_), channel_id=1, source_target_pairs={{224,0},{226,2},{228,4},{230,6},{232,8},{234,10},{236,12},{238,14}... | collective-permute-start | bytes 786440 | tf_op jit(solution)/shard_map/ppermute | solution.py:263
  49.6 12.9 %collective-permute-start = (bf16[256,512]{1,0:T(8,128)(2,1)S(1)}, bf16[256,512]{1,0:T(8,128)(2,1)S(1)}, u32[]{:S(2)}, u32[]{:S(2)}) collective-permute-start(bf16[256,512]{1,0:T(8,128)(2,1)S(1)} %all_gather.25.rest_0_), channel_id=1, source_target_pairs={{16,0},{18,2},{20,4},{22,6},{24,8},{26,10},{28,12},{30,14},{272,25... | collective-permute-start | bytes 786440 | tf_op jit(solution)/shard_map/ppermute | solution.py:263
  51.8 13.5 %collective-permute-start.1 = (bf16[256,512]{1,0:T(8,128)(2,1)S(1)}, bf16[256,512]{1,0:T(8,128)(2,1)S(1)}, u32[]{:S(2)}, u32[]{:S(2)}) collective-permute-start(bf16[256,512]{1,0:T(8,128)(2,1)S(1)} %all_gather.25.rest_0_), channel_id=1, source_target_pairs={{240,0},{242,2},{244,4},{246,6},{248,8},{250,10},{252,12},{254,14}... | collective-permute-start | bytes 786440 | tf_op jit(solution)/shard_map/ppermute | solution.py:263
  67.1 32.5 %copy-start = (bf16[1536,512]{1,0:T(8,128)(2,1)S(1)}, bf16[1536,512]{1,0:T(8,128)(2,1)}, u32[]{:S(2)}) copy-start(bf16[1536,512]{1,0:T(8,128)(2,1)} %wv.3) | copy-start | bytes 4718596
  67.1 32.5 %copy-start.1 = (bf16[1536,512]{1,0:T(8,128)(2,1)S(1)}, bf16[1536,512]{1,0:T(8,128)(2,1)}, u32[]{:S(2)}) copy-start(bf16[1536,512]{1,0:T(8,128)(2,1)} %ws.3) | copy-start | bytes 4718596

commit v18 on v12

--- a/solution.py
+++ b/solution.py
@@ -27,15 +27,6 @@
 def normalize(embed):
     inv = lax.rsqrt(jnp.sum(embed * embed, axis=1, keepdims=True) + EPS)
     return (inv, embed * inv)
-
-
-def far_groups(sizes):
-    ids = np.arange(math.prod(sizes)).reshape(sizes)
-    groups = []
-    for core in range(2):
-        part = np.moveaxis(ids[..., core], 1, -1).reshape(-1, sizes[1])
-        groups += (part[:, ::-1] if core == 1 else part).tolist()
-    return groups
 
 
 def from_line(sizes, steps):
@@ -162,9 +153,7 @@
         out_ref = rest[-1]
         t = t_ref[0]
         slope, start = -LOG2E * t, -LOG2E * b_ref[0]
-        zhi, last = lax.axis_index("zhi"), lax.axis_size("zhi") - 1
-        mine_at = lax.axis_index(PLANE) * own
-        other_at = jnp.where(lax.axis_index("core") == 0, zhi, last - zhi) * own
+        mine_at, other_at = lax.axis_index(PLANE) * own, lax.axis_index("zhi") * own
         for i in range(blocks):
             at = pl.multiple_of(lax.rem(mine_at // block + 1 + i, blocks) * block, block)
             sums = None if total is None else rest[len(others)][pl.ds(at, block)]
@@ -258,7 +247,7 @@
 
     wide, line = lax.optimization_barrier((wide, line))
     mine = lax.all_to_all(wide, PLANE, 0, 0).reshape(peers * own, width)
-    line = lax.all_gather(line, AXES, axis=0, tiled=True, axis_index_groups=far_groups(sizes))
+    line = lax.all_gather(line, "zhi", axis=0, tiled=True)
     first, second, third = (
         lax.ppermute(line, AXES, from_line(sizes, steps)) for steps in ((1, 1), (-1, -1), (2, -2))
     )

time: 97.8 us -> 97.7 us (level)
  no operation moved by 1% of the time
where the time goes in v18:
time: 97.7 us; the launch traced here: 97.4 us
  blocking collectives  69.9 us (72%)
  starting transfers between devices  12.6 us (13%)
  Pallas kernels  9.83 us (10%)
  waiting for transfers between devices  3.01 us (3%)
  between operations  2.03 us (2%)
    all_gather x1, blocking collectives, shards(): line = lax.all_gather(line, 'zhi', axis=0, tiled=True)  22.6 us
    all_to_all x1, blocking collectives, shards(): grad = lax.all_to_all(grad.reshape(peers, own, width), PLANE, 0, 0)  18.9 us
    all_gather x1, blocking collectives, shards(): delta = lax.all_gather(finish(grad, embed), GROUP, axis=0)  12.8 us
    ppermute x3, starting transfers between devices, shards(): lax.ppermute(line, AXES, from_line(sizes, steps))  8.95 us
    all_gather x1, blocking collectives, shards(): lax.all_gather(heads(vision, sentence, vision_map, sentence_map), 'core',...  8.69 us
    all_gather x1, blocking collectives, shards(): wide, line, embed = units(kept, lax.all_gather(given, 'yhi', axis=0), peers)  6.89 us
    pallas_call x3, Pallas kernels, tile(): pl.pallas_call(kernel, out_shape=pltpu.VMEM((n, width), BF if final else...  4 us
    all_to_all x1, starting transfers between devices, shards(): mine = lax.all_to_all(wide, PLANE, 0, 0).reshape(peers * own, width)  3.66 us
  transfers between devices with their start and end apart: 4, of which 1 were waited for; matrix products, arithmetic and copies ran while one was open for 0% of the time, Pallas kernels for 2%

profile of v18, /device:TPU:1, one launch (start us, length us, event | category | flops | bytes accessed | tf_op | source)
XLA Modules:
  0.0 97.4 jit_solution(16934007571513051971)
XLA Ops:
  0.6 2.5 %heads.1 = bf16[2,64,1024]{2,1,0:T(8,128)(2,1)S(1)} custom-call(bf16[128,1536]{1,0:T(8,128)(2,1)} %v.1, bf16[128,1536]{1,0:T(8,128)(2,1)} %s.1, bf16[1536,512]{1,0:T(8,128)(2,1)} %wv.3, bf16[1536,512]{1,0:T(8,128)(2,1)} %ws.3), custom_call_target="tpu_custom_call" | custom-call | tf_op jit(solution)/shard_map/heads/pallas_call | solution.py:72
  3.1 8.7 %all-gather = bf16[4,64,1024]{2,1,0:T(8,128)(2,1)S(1)} all-gather(bf16[2,64,1024]{2,1,0:T(8,128)(2,1)S(1)} %heads.1), channel_id=2, replica_groups=mesh['ylo'=2,'zhi'=4,'zlo'=4,'x'=4,'yhi'=2,'core'=2] {'core'}, dimensions={0}, use_global_device_ids=true | all-gather | bytes 786432 | tf_op jit(solution)/shard_map/all_gather | solution.py:244
  11.8 0.1 chip_sums.1
  11.8 6.9 %all-gather.1 = bf16[128,1024]{1,0:T(8,128)(2,1)S(1)} all-gather(bf16[64,1024]{1,0:T(8,128)(2,1)S(1)} %get-tuple-element.10), channel_id=3, replica_groups=mesh['ylo'=2,'zhi'=4,'zlo'=4,'x'=4,'yhi'=2,'core'=2] {'yhi'}, dimensions={0}, use_global_device_ids=true | all-gather | bytes 393216 | tf_op jit(solution)/shard_map/all_gather | solution.py:246
  18.7 1.2 %units.1 = (bf16[16,64,512]{2,1,0:T(8,128)(2,1)}, bf16[64,512]{1,0:T(8,128)(2,1)S(1)}, f32[64,512]{1,0:T(8,128)S(1)}) custom-call(f32[64,1024]{1,0:T(8,128)S(1)} %get-tuple-element.9.kept_ref, bf16[2,64,1024]{2,1,0:T(8,128)(2,1)S(1)} %bitcast.10), custom_call_target="tpu_custom_call" | custom-call | tf_op jit(solution)/shard_map/units/pallas_call | solution.py:132
  20.0 3.7 %all-to-all-start = ((bf16[16,64,512]{2,1,0:T(8,128)(2,1)}), bf16[16,64,512]{2,1,0:T(8,128)(2,1)S(1)}, u32[]{:S(2)}, u32[]{:S(2)}) async-start(bf16[16,64,512]{2,1,0:T(8,128)(2,1)} %get-tuple-element.13), calls=%async_computation | async-start | bytes 2097152 | tf_op jit(solution)/shard_map/all_to_all | solution.py:249
  23.6 22.6 %all_gather.25.rest_0_ = bf16[256,512]{1,0:T(8,128)(2,1)S(1)} all-gather(bf16[64,512]{1,0:T(8,128)(2,1)S(1)} %get-tuple-element.14), channel_id=1, replica_groups=mesh['ylo'=2,'zhi'=4,'zlo'=4,'x'=4,'yhi'=2,'core'=2] {'zhi'}, dimensions={0}, use_global_device_ids=true | all-gather | bytes 327680 | tf_op jit(solution)/shard_map/all_gather | solution.py:250
  46.3 3.0 %collective-permute-start.2 = (bf16[256,512]{1,0:T(8,128)(2,1)S(1)}, bf16[256,512]{1,0:T(8,128)(2,1)S(1)}, u32[]{:S(2)}, u32[]{:S(2)}) collective-permute-start(bf16[256,512]{1,0:T(8,128)(2,1)S(1)} %all_gather.25.rest_0_), channel_id=1, source_target_pairs={{32,0},{34,2},{36,4},{38,6},{40,8},{42,10},{44,12},{46,14},{288,25... | collective-permute-start | bytes 786440 | tf_op jit(solution)/shard_map/ppermute | solution.py:252
  49.3 4.0 %collective-permute-start = (bf16[256,512]{1,0:T(8,128)(2,1)S(1)}, bf16[256,512]{1,0:T(8,128)(2,1)S(1)}, u32[]{:S(2)}, u32[]{:S(2)}) collective-permute-start(bf16[256,512]{1,0:T(8,128)(2,1)S(1)} %all_gather.25.rest_0_), channel_id=1, source_target_pairs={{16,0},{18,2},{20,4},{22,6},{24,8},{26,10},{28,12},{30,14},{272,25... | collective-permute-start | bytes 786440 | tf_op jit(solution)/shard_map/ppermute | solution.py:252
  53.3 1.9 %collective-permute-start.1 = (bf16[256,512]{1,0:T(8,128)(2,1)S(1)}, bf16[256,512]{1,0:T(8,128)(2,1)S(1)}, u32[]{:S(2)}, u32[]{:S(2)}) collective-permute-start(bf16[256,512]{1,0:T(8,128)(2,1)S(1)} %all_gather.25.rest_0_), channel_id=1, source_target_pairs={{240,0},{242,2},{244,4},{246,6},{248,8},{250,10},{252,12},{254,14}... | collective-permute-start | bytes 786440 | tf_op jit(solution)/shard_map/ppermute | solution.py:252
  56.5 0.0 all-to-all-done
  56.5 1.1 %tile.3.rest_1_ = f32[1024,512]{1,0:T(8,128)S(1)} custom-call(f32[1]{0:T(128)S(6)} %copy.8.t_ref, f32[1]{0:T(128)S(6)} %copy.9.b_ref, bf16[1024,512]{1,0:T(8,128)(2,1)S(1)} %bitcast.5, bf16[256,512]{1,0:T(8,128)(2,1)S(1)} %all_gather.25.rest_0_), custom_call_target="tpu_custom_call" | custom-call | flops 536870912 | bytes 1310720 | tf_op jit(solution)/shard_map/tile/pallas_call | solution.py:176
  57.7 0.0 collective-permute-done.2.rest_0_
  57.7 1.1 %tile.4.rest_2_ = f32[1024,512]{1,0:T(8,128)S(1)} custom-call(f32[1]{0:T(128)S(6)} %copy.8.t_ref, f32[1]{0:T(128)S(6)} %copy.9.b_ref, bf16[1024,512]{1,0:T(8,128)(2,1)S(1)} %bitcast.6, bf16[256,512]{1,0:T(8,128)(2,1)S(1)} %collective-permute-done.2.rest_0_, f32[1024,512]{1,0:T(8,128)S(1)} %tile.3.rest_1_), custom_call_target="tpu_custom_call" | custom-call | flops 536870912 | bytes 1310720 | tf_op jit(solution)/shard_map/tile/pallas_call | solution.py:176
  58.8 3.0 %collective-permute-done.rest_0_ = bf16[256,512]{1,0:T(8,128)(2,1)S(1)} collective-permute-done((bf16[256,512]{1,0:T(8,128)(2,1)S(1)}, bf16[256,512]{1,0:T(8,128)(2,1)S(1)}, u32[]{:S(2)}, u32[]{:S(2)}) %collective-permute-start) | collective-permute-done | bytes 262176 | tf_op jit(solution)/shard_map/ppermute | solution.py:252
  61.8 0.0 collective-permute-done.1.rest_1_
  61.8 1.7 %tile.5 = bf16[1024,512]{1,0:T(8,128)(2,1)S(1)} custom-call(f32[1]{0:T(128)S(6)} %copy.8.t_ref, f32[1]{0:T(128)S(6)} %copy.9.b_ref, bf16[1024,512]{1,0:T(8,128)(2,1)S(1)} %bitcast.7, bf16[256,512]{1,0:T(8,128)(2,1)S(1)} %collective-permute-done.rest_0_, bf16[256,512]{1,0:T(8,128)(2,1)S(1)} %collective-permute-done.1.rest_1_, f32[1024,512]{1,0:T(8,128)S(1)} %tile.4.rest_2_), custom_call_target="tpu_custom_call" | custom-call | flops 1073741824 | bytes 1572864 | tf_op jit(solution)/shard_map/tile/pallas_call | solution.py:176
  63.6 0.0 copy-start
  63.6 0.0 copy-start.1
  63.6 18.9 %all_to_all.10.sums_ref = bf16[16,64,512]{2,1,0:T(8,128)(2,1)S(1)} all-to-all(bf16[16,64,512]{2,1,0:T(8,128)(2,1)S(1)} %bitcast.8), channel_id=1, replica_groups=mesh['ylo'=2,'zhi'=4,'zlo'=4,'x'=4,'yhi'=2,'core'=2] {'ylo','x','yhi'}, dimensions={0} | all-to-all | bytes 2097152 | tf_op jit(solution)/shard_map/all_to_all | solution.py:258
  82.5 0.2 finish.1
  82.7 12.8 %all-gather.2 = bf16[256,512]{1,0:T(8,128)(2,1)S(1)} all-gather(bf16[64,512]{1,0:T(8,128)(2,1)S(1)} %finish.1), channel_id=4, replica_groups=mesh['ylo'=2,'zhi'=4,'zlo'=4,'x'=4,'yhi'=2,'core'=2] {'yhi','core'}, dimensions={0}, use_global_device_ids=true | all-gather | bytes 327680 | tf_op jit(solution)/shard_map/all_gather | solution.py:259
  95.5 0.0 copy-done
  95.5 0.0 copy-done.1
  95.5 1.9 %heads_back.1 = (bf16[128,1536]{1,0:T(8,128)(2,1)}, bf16[128,1536]{1,0:T(8,128)(2,1)}) custom-call(bf16[4,64,512]{2,1,0:T(8,128)(2,1)S(1)} %bitcast.11, bf16[1536,512]{1,0:T(8,128)(2,1)S(1)} %copy-done, bf16[1536,512]{1,0:T(8,128)(2,1)S(1)} %copy-done.1), custom_call_target="tpu_custom_call" | custom-call | tf_op jit(solution)/shard_map/heads_back/pallas_call | solution.py:227
Async XLA Ops:
  20.0 36.5 %all-to-all-start = ((bf16[16,64,512]{2,1,0:T(8,128)(2,1)}), bf16[16,64,512]{2,1,0:T(8,128)(2,1)S(1)}, u32[]{:S(2)}, u32[]{:S(2)}) async-start(bf16[16,64,512]{2,1,0:T(8,128)(2,1)} %get-tuple-element.13), calls=%async_computation | async-start | bytes 2097152 | tf_op jit(solution)/shard_map/all_to_all | solution.py:249
  46.3 11.4 %collective-permute-start.2 = (bf16[256,512]{1,0:T(8,128)(2,1)S(1)}, bf16[256,512]{1,0:T(8,128)(2,1)S(1)}, u32[]{:S(2)}, u32[]{:S(2)}) collective-permute-start(bf16[256,512]{1,0:T(8,128)(2,1)S(1)} %all_gather.25.rest_0_), channel_id=1, source_target_pairs={{32,0},{34,2},{36,4},{38,6},{40,8},{42,10},{44,12},{46,14},{288,25... | collective-permute-start | bytes 786440 | tf_op jit(solution)/shard_map/ppermute | solution.py:252
  49.3 12.5 %collective-permute-start = (bf16[256,512]{1,0:T(8,128)(2,1)S(1)}, bf16[256,512]{1,0:T(8,128)(2,1)S(1)}, u32[]{:S(2)}, u32[]{:S(2)}) collective-permute-start(bf16[256,512]{1,0:T(8,128)(2,1)S(1)} %all_gather.25.rest_0_), channel_id=1, source_target_pairs={{16,0},{18,2},{20,4},{22,6},{24,8},{26,10},{28,12},{30,14},{272,25... | collective-permute-start | bytes 786440 | tf_op jit(solution)/shard_map/ppermute | solution.py:252
  53.3 8.5 %collective-permute-start.1 = (bf16[256,512]{1,0:T(8,128)(2,1)S(1)}, bf16[256,512]{1,0:T(8,128)(2,1)S(1)}, u32[]{:S(2)}, u32[]{:S(2)}) collective-permute-start(bf16[256,512]{1,0:T(8,128)(2,1)S(1)} %all_gather.25.rest_0_), channel_id=1, source_target_pairs={{240,0},{242,2},{244,4},{246,6},{248,8},{250,10},{252,12},{254,14}... | collective-permute-start | bytes 786440 | tf_op jit(solution)/shard_map/ppermute | solution.py:252
  63.6 32.0 %copy-start = (bf16[1536,512]{1,0:T(8,128)(2,1)S(1)}, bf16[1536,512]{1,0:T(8,128)(2,1)}, u32[]{:S(2)}) copy-start(bf16[1536,512]{1,0:T(8,128)(2,1)} %wv.3) | copy-start | bytes 4718596
  63.6 32.0 %copy-start.1 = (bf16[1536,512]{1,0:T(8,128)(2,1)S(1)}, bf16[1536,512]{1,0:T(8,128)(2,1)}, u32[]{:S(2)}) copy-start(bf16[1536,512]{1,0:T(8,128)(2,1)} %ws.3) | copy-start | bytes 4718596

commit v19 on v18

--- a/solution.py
+++ b/solution.py
@@ -245,9 +245,9 @@
     given, kept = chip_sums(parts)
     wide, line, embed = units(kept, lax.all_gather(given, "yhi", axis=0), peers)
 
+    line = lax.all_gather(line, "zhi", axis=0, tiled=True)
     wide, line = lax.optimization_barrier((wide, line))
     mine = lax.all_to_all(wide, PLANE, 0, 0).reshape(peers * own, width)
-    line = lax.all_gather(line, "zhi", axis=0, tiled=True)
     first, second, third = (
         lax.ppermute(line, AXES, from_line(sizes, steps)) for steps in ((1, 1), (-1, -1), (2, -2))
     )

time: 97.7 us -> 98.1 us (level)
  starting transfers between devices: 12.6 us -> 15.7 us
  blocking collectives: 69.9 us -> 67 us
    all_gather x1, blocking collectives: 22.6 us -> 19.1 us  [shards(): line = lax.all_gather(line, 'zhi', axis=0, tiled=True)]
    all_to_all x1, waiting for transfers between devices: 0.01 us -> 3.05 us  [shards(): mine = lax.all_to_all(wide, PLANE, 0, 0).reshape(peers * own, width)]
    all_to_all x1, starting transfers between devices: 3.66 us -> 6.66 us  [shards(): mine = lax.all_to_all(wide, PLANE, 0, 0).reshape(peers * own, width)]
    ppermute x3, waiting for transfers between devices: 3.01 us -> 0.07 us  [shards(): lax.ppermute(line, AXES, from_line(sizes, steps))]
    all_to_all x1, blocking collectives: 18.9 us -> 20 us  [shards(): grad = lax.all_to_all(grad.reshape(peers, own, width), PLANE, 0, 0)]
  transfers between devices with their start and end apart: 4 -> 4, of which waited for: 1 -> 2; matrix products, arithmetic and copies ran while one was open for 0% -> 0% of each run, Pallas kernels for 2% -> 2%
where the time goes in v19:
time: 98.1 us; the launch traced here: 97.7 us
  blocking collectives  67 us (68%)
  starting transfers between devices  15.7 us (16%)
  Pallas kernels  9.83 us (10%)
  waiting for transfers between devices  3.12 us (3%)
  between operations  2.03 us (2%)
    all_to_all x1, blocking collectives, shards(): grad = lax.all_to_all(grad.reshape(peers, own, width), PLANE, 0, 0)  20 us
    all_gather x1, blocking collectives, shards(): line = lax.all_gather(line, 'zhi', axis=0, tiled=True)  19.1 us
    all_gather x1, blocking collectives, shards(): delta = lax.all_gather(finish(grad, embed), GROUP, axis=0)  12.4 us
    ppermute x3, starting transfers between devices, shards(): lax.ppermute(line, AXES, from_line(sizes, steps))  9.03 us
    all_gather x1, blocking collectives, shards(): lax.all_gather(heads(vision, sentence, vision_map, sentence_map), 'core',...  8.69 us
    all_gather x1, blocking collectives, shards(): wide, line, embed = units(kept, lax.all_gather(given, 'yhi', axis=0), peers)  6.89 us
    all_to_all x1, starting transfers between devices, shards(): mine = lax.all_to_all(wide, PLANE, 0, 0).reshape(peers * own, width)  6.66 us
    pallas_call x3, Pallas kernels, tile(): pl.pallas_call(kernel, out_shape=pltpu.VMEM((n, width), BF if final else...  3.99 us
  transfers between devices with their start and end apart: 4, of which 2 were waited for; matrix products, arithmetic and copies ran while one was open for 0% of the time, Pallas kernels for 2%

profile of v19, /device:TPU:1, one launch (start us, length us, event | category | flops | bytes accessed | tf_op | source)
XLA Modules:
  0.0 97.7 jit_solution(14402319230395898838)
XLA Ops:
  0.6 2.5 %heads.1 = bf16[2,64,1024]{2,1,0:T(8,128)(2,1)S(1)} custom-call(bf16[128,1536]{1,0:T(8,128)(2,1)} %v.1, bf16[128,1536]{1,0:T(8,128)(2,1)} %s.1, bf16[1536,512]{1,0:T(8,128)(2,1)} %wv.3, bf16[1536,512]{1,0:T(8,128)(2,1)} %ws.3), custom_call_target="tpu_custom_call" | custom-call | tf_op jit(solution)/shard_map/heads/pallas_call | solution.py:72
  3.1 8.7 %all-gather = bf16[4,64,1024]{2,1,0:T(8,128)(2,1)S(1)} all-gather(bf16[2,64,1024]{2,1,0:T(8,128)(2,1)S(1)} %heads.1), channel_id=2, replica_groups=mesh['ylo'=2,'zhi'=4,'zlo'=4,'x'=4,'yhi'=2,'core'=2] {'core'}, dimensions={0}, use_global_device_ids=true | all-gather | bytes 786432 | tf_op jit(solution)/shard_map/all_gather | solution.py:244
  11.8 0.1 chip_sums.1
  11.8 6.9 %all-gather.1 = bf16[128,1024]{1,0:T(8,128)(2,1)S(1)} all-gather(bf16[64,1024]{1,0:T(8,128)(2,1)S(1)} %get-tuple-element.10), channel_id=3, replica_groups=mesh['ylo'=2,'zhi'=4,'zlo'=4,'x'=4,'yhi'=2,'core'=2] {'yhi'}, dimensions={0}, use_global_device_ids=true | all-gather | bytes 393216 | tf_op jit(solution)/shard_map/all_gather | solution.py:246
  18.7 1.2 %units.1 = (bf16[16,64,512]{2,1,0:T(8,128)(2,1)}, bf16[64,512]{1,0:T(8,128)(2,1)S(1)}, f32[64,512]{1,0:T(8,128)S(1)}) custom-call(f32[64,1024]{1,0:T(8,128)S(1)} %get-tuple-element.9.kept_ref, bf16[2,64,1024]{2,1,0:T(8,128)(2,1)S(1)} %bitcast.10), custom_call_target="tpu_custom_call" | custom-call | tf_op jit(solution)/shard_map/units/pallas_call | solution.py:132
  20.0 19.1 %all_gather.25.rest_0_ = bf16[256,512]{1,0:T(8,128)(2,1)S(1)} all-gather(bf16[64,512]{1,0:T(8,128)(2,1)S(1)} %get-tuple-element.12), channel_id=1, replica_groups=mesh['ylo'=2,'zhi'=4,'zlo'=4,'x'=4,'yhi'=2,'core'=2] {'zhi'}, dimensions={0}, use_global_device_ids=true | all-gather | bytes 327680 | tf_op jit(solution)/shard_map/all_gather | solution.py:248
  39.1 6.7 %all-to-all-start = ((bf16[16,64,512]{2,1,0:T(8,128)(2,1)}), bf16[16,64,512]{2,1,0:T(8,128)(2,1)S(1)}, u32[]{:S(2)}, u32[]{:S(2)}) async-start(bf16[16,64,512]{2,1,0:T(8,128)(2,1)} %get-tuple-element.13), calls=%async_computation | async-start | bytes 2097152 | tf_op jit(solution)/shard_map/all_to_all | solution.py:250
  45.8 3.3 %collective-permute-start.2 = (bf16[256,512]{1,0:T(8,128)(2,1)S(1)}, bf16[256,512]{1,0:T(8,128)(2,1)S(1)}, u32[]{:S(2)}, u32[]{:S(2)}) collective-permute-start(bf16[256,512]{1,0:T(8,128)(2,1)S(1)} %all_gather.25.rest_0_), channel_id=1, source_target_pairs={{32,0},{34,2},{36,4},{38,6},{40,8},{42,10},{44,12},{46,14},{288,25... | collective-permute-start | bytes 786440 | tf_op jit(solution)/shard_map/ppermute | solution.py:252
  49.0 3.9 %collective-permute-start = (bf16[256,512]{1,0:T(8,128)(2,1)S(1)}, bf16[256,512]{1,0:T(8,128)(2,1)S(1)}, u32[]{:S(2)}, u32[]{:S(2)}) collective-permute-start(bf16[256,512]{1,0:T(8,128)(2,1)S(1)} %all_gather.25.rest_0_), channel_id=1, source_target_pairs={{16,0},{18,2},{20,4},{22,6},{24,8},{26,10},{28,12},{30,14},{272,25... | collective-permute-start | bytes 786440 | tf_op jit(solution)/shard_map/ppermute | solution.py:252
  52.9 1.9 %collective-permute-start.1 = (bf16[256,512]{1,0:T(8,128)(2,1)S(1)}, bf16[256,512]{1,0:T(8,128)(2,1)S(1)}, u32[]{:S(2)}, u32[]{:S(2)}) collective-permute-start(bf16[256,512]{1,0:T(8,128)(2,1)S(1)} %all_gather.25.rest_0_), channel_id=1, source_target_pairs={{240,0},{242,2},{244,4},{246,6},{248,8},{250,10},{252,12},{254,14}... | collective-permute-start | bytes 786440 | tf_op jit(solution)/shard_map/ppermute | solution.py:252
  56.1 3.1 %all-to-all-done = bf16[16,64,512]{2,1,0:T(8,128)(2,1)S(1)} async-done(((bf16[16,64,512]{2,1,0:T(8,128)(2,1)}), bf16[16,64,512]{2,1,0:T(8,128)(2,1)S(1)}, u32[]{:S(2)}, u32[]{:S(2)}) %all-to-all-start) | async-done | bytes 1048608 | tf_op jit(solution)/shard_map/all_to_all | solution.py:250
  59.2 1.1 %tile.3.rest_1_ = f32[1024,512]{1,0:T(8,128)S(1)} custom-call(f32[1]{0:T(128)S(6)} %copy.8.t_ref, f32[1]{0:T(128)S(6)} %copy.9.b_ref, bf16[1024,512]{1,0:T(8,128)(2,1)S(1)} %bitcast.5, bf16[256,512]{1,0:T(8,128)(2,1)S(1)} %all_gather.25.rest_0_), custom_call_target="tpu_custom_call" | custom-call | flops 536870912 | bytes 1310720 | tf_op jit(solution)/shard_map/tile/pallas_call | solution.py:176
  60.3 0.0 collective-permute-done.2.rest_0_
  60.3 1.1 %tile.4.rest_2_ = f32[1024,512]{1,0:T(8,128)S(1)} custom-call(f32[1]{0:T(128)S(6)} %copy.8.t_ref, f32[1]{0:T(128)S(6)} %copy.9.b_ref, bf16[1024,512]{1,0:T(8,128)(2,1)S(1)} %bitcast.6, bf16[256,512]{1,0:T(8,128)(2,1)S(1)} %collective-permute-done.2.rest_0_, f32[1024,512]{1,0:T(8,128)S(1)} %tile.3.rest_1_), custom_call_target="tpu_custom_call" | custom-call | flops 536870912 | bytes 1310720 | tf_op jit(solution)/shard_map/tile/pallas_call | solution.py:176
  61.4 0.0 collective-permute-done.rest_0_
  61.4 0.1 collective-permute-done.1.rest_1_
  61.5 1.7 %tile.5 = bf16[1024,512]{1,0:T(8,128)(2,1)S(1)} custom-call(f32[1]{0:T(128)S(6)} %copy.8.t_ref, f32[1]{0:T(128)S(6)} %copy.9.b_ref, bf16[1024,512]{1,0:T(8,128)(2,1)S(1)} %bitcast.7, bf16[256,512]{1,0:T(8,128)(2,1)S(1)} %collective-permute-done.rest_0_, bf16[256,512]{1,0:T(8,128)(2,1)S(1)} %collective-permute-done.1.rest_1_, f32[1024,512]{1,0:T(8,128)S(1)} %tile.4.rest_2_), custom_call_target="tpu_custom_call" | custom-call | flops 1073741824 | bytes 1572864 | tf_op jit(solution)/shard_map/tile/pallas_call | solution.py:176
  63.2 0.0 copy-start
  63.3 0.0 copy-start.1
  63.3 20.0 %all_to_all.10.sums_ref = bf16[16,64,512]{2,1,0:T(8,128)(2,1)S(1)} all-to-all(bf16[16,64,512]{2,1,0:T(8,128)(2,1)S(1)} %bitcast.8), channel_id=1, replica_groups=mesh['ylo'=2,'zhi'=4,'zlo'=4,'x'=4,'yhi'=2,'core'=2] {'ylo','x','yhi'}, dimensions={0} | all-to-all | bytes 2097152 | tf_op jit(solution)/shard_map/all_to_all | solution.py:258
  83.3 0.2 finish.1
  83.5 12.4 %all-gather.2 = bf16[256,512]{1,0:T(8,128)(2,1)S(1)} all-gather(bf16[64,512]{1,0:T(8,128)(2,1)S(1)} %finish.1), channel_id=4, replica_groups=mesh['ylo'=2,'zhi'=4,'zlo'=4,'x'=4,'yhi'=2,'core'=2] {'yhi','core'}, dimensions={0}, use_global_device_ids=true | all-gather | bytes 327680 | tf_op jit(solution)/shard_map/all_gather | solution.py:259
  95.9 0.0 copy-done
  95.9 0.0 copy-done.1
  95.9 1.9 %heads_back.1 = (bf16[128,1536]{1,0:T(8,128)(2,1)}, bf16[128,1536]{1,0:T(8,128)(2,1)}) custom-call(bf16[4,64,512]{2,1,0:T(8,128)(2,1)S(1)} %bitcast.11, bf16[1536,512]{1,0:T(8,128)(2,1)S(1)} %copy-done, bf16[1536,512]{1,0:T(8,128)(2,1)S(1)} %copy-done.1), custom_call_target="tpu_custom_call" | custom-call | tf_op jit(solution)/shard_map/heads_back/pallas_call | solution.py:227
Async XLA Ops:
  39.1 20.1 %all-to-all-start = ((bf16[16,64,512]{2,1,0:T(8,128)(2,1)}), bf16[16,64,512]{2,1,0:T(8,128)(2,1)S(1)}, u32[]{:S(2)}, u32[]{:S(2)}) async-start(bf16[16,64,512]{2,1,0:T(8,128)(2,1)} %get-tuple-element.13), calls=%async_computation | async-start | bytes 2097152 | tf_op jit(solution)/shard_map/all_to_all | solution.py:250
  45.8 14.5 %collective-permute-start.2 = (bf16[256,512]{1,0:T(8,128)(2,1)S(1)}, bf16[256,512]{1,0:T(8,128)(2,1)S(1)}, u32[]{:S(2)}, u32[]{:S(2)}) collective-permute-start(bf16[256,512]{1,0:T(8,128)(2,1)S(1)} %all_gather.25.rest_0_), channel_id=1, source_target_pairs={{32,0},{34,2},{36,4},{38,6},{40,8},{42,10},{44,12},{46,14},{288,25... | collective-permute-start | bytes 786440 | tf_op jit(solution)/shard_map/ppermute | solution.py:252
  49.0 12.4 %collective-permute-start = (bf16[256,512]{1,0:T(8,128)(2,1)S(1)}, bf16[256,512]{1,0:T(8,128)(2,1)S(1)}, u32[]{:S(2)}, u32[]{:S(2)}) collective-permute-start(bf16[256,512]{1,0:T(8,128)(2,1)S(1)} %all_gather.25.rest_0_), channel_id=1, source_target_pairs={{16,0},{18,2},{20,4},{22,6},{24,8},{26,10},{28,12},{30,14},{272,25... | collective-permute-start | bytes 786440 | tf_op jit(solution)/shard_map/ppermute | solution.py:252
  52.9 8.6 %collective-permute-start.1 = (bf16[256,512]{1,0:T(8,128)(2,1)S(1)}, bf16[256,512]{1,0:T(8,128)(2,1)S(1)}, u32[]{:S(2)}, u32[]{:S(2)}) collective-permute-start(bf16[256,512]{1,0:T(8,128)(2,1)S(1)} %all_gather.25.rest_0_), channel_id=1, source_target_pairs={{240,0},{242,2},{244,4},{246,6},{248,8},{250,10},{252,12},{254,14}... | collective-permute-start | bytes 786440 | tf_op jit(solution)/shard_map/ppermute | solution.py:252
  63.2 32.6 %copy-start = (bf16[1536,512]{1,0:T(8,128)(2,1)S(1)}, bf16[1536,512]{1,0:T(8,128)(2,1)}, u32[]{:S(2)}) copy-start(bf16[1536,512]{1,0:T(8,128)(2,1)} %wv.3) | copy-start | bytes 4718596
  63.3 32.6 %copy-start.1 = (bf16[1536,512]{1,0:T(8,128)(2,1)S(1)}, bf16[1536,512]{1,0:T(8,128)(2,1)}, u32[]{:S(2)}) copy-start(bf16[1536,512]{1,0:T(8,128)(2,1)} %ws.3) | copy-start | bytes 4718596

commit v20 on v14

--- a/solution.py
+++ b/solution.py
@@ -27,15 +27,6 @@
 def normalize(embed):
     inv = lax.rsqrt(jnp.sum(embed * embed, axis=1, keepdims=True) + EPS)
     return (inv, embed * inv)
-
-
-def far_groups(sizes):
-    ids = np.arange(math.prod(sizes)).reshape(sizes)
-    groups = []
-    for core in range(2):
-        part = np.moveaxis(ids[..., core], 1, -1).reshape(-1, sizes[1])
-        groups += (part[:, ::-1] if core == 1 else part).tolist()
-    return groups
 
 
 def from_line(sizes, steps):
@@ -157,9 +148,7 @@
         out_ref = rest[-1]
         t = t_ref[0]
         slope, start = -LOG2E * t, -LOG2E * b_ref[0]
-        zhi, last = lax.axis_index("zhi"), lax.axis_size("zhi") - 1
-        mine_at = lax.axis_index(PLANE) * own
-        other_at = jnp.where(lax.axis_index("core") == 0, zhi, last - zhi) * own
+        mine_at, other_at = lax.axis_index(PLANE) * own, lax.axis_index("zhi") * own
         for i in range(blocks):
             at = pl.multiple_of(lax.rem(mine_at // block + 1 + i, blocks) * block, block)
             sums = None if total is None else rest[len(others)][pl.ds(at, block)]
@@ -253,13 +242,13 @@
 
     wide, line = lax.optimization_barrier((wide, line))
     mine = lax.all_to_all(wide, PLANE, 0, 0).reshape(peers * own, width)
-    line = lax.all_gather(line, AXES, axis=0, tiled=True, axis_index_groups=far_groups(sizes))
+    line = lax.all_gather(line, "zhi", axis=0, tiled=True)
     first, second, third = (
         lax.ppermute(line, AXES, from_line(sizes, steps)) for steps in ((1, 1), (-1, -1), (2, -2))
     )
     grad = tile(sharpness, offset, mine, [line], None, own, positives=True)
     grad = tile(sharpness, offset, mine, [third], grad, own)
-    grad = tile(sharpness, offset, mine, [second, first], grad, own, final=True)
+    grad = tile(sharpness, offset, mine, [first, second], grad, own, final=True, block=1024)
 
     grad = lax.all_to_all(grad.reshape(peers, own, width), PLANE, 0, 0)
     delta = lax.all_gather(finish(grad, embed), GROUP, axis=0)

time: 100 us -> 97.6 us (0.976)
  waiting for transfers between devices: 4.95 us -> 3.01 us
    all_to_all x1, blocking collectives: 21.4 us -> 18.9 us  [shards(): grad = lax.all_to_all(grad.reshape(peers, own, width), PLANE, 0, 0)]
    all_gather x1, blocking collectives: 10.5 us -> 12.8 us  [shards(): delta = lax.all_gather(finish(grad, embed), GROUP, axis=0)]
    ppermute x3, waiting for transfers between devices: 4.95 us -> 3.01 us  [shards(): lax.ppermute(line, AXES, from_line(sizes, steps))]
  transfers between devices with their start and end apart: 4 -> 4, of which waited for: 2 -> 1; matrix products, arithmetic and copies ran while one was open for 0% -> 0% of each run, Pallas kernels for 2% -> 2%
where the time goes in v20:
time: 97.6 us; the launch traced here: 97.3 us
  blocking collectives  69.9 us (72%)
  starting transfers between devices  12.6 us (13%)
  Pallas kernels  9.71 us (10%)
  waiting for transfers between devices  3.01 us (3%)
  between operations  2.02 us (2%)
    all_gather x1, blocking collectives, shards(): line = lax.all_gather(line, 'zhi', axis=0, tiled=True)  22.6 us
    all_to_all x1, blocking collectives, shards(): grad = lax.all_to_all(grad.reshape(peers, own, width), PLANE, 0, 0)  18.9 us
    all_gather x1, blocking collectives, shards(): delta = lax.all_gather(finish(grad, embed), GROUP, axis=0)  12.8 us
    ppermute x3, starting transfers between devices, shards(): lax.ppermute(line, AXES, from_line(sizes, steps))  8.95 us
    all_gather x1, blocking collectives, shards(): lax.all_gather(heads(vision, sentence, vision_map, sentence_map), 'core',...  8.69 us
    all_gather x1, blocking collectives, shards(): wide, line, embed = units(kept, lax.all_gather(given, 'yhi', axis=0), peers)  6.89 us
    pallas_call x3, Pallas kernels, tile(): pl.pallas_call(kernel, out_shape=pltpu.VMEM((n, width), BF if final else...  3.97 us
    all_to_all x1, starting transfers between devices, shards(): mine = lax.all_to_all(wide, PLANE, 0, 0).reshape(peers * own, width)  3.65 us
  transfers between devices with their start and end apart: 4, of which 1 were waited for; matrix products, arithmetic and copies ran while one was open for 0% of the time, Pallas kernels for 2%

profile of v20, /device:TPU:1, one launch (start us, length us, event | category | flops | bytes accessed | tf_op | source)
XLA Modules:
  0.0 97.3 jit_solution(12067693791202477096)
XLA Ops:
  0.6 2.5 %heads.1 = bf16[2,64,1024]{2,1,0:T(8,128)(2,1)S(1)} custom-call(bf16[128,1536]{1,0:T(8,128)(2,1)} %v.1, bf16[128,1536]{1,0:T(8,128)(2,1)} %s.1, bf16[1536,512]{1,0:T(8,128)(2,1)} %wv.3, bf16[1536,512]{1,0:T(8,128)(2,1)} %ws.3), custom_call_target="tpu_custom_call" | custom-call | tf_op jit(solution)/shard_map/heads/pallas_call | solution.py:72
  3.1 8.7 %all-gather = bf16[4,64,1024]{2,1,0:T(8,128)(2,1)S(1)} all-gather(bf16[2,64,1024]{2,1,0:T(8,128)(2,1)S(1)} %heads.1), channel_id=2, replica_groups=mesh['ylo'=2,'zhi'=4,'zlo'=4,'x'=4,'yhi'=2,'core'=2] {'core'}, dimensions={0}, use_global_device_ids=true | all-gather | bytes 786432 | tf_op jit(solution)/shard_map/all_gather | solution.py:239
  11.8 0.1 chip_sums.1
  11.8 6.9 %all-gather.1 = bf16[128,1024]{1,0:T(8,128)(2,1)S(1)} all-gather(bf16[64,1024]{1,0:T(8,128)(2,1)S(1)} %get-tuple-element.10), channel_id=3, replica_groups=mesh['ylo'=2,'zhi'=4,'zlo'=4,'x'=4,'yhi'=2,'core'=2] {'yhi'}, dimensions={0}, use_global_device_ids=true | all-gather | bytes 393216 | tf_op jit(solution)/shard_map/all_gather | solution.py:241
  18.7 1.1 %units.1 = (bf16[16,64,512]{2,1,0:T(8,128)(2,1)}, bf16[64,512]{1,0:T(8,128)(2,1)S(1)}, f32[64,512]{1,0:T(8,128)S(1)}) custom-call(f32[64,1024]{1,0:T(8,128)S(1)} %get-tuple-element.9.kept_ref, bf16[2,64,1024]{2,1,0:T(8,128)(2,1)S(1)} %bitcast.10), custom_call_target="tpu_custom_call" | custom-call | tf_op jit(solution)/shard_map/units/pallas_call | solution.py:128
  19.9 3.7 %all-to-all-start = ((bf16[16,64,512]{2,1,0:T(8,128)(2,1)}), bf16[16,64,512]{2,1,0:T(8,128)(2,1)S(1)}, u32[]{:S(2)}, u32[]{:S(2)}) async-start(bf16[16,64,512]{2,1,0:T(8,128)(2,1)} %get-tuple-element.13), calls=%async_computation | async-start | bytes 2097152 | tf_op jit(solution)/shard_map/all_to_all | solution.py:244
  23.5 22.6 %all_gather.25.rest_0_ = bf16[256,512]{1,0:T(8,128)(2,1)S(1)} all-gather(bf16[64,512]{1,0:T(8,128)(2,1)S(1)} %get-tuple-element.14), channel_id=1, replica_groups=mesh['ylo'=2,'zhi'=4,'zlo'=4,'x'=4,'yhi'=2,'core'=2] {'zhi'}, dimensions={0}, use_global_device_ids=true | all-gather | bytes 327680 | tf_op jit(solution)/shard_map/all_gather | solution.py:245
  46.1 3.0 %collective-permute-start.2 = (bf16[256,512]{1,0:T(8,128)(2,1)S(1)}, bf16[256,512]{1,0:T(8,128)(2,1)S(1)}, u32[]{:S(2)}, u32[]{:S(2)}) collective-permute-start(bf16[256,512]{1,0:T(8,128)(2,1)S(1)} %all_gather.25.rest_0_), channel_id=1, source_target_pairs={{32,0},{34,2},{36,4},{38,6},{40,8},{42,10},{44,12},{46,14},{288,25... | collective-permute-start | bytes 786440 | tf_op jit(solution)/shard_map/ppermute | solution.py:247
  49.2 4.0 %collective-permute-start = (bf16[256,512]{1,0:T(8,128)(2,1)S(1)}, bf16[256,512]{1,0:T(8,128)(2,1)S(1)}, u32[]{:S(2)}, u32[]{:S(2)}) collective-permute-start(bf16[256,512]{1,0:T(8,128)(2,1)S(1)} %all_gather.25.rest_0_), channel_id=1, source_target_pairs={{16,0},{18,2},{20,4},{22,6},{24,8},{26,10},{28,12},{30,14},{272,25... | collective-permute-start | bytes 786440 | tf_op jit(solution)/shard_map/ppermute | solution.py:247
  53.2 1.9 %collective-permute-start.1 = (bf16[256,512]{1,0:T(8,128)(2,1)S(1)}, bf16[256,512]{1,0:T(8,128)(2,1)S(1)}, u32[]{:S(2)}, u32[]{:S(2)}) collective-permute-start(bf16[256,512]{1,0:T(8,128)(2,1)S(1)} %all_gather.25.rest_0_), channel_id=1, source_target_pairs={{240,0},{242,2},{244,4},{246,6},{248,8},{250,10},{252,12},{254,14}... | collective-permute-start | bytes 786440 | tf_op jit(solution)/shard_map/ppermute | solution.py:247
  56.4 0.0 all-to-all-done
  56.4 1.1 %tile.3.rest_1_ = f32[1024,512]{1,0:T(8,128)S(1)} custom-call(f32[1]{0:T(128)S(6)} %copy.8.t_ref, f32[1]{0:T(128)S(6)} %copy.9.b_ref, bf16[1024,512]{1,0:T(8,128)(2,1)S(1)} %bitcast.5, bf16[256,512]{1,0:T(8,128)(2,1)S(1)} %all_gather.25.rest_0_), custom_call_target="tpu_custom_call" | custom-call | flops 536870912 | bytes 1310720 | tf_op jit(solution)/shard_map/tile/pallas_call | solution.py:171
  57.5 0.0 collective-permute-done.2.rest_0_
  57.6 1.1 %tile.4.rest_2_ = f32[1024,512]{1,0:T(8,128)S(1)} custom-call(f32[1]{0:T(128)S(6)} %copy.8.t_ref, f32[1]{0:T(128)S(6)} %copy.9.b_ref, bf16[1024,512]{1,0:T(8,128)(2,1)S(1)} %bitcast.6, bf16[256,512]{1,0:T(8,128)(2,1)S(1)} %collective-permute-done.2.rest_0_, f32[1024,512]{1,0:T(8,128)S(1)} %tile.3.rest_1_), custom_call_target="tpu_custom_call" | custom-call | flops 536870912 | bytes 1310720 | tf_op jit(solution)/shard_map/tile/pallas_call | solution.py:171
  58.7 3.0 %collective-permute-done.rest_0_ = bf16[256,512]{1,0:T(8,128)(2,1)S(1)} collective-permute-done((bf16[256,512]{1,0:T(8,128)(2,1)S(1)}, bf16[256,512]{1,0:T(8,128)(2,1)S(1)}, u32[]{:S(2)}, u32[]{:S(2)}) %collective-permute-start) | collective-permute-done | bytes 262176 | tf_op jit(solution)/shard_map/ppermute | solution.py:247
  61.7 0.0 collective-permute-done.1.rest_1_
  61.7 1.7 %tile.5 = bf16[1024,512]{1,0:T(8,128)(2,1)S(1)} custom-call(f32[1]{0:T(128)S(6)} %copy.8.t_ref, f32[1]{0:T(128)S(6)} %copy.9.b_ref, bf16[1024,512]{1,0:T(8,128)(2,1)S(1)} %bitcast.7, bf16[256,512]{1,0:T(8,128)(2,1)S(1)} %collective-permute-done.rest_0_, bf16[256,512]{1,0:T(8,128)(2,1)S(1)} %collective-permute-done.1.rest_1_, f32[1024,512]{1,0:T(8,128)S(1)} %tile.4.rest_2_), custom_call_target="tpu_custom_call" | custom-call | flops 1073741824 | bytes 1572864 | tf_op jit(solution)/shard_map/tile/pallas_call | solution.py:171
  63.4 0.0 copy-start
  63.4 0.0 copy-start.1
  63.4 18.9 %all_to_all.10.sums_ref = bf16[16,64,512]{2,1,0:T(8,128)(2,1)S(1)} all-to-all(bf16[16,64,512]{2,1,0:T(8,128)(2,1)S(1)} %bitcast.8), channel_id=1, replica_groups=mesh['ylo'=2,'zhi'=4,'zlo'=4,'x'=4,'yhi'=2,'core'=2] {'ylo','x','yhi'}, dimensions={0} | all-to-all | bytes 2097152 | tf_op jit(solution)/shard_map/all_to_all | solution.py:253
  82.3 0.2 finish.1
  82.6 12.8 %all-gather.2 = bf16[256,512]{1,0:T(8,128)(2,1)S(1)} all-gather(bf16[64,512]{1,0:T(8,128)(2,1)S(1)} %finish.1), channel_id=4, replica_groups=mesh['ylo'=2,'zhi'=4,'zlo'=4,'x'=4,'yhi'=2,'core'=2] {'yhi','core'}, dimensions={0}, use_global_device_ids=true | all-gather | bytes 327680 | tf_op jit(solution)/shard_map/all_gather | solution.py:254
  95.4 0.0 copy-done
  95.4 0.0 copy-done.1
  95.4 1.8 %heads_back.1 = (bf16[128,1536]{1,0:T(8,128)(2,1)}, bf16[128,1536]{1,0:T(8,128)(2,1)}) custom-call(bf16[4,64,512]{2,1,0:T(8,128)(2,1)S(1)} %bitcast.11, bf16[1536,512]{1,0:T(8,128)(2,1)S(1)} %copy-done, bf16[1536,512]{1,0:T(8,128)(2,1)S(1)} %copy-done.1), custom_call_target="tpu_custom_call" | custom-call | tf_op jit(solution)/shard_map/heads_back/pallas_call | solution.py:222
Async XLA Ops:
  19.9 36.5 %all-to-all-start = ((bf16[16,64,512]{2,1,0:T(8,128)(2,1)}), bf16[16,64,512]{2,1,0:T(8,128)(2,1)S(1)}, u32[]{:S(2)}, u32[]{:S(2)}) async-start(bf16[16,64,512]{2,1,0:T(8,128)(2,1)} %get-tuple-element.13), calls=%async_computation | async-start | bytes 2097152 | tf_op jit(solution)/shard_map/all_to_all | solution.py:244
  46.1 11.4 %collective-permute-start.2 = (bf16[256,512]{1,0:T(8,128)(2,1)S(1)}, bf16[256,512]{1,0:T(8,128)(2,1)S(1)}, u32[]{:S(2)}, u32[]{:S(2)}) collective-permute-start(bf16[256,512]{1,0:T(8,128)(2,1)S(1)} %all_gather.25.rest_0_), channel_id=1, source_target_pairs={{32,0},{34,2},{36,4},{38,6},{40,8},{42,10},{44,12},{46,14},{288,25... | collective-permute-start | bytes 786440 | tf_op jit(solution)/shard_map/ppermute | solution.py:247
  49.2 12.5 %collective-permute-start = (bf16[256,512]{1,0:T(8,128)(2,1)S(1)}, bf16[256,512]{1,0:T(8,128)(2,1)S(1)}, u32[]{:S(2)}, u32[]{:S(2)}) collective-permute-start(bf16[256,512]{1,0:T(8,128)(2,1)S(1)} %all_gather.25.rest_0_), channel_id=1, source_target_pairs={{16,0},{18,2},{20,4},{22,6},{24,8},{26,10},{28,12},{30,14},{272,25... | collective-permute-start | bytes 786440 | tf_op jit(solution)/shard_map/ppermute | solution.py:247
  53.2 8.5 %collective-permute-start.1 = (bf16[256,512]{1,0:T(8,128)(2,1)S(1)}, bf16[256,512]{1,0:T(8,128)(2,1)S(1)}, u32[]{:S(2)}, u32[]{:S(2)}) collective-permute-start(bf16[256,512]{1,0:T(8,128)(2,1)S(1)} %all_gather.25.rest_0_), channel_id=1, source_target_pairs={{240,0},{242,2},{244,4},{246,6},{248,8},{250,10},{252,12},{254,14}... | collective-permute-start | bytes 786440 | tf_op jit(solution)/shard_map/ppermute | solution.py:247
  63.4 32.0 %copy-start = (bf16[1536,512]{1,0:T(8,128)(2,1)S(1)}, bf16[1536,512]{1,0:T(8,128)(2,1)}, u32[]{:S(2)}) copy-start(bf16[1536,512]{1,0:T(8,128)(2,1)} %wv.3) | copy-start | bytes 4718596
  63.4 32.0 %copy-start.1 = (bf16[1536,512]{1,0:T(8,128)(2,1)S(1)}, bf16[1536,512]{1,0:T(8,128)(2,1)}, u32[]{:S(2)}) copy-start(bf16[1536,512]{1,0:T(8,128)(2,1)} %ws.3) | copy-start | bytes 4718596
